TPU v7x, 128 devices: a whole 4x4x4 slice. The times are simulated.
128 devices in a mesh: ulysses: 8 (over z, core), ctx: 16 (over x, y).
Axes of the slice: x: 4, y: 4, z: 4, core: 2. Of those that a mesh axis runs over, the one named last changes fastest.
Arguments:
- queries: bfloat16 [8192, 4096], P(('ulysses', 'ctx')), may hold values from -160 to 160
- keys: bfloat16 [8192, 1024], P(('ulysses', 'ctx')), may hold values from -6 to 6
- values: bfloat16 [8192, 1024], P(('ulysses', 'ctx')), may hold values from -6 to 6
- attn_out: bfloat16 [8192, 4096], P(('ulysses', 'ctx')), may hold values from -4 to 4
- out_grad: bfloat16 [8192, 4096], P(('ulysses', 'ctx')), may hold values from -6 to 6
- segment: int32 [8192], replicated, may hold values from 0 to 2, as said below
- span_order: int32 [32], replicated, may hold values from 0 to 31, as said below
Outputs:
- query_grad: bfloat16 [8192, 4096], P(('ulysses', 'ctx'))
- key_grad: bfloat16 [8192, 1024], P(('ulysses', 'ctx'))
- value_grad: bfloat16 [8192, 1024], P(('ulysses', 'ctx'))
Inputs may be any that keep to these rules, and one draw needn't show every extreme that they name: `segment`: 0 marks the prompt, 1 the chosen response, 2 the rejected response; in order of position the prompt comes first, then the chosen, then the rejected response, each of them non-empty. `span_order`: a permutation of 0 to 31.
All inputs are finite; a program needn't handle non-finite values.
Results may differ from a plain program's by a relative error of at most 0.005.
Values may be sent and summed in bfloat16 or wider, within the bound.
No kernel may reach another device: no remote copies, remote signals or barrier semaphores. Data moves between devices by JAX's collectives and lax.ppermute only.
A program may use at most 64 MiB of HBM per device.

v0:
```python
import functools
import math

import jax
import jax.numpy as jnp
from jax import lax
from jax.experimental import pallas as pl
from jax.experimental.pallas import tpu as pltpu
from jax.sharding import Mesh, PartitionSpec as P

D = 128
G = 4
R = 64
SPAN = 256
NT = 32
HR = R // 2
QR = G * HR
C = 2 * QR
SCALE = D**-0.5
LOG2E = math.log2(math.e)
EXP_SCALE = SCALE * LOG2E
HIDDEN = -1e30
F32 = jnp.float32
BF16 = jnp.bfloat16
AXES = ("z", "core", "xh", "xl", "y")
HEADS = ("xh", "z")
SPREAD = ("xh", "xl", "z")
NT_DIMS = (((1,), (1,)), ((), ()))


def pack_kv_kernel(keys, values, out):
    for g in range(8):
        out[g, :R] = keys[:, g * D : (g + 1) * D]
        out[g, R:] = values[:, g * D : (g + 1) * D]


def pack_q_kernel(queries, saved, grads, out):
    ones = jnp.ones((8, D), BF16)
    row = lax.broadcasted_iota(jnp.int32, (16, D), 0)
    for g in range(8):
        for half in range(2):
            dest = (g // 4 * 2 + half) * 4 + g % 4
            rows = slice(half * HR, (half + 1) * HR)
            prods = []
            for h in range(G):
                cols = slice((g * G + h) * D, (g * G + h + 1) * D)
                grad = grads[rows, cols]
                out[dest, h * HR : (h + 1) * HR] = queries[rows, cols]
                out[dest, QR + h * HR : QR + (h + 1) * HR] = grad
                prods.append(grad.astype(F32) * saved[rows, cols].astype(F32))
            prod = jnp.concatenate(prods, axis=0)
            high = prod.astype(BF16)
            low = (prod - high.astype(F32)).astype(BF16)
            dot = lax.dot_general(ones, high, NT_DIMS, preferred_element_type=F32)
            dot = dot + lax.dot_general(ones, low, NT_DIMS, preferred_element_type=F32)
            both = jnp.concatenate([dot, dot], axis=0)
            rounded = both.astype(BF16).astype(F32)
            out[dest, 2 * QR :] = jnp.where(row == 0, rounded, both - rounded).astype(BF16)


def attention_kernel(meta, qpay, *refs):
    pieces = refs[:10]
    dq_out, mine_0, mine_p, mine_m, mine_2, other_0, other_p, other_m, other_2 = refs[10:19]
    q_s, do_s, d_s, k_s, v_s, kt_s, stash, m_blk, m_run, l_run, dk_s, dv_s, dq_s, sem = refs[19:]
    n0 = meta[64]
    n1 = meta[65]
    xl = meta[66]
    y = meta[67]
    core = meta[68]

    copies = []
    for s in range(16):
        for part, dst in ((0, q_s), (1, do_s)):
            copies.append(
                pltpu.make_async_copy(
                    qpay.at[s, pl.ds(part * QR, QR)], dst.at[s // 2, pl.ds((s % 2) * QR, QR)], sem
                )
            )
    copies.append(pltpu.make_async_copy(qpay.at[:, pl.ds(2 * QR, 16)], d_s, sem))
    for number, piece in enumerate(pieces):
        which = number % 5
        from_core = core if number < 5 else 1 - core
        dy = (0, 3, 1, 2, 2)[which]
        flips = ((0, 1), (0, 1), (0, 1), (0,), (1,))[which]
        for place, flip in enumerate(flips):
            slot = jnp.where(xl == flip, 0, 1) * 4 + (y + dy) % 4
            source = piece.at[place] if len(flips) > 1 else piece
            copies.append(
                pltpu.make_async_copy(source.at[:, pl.ds(0, R)], k_s.at[slot, :, from_core], sem)
            )
            copies.append(
                pltpu.make_async_copy(source.at[:, pl.ds(R, R)], v_s.at[slot, :, from_core], sem)
            )
    for copy in copies:
        copy.start()
    dk_s[...] = jnp.zeros_like(dk_s)
    dv_s[...] = jnp.zeros_like(dv_s)
    for copy in copies:
        copy.wait()

    def tile_of(ref, tile):
        return ref[tile // 4, pl.ds((tile % 4) * 2, 2)].reshape(SPAN, D)

    def add_to(ref, tile, term):
        place = (tile // 4, pl.ds((tile % 4) * 2, 2))
        ref[place] += term.reshape(2, 2, R, D)

    def turn(tile, carry):
        kt_s[tile] = tile_of(k_s, tile).T
        return carry

    lax.fori_loop(0, NT, turn, 0)

    def chunk_step(c, unused):
        tile_q = (((c // 2) % 2 * 4 + y) * 2 + c // 4) * 2 + c % 2
        span_q = meta[tile_q]
        first = span_q * SPAN
        has_second = first + (SPAN - 1) >= n1
        all_second = first >= n1
        lo = jnp.where(has_second, n0 // SPAN, 0)
        hi = jnp.where(has_second, (n1 + (SPAN - 1)) // SPAN, 0)
        hi = jnp.minimum(hi, span_q)
        lo = jnp.minimum(lo, hi)
        skip_at = (n0 + (SPAN - 1)) // SPAN
        skip_to = n1 // SPAN
        skip = jnp.where(all_second, jnp.maximum(skip_to - skip_at, 0), 0)
        n_masked = hi - lo - skip
        n_plain = span_q - (hi - lo)
        count = 1 + n_masked + n_plain

        def masked_at(i):
            at = lo + i
            return jnp.where(at >= skip_at, at + skip, at)

        def plain_at(i):
            return jnp.where(i < lo, i, i + (hi - lo))

        def place_at(i):
            at = jnp.where(i < n_plain, plain_at(i), masked_at(i - n_plain))
            return jnp.where(i == count - 1, span_q, at)

        q = q_s[c]
        grads = do_s[c]

        def scores_of(at):
            tile = meta[32 + at]
            scores = lax.dot_general(tile_of(k_s, tile), q, NT_DIMS, preferred_element_type=F32)
            return scores * EXP_SCALE

        def seen_at(at):
            lane = lax.broadcasted_iota(jnp.int32, (1, C), 1)
            query_pos = first + core * R + xl * HR + (lane // QR) * (2 * R) + lane % HR
            key_pos = at * SPAN + lax.broadcasted_iota(jnp.int32, (SPAN, 1), 0)
            low = jnp.where(query_pos >= n1, n0, n1)
            return (key_pos <= query_pos) & ((key_pos < low) | (key_pos >= n1))

        def add_up(weights):
            return jnp.sum(weights.reshape(SPAN // 8, 8, C), axis=0)

        def weigh(at, masked):
            top = m_run[...]
            scores = scores_of(at)
            if masked:
                scores = jnp.where(seen_at(at), scores, HIDDEN)
            weights = jnp.exp2(scores - top)
            l_run[...] += add_up(weights)
            m_blk[at] = top
            stash[at] = weights

        def weigh_diagonal():
            scores = jnp.where(seen_at(span_q), scores_of(span_q), HIDDEN)
            top = jnp.max(scores, axis=0, keepdims=True)
            weights = jnp.exp2(scores - top)
            l_run[...] = add_up(weights)
            m_run[...] = top
            m_blk[span_q] = top
            stash[span_q] = weights

        def masked_step(i, carry):
            weigh(masked_at(i), True)
            return carry

        def plain_pair(i, carry):
            weigh(plain_at(2 * i), False)
            weigh(plain_at(2 * i + 1), False)
            return carry

        weigh_diagonal()
        lax.fori_loop(0, n_masked, masked_step, 0)
        lax.fori_loop(0, n_plain // 2, plain_pair, 0)

        @pl.when(n_plain % 2 == 1)
        def _():
            weigh(plain_at(n_plain - 1), False)

        @pl.when(jnp.logical_not(jnp.max(l_run[...]) < 2.0**90))
        def _():
            m_run[...] = jnp.full_like(m_run, HIDDEN)
            l_run[...] = jnp.zeros_like(l_run)

            def careful_step(i, carry):
                at = place_at(count - 1 - i)
                scores = jnp.where(seen_at(at), scores_of(at), HIDDEN)
                old = m_run[...]
                top = jnp.maximum(old, jnp.max(scores, axis=0, keepdims=True))
                weights = jnp.exp2(scores - top)
                l_run[...] = l_run[...] * jnp.exp2(old - top) + add_up(weights)
                m_run[...] = top
                m_blk[at] = top
                stash[at] = weights
                return carry

            lax.fori_loop(0, count, careful_step, 0)

        logsum = m_run[...] + jnp.log2(jnp.sum(l_run[...], axis=0, keepdims=True))
        dots = []
        for half in range(2):
            block = d_s[2 * c + half].astype(F32)
            dots.append(block[0:1] + block[1:2])
        row_dot = jnp.concatenate(dots, axis=1)
        dq_s[...] = jnp.zeros_like(dq_s)

        def grad_tile(at):
            tile = meta[32 + at]
            weights = stash[at] * jnp.exp2(m_blk[at] - logsum)
            prob_grad = lax.dot_general(
                tile_of(v_s, tile), grads, NT_DIMS, preferred_element_type=F32
            )
            score_grad = (weights * (prob_grad - row_dot)).astype(BF16)
            add_to(dv_s, tile, jnp.dot(weights.astype(BF16), grads, preferred_element_type=F32))
            add_to(dk_s, tile, jnp.dot(score_grad, q, preferred_element_type=F32))
            return jnp.dot(kt_s[tile], score_grad, preferred_element_type=F32)

        def grad_pair(i, carry):
            first_term = grad_tile(place_at(2 * i))
            second_term = grad_tile(place_at(2 * i + 1))
            dq_s[...] += first_term + second_term
            return carry

        lax.fori_loop(0, count // 2, grad_pair, 0)

        @pl.when(count % 2 == 1)
        def _():
            dq_s[...] += grad_tile(span_q)

        dq = (dq_s[...] * SCALE).T.astype(BF16)
        dq_out[2 * c] = dq[:QR]
        dq_out[2 * c + 1] = dq[QR:]
        return unused

    lax.fori_loop(0, 8, chunk_step, 0)

    for from_core, outs in (
        (core, (mine_0, mine_p, mine_m, mine_2)),
        (1 - core, (other_0, other_p, other_m, other_2)),
    ):
        for dy, out in zip((0, 1, 3, 2), outs):
            for flip in range(2):
                slot = jnp.where(xl == flip, 0, 1) * 4 + (y + dy) % 4
                out[flip, :, :R] = (dk_s[slot, :, from_core] * SCALE).astype(BF16)
                out[flip, :, R:] = dv_s[slot, :, from_core].astype(BF16)


def last_sum_kernel(mine, got, behind, ahead, dq, keep, send, out):
    for flip, total in enumerate((keep, send)):
        parts = [ref[flip].astype(F32) for ref in (mine, got, behind, ahead)]
        total[...] = ((parts[0] + parts[1]) + (parts[2] + parts[3])).astype(total.dtype)
    for g in range(8):
        for half in range(2):
            dest = (g // 4 * 2 + half) * 4 + g % 4
            for h in range(G):
                cols = slice((g * G + h) * D, (g * G + h + 1) * D)
                out[half * HR : (half + 1) * HR, cols] = dq[dest, h * HR : (h + 1) * HR]


def unpack_kv_kernel(got, key_grad, value_grad):
    for g in range(8):
        key_grad[:, g * D : (g + 1) * D] = got[g, :R]
        value_grad[:, g * D : (g + 1) * D] = got[g, R:]


def on_vmem(kernel, outs, *args):
    return pl.pallas_call(
        kernel,
        out_shape=outs,
        compiler_params=pltpu.CompilerParams(vmem_limit_bytes=16 << 20),
    )(*args)


def exchange(array, axes):
    return lax.all_to_all(array, axes, split_axis=0, concat_axis=0, tiled=True)


def shift(array, by):
    return lax.ppermute(array, "y", [(i, (i + by) % 4) for i in range(4)])


def flip(array, axis):
    return lax.ppermute(array, axis, [(0, 1), (1, 0)])


def gather_kv(own):
    both = jnp.stack([own, flip(own, "xl")])
    behind = shift(both, 1)
    ahead = shift(both, -1)
    far_same = shift(behind[0], 1)
    far_flip = shift(ahead[1], -1)
    mine = (both, behind, ahead, far_same, far_flip)
    return mine + tuple(flip(array, "core") for array in mine)


def add(*terms):
    total = terms[0].astype(F32)
    for term in terms[1:]:
        total = total + term.astype(F32)
    return total


def reduce_kv(mine, other, dq):
    got_0, got_p, got_m, got_2 = [flip(array, "core") for array in other]
    mine_0, mine_p, mine_m, mine_2 = mine
    far = add(mine_2, got_2).astype(BF16)
    from_behind = shift(far[0], 1)
    from_ahead = shift(far[1], -1)
    to_ahead = jnp.stack([add(mine_p[0], got_p[0], from_behind), add(mine_p[1], got_p[1])])
    to_behind = jnp.stack([add(mine_m[0], got_m[0]), add(mine_m[1], got_m[1], from_ahead)])
    near_behind = shift(to_ahead.astype(BF16), 1)
    near_ahead = shift(to_behind.astype(BF16), -1)
    piece = (8, 2 * R, D)
    keep, send, query_grad = on_vmem(
        last_sum_kernel,
        [
            jax.ShapeDtypeStruct(piece, F32),
            jax.ShapeDtypeStruct(piece, BF16),
            jax.ShapeDtypeStruct((R, 8 * G * D), BF16),
        ],
        mine_0,
        got_0,
        near_behind,
        near_ahead,
        dq,
    )
    return add(keep, flip(send, "xl")).astype(BF16), query_grad


def body(queries, keys, values, attn_out, out_grad, segment, span_order):
    kv_own = exchange(
        on_vmem(pack_kv_kernel, jax.ShapeDtypeStruct((8, 2 * R, D), BF16), keys, values), HEADS
    )
    q_own = exchange(
        on_vmem(
            pack_q_kernel,
            jax.ShapeDtypeStruct((16, 2 * QR + 16, D), BF16),
            queries,
            attn_out,
            out_grad,
        ),
        SPREAD,
    )
    span_of_tile = span_order.reshape(2, 2, 4, 2).transpose(1, 2, 0, 3).reshape(NT)
    number = jnp.arange(NT, dtype=jnp.int32)
    tile_of_span = jnp.sum(
        jnp.where(span_of_tile[None, :] == number[:, None], number[None, :], 0), axis=1
    ).astype(jnp.int32)
    n0 = jnp.sum((segment == 0).astype(jnp.int32))
    n1 = jnp.sum((segment != 2).astype(jnp.int32))
    scalars = jnp.stack(
        [n0, n1, lax.axis_index("xl"), lax.axis_index("y"), lax.axis_index("core")]
    ).astype(jnp.int32)
    meta = jnp.concatenate([span_of_tile, tile_of_span, scalars])

    pieces = gather_kv(kv_own)
    group = jax.ShapeDtypeStruct((2, 8, 2 * R, D), BF16)
    outs = pl.pallas_call(
        attention_kernel,
        out_shape=[jax.ShapeDtypeStruct((16, QR, D), BF16)] + [group] * 8,
        in_specs=[pl.BlockSpec(memory_space=pltpu.SMEM)] + [pl.BlockSpec(memory_space=pl.ANY)] * 11,
        scratch_shapes=[
            pltpu.VMEM((8, C, D), BF16),
            pltpu.VMEM((8, C, D), BF16),
            pltpu.VMEM((16, 16, D), BF16),
            pltpu.VMEM((8, 8, 2, R, D), BF16),
            pltpu.VMEM((8, 8, 2, R, D), BF16),
            pltpu.VMEM((NT, D, SPAN), BF16),
            pltpu.VMEM((NT, SPAN, C), F32),
            pltpu.VMEM((NT, 1, C), F32),
            pltpu.VMEM((1, C), F32),
            pltpu.VMEM((8, C), F32),
            pltpu.VMEM((8, 8, 2, R, D), F32),
            pltpu.VMEM((8, 8, 2, R, D), F32),
            pltpu.VMEM((D, C), F32),
            pltpu.SemaphoreType.DMA,
        ],
        compiler_params=pltpu.CompilerParams(vmem_limit_bytes=48 << 20),
    )(meta, q_own, *pieces)
    dkv, query_grad = reduce_kv(outs[1:5], outs[5:9], exchange(outs[0], SPREAD))
    key_grad, value_grad = on_vmem(
        unpack_kv_kernel, [jax.ShapeDtypeStruct((R, 8 * D), BF16)] * 2, exchange(dkv, HEADS)
    )
    return query_grad, key_grad, value_grad


def solution(mesh):
    fine = Mesh(mesh.devices.reshape(4, 2, 2, 2, 4), AXES)
    rows = P(AXES, None)
    return jax.shard_map(
        body,
        mesh=fine,
        in_specs=(rows,) * 5 + (P(), P()),
        out_specs=(rows,) * 3,
        check_vma=False,
    )
```

profile of v0, /device:TPU:0, one launch (start us, length us, event | category | flops | bytes accessed | tf_op | source)
XLA Modules:
  0.0 162.8 jit_solution(2578796950353836271)
XLA Ops:
  0.7 1.0 copy-done.3
  1.7 0.9 copy-done.4
  2.6 16.4 %all_to_all.20 = bf16[8,128,128]{2,1,0:T(8,128)(2,1)S(1)} all-to-all(bf16[8,128,128]{2,1,0:T(8,128)(2,1)S(1)} %shard_map.95), channel_id=1, replica_groups=mesh['z'=4,'core'=2,'xh'=2,'xl'=2,'y'=4] {'xh','z'}, dimensions={0} | all-to-all | bytes 524288 | tf_op jit(solution)/shard_map/all_to_all | solution.py:291
  19.0 0.6 collective-permute-start
  19.6 6.0 %collective-permute-done = bf16[8,128,128]{2,1,0:T(8,128)(2,1)S(1)} collective-permute-done((bf16[8,128,128]{2,1,0:T(8,128)(2,1)S(1)}, bf16[8,128,128]{2,1,0:T(8,128)(2,1)S(1)}, u32[]{:S(2)}, u32[]{:S(2)}) %collective-permute-start) | collective-permute-done | bytes 262176 | tf_op jit(solution)/shard_map/ppermute | solution.py:299
  25.6 0.1 pad_maximum_fusion.refs_0_
  25.7 3.1 %collective-permute-start.2 = (bf16[2,8,128,128]{3,2,1,0:T(8,128)(2,1)S(1)}, bf16[2,8,128,128]{3,2,1,0:T(8,128)(2,1)S(1)}, u32[]{:S(2)}, u32[]{:S(2)}) collective-permute-start(bf16[2,8,128,128]{3,2,1,0:T(8,128)(2,1)S(1)} %pad_maximum_fusion.refs_0_), channel_id=1, source_target_pairs={{0,3},{1,0},{2,1},{3,2},{4,7},{5,4},{6,5},{7,6},{8,11},{9,8},{10,9... | collective-permute-start | bytes 1572872 | tf_op jit(solution)/shard_map/ppermute | solution.py:295
  28.8 1.7 %shard_map.94 = bf16[16,272,128]{2,1,0:T(8,128)(2,1)} custom-call(bf16[64,4096]{1,0:T(8,128)(2,1)S(1)} %copy-done, bf16[64,4096]{1,0:T(8,128)(2,1)S(1)} %copy-done.1, bf16[64,4096]{1,0:T(8,128)(2,1)S(1)} %copy-done.2), custom_call_target="tpu_custom_call" | custom-call | tf_op jit(solution)/shard_map/pallas_call | solution.py:283
  30.5 3.8 %all-to-all-start = ((bf16[16,272,128]{2,1,0:T(8,128)(2,1)}), bf16[16,272,128]{2,1,0:T(8,128)(2,1)S(1)}, u32[]{:S(2)}, u32[]{:S(2)}) async-start(bf16[16,272,128]{2,1,0:T(8,128)(2,1)} %shard_map.94), calls=%async_computation | async-start | bytes 2228224 | tf_op jit(solution)/shard_map/all_to_all | solution.py:291
  34.3 0.1 collective-permute-start.5
  34.4 3.2 %collective-permute-done.2.refs_2_ = bf16[2,8,128,128]{3,2,1,0:T(8,128)(2,1)S(1)} collective-permute-done((bf16[2,8,128,128]{3,2,1,0:T(8,128)(2,1)S(1)}, bf16[2,8,128,128]{3,2,1,0:T(8,128)(2,1)S(1)}, u32[]{:S(2)}, u32[]{:S(2)}) %collective-permute-start.2) | collective-permute-done | bytes 524320 | tf_op jit(solution)/shard_map/ppermute | solution.py:295
  37.6 3.8 %collective-permute-start.4 = (bf16[8,128,128]{2,1,0:T(8,128)(2,1)S(1)}, bf16[8,128,128]{2,1,0:T(8,128)(2,1)S(1)}, u32[]{:S(2)}, u32[]{:S(2)}) collective-permute-start(bf16[8,128,128]{2,1,0:T(8,128)(2,1)S(1)} %slice_bitcast_fusion.2), channel_id=1, source_target_pairs={{0,3},{1,0},{2,1},{3,2},{4,7},{5,4},{6,5},{7,6},{8,11},{9,8},{10,9... | collective-permute-start | bytes 786440 | tf_op jit(solution)/shard_map/ppermute | solution.py:295
  41.4 1.0 slice_bitcast_fusion.3
  42.4 0.1 collective-permute-start.3
  42.5 0.1 collective-permute-start.7
  42.6 0.5 collective-permute-start.6
  43.0 2.2 %collective-permute-done.4.refs_4_ = bf16[8,128,128]{2,1,0:T(8,128)(2,1)S(1)} collective-permute-done((bf16[8,128,128]{2,1,0:T(8,128)(2,1)S(1)}, bf16[8,128,128]{2,1,0:T(8,128)(2,1)S(1)}, u32[]{:S(2)}, u32[]{:S(2)}) %collective-permute-start.4) | collective-permute-done | bytes 262176 | tf_op jit(solution)/shard_map/ppermute | solution.py:295
  45.3 4.7 %collective-permute-done.3.refs_3_ = bf16[8,128,128]{2,1,0:T(8,128)(2,1)S(1)} collective-permute-done((bf16[8,128,128]{2,1,0:T(8,128)(2,1)S(1)}, bf16[8,128,128]{2,1,0:T(8,128)(2,1)S(1)}, u32[]{:S(2)}, u32[]{:S(2)}) %collective-permute-start.3) | collective-permute-done | bytes 262176 | tf_op jit(solution)/shard_map/ppermute | solution.py:295
  50.0 0.1 reshape.19
  50.1 0.1 reshape.20
  50.2 0.1 select_reduce_fusion
  50.4 0.6 convert_reduce_fusion
  51.0 1.4 concatenate.3.meta
  52.5 1.0 copy-done.5
  53.4 57.3 %shard_map.96 = (bf16[16,128,128]{2,1,0:T(8,128)(2,1)S(1)}, bf16[2,8,128,128]{3,2,1,0:T(8,128)(2,1)S(1)}, bf16[2,8,128,128]{3,2,1,0:T(8,128)(2,1)S(1)}, bf16[2,8...) custom-call(s32[69]{0:T(128)S(1)} %concatenate.3.meta, ...), custom_call_target="tpu_custom_call" | custom-call | tf_op jit(solution)/shard_map/pallas_call | solution.py:374
  110.8 0.6 collective-permute-start.12
  111.3 0.1 collective-permute-start.11
  111.4 0.4 collective-permute-start.10
  111.9 0.1 collective-permute-start.15
  111.9 0.9 collective-permute-done.12
  112.9 0.1 add_convert_fusion
  113.1 0.1 collective-permute-start.16
  113.2 2.0 %collective-permute-start.13 = (bf16[8,128,128]{2,1,0:T(8,128)(2,1)S(1)}, bf16[8,128,128]{2,1,0:T(8,128)(2,1)S(1)}, u32[]{:S(2)}, u32[]{:S(2)}) collective-permute-start(bf16[8,128,128]{2,1,0:T(8,128)(2,1)S(1)} %get-tuple-element.34), channel_id=1, source_target_pairs={{0,1},{1,2},{2,3},{3,0},{4,5},{5,6},{6,7},{7,4},{8,9},{9,10},{10,1... | collective-permute-start | bytes 786440 | tf_op jit(solution)/shard_map/ppermute | solution.py:295
  115.2 0.1 add_convert_fusion.3
  115.3 0.1 add_convert_fusion.2
  115.4 7.7 %collective-permute-done.13 = bf16[8,128,128]{2,1,0:T(8,128)(2,1)S(1)} collective-permute-done((bf16[8,128,128]{2,1,0:T(8,128)(2,1)S(1)}, bf16[8,128,128]{2,1,0:T(8,128)(2,1)S(1)}, u32[]{:S(2)}, u32[]{:S(2)}) %collective-permute-start.13) | collective-permute-done | bytes 262176 | tf_op jit(solution)/shard_map/ppermute | solution.py:295
  123.0 0.1 fusion.2
  123.1 0.1 pad_maximum_fusion.1
  123.2 0.5 collective-permute-start.14
  123.7 0.1 fusion.3
  123.8 0.1 pad_maximum_fusion.2
  123.9 2.9 %collective-permute-start.17 = (bf16[2,8,128,128]{3,2,1,0:T(8,128)(2,1)S(1)}, bf16[2,8,128,128]{3,2,1,0:T(8,128)(2,1)S(1)}, u32[]{:S(2)}, u32[]{:S(2)}) collective-permute-start(bf16[2,8,128,128]{3,2,1,0:T(8,128)(2,1)S(1)} %pad_maximum_fusion.2), channel_id=1, source_target_pairs={{0,3},{1,0},{2,1},{3,2},{4,7},{5,4},{6,5},{7,6},{8,11},{9,8},{10,9... | collective-permute-start | bytes 1572872 | tf_op jit(solution)/shard_map/ppermute | solution.py:295
  126.7 16.0 %all_to_all.21.dq = bf16[16,128,128]{2,1,0:T(8,128)(2,1)S(1)} all-to-all(bf16[16,128,128]{2,1,0:T(8,128)(2,1)S(1)} %get-tuple-element.25), channel_id=1, replica_groups=mesh['z'=4,'core'=2,'xh'=2,'xl'=2,'y'=4] {'xh','xl','z'}, dimensions={0} | all-to-all | bytes 1048576 | tf_op jit(solution)/shard_map/all_to_all | solution.py:291
  142.8 1.0 shard_map.97
  143.8 6.4 %collective-permute-done.18 = bf16[8,128,128]{2,1,0:T(8,128)(2,1)S(1)} collective-permute-done((bf16[8,128,128]{2,1,0:T(8,128)(2,1)S(1)}, bf16[8,128,128]{2,1,0:T(8,128)(2,1)S(1)}, u32[]{:S(2)}, u32[]{:S(2)}) %collective-permute-start.18) | collective-permute-done | bytes 262176 | tf_op jit(solution)/shard_map/ppermute | solution.py:299
  150.1 0.1 add_convert_fusion.1
  150.2 11.9 %all_to_all.22.got = bf16[8,128,128]{2,1,0:T(8,128)(2,1)S(1)} all-to-all(bf16[8,128,128]{2,1,0:T(8,128)(2,1)S(1)} %add_convert_fusion.1), channel_id=1, replica_groups=mesh['z'=4,'core'=2,'xh'=2,'xl'=2,'y'=4] {'xh','z'}, dimensions={0} | all-to-all | bytes 524288 | tf_op jit(solution)/shard_map/all_to_all | solution.py:291
  162.1 0.8 shard_map.98
  (38 shorter events, 0.2 us)
Async XLA Ops:
  0.6 28.2 %copy-start.2 = (bf16[64,4096]{1,0:T(8,128)(2,1)S(1)}, bf16[64,4096]{1,0:T(8,128)(2,1)}, u32[]{:S(2)}) copy-start(bf16[64,4096]{1,0:T(8,128)(2,1)} %grads.1) | copy-start | bytes 1572868
  0.6 28.2 %copy-start.1 = (bf16[64,4096]{1,0:T(8,128)(2,1)S(1)}, bf16[64,4096]{1,0:T(8,128)(2,1)}, u32[]{:S(2)}) copy-start(bf16[64,4096]{1,0:T(8,128)(2,1)} %saved.1) | copy-start | bytes 1572868
  0.7 28.1 %copy-start = (bf16[64,4096]{1,0:T(8,128)(2,1)S(1)}, bf16[64,4096]{1,0:T(8,128)(2,1)}, u32[]{:S(2)}) copy-start(bf16[64,4096]{1,0:T(8,128)(2,1)} %queries.1) | copy-start | bytes 1572868
  0.7 1.0 copy-start.3
  1.7 0.9 copy-start.4
  19.0 6.6 %collective-permute-start = (bf16[8,128,128]{2,1,0:T(8,128)(2,1)S(1)}, bf16[8,128,128]{2,1,0:T(8,128)(2,1)S(1)}, u32[]{:S(2)}, u32[]{:S(2)}) collective-permute-start(bf16[8,128,128]{2,1,0:T(8,128)(2,1)S(1)} %all_to_all.20), channel_id=1, source_target_pairs={{0,4},{4,0},{1,5},{5,1},{2,6},{6,2},{3,7},{7,3},{8,12},{12,8},{9,1... | collective-permute-start | bytes 786440 | tf_op jit(solution)/shard_map/ppermute | solution.py:299
  25.7 8.6 %copy-start.6 = (bf16[2,8,128,128]{3,2,1,0:T(8,128)(2,1)}, bf16[2,8,128,128]{3,2,1,0:T(8,128)(2,1)S(1)}, u32[]{:S(2)}) copy-start(bf16[2,8,128,128]{3,2,1,0:T(8,128)(2,1)S(1)} %pad_maximum_fusion.refs_0_) | copy-start | bytes 1572868
  25.7 11.9 %collective-permute-start.2 = (bf16[2,8,128,128]{3,2,1,0:T(8,128)(2,1)S(1)}, bf16[2,8,128,128]{3,2,1,0:T(8,128)(2,1)S(1)}, u32[]{:S(2)}, u32[]{:S(2)}) collective-permute-start(bf16[2,8,128,128]{3,2,1,0:T(8,128)(2,1)S(1)} %pad_maximum_fusion.refs_0_), channel_id=1, source_target_pairs={{0,3},{1,0},{2,1},{3,2},{4,7},{5,4},{6,5},{7,6},{8,11},{9,8},{10,9... | collective-permute-start | bytes 1572872 | tf_op jit(solution)/shard_map/ppermute | solution.py:295
  28.8 12.6 %collective-permute-start.1 = (bf16[2,8,128,128]{3,2,1,0:T(8,128)(2,1)S(1)}, bf16[2,8,128,128]{3,2,1,0:T(8,128)(2,1)}, u32[]{:S(2)}, u32[]{:S(2)}) collective-permute-start(bf16[2,8,128,128]{3,2,1,0:T(8,128)(2,1)S(1)} %pad_maximum_fusion.refs_0_), channel_id=1, source_target_pairs={{0,1},{1,2},{2,3},{3,0},{4,5},{5,6},{6,7},{7,4},{8,9},{9,10},{10,1... | collective-permute-start | bytes 1572872 | tf_op jit(solution)/shard_map/ppermute | solution.py:295
  30.5 19.5 %copy-start.9 = (s32[32]{0:T(128)S(1)}, s32[32]{0:T(128)}, u32[]{:S(2)}) copy-start(s32[32]{0:T(128)} %param.13) | copy-start | bytes 388
  30.5 19.9 %copy-start.8 = (s32[8192]{0:T(1024)S(1)}, s32[8192]{0:T(1024)}, u32[]{:S(2)}) copy-start(s32[8192]{0:T(1024)} %param.12) | copy-start | bytes 98308
  30.5 21.9 %all-to-all-start = ((bf16[16,272,128]{2,1,0:T(8,128)(2,1)}), bf16[16,272,128]{2,1,0:T(8,128)(2,1)S(1)}, u32[]{:S(2)}, u32[]{:S(2)}) async-start(bf16[16,272,128]{2,1,0:T(8,128)(2,1)} %shard_map.94), calls=%async_computation | async-start | bytes 2228224 | tf_op jit(solution)/shard_map/all_to_all | solution.py:291
  34.3 18.0 %collective-permute-start.5 = (bf16[2,8,128,128]{3,2,1,0:T(8,128)(2,1)S(1)}, bf16[2,8,128,128]{3,2,1,0:T(8,128)(2,1)}, u32[]{:S(2)}, u32[]{:S(2)}) collective-permute-start(bf16[2,8,128,128]{3,2,1,0:T(8,128)(2,1)S(1)} %pad_maximum_fusion.refs_0_), channel_id=1, source_target_pairs={{0,16},{16,0},{1,17},{17,1},{2,18},{18,2},{3,19},{19,3},{4,20},{20... | collective-permute-start | bytes 1572872 | tf_op jit(solution)/shard_map/ppermute | solution.py:299
  37.6 14.8 %copy-start.7 = (bf16[2,8,128,128]{3,2,1,0:T(8,128)(2,1)}, bf16[2,8,128,128]{3,2,1,0:T(8,128)(2,1)S(1)}, u32[]{:S(2)}) copy-start(bf16[2,8,128,128]{3,2,1,0:T(8,128)(2,1)S(1)} %collective-permute-done.2.refs_2_) | copy-start | bytes 1572868
  37.6 7.7 %collective-permute-start.4 = (bf16[8,128,128]{2,1,0:T(8,128)(2,1)S(1)}, bf16[8,128,128]{2,1,0:T(8,128)(2,1)S(1)}, u32[]{:S(2)}, u32[]{:S(2)}) collective-permute-start(bf16[8,128,128]{2,1,0:T(8,128)(2,1)S(1)} %slice_bitcast_fusion.2), channel_id=1, source_target_pairs={{0,3},{1,0},{2,1},{3,2},{4,7},{5,4},{6,5},{7,6},{8,11},{9,8},{10,9... | collective-permute-start | bytes 786440 | tf_op jit(solution)/shard_map/ppermute | solution.py:295
  42.4 7.7 %collective-permute-start.3 = (bf16[8,128,128]{2,1,0:T(8,128)(2,1)S(1)}, bf16[8,128,128]{2,1,0:T(8,128)(2,1)S(1)}, u32[]{:S(2)}, u32[]{:S(2)}) collective-permute-start(bf16[8,128,128]{2,1,0:T(8,128)(2,1)S(1)} %slice_bitcast_fusion.3), channel_id=1, source_target_pairs={{0,1},{1,2},{2,3},{3,0},{4,5},{5,6},{6,7},{7,4},{8,9},{9,10},{10,1... | collective-permute-start | bytes 786440 | tf_op jit(solution)/shard_map/ppermute | solution.py:295
  42.5 10.0 %collective-permute-start.7 = (bf16[2,8,128,128]{3,2,1,0:T(8,128)(2,1)S(1)}, bf16[2,8,128,128]{3,2,1,0:T(8,128)(2,1)}, u32[]{:S(2)}, u32[]{:S(2)}) collective-permute-start(bf16[2,8,128,128]{3,2,1,0:T(8,128)(2,1)S(1)} %collective-permute-done.2.refs_2_), channel_id=1, source_target_pairs={{0,16},{16,0},{1,17},{17,1},{2,18},{18,2},{3,19},{19,3},{4,20},{20... | collective-permute-start | bytes 1572872 | tf_op jit(solution)/shard_map/ppermute | solution.py:299
  42.6 9.9 %collective-permute-start.6 = (bf16[2,8,128,128]{3,2,1,0:T(8,128)(2,1)}, bf16[2,8,128,128]{3,2,1,0:T(8,128)(2,1)}, u32[]{:S(2)}, u32[]{:S(2)}) collective-permute-start(bf16[2,8,128,128]{3,2,1,0:T(8,128)(2,1)} %collective-permute-done.1.refs_1_), channel_id=1, source_target_pairs={{0,16},{16,0},{1,17},{17,1},{2,18},{18,2},{3,19},{19,3},{4,20},{20... | collective-permute-start | bytes 1572872 | tf_op jit(solution)/shard_map/ppermute | solution.py:299
  45.3 7.1 %collective-permute-start.9 = (bf16[8,128,128]{2,1,0:T(8,128)(2,1)S(1)}, bf16[8,128,128]{2,1,0:T(8,128)(2,1)S(1)}, u32[]{:S(2)}, u32[]{:S(2)}) collective-permute-start(bf16[8,128,128]{2,1,0:T(8,128)(2,1)S(1)} %collective-permute-done.4.refs_4_), channel_id=1, source_target_pairs={{0,16},{16,0},{1,17},{17,1},{2,18},{18,2},{3,19},{19,3},{4,20},{20... | collective-permute-start | bytes 786440 | tf_op jit(solution)/shard_map/ppermute | solution.py:299
  50.0 2.4 %collective-permute-start.8 = (bf16[8,128,128]{2,1,0:T(8,128)(2,1)S(1)}, bf16[8,128,128]{2,1,0:T(8,128)(2,1)S(1)}, u32[]{:S(2)}, u32[]{:S(2)}) collective-permute-start(bf16[8,128,128]{2,1,0:T(8,128)(2,1)S(1)} %collective-permute-done.3.refs_3_), channel_id=1, source_target_pairs={{0,16},{16,0},{1,17},{17,1},{2,18},{18,2},{3,19},{19,3},{4,20},{20... | collective-permute-start | bytes 786440 | tf_op jit(solution)/shard_map/ppermute | solution.py:299
  52.4 1.0 copy-start.5
  110.8 2.1 %collective-permute-start.12 = (bf16[2,8,128,128]{3,2,1,0:T(8,128)(2,1)S(1)}, bf16[2,8,128,128]{3,2,1,0:T(8,128)(2,1)S(1)}, u32[]{:S(2)}, u32[]{:S(2)}) collective-permute-start(bf16[2,8,128,128]{3,2,1,0:T(8,128)(2,1)S(1)} %get-tuple-element.22), channel_id=1, source_target_pairs={{0,16},{16,0},{1,17},{17,1},{2,18},{18,2},{3,19},{19,3},{4,20},{20... | collective-permute-start | bytes 1572872 | tf_op jit(solution)/shard_map/ppermute | solution.py:299
  111.3 3.8 %collective-permute-start.11 = (bf16[2,8,128,128]{3,2,1,0:T(8,128)(2,1)S(1)}, bf16[2,8,128,128]{3,2,1,0:T(8,128)(2,1)S(1)}, u32[]{:S(2)}, u32[]{:S(2)}) collective-permute-start(bf16[2,8,128,128]{3,2,1,0:T(8,128)(2,1)S(1)} %get-tuple-element.20), channel_id=1, source_target_pairs={{0,16},{16,0},{1,17},{17,1},{2,18},{18,2},{3,19},{19,3},{4,20},{20... | collective-permute-start | bytes 1572872 | tf_op jit(solution)/shard_map/ppermute | solution.py:299
  111.4 31.3 %collective-permute-start.10 = (bf16[2,8,128,128]{3,2,1,0:T(8,128)(2,1)S(1)}, bf16[2,8,128,128]{3,2,1,0:T(8,128)(2,1)S(1)}, u32[]{:S(2)}, u32[]{:S(2)}) collective-permute-start(bf16[2,8,128,128]{3,2,1,0:T(8,128)(2,1)S(1)} %get-tuple-element.18), channel_id=1, source_target_pairs={{0,16},{16,0},{1,17},{17,1},{2,18},{18,2},{3,19},{19,3},{4,20},{20... | collective-permute-start | bytes 1572872 | tf_op jit(solution)/shard_map/ppermute | solution.py:299
  111.9 3.4 %collective-permute-start.15 = (bf16[2,8,128,128]{3,2,1,0:T(8,128)(2,1)S(1)}, bf16[2,8,128,128]{3,2,1,0:T(8,128)(2,1)S(1)}, u32[]{:S(2)}, u32[]{:S(2)}) collective-permute-start(bf16[2,8,128,128]{3,2,1,0:T(8,128)(2,1)S(1)} %get-tuple-element.24), channel_id=1, source_target_pairs={{0,16},{16,0},{1,17},{17,1},{2,18},{18,2},{3,19},{19,3},{4,20},{20... | collective-permute-start | bytes 1572872 | tf_op jit(solution)/shard_map/ppermute | solution.py:299
  113.1 10.6 %collective-permute-start.16 = (bf16[8,128,128]{2,1,0:T(8,128)(2,1)S(1)}, bf16[8,128,128]{2,1,0:T(8,128)(2,1)S(1)}, u32[]{:S(2)}, u32[]{:S(2)}) collective-permute-start(bf16[8,128,128]{2,1,0:T(8,128)(2,1)S(1)} %get-tuple-element.33), channel_id=1, source_target_pairs={{0,3},{1,0},{2,1},{3,2},{4,7},{5,4},{6,5},{7,6},{8,11},{9,8},{10,9... | collective-permute-start | bytes 786440 | tf_op jit(solution)/shard_map/ppermute | solution.py:295
  113.2 9.9 %collective-permute-start.13 = (bf16[8,128,128]{2,1,0:T(8,128)(2,1)S(1)}, bf16[8,128,128]{2,1,0:T(8,128)(2,1)S(1)}, u32[]{:S(2)}, u32[]{:S(2)}) collective-permute-start(bf16[8,128,128]{2,1,0:T(8,128)(2,1)S(1)} %get-tuple-element.34), channel_id=1, source_target_pairs={{0,1},{1,2},{2,3},{3,0},{4,5},{5,6},{6,7},{7,4},{8,9},{9,10},{10,1... | collective-permute-start | bytes 786440 | tf_op jit(solution)/shard_map/ppermute | solution.py:295
  123.2 19.6 %collective-permute-start.14 = (bf16[2,8,128,128]{3,2,1,0:T(8,128)(2,1)S(1)}, bf16[2,8,128,128]{3,2,1,0:T(8,128)(2,1)S(1)}, u32[]{:S(2)}, u32[]{:S(2)}) collective-permute-start(bf16[2,8,128,128]{3,2,1,0:T(8,128)(2,1)S(1)} %pad_maximum_fusion.1), channel_id=1, source_target_pairs={{0,1},{1,2},{2,3},{3,0},{4,5},{5,6},{6,7},{7,4},{8,9},{9,10},{10,1... | collective-permute-start | bytes 1572872 | tf_op jit(solution)/shard_map/ppermute | solution.py:295
  123.9 18.9 %collective-permute-start.17 = (bf16[2,8,128,128]{3,2,1,0:T(8,128)(2,1)S(1)}, bf16[2,8,128,128]{3,2,1,0:T(8,128)(2,1)S(1)}, u32[]{:S(2)}, u32[]{:S(2)}) collective-permute-start(bf16[2,8,128,128]{3,2,1,0:T(8,128)(2,1)S(1)} %pad_maximum_fusion.2), channel_id=1, source_target_pairs={{0,3},{1,0},{2,1},{3,2},{4,7},{5,4},{6,5},{7,6},{8,11},{9,8},{10,9... | collective-permute-start | bytes 1572872 | tf_op jit(solution)/shard_map/ppermute | solution.py:295
  143.8 6.4 %collective-permute-start.18 = (bf16[8,128,128]{2,1,0:T(8,128)(2,1)S(1)}, bf16[8,128,128]{2,1,0:T(8,128)(2,1)S(1)}, u32[]{:S(2)}, u32[]{:S(2)}) collective-permute-start(bf16[8,128,128]{2,1,0:T(8,128)(2,1)S(1)} %get-tuple-element.28), channel_id=1, source_target_pairs={{0,4},{4,0},{1,5},{5,1},{2,6},{6,2},{3,7},{7,3},{8,12},{12,8},{9,1... | collective-permute-start | bytes 786440 | tf_op jit(solution)/shard_map/ppermute | solution.py:299
where the time goes:
time: 161 us; the launch traced here: 163 us
  Pallas kernels  60.9 us (38%)
  blocking collectives  44.3 us (28%)
  waiting for transfers between devices  31.2 us (19%)
  starting transfers between devices  18.7 us (12%)
  local copies, waits for them, and re-layouts  5.5 us (3%)
    pallas_call x1, Pallas kernels, body(): pl.pallas_call(attention_kernel, out_shape=[jax.ShapeDtypeStruct((16, QR,...  57.3 us
    all_to_all x3, blocking collectives, exchange(): return lax.all_to_all(array, axes, split_axis=0, concat_axis=0, tiled=True)  44.3 us
    ppermute x8, waiting for transfers between devices, shift(): return lax.ppermute(array, 'y', [(i, (i + by) % 4) for i in range(4)])  17.8 us
    ppermute x11, waiting for transfers between devices, flip(): return lax.ppermute(array, axis, [(0, 1), (1, 0)])  13.3 us
    ppermute x8, starting transfers between devices, shift(): return lax.ppermute(array, 'y', [(i, (i + by) % 4) for i in range(4)])  12.4 us
    all_to_all x1, starting transfers between devices, exchange(): return lax.all_to_all(array, axes, split_axis=0, concat_axis=0, tiled=True)  3.83 us
    pallas_call x4, Pallas kernels, on_vmem(): pl.pallas_call(kernel, out_shape=outs, compiler_params=pltpu.CompilerPara...  3.52 us
  transfers between devices with their start and end apart: 20, of which 7 were waited for; matrix products, arithmetic and copies ran while one was open for 2% of the time, Pallas kernels for 1%

commit v1 on v0

v1 whole, which is shorter than its diff:
```python
import functools
import math

import jax
import jax.numpy as jnp
from jax import lax
from jax.experimental import pallas as pl
from jax.experimental.pallas import tpu as pltpu
from jax.sharding import Mesh, PartitionSpec as P

D = 128
G = 4
R = 64
SPAN = 256
KB = 2 * SPAN
NT = 32
HR = R // 2
QR = G * HR
C = 2 * QR
SCALE = D**-0.5
LOG2E = math.log2(math.e)
EXP_SCALE = SCALE * LOG2E
HIDDEN = -1e30
F32 = jnp.float32
BF16 = jnp.bfloat16
AXES = ("z", "core", "xh", "xl", "y")
HEADS = ("xh", "z")
SPREAD = ("xh", "xl", "z")
NT_DIMS = (((1,), (1,)), ((), ()))


def pack_kv_kernel(keys, values, segment, out, counts):
    counts[0] = jnp.sum((segment[...] == 0).astype(jnp.int32))
    counts[1] = jnp.sum((segment[...] != 2).astype(jnp.int32))
    for g in range(8):
        out[g, :R] = keys[:, g * D : (g + 1) * D]
        out[g, R:] = values[:, g * D : (g + 1) * D]


def pack_q_kernel(queries, saved, grads, out):
    ones = jnp.ones((8, D), BF16)
    row = lax.broadcasted_iota(jnp.int32, (16, D), 0)
    for g in range(8):
        for half in range(2):
            dest = (g // 4 * 2 + half) * 4 + g % 4
            rows = slice(half * HR, (half + 1) * HR)
            prods = []
            for h in range(G):
                cols = slice((g * G + h) * D, (g * G + h + 1) * D)
                grad = grads[rows, cols]
                out[dest, h * HR : (h + 1) * HR] = queries[rows, cols]
                out[dest, QR + h * HR : QR + (h + 1) * HR] = grad
                prods.append(grad.astype(F32) * saved[rows, cols].astype(F32))
            prod = jnp.concatenate(prods, axis=0)
            high = prod.astype(BF16)
            low = (prod - high.astype(F32)).astype(BF16)
            dot = lax.dot_general(ones, high, NT_DIMS, preferred_element_type=F32)
            dot = dot + lax.dot_general(ones, low, NT_DIMS, preferred_element_type=F32)
            both = jnp.concatenate([dot, dot], axis=0)
            rounded = both.astype(BF16).astype(F32)
            out[dest, 2 * QR :] = jnp.where(row == 0, rounded, both - rounded).astype(BF16)


def span_id(xh, xl, y, zh):
    return ((xh * 2 + xl) * 4 + y) * 2 + zh


def attention_kernel(order, counts, qpay, *refs):
    pieces = refs[:10]
    dq_out, outs = refs[10], (refs[11:15], refs[15:19])
    (q_s, do_s, d_s, k_s, v_s, kt_s, stash, m_blk, m_run, l_run, dk_s, dv_s, dq_s, sem) = refs[19:]
    n0 = counts[0]
    n1 = counts[1]
    xl = lax.axis_index("xl")
    y = lax.axis_index("y")
    core = lax.axis_index("core")

    def place(flip, dy, j):
        return order[span_id(j // 2, xl ^ flip, y ^ dy, j % 2)]

    copies = []
    for s in range(16):
        for part, dst in ((0, q_s), (1, do_s)):
            copies.append(
                pltpu.make_async_copy(
                    qpay.at[s, pl.ds(part * QR, QR)], dst.at[s // 2, pl.ds((s % 2) * QR, QR)], sem
                )
            )
    copies.append(pltpu.make_async_copy(qpay.at[:, pl.ds(2 * QR, 16)], d_s, sem))
    for number, piece in enumerate(pieces):
        which = number % 5
        from_core = core if number < 5 else 1 - core
        dy = (0, 1, 3, 2, 2)[which]
        flips = ((0, 1), (0, 1), (0, 1), (0,), (1,))[which]
        for at, flip in enumerate(flips):
            source = piece.at[at] if len(flips) > 1 else piece
            for j in range(4):
                rank = place(flip, dy, j)
                rows = source.at[pl.ds(2 * j, 2)]
                copies.append(
                    pltpu.make_async_copy(rows.at[:, pl.ds(0, R)], k_s.at[rank, :, from_core], sem)
                )
                copies.append(
                    pltpu.make_async_copy(rows.at[:, pl.ds(R, R)], v_s.at[rank, :, from_core], sem)
                )
    for copy in copies:
        copy.start()
    dk_s[...] = jnp.zeros_like(dk_s)
    dv_s[...] = jnp.zeros_like(dv_s)
    for copy in copies:
        copy.wait()

    def block_of(ref, b):
        return ref[pl.ds(2 * b, 2)].reshape(KB, D)

    def turn(b, carry):
        kt_s[b] = block_of(k_s, b).T
        return carry

    lax.fori_loop(0, NT // 2, turn, 0)

    def chunk_step(c, unused):
        span_q = order[span_id(c // 4, c // 2 % 2, y, c % 2)]
        first = span_q * SPAN
        has_second = first + (SPAN - 1) >= n1
        all_second = first >= n1
        n_full = span_q // 2
        lo = jnp.where(has_second, n0 // KB, 0)
        hi = jnp.where(has_second, (n1 + (KB - 1)) // KB, 0)
        hi = jnp.minimum(hi, n_full)
        lo = jnp.minimum(lo, hi)
        skip_at = (n0 + (KB - 1)) // KB
        skip = jnp.where(all_second, jnp.maximum(jnp.minimum(n1 // KB, hi) - skip_at, 0), 0)
        n_masked = hi - lo - skip
        n_plain = n_full - (hi - lo)
        count = n_plain + n_masked + 1

        def masked_at(i):
            at = lo + i
            return jnp.where(at >= skip_at, at + skip, at)

        def plain_at(i):
            return jnp.where(i < lo, i, i + (hi - lo))

        def place_at(i):
            at = jnp.where(i < n_plain, plain_at(i), masked_at(i - n_plain))
            return jnp.where(i == count - 1, n_full, at)

        q = q_s[c]
        grads = do_s[c]

        def scores_of(b):
            scores = lax.dot_general(block_of(k_s, b), q, NT_DIMS, preferred_element_type=F32)
            return scores * EXP_SCALE

        def seen_at(b):
            lane = lax.broadcasted_iota(jnp.int32, (1, C), 1)
            query_pos = first + core * R + xl * HR + (lane // QR) * (2 * R) + lane % HR
            key_pos = b * KB + lax.broadcasted_iota(jnp.int32, (KB, 1), 0)
            low = jnp.where(query_pos >= n1, n0, n1)
            return (key_pos <= query_pos) & ((key_pos < low) | (key_pos >= n1))

        def add_up(weights):
            return jnp.sum(weights.reshape(KB // 8, 8, C), axis=0)

        def weigh(b, masked):
            top = m_run[...]
            scores = scores_of(b)
            if masked:
                scores = jnp.where(seen_at(b), scores, HIDDEN)
            weights = jnp.exp2(scores - top)
            l_run[...] += add_up(weights)
            m_blk[b] = top
            stash[b] = weights

        def weigh_diagonal():
            scores = jnp.where(seen_at(n_full), scores_of(n_full), HIDDEN)
            top = jnp.max(scores, axis=0, keepdims=True)
            weights = jnp.exp2(scores - top)
            l_run[...] = add_up(weights)
            m_run[...] = top
            m_blk[n_full] = top
            stash[n_full] = weights

        def masked_step(i, carry):
            weigh(masked_at(i), True)
            return carry

        def plain_pair(i, carry):
            weigh(plain_at(2 * i), False)
            weigh(plain_at(2 * i + 1), False)
            return carry

        weigh_diagonal()
        lax.fori_loop(0, n_masked, masked_step, 0)
        lax.fori_loop(0, n_plain // 2, plain_pair, 0)

        @pl.when(n_plain % 2 == 1)
        def _():
            weigh(plain_at(n_plain - 1), False)

        @pl.when(jnp.logical_not(jnp.max(l_run[...]) < 2.0**90))
        def _():
            m_run[...] = jnp.full_like(m_run, HIDDEN)
            l_run[...] = jnp.zeros_like(l_run)

            def careful_step(i, carry):
                b = place_at(count - 1 - i)
                scores = jnp.where(seen_at(b), scores_of(b), HIDDEN)
                old = m_run[...]
                top = jnp.maximum(old, jnp.max(scores, axis=0, keepdims=True))
                weights = jnp.exp2(scores - top)
                l_run[...] = l_run[...] * jnp.exp2(old - top) + add_up(weights)
                m_run[...] = top
                m_blk[b] = top
                stash[b] = weights
                return carry

            lax.fori_loop(0, count, careful_step, 0)

        logsum = m_run[...] + jnp.log2(jnp.sum(l_run[...], axis=0, keepdims=True))
        dots = []
        for half in range(2):
            block = d_s[2 * c + half].astype(F32)
            dots.append(block[0:1] + block[1:2])
        row_dot = jnp.concatenate(dots, axis=1)
        dq_s[...] = jnp.zeros_like(dq_s)

        def grad_block(b):
            weights = stash[b] * jnp.exp2(m_blk[b] - logsum)
            prob_grad = lax.dot_general(
                block_of(v_s, b), grads, NT_DIMS, preferred_element_type=F32
            )
            score_grad = (weights * (prob_grad - row_dot)).astype(BF16)
            for ref, term in (
                (dv_s, jnp.dot(weights.astype(BF16), grads, preferred_element_type=F32)),
                (dk_s, jnp.dot(score_grad, q, preferred_element_type=F32)),
            ):
                ref[pl.ds(2 * b, 2)] += term.reshape(2, 2, 2, R, D)
            return jnp.dot(kt_s[b], score_grad, preferred_element_type=F32)

        def grad_pair(i, carry):
            first_term = grad_block(place_at(2 * i))
            second_term = grad_block(place_at(2 * i + 1))
            dq_s[...] += first_term + second_term
            return carry

        lax.fori_loop(0, count // 2, grad_pair, 0)

        @pl.when(count % 2 == 1)
        def _():
            dq_s[...] += grad_block(n_full)

        dq = (dq_s[...] * SCALE).T.astype(BF16)
        dq_out[2 * c] = dq[:QR]
        dq_out[2 * c + 1] = dq[QR:]
        return unused

    lax.fori_loop(0, 8, chunk_step, 0)

    for from_core, group in ((core, outs[0]), (1 - core, outs[1])):
        for dy, out in zip((0, 1, 3, 2), group):
            for flip in range(2):
                for j in range(4):
                    rank = place(flip, dy, j)
                    rows = slice(2 * j, 2 * j + 2)
                    out[flip, rows, :R] = (dk_s[rank, :, from_core] * SCALE).astype(BF16)
                    out[flip, rows, R:] = dv_s[rank, :, from_core].astype(BF16)


def last_sum_kernel(mine, got, near_1, near_3, dq, keep, send, out):
    for flip, total in enumerate((keep, send)):
        parts = [ref[flip].astype(F32) for ref in (mine, got, near_1, near_3)]
        total[...] = ((parts[0] + parts[1]) + (parts[2] + parts[3])).astype(total.dtype)
    for g in range(8):
        for half in range(2):
            dest = (g // 4 * 2 + half) * 4 + g % 4
            for h in range(G):
                cols = slice((g * G + h) * D, (g * G + h + 1) * D)
                out[half * HR : (half + 1) * HR, cols] = dq[dest, h * HR : (h + 1) * HR]


def unpack_kv_kernel(got, key_grad, value_grad):
    for g in range(8):
        key_grad[:, g * D : (g + 1) * D] = got[g, :R]
        value_grad[:, g * D : (g + 1) * D] = got[g, R:]


def on_vmem(kernel, outs, *args):
    return pl.pallas_call(
        kernel,
        out_shape=outs,
        compiler_params=pltpu.CompilerParams(vmem_limit_bytes=16 << 20),
    )(*args)


def exchange(array, axes):
    return lax.all_to_all(array, axes, split_axis=0, concat_axis=0, tiled=True)


def flip(array, axis):
    return lax.ppermute(array, axis, [(0, 1), (1, 0)])


def swap(array, distance):
    return lax.ppermute(array, "y", [(i, i ^ distance) for i in range(4)])


def gather_kv(own):
    both = jnp.stack([own, flip(own, "xl")])
    near_1 = swap(both, 1)
    near_3 = swap(both, 3)
    far_same = swap(near_3[0], 1)
    far_flip = swap(near_1[1], 3)
    mine = (both, near_1, near_3, far_same, far_flip)
    return mine + tuple(flip(array, "core") for array in mine)


def add(*terms):
    total = terms[0].astype(F32)
    for term in terms[1:]:
        total = total + term.astype(F32)
    return total


def reduce_kv(mine, other, dq):
    got_0, got_1, got_3, got_2 = [flip(array, "core") for array in other]
    mine_0, mine_1, mine_3, mine_2 = mine
    far = add(mine_2, got_2).astype(BF16)
    from_1 = swap(far[0], 1)
    from_3 = swap(far[1], 3)
    to_3 = jnp.stack([add(mine_3[0], got_3[0], from_1), add(mine_3[1], got_3[1])])
    to_1 = jnp.stack([add(mine_1[0], got_1[0]), add(mine_1[1], got_1[1], from_3)])
    near_3 = swap(to_3.astype(BF16), 3)
    near_1 = swap(to_1.astype(BF16), 1)
    piece = (8, 2 * R, D)
    keep, send, query_grad = on_vmem(
        last_sum_kernel,
        [
            jax.ShapeDtypeStruct(piece, F32),
            jax.ShapeDtypeStruct(piece, BF16),
            jax.ShapeDtypeStruct((R, 8 * G * D), BF16),
        ],
        mine_0,
        got_0,
        near_1,
        near_3,
        dq,
    )
    return add(keep, flip(send, "xl")).astype(BF16), query_grad


def body(queries, keys, values, attn_out, out_grad, segment, span_order):
    kv_packed, counts = pl.pallas_call(
        pack_kv_kernel,
        out_shape=[jax.ShapeDtypeStruct((8, 2 * R, D), BF16), jax.ShapeDtypeStruct((2,), jnp.int32)],
        out_specs=[pl.BlockSpec(memory_space=pltpu.VMEM), pl.BlockSpec(memory_space=pltpu.SMEM)],
        compiler_params=pltpu.CompilerParams(vmem_limit_bytes=16 << 20),
    )(keys, values, segment.reshape(64, 128))
    kv_own = exchange(kv_packed, HEADS)
    q_own = exchange(
        on_vmem(
            pack_q_kernel,
            jax.ShapeDtypeStruct((16, 2 * QR + 16, D), BF16),
            queries,
            attn_out,
            out_grad,
        ),
        SPREAD,
    )
    pieces = gather_kv(kv_own)
    group = jax.ShapeDtypeStruct((2, 8, 2 * R, D), BF16)
    outs = pl.pallas_call(
        attention_kernel,
        out_shape=[jax.ShapeDtypeStruct((16, QR, D), BF16)] + [group] * 8,
        in_specs=[pl.BlockSpec(memory_space=pltpu.SMEM)] * 2
        + [pl.BlockSpec(memory_space=pl.ANY)] * 11,
        scratch_shapes=[
            pltpu.VMEM((8, C, D), BF16),
            pltpu.VMEM((8, C, D), BF16),
            pltpu.VMEM((16, 16, D), BF16),
            pltpu.VMEM((NT, 2, 2, R, D), BF16),
            pltpu.VMEM((NT, 2, 2, R, D), BF16),
            pltpu.VMEM((NT // 2, D, KB), BF16),
            pltpu.VMEM((NT // 2, KB, C), F32),
            pltpu.VMEM((NT // 2, 1, C), F32),
            pltpu.VMEM((1, C), F32),
            pltpu.VMEM((8, C), F32),
            pltpu.VMEM((NT, 2, 2, R, D), F32),
            pltpu.VMEM((NT, 2, 2, R, D), F32),
            pltpu.VMEM((D, C), F32),
            pltpu.SemaphoreType.DMA,
        ],
        compiler_params=pltpu.CompilerParams(vmem_limit_bytes=48 << 20),
    )(span_order, counts, q_own, *pieces)
    dkv, query_grad = reduce_kv(outs[1:5], outs[5:9], exchange(outs[0], SPREAD))
    key_grad, value_grad = on_vmem(
        unpack_kv_kernel, [jax.ShapeDtypeStruct((R, 8 * D), BF16)] * 2, exchange(dkv, HEADS)
    )
    return query_grad, key_grad, value_grad


def solution(mesh):
    fine = Mesh(mesh.devices.reshape(4, 2, 2, 2, 4), AXES)
    rows = P(AXES, None)
    return jax.shard_map(
        body,
        mesh=fine,
        in_specs=(rows,) * 5 + (P(), P()),
        out_specs=(rows,) * 3,
        check_vma=False,
    )
```

time: 161 us -> 143 us (0.89); the launches traced: 163 us -> 143 us
  Pallas kernels: 60.9 us -> 45.5 us
  starting transfers between devices: 18.7 us -> 12.9 us
  waiting for transfers between devices: 31.2 us -> 36.9 us
  local copies, waits for them, and re-layouts: 5.5 us -> 3.73 us
  blocking collectives: 44.3 us -> 42.6 us
    pallas_call x1, Pallas kernels: 57.3 us -> 41.3 us  [body(): pl.pallas_call(attention_kernel, out_shape=[jax.ShapeDtypeStruct((16, QR,...]
    ppermute x8, starting transfers between devices: 12.4 us -> 6.72 us  [swap(): return lax.ppermute(array, 'y', [(i, i ^ distance) for i in range(4)])]
    ppermute x8, waiting for transfers between devices: 17.8 us -> 21.4 us  [swap(): return lax.ppermute(array, 'y', [(i, i ^ distance) for i in range(4)])]
    ppermute x11, waiting for transfers between devices: 13.3 us -> 15.5 us  [flip(): return lax.ppermute(array, axis, [(0, 1), (1, 0)])]
    all_to_all x3, blocking collectives: 44.3 us -> 42.6 us  [exchange(): return lax.all_to_all(array, axes, split_axis=0, concat_axis=0, tiled=True)]
    pallas_call x4 -> x3, Pallas kernels: 3.52 us -> 3.46 us  [on_vmem(): pl.pallas_call(kernel, out_shape=outs, compiler_params=pltpu.CompilerPara...]
  transfers between devices with their start and end apart: 20 -> 20, of which waited for: 7 -> 10; matrix products, arithmetic and copies ran while one was open for 2% -> 1% of each run, Pallas kernels for 1% -> 1%
where the time goes in v1:
time: 143 us
  Pallas kernels  45.5 us (32%)
  blocking collectives  42.6 us (30%)
  waiting for transfers between devices  36.9 us (26%)
  starting transfers between devices  12.9 us (9%)
  local copies, waits for them, and re-layouts  3.73 us (3%)
    all_to_all x3, blocking collectives, exchange(): return lax.all_to_all(array, axes, split_axis=0, concat_axis=0, tiled=True)  42.6 us
    pallas_call x1, Pallas kernels, body(): pl.pallas_call(attention_kernel, out_shape=[jax.ShapeDtypeStruct((16, QR,...  41.3 us
    ppermute x8, waiting for transfers between devices, swap(): return lax.ppermute(array, 'y', [(i, i ^ distance) for i in range(4)])  21.4 us
    ppermute x11, waiting for transfers between devices, flip(): return lax.ppermute(array, axis, [(0, 1), (1, 0)])  15.5 us
    ppermute x8, starting transfers between devices, swap(): return lax.ppermute(array, 'y', [(i, i ^ distance) for i in range(4)])  6.72 us
    all_to_all x1, starting transfers between devices, exchange(): return lax.all_to_all(array, axes, split_axis=0, concat_axis=0, tiled=True)  3.83 us
    pallas_call x3, Pallas kernels, on_vmem(): pl.pallas_call(kernel, out_shape=outs, compiler_params=pltpu.CompilerPara...  3.46 us
  transfers between devices with their start and end apart: 20, of which 10 were waited for; matrix products, arithmetic and copies ran while one was open for 1% of the time, Pallas kernels for 1%

profile of v1, /device:TPU:0, one launch (start us, length us, event | category | flops | bytes accessed | tf_op | source)
XLA Modules:
  0.0 143.1 jit_solution(10378830123102565781)
XLA Ops:
  0.7 1.0 copy-done.3
  1.7 0.9 copy-done.4
  2.6 0.8 copy-done.5
  3.3 0.7 shard_map.94
  4.1 16.4 %all_to_all.20 = bf16[8,128,128]{2,1,0:T(8,128)(2,1)S(1)} all-to-all(bf16[8,128,128]{2,1,0:T(8,128)(2,1)S(1)} %get-tuple-element.20), channel_id=1, replica_groups=mesh['z'=4,'core'=2,'xh'=2,'xl'=2,'y'=4] {'xh','z'}, dimensions={0} | all-to-all | bytes 524288 | tf_op jit(solution)/shard_map/all_to_all | solution.py:298
  20.5 0.6 collective-permute-start
  21.1 6.0 %collective-permute-done = bf16[8,128,128]{2,1,0:T(8,128)(2,1)S(1)} collective-permute-done((bf16[8,128,128]{2,1,0:T(8,128)(2,1)S(1)}, bf16[8,128,128]{2,1,0:T(8,128)(2,1)S(1)}, u32[]{:S(2)}, u32[]{:S(2)}) %collective-permute-start) | collective-permute-done | bytes 262176 | tf_op jit(solution)/shard_map/ppermute | solution.py:302
  27.1 0.1 pad_maximum_fusion.refs_0_
  27.1 3.1 %collective-permute-start.2 = (bf16[2,8,128,128]{3,2,1,0:T(8,128)(2,1)S(1)}, bf16[2,8,128,128]{3,2,1,0:T(8,128)(2,1)S(1)}, u32[]{:S(2)}, u32[]{:S(2)}) collective-permute-start(bf16[2,8,128,128]{3,2,1,0:T(8,128)(2,1)S(1)} %pad_maximum_fusion.refs_0_), channel_id=1, source_target_pairs={{0,3},{1,2},{2,1},{3,0},{4,7},{5,6},{6,5},{7,4},{8,11},{9,10},{10,... | collective-permute-start | bytes 1572872 | tf_op jit(solution)/shard_map/ppermute | solution.py:306
  30.2 0.1 collective-permute-start.1
  30.4 1.7 %shard_map.95 = bf16[16,272,128]{2,1,0:T(8,128)(2,1)} custom-call(bf16[64,4096]{1,0:T(8,128)(2,1)S(1)} %copy-done, bf16[64,4096]{1,0:T(8,128)(2,1)S(1)} %copy-done.1, bf16[64,4096]{1,0:T(8,128)(2,1)S(1)} %copy-done.2), custom_call_target="tpu_custom_call" | custom-call | tf_op jit(solution)/shard_map/pallas_call | solution.py:290
  32.1 3.8 %all-to-all-start = ((bf16[16,272,128]{2,1,0:T(8,128)(2,1)}), bf16[16,272,128]{2,1,0:T(8,128)(2,1)S(1)}, u32[]{:S(2)}, u32[]{:S(2)}) async-start(bf16[16,272,128]{2,1,0:T(8,128)(2,1)} %shard_map.95), calls=%async_computation | async-start | bytes 2228224 | tf_op jit(solution)/shard_map/all_to_all | solution.py:298
  35.9 0.1 collective-permute-start.5
  36.0 3.8 %collective-permute-done.2.refs_2_ = bf16[2,8,128,128]{3,2,1,0:T(8,128)(2,1)S(1)} collective-permute-done((bf16[2,8,128,128]{3,2,1,0:T(8,128)(2,1)S(1)}, bf16[2,8,128,128]{3,2,1,0:T(8,128)(2,1)S(1)}, u32[]{:S(2)}, u32[]{:S(2)}) %collective-permute-start.2) | collective-permute-done | bytes 524320 | tf_op jit(solution)/shard_map/ppermute | solution.py:306
  39.8 0.4 collective-permute-start.3
  40.2 3.0 %collective-permute-done.1.refs_1_ = bf16[2,8,128,128]{3,2,1,0:T(8,128)(2,1)} collective-permute-done((bf16[2,8,128,128]{3,2,1,0:T(8,128)(2,1)S(1)}, bf16[2,8,128,128]{3,2,1,0:T(8,128)(2,1)}, u32[]{:S(2)}, u32[]{:S(2)}) %collective-permute-start.1) | collective-permute-done | bytes 524320 | tf_op jit(solution)/shard_map/ppermute | solution.py:306
  43.2 1.0 slice_bitcast_fusion.2
  44.2 0.1 collective-permute-start.4
  44.3 0.1 collective-permute-start.7
  44.4 0.5 collective-permute-start.6
  44.9 2.0 %collective-permute-done.3.refs_3_ = bf16[8,128,128]{2,1,0:T(8,128)(2,1)S(1)} collective-permute-done((bf16[8,128,128]{2,1,0:T(8,128)(2,1)S(1)}, bf16[8,128,128]{2,1,0:T(8,128)(2,1)S(1)}, u32[]{:S(2)}, u32[]{:S(2)}) %collective-permute-start.3) | collective-permute-done | bytes 262176 | tf_op jit(solution)/shard_map/ppermute | solution.py:306
  46.9 5.0 %collective-permute-done.4.refs_4_ = bf16[8,128,128]{2,1,0:T(8,128)(2,1)S(1)} collective-permute-done((bf16[8,128,128]{2,1,0:T(8,128)(2,1)S(1)}, bf16[8,128,128]{2,1,0:T(8,128)(2,1)S(1)}, u32[]{:S(2)}, u32[]{:S(2)}) %collective-permute-start.4) | collective-permute-done | bytes 262176 | tf_op jit(solution)/shard_map/ppermute | solution.py:306
  51.9 1.5 %collective-permute-done.9.refs_9_ = bf16[8,128,128]{2,1,0:T(8,128)(2,1)S(1)} collective-permute-done((bf16[8,128,128]{2,1,0:T(8,128)(2,1)S(1)}, bf16[8,128,128]{2,1,0:T(8,128)(2,1)S(1)}, u32[]{:S(2)}, u32[]{:S(2)}) %collective-permute-start.9) | collective-permute-done | bytes 262176 | tf_op jit(solution)/shard_map/ppermute | solution.py:302
  53.4 41.3 %shard_map.96 = (bf16[16,128,128]{2,1,0:T(8,128)(2,1)S(1)}, bf16[2,8,128,128]{3,2,1,0:T(8,128)(2,1)S(1)}, bf16[2,8,128,128]{3,2,1,0:T(8,128)(2,1)S(1)}, bf16[2,8...) custom-call(s32[32]{0:T(128)S(1)} %copy-done.6, ...), custom_call_target="tpu_custom_call" | custom-call | tf_op jit(solution)/shard_map/pallas_call | solution.py:373
  94.7 0.2 collective-permute-start.12
  94.9 0.4 collective-permute-start.11
  95.3 0.1 collective-permute-start.10
  95.4 0.4 collective-permute-start.15
  95.8 0.9 collective-permute-done.12
  96.7 0.1 add_convert_fusion
  96.9 0.1 collective-permute-start.16
  97.0 1.2 collective-permute-start.13
  98.2 0.1 add_convert_fusion.3
  98.3 0.7 collective-permute-done.15
  99.0 0.1 add_convert_fusion.2
  99.0 7.6 %collective-permute-done.13 = bf16[8,128,128]{2,1,0:T(8,128)(2,1)S(1)} collective-permute-done((bf16[8,128,128]{2,1,0:T(8,128)(2,1)S(1)}, bf16[8,128,128]{2,1,0:T(8,128)(2,1)S(1)}, u32[]{:S(2)}, u32[]{:S(2)}) %collective-permute-start.13) | collective-permute-done | bytes 262176 | tf_op jit(solution)/shard_map/ppermute | solution.py:306
  106.6 0.1 fusion.2
  106.7 0.1 pad_maximum_fusion.1
  106.8 0.5 collective-permute-start.14
  107.3 0.1 fusion.3
  107.4 0.1 pad_maximum_fusion.2
  107.5 1.2 collective-permute-start.17
  108.7 14.3 %all_to_all.21.dq = bf16[16,128,128]{2,1,0:T(8,128)(2,1)S(1)} all-to-all(bf16[16,128,128]{2,1,0:T(8,128)(2,1)S(1)} %get-tuple-element.29), channel_id=1, replica_groups=mesh['z'=4,'core'=2,'xh'=2,'xl'=2,'y'=4] {'xh','xl','z'}, dimensions={0} | all-to-all | bytes 1048576 | tf_op jit(solution)/shard_map/all_to_all | solution.py:298
  123.0 1.0 shard_map.97
  124.1 6.4 %collective-permute-done.18 = bf16[8,128,128]{2,1,0:T(8,128)(2,1)S(1)} collective-permute-done((bf16[8,128,128]{2,1,0:T(8,128)(2,1)S(1)}, bf16[8,128,128]{2,1,0:T(8,128)(2,1)S(1)}, u32[]{:S(2)}, u32[]{:S(2)}) %collective-permute-start.18) | collective-permute-done | bytes 262176 | tf_op jit(solution)/shard_map/ppermute | solution.py:302
  130.4 0.1 add_convert_fusion.1
  130.5 11.9 %all_to_all.22.got = bf16[8,128,128]{2,1,0:T(8,128)(2,1)S(1)} all-to-all(bf16[8,128,128]{2,1,0:T(8,128)(2,1)S(1)} %add_convert_fusion.1), channel_id=1, replica_groups=mesh['z'=4,'core'=2,'xh'=2,'xl'=2,'y'=4] {'xh','z'}, dimensions={0} | all-to-all | bytes 524288 | tf_op jit(solution)/shard_map/all_to_all | solution.py:298
  142.4 0.8 shard_map.98
  (32 shorter events, 0.1 us)
Async XLA Ops:
  0.6 29.7 %copy-start.2 = (bf16[64,4096]{1,0:T(8,128)(2,1)S(1)}, bf16[64,4096]{1,0:T(8,128)(2,1)}, u32[]{:S(2)}) copy-start(bf16[64,4096]{1,0:T(8,128)(2,1)} %grads.1) | copy-start | bytes 1572868
  0.6 29.7 %copy-start.1 = (bf16[64,4096]{1,0:T(8,128)(2,1)S(1)}, bf16[64,4096]{1,0:T(8,128)(2,1)}, u32[]{:S(2)}) copy-start(bf16[64,4096]{1,0:T(8,128)(2,1)} %saved.1) | copy-start | bytes 1572868
  0.7 29.7 %copy-start = (bf16[64,4096]{1,0:T(8,128)(2,1)S(1)}, bf16[64,4096]{1,0:T(8,128)(2,1)}, u32[]{:S(2)}) copy-start(bf16[64,4096]{1,0:T(8,128)(2,1)} %queries.1) | copy-start | bytes 1572868
  0.7 1.0 copy-start.3
  1.7 0.9 copy-start.4
  2.6 0.8 copy-start.5
  20.5 6.6 %collective-permute-start = (bf16[8,128,128]{2,1,0:T(8,128)(2,1)S(1)}, bf16[8,128,128]{2,1,0:T(8,128)(2,1)S(1)}, u32[]{:S(2)}, u32[]{:S(2)}) collective-permute-start(bf16[8,128,128]{2,1,0:T(8,128)(2,1)S(1)} %all_to_all.20), channel_id=1, source_target_pairs={{0,4},{4,0},{1,5},{5,1},{2,6},{6,2},{3,7},{7,3},{8,12},{12,8},{9,1... | collective-permute-start | bytes 786440 | tf_op jit(solution)/shard_map/ppermute | solution.py:302
  27.1 8.8 %copy-start.8 = (bf16[2,8,128,128]{3,2,1,0:T(8,128)(2,1)}, bf16[2,8,128,128]{3,2,1,0:T(8,128)(2,1)S(1)}, u32[]{:S(2)}) copy-start(bf16[2,8,128,128]{3,2,1,0:T(8,128)(2,1)S(1)} %pad_maximum_fusion.refs_0_) | copy-start | bytes 1572868
  27.1 12.7 %collective-permute-start.2 = (bf16[2,8,128,128]{3,2,1,0:T(8,128)(2,1)S(1)}, bf16[2,8,128,128]{3,2,1,0:T(8,128)(2,1)S(1)}, u32[]{:S(2)}, u32[]{:S(2)}) collective-permute-start(bf16[2,8,128,128]{3,2,1,0:T(8,128)(2,1)S(1)} %pad_maximum_fusion.refs_0_), channel_id=1, source_target_pairs={{0,3},{1,2},{2,1},{3,0},{4,7},{5,6},{6,5},{7,4},{8,11},{9,10},{10,... | collective-permute-start | bytes 1572872 | tf_op jit(solution)/shard_map/ppermute | solution.py:306
  30.2 13.0 %collective-permute-start.1 = (bf16[2,8,128,128]{3,2,1,0:T(8,128)(2,1)S(1)}, bf16[2,8,128,128]{3,2,1,0:T(8,128)(2,1)}, u32[]{:S(2)}, u32[]{:S(2)}) collective-permute-start(bf16[2,8,128,128]{3,2,1,0:T(8,128)(2,1)S(1)} %pad_maximum_fusion.refs_0_), channel_id=1, source_target_pairs={{0,1},{1,0},{2,3},{3,2},{4,5},{5,4},{6,7},{7,6},{8,9},{9,8},{10,11... | collective-permute-start | bytes 1572872 | tf_op jit(solution)/shard_map/ppermute | solution.py:306
  32.1 21.3 %copy-start.6 = (s32[32]{0:T(128)S(1)}, s32[32]{0:T(128)}, u32[]{:S(2)}) copy-start(s32[32]{0:T(128)} %order.1) | copy-start | bytes 388
  32.1 19.8 %all-to-all-start = ((bf16[16,272,128]{2,1,0:T(8,128)(2,1)}), bf16[16,272,128]{2,1,0:T(8,128)(2,1)S(1)}, u32[]{:S(2)}, u32[]{:S(2)}) async-start(bf16[16,272,128]{2,1,0:T(8,128)(2,1)} %shard_map.95), calls=%async_computation | async-start | bytes 2228224 | tf_op jit(solution)/shard_map/all_to_all | solution.py:298
  35.9 16.0 %collective-permute-start.5 = (bf16[2,8,128,128]{3,2,1,0:T(8,128)(2,1)S(1)}, bf16[2,8,128,128]{3,2,1,0:T(8,128)(2,1)}, u32[]{:S(2)}, u32[]{:S(2)}) collective-permute-start(bf16[2,8,128,128]{3,2,1,0:T(8,128)(2,1)S(1)} %pad_maximum_fusion.refs_0_), channel_id=1, source_target_pairs={{0,16},{16,0},{1,17},{17,1},{2,18},{18,2},{3,19},{19,3},{4,20},{20... | collective-permute-start | bytes 1572872 | tf_op jit(solution)/shard_map/ppermute | solution.py:302
  39.8 13.6 %copy-start.9 = (bf16[2,8,128,128]{3,2,1,0:T(8,128)(2,1)}, bf16[2,8,128,128]{3,2,1,0:T(8,128)(2,1)S(1)}, u32[]{:S(2)}) copy-start(bf16[2,8,128,128]{3,2,1,0:T(8,128)(2,1)S(1)} %collective-permute-done.2.refs_2_) | copy-start | bytes 1572868
  39.8 7.1 %collective-permute-start.3 = (bf16[8,128,128]{2,1,0:T(8,128)(2,1)S(1)}, bf16[8,128,128]{2,1,0:T(8,128)(2,1)S(1)}, u32[]{:S(2)}, u32[]{:S(2)}) collective-permute-start(bf16[8,128,128]{2,1,0:T(8,128)(2,1)S(1)} %slice_bitcast_fusion.3), channel_id=1, source_target_pairs={{0,1},{1,0},{2,3},{3,2},{4,5},{5,4},{6,7},{7,6},{8,9},{9,8},{10,11... | collective-permute-start | bytes 786440 | tf_op jit(solution)/shard_map/ppermute | solution.py:306
  44.2 7.7 %collective-permute-start.4 = (bf16[8,128,128]{2,1,0:T(8,128)(2,1)S(1)}, bf16[8,128,128]{2,1,0:T(8,128)(2,1)S(1)}, u32[]{:S(2)}, u32[]{:S(2)}) collective-permute-start(bf16[8,128,128]{2,1,0:T(8,128)(2,1)S(1)} %slice_bitcast_fusion.2), channel_id=1, source_target_pairs={{0,3},{1,2},{2,1},{3,0},{4,7},{5,6},{6,5},{7,4},{8,11},{9,10},{10,... | collective-permute-start | bytes 786440 | tf_op jit(solution)/shard_map/ppermute | solution.py:306
  44.3 7.6 %collective-permute-start.7 = (bf16[2,8,128,128]{3,2,1,0:T(8,128)(2,1)S(1)}, bf16[2,8,128,128]{3,2,1,0:T(8,128)(2,1)}, u32[]{:S(2)}, u32[]{:S(2)}) collective-permute-start(bf16[2,8,128,128]{3,2,1,0:T(8,128)(2,1)S(1)} %collective-permute-done.2.refs_2_), channel_id=1, source_target_pairs={{0,16},{16,0},{1,17},{17,1},{2,18},{18,2},{3,19},{19,3},{4,20},{20... | collective-permute-start | bytes 1572872 | tf_op jit(solution)/shard_map/ppermute | solution.py:302
  44.4 9.0 %collective-permute-start.6 = (bf16[2,8,128,128]{3,2,1,0:T(8,128)(2,1)}, bf16[2,8,128,128]{3,2,1,0:T(8,128)(2,1)}, u32[]{:S(2)}, u32[]{:S(2)}) collective-permute-start(bf16[2,8,128,128]{3,2,1,0:T(8,128)(2,1)} %collective-permute-done.1.refs_1_), channel_id=1, source_target_pairs={{0,16},{16,0},{1,17},{17,1},{2,18},{18,2},{3,19},{19,3},{4,20},{20... | collective-permute-start | bytes 1572872 | tf_op jit(solution)/shard_map/ppermute | solution.py:302
  46.9 5.0 %collective-permute-start.8 = (bf16[8,128,128]{2,1,0:T(8,128)(2,1)S(1)}, bf16[8,128,128]{2,1,0:T(8,128)(2,1)S(1)}, u32[]{:S(2)}, u32[]{:S(2)}) collective-permute-start(bf16[8,128,128]{2,1,0:T(8,128)(2,1)S(1)} %collective-permute-done.3.refs_3_), channel_id=1, source_target_pairs={{0,16},{16,0},{1,17},{17,1},{2,18},{18,2},{3,19},{19,3},{4,20},{20... | collective-permute-start | bytes 786440 | tf_op jit(solution)/shard_map/ppermute | solution.py:302
  51.9 1.5 %collective-permute-start.9 = (bf16[8,128,128]{2,1,0:T(8,128)(2,1)S(1)}, bf16[8,128,128]{2,1,0:T(8,128)(2,1)S(1)}, u32[]{:S(2)}, u32[]{:S(2)}) collective-permute-start(bf16[8,128,128]{2,1,0:T(8,128)(2,1)S(1)} %collective-permute-done.4.refs_4_), channel_id=1, source_target_pairs={{0,16},{16,0},{1,17},{17,1},{2,18},{18,2},{3,19},{19,3},{4,20},{20... | collective-permute-start | bytes 786440 | tf_op jit(solution)/shard_map/ppermute | solution.py:302
  51.9 1.5 %copy-start.7 = (bf16[16,272,128]{2,1,0:T(8,128)(2,1)}, bf16[16,272,128]{2,1,0:T(8,128)(2,1)S(1)}, u32[]{:S(2)}) copy-start(bf16[16,272,128]{2,1,0:T(8,128)(2,1)S(1)} %all-to-all-done.qpay) | copy-start | bytes 3342340
  94.7 2.0 %collective-permute-start.12 = (bf16[2,8,128,128]{3,2,1,0:T(8,128)(2,1)S(1)}, bf16[2,8,128,128]{3,2,1,0:T(8,128)(2,1)S(1)}, u32[]{:S(2)}, u32[]{:S(2)}) collective-permute-start(bf16[2,8,128,128]{3,2,1,0:T(8,128)(2,1)S(1)} %get-tuple-element.26), channel_id=1, source_target_pairs={{0,16},{16,0},{1,17},{17,1},{2,18},{18,2},{3,19},{19,3},{4,20},{20... | collective-permute-start | bytes 1572872 | tf_op jit(solution)/shard_map/ppermute | solution.py:302
  94.9 3.3 %collective-permute-start.11 = (bf16[2,8,128,128]{3,2,1,0:T(8,128)(2,1)S(1)}, bf16[2,8,128,128]{3,2,1,0:T(8,128)(2,1)S(1)}, u32[]{:S(2)}, u32[]{:S(2)}) collective-permute-start(bf16[2,8,128,128]{3,2,1,0:T(8,128)(2,1)S(1)} %get-tuple-element.24), channel_id=1, source_target_pairs={{0,16},{16,0},{1,17},{17,1},{2,18},{18,2},{3,19},{19,3},{4,20},{20... | collective-permute-start | bytes 1572872 | tf_op jit(solution)/shard_map/ppermute | solution.py:302
  95.3 27.7 %collective-permute-start.10 = (bf16[2,8,128,128]{3,2,1,0:T(8,128)(2,1)S(1)}, bf16[2,8,128,128]{3,2,1,0:T(8,128)(2,1)S(1)}, u32[]{:S(2)}, u32[]{:S(2)}) collective-permute-start(bf16[2,8,128,128]{3,2,1,0:T(8,128)(2,1)S(1)} %get-tuple-element.22), channel_id=1, source_target_pairs={{0,16},{16,0},{1,17},{17,1},{2,18},{18,2},{3,19},{19,3},{4,20},{20... | collective-permute-start | bytes 1572872 | tf_op jit(solution)/shard_map/ppermute | solution.py:302
  95.4 3.5 %collective-permute-start.15 = (bf16[2,8,128,128]{3,2,1,0:T(8,128)(2,1)S(1)}, bf16[2,8,128,128]{3,2,1,0:T(8,128)(2,1)S(1)}, u32[]{:S(2)}, u32[]{:S(2)}) collective-permute-start(bf16[2,8,128,128]{3,2,1,0:T(8,128)(2,1)S(1)} %get-tuple-element.28), channel_id=1, source_target_pairs={{0,16},{16,0},{1,17},{17,1},{2,18},{18,2},{3,19},{19,3},{4,20},{20... | collective-permute-start | bytes 1572872 | tf_op jit(solution)/shard_map/ppermute | solution.py:302
  96.9 10.4 %collective-permute-start.16 = (bf16[8,128,128]{2,1,0:T(8,128)(2,1)S(1)}, bf16[8,128,128]{2,1,0:T(8,128)(2,1)S(1)}, u32[]{:S(2)}, u32[]{:S(2)}) collective-permute-start(bf16[8,128,128]{2,1,0:T(8,128)(2,1)S(1)} %get-tuple-element.35), channel_id=1, source_target_pairs={{0,1},{1,0},{2,3},{3,2},{4,5},{5,4},{6,7},{7,6},{8,9},{9,8},{10,11... | collective-permute-start | bytes 786440 | tf_op jit(solution)/shard_map/ppermute | solution.py:306
  97.0 9.6 %collective-permute-start.13 = (bf16[8,128,128]{2,1,0:T(8,128)(2,1)S(1)}, bf16[8,128,128]{2,1,0:T(8,128)(2,1)S(1)}, u32[]{:S(2)}, u32[]{:S(2)}) collective-permute-start(bf16[8,128,128]{2,1,0:T(8,128)(2,1)S(1)} %get-tuple-element.36), channel_id=1, source_target_pairs={{0,3},{1,2},{2,1},{3,0},{4,7},{5,6},{6,5},{7,4},{8,11},{9,10},{10,... | collective-permute-start | bytes 786440 | tf_op jit(solution)/shard_map/ppermute | solution.py:306
  106.8 16.2 %collective-permute-start.14 = (bf16[2,8,128,128]{3,2,1,0:T(8,128)(2,1)S(1)}, bf16[2,8,128,128]{3,2,1,0:T(8,128)(2,1)S(1)}, u32[]{:S(2)}, u32[]{:S(2)}) collective-permute-start(bf16[2,8,128,128]{3,2,1,0:T(8,128)(2,1)S(1)} %pad_maximum_fusion.1), channel_id=1, source_target_pairs={{0,1},{1,0},{2,3},{3,2},{4,5},{5,4},{6,7},{7,6},{8,9},{9,8},{10,11... | collective-permute-start | bytes 1572872 | tf_op jit(solution)/shard_map/ppermute | solution.py:306
  107.5 15.5 %collective-permute-start.17 = (bf16[2,8,128,128]{3,2,1,0:T(8,128)(2,1)S(1)}, bf16[2,8,128,128]{3,2,1,0:T(8,128)(2,1)S(1)}, u32[]{:S(2)}, u32[]{:S(2)}) collective-permute-start(bf16[2,8,128,128]{3,2,1,0:T(8,128)(2,1)S(1)} %pad_maximum_fusion.2), channel_id=1, source_target_pairs={{0,3},{1,2},{2,1},{3,0},{4,7},{5,6},{6,5},{7,4},{8,11},{9,10},{10,... | collective-permute-start | bytes 1572872 | tf_op jit(solution)/shard_map/ppermute | solution.py:306
  124.1 6.4 %collective-permute-start.18 = (bf16[8,128,128]{2,1,0:T(8,128)(2,1)S(1)}, bf16[8,128,128]{2,1,0:T(8,128)(2,1)S(1)}, u32[]{:S(2)}, u32[]{:S(2)}) collective-permute-start(bf16[8,128,128]{2,1,0:T(8,128)(2,1)S(1)} %get-tuple-element.32), channel_id=1, source_target_pairs={{0,4},{4,0},{1,5},{5,1},{2,6},{6,2},{3,7},{7,3},{8,12},{12,8},{9,1... | collective-permute-start | bytes 786440 | tf_op jit(solution)/shard_map/ppermute | solution.py:302

commit v2 on v1

--- a/solution.py
+++ b/solution.py
@@ -68,7 +68,9 @@
 def attention_kernel(order, counts, qpay, *refs):
     pieces = refs[:10]
     dq_out, outs = refs[10], (refs[11:15], refs[15:19])
-    (q_s, do_s, d_s, k_s, v_s, kt_s, stash, m_blk, m_run, l_run, dk_s, dv_s, dq_s, sem) = refs[19:]
+    (q_s, do_s, d_s, k_s, v_s, kt_s, qa_s, ga_s, stash, m_blk, m_run, l_run, dk_s, dv_s, dq_s, sem) = (
+        refs[19:]
+    )
     n0 = counts[0]
     n1 = counts[1]
     xl = lax.axis_index("xl")
@@ -98,23 +100,35 @@
                 rank = place(flip, dy, j)
                 rows = source.at[pl.ds(2 * j, 2)]
                 copies.append(
-                    pltpu.make_async_copy(rows.at[:, pl.ds(0, R)], k_s.at[rank, :, from_core], sem)
+                    pltpu.make_async_copy(rows.at[:, pl.ds(0, R)], k_s.at[rank, :, from_core, :, pl.ds(0, D)], sem)
                 )
                 copies.append(
-                    pltpu.make_async_copy(rows.at[:, pl.ds(R, R)], v_s.at[rank, :, from_core], sem)
+                    pltpu.make_async_copy(rows.at[:, pl.ds(R, R)], v_s.at[rank, :, from_core, :, pl.ds(0, D)], sem)
                 )
     for copy in copies:
         copy.start()
     dk_s[...] = jnp.zeros_like(dk_s)
     dv_s[...] = jnp.zeros_like(dv_s)
+    beside = lax.broadcasted_iota(jnp.int32, (1, 1, 1, 1, D), 4) < 2
+    beside = jnp.broadcast_to(beside.astype(F32), (1, 2, 2, R, D)).astype(BF16)
+
+    def put_beside(i, carry):
+        k_s[pl.ds(i, 1), :, :, :, D:] = beside
+        v_s[pl.ds(i, 1), :, :, :, D:] = beside
+        return carry
+
+    lax.fori_loop(0, NT, put_beside, 0)
     for copy in copies:
         copy.wait()
 
     def block_of(ref, b):
-        return ref[pl.ds(2 * b, 2)].reshape(KB, D)
+        return ref[pl.ds(2 * b, 2)].reshape(KB, 2 * D)
+
+    def keys_of(b):
+        return k_s[pl.ds(2 * b, 2), :, :, :, :D].reshape(KB, D)
 
     def turn(b, carry):
-        kt_s[b] = block_of(k_s, b).T
+        kt_s[b] = keys_of(b).T
         return carry
 
     lax.fori_loop(0, NT // 2, turn, 0)
@@ -149,9 +163,24 @@
         q = q_s[c]
         grads = do_s[c]
 
-        def scores_of(b):
-            scores = lax.dot_general(block_of(k_s, b), q, NT_DIMS, preferred_element_type=F32)
-            return scores * EXP_SCALE
+        def put_under(ref, *rows):
+            number = lax.broadcasted_iota(jnp.int32, (D, C), 0)
+            block = jnp.zeros((D, C), F32)
+            for i, values in enumerate(rows):
+                block = jnp.where(number == i, values, block)
+            ref[D:] = block.astype(BF16)
+
+        def raw_scores(b):
+            return jnp.dot(keys_of(b), qa_s[:D], preferred_element_type=F32)
+
+        qa_s[:D] = q.T
+        ga_s[:D] = grads.T
+        halves = [d_s[2 * c + half].astype(F32) for half in range(2)]
+        put_under(
+            ga_s,
+            -jnp.concatenate([half[0:1] for half in halves], axis=1),
+            -jnp.concatenate([half[1:2] for half in halves], axis=1),
+        )
 
         def seen_at(b):
             lane = lax.broadcasted_iota(jnp.int32, (1, C), 1)
@@ -164,22 +193,22 @@
             return jnp.sum(weights.reshape(KB // 8, 8, C), axis=0)
 
         def weigh(b, masked):
-            top = m_run[...]
-            scores = scores_of(b)
+            scores = jnp.dot(block_of(k_s, b), qa_s[...], preferred_element_type=F32)
             if masked:
                 scores = jnp.where(seen_at(b), scores, HIDDEN)
-            weights = jnp.exp2(scores - top)
+            weights = jnp.exp2(scores * EXP_SCALE)
             l_run[...] += add_up(weights)
-            m_blk[b] = top
+            m_blk[b] = m_run[...]
             stash[b] = weights
 
         def weigh_diagonal():
-            scores = jnp.where(seen_at(n_full), scores_of(n_full), HIDDEN)
-            top = jnp.max(scores, axis=0, keepdims=True)
-            weights = jnp.exp2(scores - top)
+            scores = jnp.where(seen_at(n_full), raw_scores(n_full), HIDDEN)
+            top = jnp.max(scores, axis=0, keepdims=True).astype(BF16).astype(F32)
+            put_under(qa_s, -top)
+            weights = jnp.exp2((scores - top) * EXP_SCALE)
             l_run[...] = add_up(weights)
-            m_run[...] = top
-            m_blk[n_full] = top
+            m_run[...] = top * EXP_SCALE
+            m_blk[n_full] = top * EXP_SCALE
             stash[n_full] = weights
 
         def masked_step(i, carry):
@@ -206,7 +235,7 @@
 
             def careful_step(i, carry):
                 b = place_at(count - 1 - i)
-                scores = jnp.where(seen_at(b), scores_of(b), HIDDEN)
+                scores = jnp.where(seen_at(b), raw_scores(b) * EXP_SCALE, HIDDEN)
                 old = m_run[...]
                 top = jnp.maximum(old, jnp.max(scores, axis=0, keepdims=True))
                 weights = jnp.exp2(scores - top)
@@ -219,19 +248,12 @@
             lax.fori_loop(0, count, careful_step, 0)
 
         logsum = m_run[...] + jnp.log2(jnp.sum(l_run[...], axis=0, keepdims=True))
-        dots = []
-        for half in range(2):
-            block = d_s[2 * c + half].astype(F32)
-            dots.append(block[0:1] + block[1:2])
-        row_dot = jnp.concatenate(dots, axis=1)
         dq_s[...] = jnp.zeros_like(dq_s)
 
         def grad_block(b):
             weights = stash[b] * jnp.exp2(m_blk[b] - logsum)
-            prob_grad = lax.dot_general(
-                block_of(v_s, b), grads, NT_DIMS, preferred_element_type=F32
-            )
-            score_grad = (weights * (prob_grad - row_dot)).astype(BF16)
+            above = jnp.dot(block_of(v_s, b), ga_s[...], preferred_element_type=F32)
+            score_grad = (weights * above).astype(BF16)
             for ref, term in (
                 (dv_s, jnp.dot(weights.astype(BF16), grads, preferred_element_type=F32)),
                 (dk_s, jnp.dot(score_grad, q, preferred_element_type=F32)),
@@ -268,10 +290,13 @@
                     out[flip, rows, R:] = dv_s[rank, :, from_core].astype(BF16)
 
 
-def last_sum_kernel(mine, got, near_1, near_3, dq, keep, send, out):
-    for flip, total in enumerate((keep, send)):
-        parts = [ref[flip].astype(F32) for ref in (mine, got, near_1, near_3)]
-        total[...] = ((parts[0] + parts[1]) + (parts[2] + parts[3])).astype(total.dtype)
+def last_sum_kernel(mine, got, near_1, near_3, dq, sums, out):
+    for flip in range(2):
+        for xh in range(2):
+            rows = slice(xh * 4, xh * 4 + 4)
+            parts = [ref[flip, rows].astype(F32) for ref in (mine, got, near_1, near_3)]
+            total = (parts[0] + parts[1]) + (parts[2] + parts[3])
+            sums[xh, lax.axis_index("xl") ^ flip] = total.astype(BF16)
     for g in range(8):
         for half in range(2):
             dest = (g // 4 * 2 + half) * 4 + g % 4
@@ -282,8 +307,11 @@
 
 def unpack_kv_kernel(got, key_grad, value_grad):
     for g in range(8):
-        key_grad[:, g * D : (g + 1) * D] = got[g, :R]
-        value_grad[:, g * D : (g + 1) * D] = got[g, R:]
+        pair = [(g // 4 * 2 + xl) * 4 + g % 4 for xl in range(2)]
+        for start, out in ((0, key_grad), (R, value_grad)):
+            rows = slice(start, start + R)
+            total = got[pair[0], rows].astype(F32) + got[pair[1], rows].astype(F32)
+            out[:, g * D : (g + 1) * D] = total.astype(BF16)
 
 
 def on_vmem(kernel, outs, *args):
@@ -333,21 +361,17 @@
     to_1 = jnp.stack([add(mine_1[0], got_1[0]), add(mine_1[1], got_1[1], from_3)])
     near_3 = swap(to_3.astype(BF16), 3)
     near_1 = swap(to_1.astype(BF16), 1)
-    piece = (8, 2 * R, D)
-    keep, send, query_grad = on_vmem(
+    pair = (2, 2, 4, 2 * R, D)
+    sums, query_grad = on_vmem(
         last_sum_kernel,
-        [
-            jax.ShapeDtypeStruct(piece, F32),
-            jax.ShapeDtypeStruct(piece, BF16),
-            jax.ShapeDtypeStruct((R, 8 * G * D), BF16),
-        ],
+        [jax.ShapeDtypeStruct(pair, BF16), jax.ShapeDtypeStruct((R, 8 * G * D), BF16)],
         mine_0,
         got_0,
         near_1,
         near_3,
         dq,
     )
-    return add(keep, flip(send, "xl")).astype(BF16), query_grad
+    return sums.reshape(16, 2 * R, D), query_grad
 
 
 def body(queries, keys, values, attn_out, out_grad, segment, span_order):
@@ -379,9 +403,11 @@
             pltpu.VMEM((8, C, D), BF16),
             pltpu.VMEM((8, C, D), BF16),
             pltpu.VMEM((16, 16, D), BF16),
-            pltpu.VMEM((NT, 2, 2, R, D), BF16),
-            pltpu.VMEM((NT, 2, 2, R, D), BF16),
+            pltpu.VMEM((NT, 2, 2, R, 2 * D), BF16),
+            pltpu.VMEM((NT, 2, 2, R, 2 * D), BF16),
             pltpu.VMEM((NT // 2, D, KB), BF16),
+            pltpu.VMEM((2 * D, C), BF16),
+            pltpu.VMEM((2 * D, C), BF16),
             pltpu.VMEM((NT // 2, KB, C), F32),
             pltpu.VMEM((NT // 2, 1, C), F32),
             pltpu.VMEM((1, C), F32),
@@ -395,7 +421,7 @@
     )(span_order, counts, q_own, *pieces)
     dkv, query_grad = reduce_kv(outs[1:5], outs[5:9], exchange(outs[0], SPREAD))
     key_grad, value_grad = on_vmem(
-        unpack_kv_kernel, [jax.ShapeDtypeStruct((R, 8 * D), BF16)] * 2, exchange(dkv, HEADS)
+        unpack_kv_kernel, [jax.ShapeDtypeStruct((R, 8 * D), BF16)] * 2, exchange(dkv, SPREAD)
     )
     return query_grad, key_grad, value_grad
 

time: 143 us -> 140 us (0.979)
  waiting for transfers between devices: 36.9 us -> 28.7 us
  starting transfers between devices: 12.9 us -> 18.5 us
  Pallas kernels: 45.5 us -> 43.2 us
    ppermute x11 -> x10, waiting for transfers between devices: 15.5 us -> 8.42 us  [flip(): return lax.ppermute(array, axis, [(0, 1), (1, 0)])]
    ppermute x8, starting transfers between devices: 6.72 us -> 12.3 us  [swap(): return lax.ppermute(array, 'y', [(i, i ^ distance) for i in range(4)])]
    pallas_call x1, Pallas kernels: 41.3 us -> 39.1 us  [body(): pl.pallas_call(attention_kernel, out_shape=[jax.ShapeDtypeStruct((16, QR,...]
    all_to_all x3, blocking collectives: 42.6 us -> 44 us  [exchange(): return lax.all_to_all(array, axes, split_axis=0, concat_axis=0, tiled=True)]
  transfers between devices with their start and end apart: 20 -> 19, of which waited for: 10 -> 8; matrix products, arithmetic and copies ran while one was open for 1% -> 1% of each run, Pallas kernels for 1% -> 1%
where the time goes in v2:
time: 140 us
  blocking collectives  44 us (31%)
  Pallas kernels  43.2 us (31%)
  waiting for transfers between devices  28.7 us (20%)
  starting transfers between devices  18.5 us (13%)
  local copies, waits for them, and re-layouts  3.73 us (3%)
    all_to_all x3, blocking collectives, exchange(): return lax.all_to_all(array, axes, split_axis=0, concat_axis=0, tiled=True)  44 us
    pallas_call x1, Pallas kernels, body(): pl.pallas_call(attention_kernel, out_shape=[jax.ShapeDtypeStruct((16, QR,...  39.1 us
    ppermute x8, waiting for transfers between devices, swap(): return lax.ppermute(array, 'y', [(i, i ^ distance) for i in range(4)])  20.3 us
    ppermute x8, starting transfers between devices, swap(): return lax.ppermute(array, 'y', [(i, i ^ distance) for i in range(4)])  12.3 us
    ppermute x10, waiting for transfers between devices, flip(): return lax.ppermute(array, axis, [(0, 1), (1, 0)])  8.42 us
    all_to_all x1, starting transfers between devices, exchange(): return lax.all_to_all(array, axes, split_axis=0, concat_axis=0, tiled=True)  3.83 us
    pallas_call x3, Pallas kernels, on_vmem(): pl.pallas_call(kernel, out_shape=outs, compiler_params=pltpu.CompilerPara...  3.41 us
  transfers between devices with their start and end apart: 19, of which 8 were waited for; matrix products, arithmetic and copies ran while one was open for 1% of the time, Pallas kernels for 1%

profile of v2, /device:TPU:0, one launch (start us, length us, event | category | flops | bytes accessed | tf_op | source)
XLA Modules:
  0.0 139.7 jit_solution(14768764601424292044)
XLA Ops:
  0.7 1.0 copy-done.3
  1.7 0.9 copy-done.4
  2.6 0.8 copy-done.5
  3.3 0.7 shard_map.94
  4.1 16.4 %all_to_all.20 = bf16[8,128,128]{2,1,0:T(8,128)(2,1)S(1)} all-to-all(bf16[8,128,128]{2,1,0:T(8,128)(2,1)S(1)} %get-tuple-element.19), channel_id=1, replica_groups=mesh['z'=4,'core'=2,'xh'=2,'xl'=2,'y'=4] {'xh','z'}, dimensions={0} | all-to-all | bytes 524288 | tf_op jit(solution)/shard_map/all_to_all | solution.py:326
  20.5 0.6 collective-permute-start
  21.1 6.0 %collective-permute-done = bf16[8,128,128]{2,1,0:T(8,128)(2,1)S(1)} collective-permute-done((bf16[8,128,128]{2,1,0:T(8,128)(2,1)S(1)}, bf16[8,128,128]{2,1,0:T(8,128)(2,1)S(1)}, u32[]{:S(2)}, u32[]{:S(2)}) %collective-permute-start) | collective-permute-done | bytes 262176 | tf_op jit(solution)/shard_map/ppermute | solution.py:330
  27.1 0.1 pad_maximum_fusion.refs_0_
  27.1 0.0 copy-start.8
  27.1 3.1 %collective-permute-start.2 = (bf16[2,8,128,128]{3,2,1,0:T(8,128)(2,1)S(1)}, bf16[2,8,128,128]{3,2,1,0:T(8,128)(2,1)S(1)}, u32[]{:S(2)}, u32[]{:S(2)}) collective-permute-start(bf16[2,8,128,128]{3,2,1,0:T(8,128)(2,1)S(1)} %pad_maximum_fusion.refs_0_), channel_id=1, source_target_pairs={{0,3},{1,2},{2,1},{3,0},{4,7},{5,6},{6,5},{7,4},{8,11},{9,10},{10,... | collective-permute-start | bytes 1572872 | tf_op jit(solution)/shard_map/ppermute | solution.py:334
  30.2 0.1 collective-permute-start.1
  30.4 1.7 %shard_map.95 = bf16[16,272,128]{2,1,0:T(8,128)(2,1)} custom-call(bf16[64,4096]{1,0:T(8,128)(2,1)S(1)} %copy-done, bf16[64,4096]{1,0:T(8,128)(2,1)S(1)} %copy-done.1, bf16[64,4096]{1,0:T(8,128)(2,1)S(1)} %copy-done.2), custom_call_target="tpu_custom_call" | custom-call | tf_op jit(solution)/shard_map/pallas_call | solution.py:318
  32.0 3.8 %all-to-all-start = ((bf16[16,272,128]{2,1,0:T(8,128)(2,1)}), bf16[16,272,128]{2,1,0:T(8,128)(2,1)S(1)}, u32[]{:S(2)}, u32[]{:S(2)}) async-start(bf16[16,272,128]{2,1,0:T(8,128)(2,1)} %shard_map.95), calls=%async_computation | async-start | bytes 2228224 | tf_op jit(solution)/shard_map/all_to_all | solution.py:326
  35.9 0.1 collective-permute-start.5
  36.0 3.8 %collective-permute-done.2.refs_2_ = bf16[2,8,128,128]{3,2,1,0:T(8,128)(2,1)S(1)} collective-permute-done((bf16[2,8,128,128]{3,2,1,0:T(8,128)(2,1)S(1)}, bf16[2,8,128,128]{3,2,1,0:T(8,128)(2,1)S(1)}, u32[]{:S(2)}, u32[]{:S(2)}) %collective-permute-start.2) | collective-permute-done | bytes 524320 | tf_op jit(solution)/shard_map/ppermute | solution.py:334
  39.8 0.4 collective-permute-start.3
  40.2 3.0 %collective-permute-done.1.refs_1_ = bf16[2,8,128,128]{3,2,1,0:T(8,128)(2,1)} collective-permute-done((bf16[2,8,128,128]{3,2,1,0:T(8,128)(2,1)S(1)}, bf16[2,8,128,128]{3,2,1,0:T(8,128)(2,1)}, u32[]{:S(2)}, u32[]{:S(2)}) %collective-permute-start.1) | collective-permute-done | bytes 524320 | tf_op jit(solution)/shard_map/ppermute | solution.py:334
  43.2 1.0 slice_bitcast_fusion.2
  44.2 0.1 collective-permute-start.4
  44.3 0.1 collective-permute-start.7
  44.4 0.5 collective-permute-start.6
  44.9 2.0 %collective-permute-done.3.refs_3_ = bf16[8,128,128]{2,1,0:T(8,128)(2,1)S(1)} collective-permute-done((bf16[8,128,128]{2,1,0:T(8,128)(2,1)S(1)}, bf16[8,128,128]{2,1,0:T(8,128)(2,1)S(1)}, u32[]{:S(2)}, u32[]{:S(2)}) %collective-permute-start.3) | collective-permute-done | bytes 262176 | tf_op jit(solution)/shard_map/ppermute | solution.py:334
  46.9 5.0 %collective-permute-done.4.refs_4_ = bf16[8,128,128]{2,1,0:T(8,128)(2,1)S(1)} collective-permute-done((bf16[8,128,128]{2,1,0:T(8,128)(2,1)S(1)}, bf16[8,128,128]{2,1,0:T(8,128)(2,1)S(1)}, u32[]{:S(2)}, u32[]{:S(2)}) %collective-permute-start.4) | collective-permute-done | bytes 262176 | tf_op jit(solution)/shard_map/ppermute | solution.py:334
  51.9 0.0 all-to-all-done.qpay
  51.9 0.0 collective-permute-done.8.refs_8_
  51.9 1.5 %collective-permute-done.9.refs_9_ = bf16[8,128,128]{2,1,0:T(8,128)(2,1)S(1)} collective-permute-done((bf16[8,128,128]{2,1,0:T(8,128)(2,1)S(1)}, bf16[8,128,128]{2,1,0:T(8,128)(2,1)S(1)}, u32[]{:S(2)}, u32[]{:S(2)}) %collective-permute-start.9) | collective-permute-done | bytes 262176 | tf_op jit(solution)/shard_map/ppermute | solution.py:330
  53.4 39.1 %shard_map.96 = (bf16[16,128,128]{2,1,0:T(8,128)(2,1)S(1)}, bf16[2,8,128,128]{3,2,1,0:T(8,128)(2,1)S(1)}, bf16[2,8,128,128]{3,2,1,0:T(8,128)(2,1)S(1)}, bf16[2,8...) custom-call(s32[32]{0:T(128)S(1)} %copy-done.6, ...), custom_call_target="tpu_custom_call" | custom-call | tf_op jit(solution)/shard_map/pallas_call | solution.py:397
  92.5 0.2 collective-permute-start.12
  92.7 0.4 collective-permute-start.11
  93.1 0.1 collective-permute-start.10
  93.2 0.4 collective-permute-start.15
  93.6 0.9 collective-permute-done.12
  94.5 0.1 add_convert_fusion
  94.7 0.1 collective-permute-start.16
  94.8 5.0 %collective-permute-start.13 = (bf16[8,128,128]{2,1,0:T(8,128)(2,1)S(1)}, bf16[8,128,128]{2,1,0:T(8,128)(2,1)S(1)}, u32[]{:S(2)}, u32[]{:S(2)}) collective-permute-start(bf16[8,128,128]{2,1,0:T(8,128)(2,1)S(1)} %get-tuple-element.34), channel_id=1, source_target_pairs={{0,3},{1,2},{2,1},{3,0},{4,7},{5,6},{6,5},{7,4},{8,11},{9,10},{10,... | collective-permute-start | bytes 786440 | tf_op jit(solution)/shard_map/ppermute | solution.py:334
  99.8 0.1 add_convert_fusion.2
  99.9 0.1 add_convert_fusion.1
  100.0 6.4 %collective-permute-done.13 = bf16[8,128,128]{2,1,0:T(8,128)(2,1)S(1)} collective-permute-done((bf16[8,128,128]{2,1,0:T(8,128)(2,1)S(1)}, bf16[8,128,128]{2,1,0:T(8,128)(2,1)S(1)}, u32[]{:S(2)}, u32[]{:S(2)}) %collective-permute-start.13) | collective-permute-done | bytes 262176 | tf_op jit(solution)/shard_map/ppermute | solution.py:334
  106.4 0.1 fusion.2
  106.5 0.1 pad_maximum_fusion.1
  106.6 1.1 collective-permute-start.14
  107.7 0.1 fusion.3
  107.8 0.1 pad_maximum_fusion.2
  107.9 2.4 %collective-permute-start.17 = (bf16[2,8,128,128]{3,2,1,0:T(8,128)(2,1)S(1)}, bf16[2,8,128,128]{3,2,1,0:T(8,128)(2,1)S(1)}, u32[]{:S(2)}, u32[]{:S(2)}) collective-permute-start(bf16[2,8,128,128]{3,2,1,0:T(8,128)(2,1)S(1)} %pad_maximum_fusion.2), channel_id=1, source_target_pairs={{0,3},{1,2},{2,1},{3,0},{4,7},{5,6},{6,5},{7,4},{8,11},{9,10},{10,... | collective-permute-start | bytes 1572872 | tf_op jit(solution)/shard_map/ppermute | solution.py:334
  110.3 14.3 %all_to_all.21.dq = bf16[16,128,128]{2,1,0:T(8,128)(2,1)S(1)} all-to-all(bf16[16,128,128]{2,1,0:T(8,128)(2,1)S(1)} %get-tuple-element.28), channel_id=1, replica_groups=mesh['z'=4,'core'=2,'xh'=2,'xl'=2,'y'=4] {'xh','xl','z'}, dimensions={0} | all-to-all | bytes 1048576 | tf_op jit(solution)/shard_map/all_to_all | solution.py:326
  124.6 1.0 shard_map.97
  125.6 13.3 %all_to_all.22.got = bf16[16,128,128]{2,1,0:T(8,128)(2,1)S(1)} all-to-all(bf16[16,128,128]{2,1,0:T(8,128)(2,1)S(1)} %bitcast.28), channel_id=1, replica_groups=mesh['z'=4,'core'=2,'xh'=2,'xl'=2,'y'=4] {'xh','xl','z'}, dimensions={0} | all-to-all | bytes 1048576 | tf_op jit(solution)/shard_map/all_to_all | solution.py:326
  138.9 0.8 shard_map.98
  (29 shorter events, 0.1 us)
Async XLA Ops:
  0.6 29.7 %copy-start.2 = (bf16[64,4096]{1,0:T(8,128)(2,1)S(1)}, bf16[64,4096]{1,0:T(8,128)(2,1)}, u32[]{:S(2)}) copy-start(bf16[64,4096]{1,0:T(8,128)(2,1)} %grads.1) | copy-start | bytes 1572868
  0.6 29.7 %copy-start.1 = (bf16[64,4096]{1,0:T(8,128)(2,1)S(1)}, bf16[64,4096]{1,0:T(8,128)(2,1)}, u32[]{:S(2)}) copy-start(bf16[64,4096]{1,0:T(8,128)(2,1)} %saved.1) | copy-start | bytes 1572868
  0.7 29.7 %copy-start = (bf16[64,4096]{1,0:T(8,128)(2,1)S(1)}, bf16[64,4096]{1,0:T(8,128)(2,1)}, u32[]{:S(2)}) copy-start(bf16[64,4096]{1,0:T(8,128)(2,1)} %queries.1) | copy-start | bytes 1572868
  0.7 1.0 copy-start.3
  1.7 0.9 copy-start.4
  2.6 0.8 copy-start.5
  20.5 6.6 %collective-permute-start = (bf16[8,128,128]{2,1,0:T(8,128)(2,1)S(1)}, bf16[8,128,128]{2,1,0:T(8,128)(2,1)S(1)}, u32[]{:S(2)}, u32[]{:S(2)}) collective-permute-start(bf16[8,128,128]{2,1,0:T(8,128)(2,1)S(1)} %all_to_all.20), channel_id=1, source_target_pairs={{0,4},{4,0},{1,5},{5,1},{2,6},{6,2},{3,7},{7,3},{8,12},{12,8},{9,1... | collective-permute-start | bytes 786440 | tf_op jit(solution)/shard_map/ppermute | solution.py:330
  27.1 8.8 %copy-start.8 = (bf16[2,8,128,128]{3,2,1,0:T(8,128)(2,1)}, bf16[2,8,128,128]{3,2,1,0:T(8,128)(2,1)S(1)}, u32[]{:S(2)}) copy-start(bf16[2,8,128,128]{3,2,1,0:T(8,128)(2,1)S(1)} %pad_maximum_fusion.refs_0_) | copy-start | bytes 1572868
  27.1 12.7 %collective-permute-start.2 = (bf16[2,8,128,128]{3,2,1,0:T(8,128)(2,1)S(1)}, bf16[2,8,128,128]{3,2,1,0:T(8,128)(2,1)S(1)}, u32[]{:S(2)}, u32[]{:S(2)}) collective-permute-start(bf16[2,8,128,128]{3,2,1,0:T(8,128)(2,1)S(1)} %pad_maximum_fusion.refs_0_), channel_id=1, source_target_pairs={{0,3},{1,2},{2,1},{3,0},{4,7},{5,6},{6,5},{7,4},{8,11},{9,10},{10,... | collective-permute-start | bytes 1572872 | tf_op jit(solution)/shard_map/ppermute | solution.py:334
  30.2 13.0 %collective-permute-start.1 = (bf16[2,8,128,128]{3,2,1,0:T(8,128)(2,1)S(1)}, bf16[2,8,128,128]{3,2,1,0:T(8,128)(2,1)}, u32[]{:S(2)}, u32[]{:S(2)}) collective-permute-start(bf16[2,8,128,128]{3,2,1,0:T(8,128)(2,1)S(1)} %pad_maximum_fusion.refs_0_), channel_id=1, source_target_pairs={{0,1},{1,0},{2,3},{3,2},{4,5},{5,4},{6,7},{7,6},{8,9},{9,8},{10,11... | collective-permute-start | bytes 1572872 | tf_op jit(solution)/shard_map/ppermute | solution.py:334
  32.0 21.4 %copy-start.6 = (s32[32]{0:T(128)S(1)}, s32[32]{0:T(128)}, u32[]{:S(2)}) copy-start(s32[32]{0:T(128)} %order.1) | copy-start | bytes 388
  32.0 19.8 %all-to-all-start = ((bf16[16,272,128]{2,1,0:T(8,128)(2,1)}), bf16[16,272,128]{2,1,0:T(8,128)(2,1)S(1)}, u32[]{:S(2)}, u32[]{:S(2)}) async-start(bf16[16,272,128]{2,1,0:T(8,128)(2,1)} %shard_map.95), calls=%async_computation | async-start | bytes 2228224 | tf_op jit(solution)/shard_map/all_to_all | solution.py:326
  35.9 16.0 %collective-permute-start.5 = (bf16[2,8,128,128]{3,2,1,0:T(8,128)(2,1)S(1)}, bf16[2,8,128,128]{3,2,1,0:T(8,128)(2,1)}, u32[]{:S(2)}, u32[]{:S(2)}) collective-permute-start(bf16[2,8,128,128]{3,2,1,0:T(8,128)(2,1)S(1)} %pad_maximum_fusion.refs_0_), channel_id=1, source_target_pairs={{0,16},{16,0},{1,17},{17,1},{2,18},{18,2},{3,19},{19,3},{4,20},{20... | collective-permute-start | bytes 1572872 | tf_op jit(solution)/shard_map/ppermute | solution.py:330
  39.8 13.6 %copy-start.9 = (bf16[2,8,128,128]{3,2,1,0:T(8,128)(2,1)}, bf16[2,8,128,128]{3,2,1,0:T(8,128)(2,1)S(1)}, u32[]{:S(2)}) copy-start(bf16[2,8,128,128]{3,2,1,0:T(8,128)(2,1)S(1)} %collective-permute-done.2.refs_2_) | copy-start | bytes 1572868
  39.8 7.1 %collective-permute-start.3 = (bf16[8,128,128]{2,1,0:T(8,128)(2,1)S(1)}, bf16[8,128,128]{2,1,0:T(8,128)(2,1)S(1)}, u32[]{:S(2)}, u32[]{:S(2)}) collective-permute-start(bf16[8,128,128]{2,1,0:T(8,128)(2,1)S(1)} %slice_bitcast_fusion.3), channel_id=1, source_target_pairs={{0,1},{1,0},{2,3},{3,2},{4,5},{5,4},{6,7},{7,6},{8,9},{9,8},{10,11... | collective-permute-start | bytes 786440 | tf_op jit(solution)/shard_map/ppermute | solution.py:334
  44.2 7.7 %collective-permute-start.4 = (bf16[8,128,128]{2,1,0:T(8,128)(2,1)S(1)}, bf16[8,128,128]{2,1,0:T(8,128)(2,1)S(1)}, u32[]{:S(2)}, u32[]{:S(2)}) collective-permute-start(bf16[8,128,128]{2,1,0:T(8,128)(2,1)S(1)} %slice_bitcast_fusion.2), channel_id=1, source_target_pairs={{0,3},{1,2},{2,1},{3,0},{4,7},{5,6},{6,5},{7,4},{8,11},{9,10},{10,... | collective-permute-start | bytes 786440 | tf_op jit(solution)/shard_map/ppermute | solution.py:334
  44.3 7.6 %collective-permute-start.7 = (bf16[2,8,128,128]{3,2,1,0:T(8,128)(2,1)S(1)}, bf16[2,8,128,128]{3,2,1,0:T(8,128)(2,1)}, u32[]{:S(2)}, u32[]{:S(2)}) collective-permute-start(bf16[2,8,128,128]{3,2,1,0:T(8,128)(2,1)S(1)} %collective-permute-done.2.refs_2_), channel_id=1, source_target_pairs={{0,16},{16,0},{1,17},{17,1},{2,18},{18,2},{3,19},{19,3},{4,20},{20... | collective-permute-start | bytes 1572872 | tf_op jit(solution)/shard_map/ppermute | solution.py:330
  44.4 9.0 %collective-permute-start.6 = (bf16[2,8,128,128]{3,2,1,0:T(8,128)(2,1)}, bf16[2,8,128,128]{3,2,1,0:T(8,128)(2,1)}, u32[]{:S(2)}, u32[]{:S(2)}) collective-permute-start(bf16[2,8,128,128]{3,2,1,0:T(8,128)(2,1)} %collective-permute-done.1.refs_1_), channel_id=1, source_target_pairs={{0,16},{16,0},{1,17},{17,1},{2,18},{18,2},{3,19},{19,3},{4,20},{20... | collective-permute-start | bytes 1572872 | tf_op jit(solution)/shard_map/ppermute | solution.py:330
  46.9 5.0 %collective-permute-start.8 = (bf16[8,128,128]{2,1,0:T(8,128)(2,1)S(1)}, bf16[8,128,128]{2,1,0:T(8,128)(2,1)S(1)}, u32[]{:S(2)}, u32[]{:S(2)}) collective-permute-start(bf16[8,128,128]{2,1,0:T(8,128)(2,1)S(1)} %collective-permute-done.3.refs_3_), channel_id=1, source_target_pairs={{0,16},{16,0},{1,17},{17,1},{2,18},{18,2},{3,19},{19,3},{4,20},{20... | collective-permute-start | bytes 786440 | tf_op jit(solution)/shard_map/ppermute | solution.py:330
  51.9 1.5 %collective-permute-start.9 = (bf16[8,128,128]{2,1,0:T(8,128)(2,1)S(1)}, bf16[8,128,128]{2,1,0:T(8,128)(2,1)S(1)}, u32[]{:S(2)}, u32[]{:S(2)}) collective-permute-start(bf16[8,128,128]{2,1,0:T(8,128)(2,1)S(1)} %collective-permute-done.4.refs_4_), channel_id=1, source_target_pairs={{0,16},{16,0},{1,17},{17,1},{2,18},{18,2},{3,19},{19,3},{4,20},{20... | collective-permute-start | bytes 786440 | tf_op jit(solution)/shard_map/ppermute | solution.py:330
  51.9 1.5 %copy-start.7 = (bf16[16,272,128]{2,1,0:T(8,128)(2,1)}, bf16[16,272,128]{2,1,0:T(8,128)(2,1)S(1)}, u32[]{:S(2)}) copy-start(bf16[16,272,128]{2,1,0:T(8,128)(2,1)S(1)} %all-to-all-done.qpay) | copy-start | bytes 3342340
  92.5 2.0 %collective-permute-start.12 = (bf16[2,8,128,128]{3,2,1,0:T(8,128)(2,1)S(1)}, bf16[2,8,128,128]{3,2,1,0:T(8,128)(2,1)S(1)}, u32[]{:S(2)}, u32[]{:S(2)}) collective-permute-start(bf16[2,8,128,128]{3,2,1,0:T(8,128)(2,1)S(1)} %get-tuple-element.25), channel_id=1, source_target_pairs={{0,16},{16,0},{1,17},{17,1},{2,18},{18,2},{3,19},{19,3},{4,20},{20... | collective-permute-start | bytes 1572872 | tf_op jit(solution)/shard_map/ppermute | solution.py:330
  92.7 7.1 %collective-permute-start.11 = (bf16[2,8,128,128]{3,2,1,0:T(8,128)(2,1)S(1)}, bf16[2,8,128,128]{3,2,1,0:T(8,128)(2,1)S(1)}, u32[]{:S(2)}, u32[]{:S(2)}) collective-permute-start(bf16[2,8,128,128]{3,2,1,0:T(8,128)(2,1)S(1)} %get-tuple-element.23), channel_id=1, source_target_pairs={{0,16},{16,0},{1,17},{17,1},{2,18},{18,2},{3,19},{19,3},{4,20},{20... | collective-permute-start | bytes 1572872 | tf_op jit(solution)/shard_map/ppermute | solution.py:330
  93.1 31.5 %collective-permute-start.10 = (bf16[2,8,128,128]{3,2,1,0:T(8,128)(2,1)S(1)}, bf16[2,8,128,128]{3,2,1,0:T(8,128)(2,1)S(1)}, u32[]{:S(2)}, u32[]{:S(2)}) collective-permute-start(bf16[2,8,128,128]{3,2,1,0:T(8,128)(2,1)S(1)} %get-tuple-element.21), channel_id=1, source_target_pairs={{0,16},{16,0},{1,17},{17,1},{2,18},{18,2},{3,19},{19,3},{4,20},{20... | collective-permute-start | bytes 1572872 | tf_op jit(solution)/shard_map/ppermute | solution.py:330
  93.2 6.7 %collective-permute-start.15 = (bf16[2,8,128,128]{3,2,1,0:T(8,128)(2,1)S(1)}, bf16[2,8,128,128]{3,2,1,0:T(8,128)(2,1)S(1)}, u32[]{:S(2)}, u32[]{:S(2)}) collective-permute-start(bf16[2,8,128,128]{3,2,1,0:T(8,128)(2,1)S(1)} %get-tuple-element.27), channel_id=1, source_target_pairs={{0,16},{16,0},{1,17},{17,1},{2,18},{18,2},{3,19},{19,3},{4,20},{20... | collective-permute-start | bytes 1572872 | tf_op jit(solution)/shard_map/ppermute | solution.py:330
  94.7 13.0 %collective-permute-start.16 = (bf16[8,128,128]{2,1,0:T(8,128)(2,1)S(1)}, bf16[8,128,128]{2,1,0:T(8,128)(2,1)S(1)}, u32[]{:S(2)}, u32[]{:S(2)}) collective-permute-start(bf16[8,128,128]{2,1,0:T(8,128)(2,1)S(1)} %get-tuple-element.33), channel_id=1, source_target_pairs={{0,1},{1,0},{2,3},{3,2},{4,5},{5,4},{6,7},{7,6},{8,9},{9,8},{10,11... | collective-permute-start | bytes 786440 | tf_op jit(solution)/shard_map/ppermute | solution.py:334
  94.8 11.6 %collective-permute-start.13 = (bf16[8,128,128]{2,1,0:T(8,128)(2,1)S(1)}, bf16[8,128,128]{2,1,0:T(8,128)(2,1)S(1)}, u32[]{:S(2)}, u32[]{:S(2)}) collective-permute-start(bf16[8,128,128]{2,1,0:T(8,128)(2,1)S(1)} %get-tuple-element.34), channel_id=1, source_target_pairs={{0,3},{1,2},{2,1},{3,0},{4,7},{5,6},{6,5},{7,4},{8,11},{9,10},{10,... | collective-permute-start | bytes 786440 | tf_op jit(solution)/shard_map/ppermute | solution.py:334
  106.6 18.0 %collective-permute-start.14 = (bf16[2,8,128,128]{3,2,1,0:T(8,128)(2,1)S(1)}, bf16[2,8,128,128]{3,2,1,0:T(8,128)(2,1)S(1)}, u32[]{:S(2)}, u32[]{:S(2)}) collective-permute-start(bf16[2,8,128,128]{3,2,1,0:T(8,128)(2,1)S(1)} %pad_maximum_fusion.1), channel_id=1, source_target_pairs={{0,1},{1,0},{2,3},{3,2},{4,5},{5,4},{6,7},{7,6},{8,9},{9,8},{10,11... | collective-permute-start | bytes 1572872 | tf_op jit(solution)/shard_map/ppermute | solution.py:334
  107.9 16.7 %collective-permute-start.17 = (bf16[2,8,128,128]{3,2,1,0:T(8,128)(2,1)S(1)}, bf16[2,8,128,128]{3,2,1,0:T(8,128)(2,1)S(1)}, u32[]{:S(2)}, u32[]{:S(2)}) collective-permute-start(bf16[2,8,128,128]{3,2,1,0:T(8,128)(2,1)S(1)} %pad_maximum_fusion.2), channel_id=1, source_target_pairs={{0,3},{1,2},{2,1},{3,0},{4,7},{5,6},{6,5},{7,4},{8,11},{9,10},{10,... | collective-permute-start | bytes 1572872 | tf_op jit(solution)/shard_map/ppermute | solution.py:334

commit v3 on v2

--- a/solution.py
+++ b/solution.py
@@ -17,10 +17,13 @@
 HR = R // 2
 QR = G * HR
 C = 2 * QR
+NC = 8
+W = 4
 SCALE = D**-0.5
 LOG2E = math.log2(math.e)
 EXP_SCALE = SCALE * LOG2E
 HIDDEN = -1e30
+LARGE = 2.0**90
 F32 = jnp.float32
 BF16 = jnp.bfloat16
 AXES = ("z", "core", "xh", "xl", "y")
@@ -68,9 +71,8 @@
 def attention_kernel(order, counts, qpay, *refs):
     pieces = refs[:10]
     dq_out, outs = refs[10], (refs[11:15], refs[15:19])
-    (q_s, do_s, d_s, k_s, v_s, kt_s, qa_s, ga_s, stash, m_blk, m_run, l_run, dk_s, dv_s, dq_s, sem) = (
-        refs[19:]
-    )
+    (plain_c, plain_b, masked_c, masked_b, q_s, do_s, d_s, k_s, v_s, kt_s, qa_s, ga_s) = refs[19:31]
+    m_s, l_s, dk_s, dv_s, dq_s, sem, value_sem = refs[31:]
     n0 = counts[0]
     n1 = counts[1]
     xl = lax.axis_index("xl")
@@ -81,6 +83,7 @@
         return order[span_id(j // 2, xl ^ flip, y ^ dy, j % 2)]
 
     copies = []
+    value_copies = []
     for s in range(16):
         for part, dst in ((0, q_s), (1, do_s)):
             copies.append(
@@ -100,16 +103,21 @@
                 rank = place(flip, dy, j)
                 rows = source.at[pl.ds(2 * j, 2)]
                 copies.append(
-                    pltpu.make_async_copy(rows.at[:, pl.ds(0, R)], k_s.at[rank, :, from_core, :, pl.ds(0, D)], sem)
+                    pltpu.make_async_copy(
+                        rows.at[:, pl.ds(0, R)], k_s.at[rank, :, from_core, :, pl.ds(0, D)], sem
+                    )
                 )
-                copies.append(
-                    pltpu.make_async_copy(rows.at[:, pl.ds(R, R)], v_s.at[rank, :, from_core, :, pl.ds(0, D)], sem)
+                value_copies.append(
+                    pltpu.make_async_copy(
+                        rows.at[:, pl.ds(R, R)],
+                        v_s.at[rank, :, from_core, :, pl.ds(0, D)],
+                        value_sem,
+                    )
                 )
-    for copy in copies:
+    for copy in copies + value_copies:
         copy.start()
-    dk_s[...] = jnp.zeros_like(dk_s)
-    dv_s[...] = jnp.zeros_like(dv_s)
-    beside = lax.broadcasted_iota(jnp.int32, (1, 1, 1, 1, D), 4) < 2
+
+    beside = lax.broadcasted_iota(jnp.int32, (1, 1, 1, 1, D), 4) < 3
     beside = jnp.broadcast_to(beside.astype(F32), (1, 2, 2, R, D)).astype(BF16)
 
     def put_beside(i, carry):
@@ -118,167 +126,217 @@
         return carry
 
     lax.fori_loop(0, NT, put_beside, 0)
-    for copy in copies:
-        copy.wait()
-
-    def block_of(ref, b):
-        return ref[pl.ds(2 * b, 2)].reshape(KB, 2 * D)
-
-    def keys_of(b):
-        return k_s[pl.ds(2 * b, 2), :, :, :, :D].reshape(KB, D)
-
-    def turn(b, carry):
-        kt_s[b] = keys_of(b).T
-        return carry
-
-    lax.fori_loop(0, NT // 2, turn, 0)
-
-    def chunk_step(c, unused):
-        span_q = order[span_id(c // 4, c // 2 % 2, y, c % 2)]
+    dk_s[...] = jnp.zeros_like(dk_s)
+    dv_s[...] = jnp.zeros_like(dv_s)
+    dq_s[...] = jnp.zeros_like(dq_s)
+
+    def span_of(c):
+        return order[span_id(c // 4, c // 2 % 2, y, c % 2)]
+
+    def list_chunk(c, sizes):
+        n_plain, n_masked = sizes
+        span_q = span_of(c)
         first = span_q * SPAN
         has_second = first + (SPAN - 1) >= n1
         all_second = first >= n1
         n_full = span_q // 2
-        lo = jnp.where(has_second, n0 // KB, 0)
-        hi = jnp.where(has_second, (n1 + (KB - 1)) // KB, 0)
-        hi = jnp.minimum(hi, n_full)
-        lo = jnp.minimum(lo, hi)
-        skip_at = (n0 + (KB - 1)) // KB
-        skip = jnp.where(all_second, jnp.maximum(jnp.minimum(n1 // KB, hi) - skip_at, 0), 0)
-        n_masked = hi - lo - skip
-        n_plain = n_full - (hi - lo)
-        count = n_plain + n_masked + 1
-
-        def masked_at(i):
-            at = lo + i
-            return jnp.where(at >= skip_at, at + skip, at)
-
-        def plain_at(i):
-            return jnp.where(i < lo, i, i + (hi - lo))
-
-        def place_at(i):
-            at = jnp.where(i < n_plain, plain_at(i), masked_at(i - n_plain))
-            return jnp.where(i == count - 1, n_full, at)
-
-        q = q_s[c]
-        grads = do_s[c]
-
-        def put_under(ref, *rows):
-            number = lax.broadcasted_iota(jnp.int32, (D, C), 0)
-            block = jnp.zeros((D, C), F32)
-            for i, values in enumerate(rows):
-                block = jnp.where(number == i, values, block)
-            ref[D:] = block.astype(BF16)
-
-        def raw_scores(b):
-            return jnp.dot(keys_of(b), qa_s[:D], preferred_element_type=F32)
-
-        qa_s[:D] = q.T
-        ga_s[:D] = grads.T
+        hi = jnp.minimum(jnp.where(has_second, (n1 + (KB - 1)) // KB, 0), n_full)
+        lo = jnp.minimum(jnp.where(has_second, n0 // KB, 0), hi)
+        skip_at = jnp.where(all_second, (n0 + (KB - 1)) // KB, hi)
+        skip_to = jnp.where(all_second, n1 // KB, 0)
+        masked_c[c] = c
+        masked_b[c] = n_full
+
+        def put_plain(b, n):
+            plain_c[n] = c
+            plain_b[n] = b
+            return n + 1
+
+        def put_masked(b, n):
+            hidden = (b >= skip_at) & (b < skip_to)
+            masked_c[n] = c
+            masked_b[n] = b
+            return jnp.where(hidden, n, n + 1)
+
+        n_plain = lax.fori_loop(0, lo, put_plain, n_plain)
+        n_plain = lax.fori_loop(hi, n_full, put_plain, n_plain)
+        return n_plain, lax.fori_loop(lo, hi, put_masked, n_masked)
+
+    n_plain, n_masked = lax.fori_loop(0, NC, list_chunk, (jnp.int32(0), jnp.int32(NC)))
+    for i in range(W - 1):
+        plain_c[n_plain + i] = NC
+        plain_b[n_plain + i] = 0
+        masked_c[n_masked + i] = NC
+        masked_b[n_masked + i] = 0
+
+    for copy in copies:
+        copy.wait()
+
+    def block_of(ref, b):
+        return ref[pl.ds(2 * b, 2)].reshape(KB, 2 * D)
+
+    def keys_of(b):
+        return k_s[pl.ds(2 * b, 2), :, :, :, :D].reshape(KB, D)
+
+    def turn_keys(b, carry):
+        kt_s[b] = keys_of(b).T
+        return carry
+
+    lax.fori_loop(0, NT // 2, turn_keys, 0)
+
+    def put_under(ref, c, *rows):
+        number = lax.broadcasted_iota(jnp.int32, (D, C), 0)
+        block = jnp.zeros((D, C), F32)
+        for i, values in enumerate(rows):
+            block = jnp.where(number == i, values, block)
+        ref[c, D:] = block.astype(BF16)
+
+    def turn_rows(c, carry):
+        qa_s[c, :D] = q_s[c].T
+        ga_s[c, :D] = do_s[c].T
         halves = [d_s[2 * c + half].astype(F32) for half in range(2)]
         put_under(
             ga_s,
+            c,
             -jnp.concatenate([half[0:1] for half in halves], axis=1),
             -jnp.concatenate([half[1:2] for half in halves], axis=1),
         )
-
-        def seen_at(b):
-            lane = lax.broadcasted_iota(jnp.int32, (1, C), 1)
-            query_pos = first + core * R + xl * HR + (lane // QR) * (2 * R) + lane % HR
-            key_pos = b * KB + lax.broadcasted_iota(jnp.int32, (KB, 1), 0)
-            low = jnp.where(query_pos >= n1, n0, n1)
-            return (key_pos <= query_pos) & ((key_pos < low) | (key_pos >= n1))
-
-        def add_up(weights):
-            return jnp.sum(weights.reshape(KB // 8, 8, C), axis=0)
-
-        def weigh(b, masked):
-            scores = jnp.dot(block_of(k_s, b), qa_s[...], preferred_element_type=F32)
-            if masked:
-                scores = jnp.where(seen_at(b), scores, HIDDEN)
-            weights = jnp.exp2(scores * EXP_SCALE)
-            l_run[...] += add_up(weights)
-            m_blk[b] = m_run[...]
-            stash[b] = weights
-
-        def weigh_diagonal():
-            scores = jnp.where(seen_at(n_full), raw_scores(n_full), HIDDEN)
+        return carry
+
+    lax.fori_loop(0, NC, turn_rows, 0)
+    qa_s[NC, :D] = jnp.zeros((D, C), BF16)
+    put_under(qa_s, NC, jnp.full((1, C), HIDDEN, F32))
+    ga_s[NC] = jnp.zeros((2 * D, C), BF16)
+    q_s[NC] = jnp.zeros((C, D), BF16)
+    do_s[NC] = jnp.zeros((C, D), BF16)
+    l_s[NC] = jnp.zeros((8, C), F32)
+
+    def seen(c, b):
+        lane = lax.broadcasted_iota(jnp.int32, (1, C), 1)
+        row = span_of(jnp.minimum(c, NC - 1)) * SPAN + core * R + xl * HR
+        query_pos = row + (lane // QR) * (2 * R) + lane % HR
+        key_pos = b * KB + lax.broadcasted_iota(jnp.int32, (KB, 1), 0)
+        low = jnp.where(query_pos >= n1, n0, n1)
+        return (key_pos <= query_pos) & ((key_pos < low) | (key_pos >= n1))
+
+    def add_up(weights):
+        return jnp.sum(weights.reshape(KB // 8, 8, C), axis=0)
+
+    def raw_scores(c, b):
+        return jnp.dot(keys_of(b), qa_s[c, :D], preferred_element_type=F32)
+
+    def weights_of(c, b, masked):
+        scores = jnp.dot(block_of(k_s, b), qa_s[c], preferred_element_type=F32)
+        if masked:
+            scores = jnp.where(seen(c, b), scores, HIDDEN)
+        return jnp.exp2(scores * EXP_SCALE)
+
+    def diagonal_step(i, carry):
+        for c in [2 * i + k for k in range(2)]:
+            b = masked_b[c]
+            scores = jnp.where(seen(c, b), raw_scores(c, b), HIDDEN)
             top = jnp.max(scores, axis=0, keepdims=True).astype(BF16).astype(F32)
-            put_under(qa_s, -top)
-            weights = jnp.exp2((scores - top) * EXP_SCALE)
-            l_run[...] = add_up(weights)
-            m_run[...] = top * EXP_SCALE
-            m_blk[n_full] = top * EXP_SCALE
-            stash[n_full] = weights
-
-        def masked_step(i, carry):
-            weigh(masked_at(i), True)
+            put_under(qa_s, c, -top)
+            m_s[c] = top * EXP_SCALE
+            l_s[c] = add_up(jnp.exp2((scores - top) * EXP_SCALE))
+        return carry
+
+    lax.fori_loop(0, NC // 2, diagonal_step, 0)
+
+    def add_weights(items, masked):
+        parts = [add_up(weights_of(c, b, masked)) for c, b in items]
+        for (c, b), part in zip(items, parts):
+            l_s[c] += part
+
+    def masked_stats(i, carry):
+        at = [NC + 2 * i + k for k in range(2)]
+        add_weights([(masked_c[n], masked_b[n]) for n in at], True)
+        return carry
+
+    def plain_stats(i, carry):
+        at = [W * i + k for k in range(W)]
+        add_weights([(plain_c[n], plain_b[n]) for n in at], False)
+        return carry
+
+    lax.fori_loop(0, (n_masked - NC + 1) // 2, masked_stats, 0)
+    lax.fori_loop(0, (n_plain + W - 1) // W, plain_stats, 0)
+
+    @pl.when(jnp.logical_not(jnp.max(l_s[...]) < LARGE))
+    def _():
+        def careful(c, b):
+            scores = jnp.where(seen(c, b), raw_scores(c, b) * EXP_SCALE, HIDDEN)
+            old = m_s[c]
+            top = jnp.maximum(old, jnp.max(scores, axis=0, keepdims=True))
+            l_s[c] = l_s[c] * jnp.exp2(old - top) + add_up(jnp.exp2(scores - top))
+            m_s[c] = top
+
+        def careful_masked(n, carry):
+            c = masked_c[n]
+
+            @pl.when(n < NC)
+            def _():
+                m_s[c] = jnp.full((1, C), HIDDEN, F32)
+                l_s[c] = jnp.zeros((8, C), F32)
+
+            careful(c, masked_b[n])
             return carry
 
-        def plain_pair(i, carry):
-            weigh(plain_at(2 * i), False)
-            weigh(plain_at(2 * i + 1), False)
+        def careful_plain(n, carry):
+            careful(plain_c[n], plain_b[n])
             return carry
 
-        weigh_diagonal()
-        lax.fori_loop(0, n_masked, masked_step, 0)
-        lax.fori_loop(0, n_plain // 2, plain_pair, 0)
-
-        @pl.when(n_plain % 2 == 1)
-        def _():
-            weigh(plain_at(n_plain - 1), False)
-
-        @pl.when(jnp.logical_not(jnp.max(l_run[...]) < 2.0**90))
-        def _():
-            m_run[...] = jnp.full_like(m_run, HIDDEN)
-            l_run[...] = jnp.zeros_like(l_run)
-
-            def careful_step(i, carry):
-                b = place_at(count - 1 - i)
-                scores = jnp.where(seen_at(b), raw_scores(b) * EXP_SCALE, HIDDEN)
-                old = m_run[...]
-                top = jnp.maximum(old, jnp.max(scores, axis=0, keepdims=True))
-                weights = jnp.exp2(scores - top)
-                l_run[...] = l_run[...] * jnp.exp2(old - top) + add_up(weights)
-                m_run[...] = top
-                m_blk[b] = top
-                stash[b] = weights
-                return carry
-
-            lax.fori_loop(0, count, careful_step, 0)
-
-        logsum = m_run[...] + jnp.log2(jnp.sum(l_run[...], axis=0, keepdims=True))
-        dq_s[...] = jnp.zeros_like(dq_s)
-
-        def grad_block(b):
-            weights = stash[b] * jnp.exp2(m_blk[b] - logsum)
-            above = jnp.dot(block_of(v_s, b), ga_s[...], preferred_element_type=F32)
-            score_grad = (weights * above).astype(BF16)
+        lax.fori_loop(0, n_masked, careful_masked, 0)
+        lax.fori_loop(0, n_plain, careful_plain, 0)
+
+    def put_logsum(c, carry):
+        logsum = m_s[c] + jnp.log2(jnp.sum(l_s[c], axis=0, keepdims=True))
+        rest = logsum * (1.0 / EXP_SCALE)
+        rows = []
+        for _ in range(3):
+            part = rest.astype(BF16).astype(F32)
+            rows.append(-part)
+            rest = rest - part
+        put_under(qa_s, c, *rows)
+        return carry
+
+    lax.fori_loop(0, NC, put_logsum, 0)
+    for copy in value_copies:
+        copy.wait()
+
+    def grad_step(items, masked):
+        weights = [weights_of(c, b, masked) for c, b in items]
+        above = [
+            jnp.dot(block_of(v_s, b), ga_s[c], preferred_element_type=F32) for c, b in items
+        ]
+        score_grads = [(w * p).astype(BF16) for w, p in zip(weights, above)]
+        for (c, b), w, score_grad in zip(items, weights, score_grads):
             for ref, term in (
-                (dv_s, jnp.dot(weights.astype(BF16), grads, preferred_element_type=F32)),
-                (dk_s, jnp.dot(score_grad, q, preferred_element_type=F32)),
+                (dv_s, jnp.dot(w.astype(BF16), do_s[c], preferred_element_type=F32)),
+                (dk_s, jnp.dot(score_grad, q_s[c], preferred_element_type=F32)),
             ):
                 ref[pl.ds(2 * b, 2)] += term.reshape(2, 2, 2, R, D)
-            return jnp.dot(kt_s[b], score_grad, preferred_element_type=F32)
-
-        def grad_pair(i, carry):
-            first_term = grad_block(place_at(2 * i))
-            second_term = grad_block(place_at(2 * i + 1))
-            dq_s[...] += first_term + second_term
-            return carry
-
-        lax.fori_loop(0, count // 2, grad_pair, 0)
-
-        @pl.when(count % 2 == 1)
-        def _():
-            dq_s[...] += grad_block(n_full)
-
-        dq = (dq_s[...] * SCALE).T.astype(BF16)
+            dq_s[c] += jnp.dot(kt_s[b], score_grad, preferred_element_type=F32)
+
+    def masked_grads(i, carry):
+        at = [2 * i + k for k in range(2)]
+        grad_step([(masked_c[n], masked_b[n]) for n in at], True)
+        return carry
+
+    def plain_grads(i, carry):
+        at = [W * i + k for k in range(W)]
+        grad_step([(plain_c[n], plain_b[n]) for n in at], False)
+        return carry
+
+    lax.fori_loop(0, (n_masked + 1) // 2, masked_grads, 0)
+    lax.fori_loop(0, (n_plain + W - 1) // W, plain_grads, 0)
+
+    def finish(c, carry):
+        dq = (dq_s[c] * SCALE).T.astype(BF16)
         dq_out[2 * c] = dq[:QR]
         dq_out[2 * c + 1] = dq[QR:]
-        return unused
-
-    lax.fori_loop(0, 8, chunk_step, 0)
+        return carry
+
+    lax.fori_loop(0, NC, finish, 0)
 
     for from_core, group in ((core, outs[0]), (1 - core, outs[1])):
         for dy, out in zip((0, 1, 3, 2), group):
@@ -400,21 +458,24 @@
         in_specs=[pl.BlockSpec(memory_space=pltpu.SMEM)] * 2
         + [pl.BlockSpec(memory_space=pl.ANY)] * 11,
         scratch_shapes=[
-            pltpu.VMEM((8, C, D), BF16),
-            pltpu.VMEM((8, C, D), BF16),
+            pltpu.SMEM((NC * NT // 2 + W,), jnp.int32),
+            pltpu.SMEM((NC * NT // 2 + W,), jnp.int32),
+            pltpu.SMEM((NC * NT // 2 + NC + W,), jnp.int32),
+            pltpu.SMEM((NC * NT // 2 + NC + W,), jnp.int32),
+            pltpu.VMEM((NC + 1, C, D), BF16),
+            pltpu.VMEM((NC + 1, C, D), BF16),
             pltpu.VMEM((16, 16, D), BF16),
             pltpu.VMEM((NT, 2, 2, R, 2 * D), BF16),
             pltpu.VMEM((NT, 2, 2, R, 2 * D), BF16),
             pltpu.VMEM((NT // 2, D, KB), BF16),
-            pltpu.VMEM((2 * D, C), BF16),
-            pltpu.VMEM((2 * D, C), BF16),
-            pltpu.VMEM((NT // 2, KB, C), F32),
-            pltpu.VMEM((NT // 2, 1, C), F32),
-            pltpu.VMEM((1, C), F32),
-            pltpu.VMEM((8, C), F32),
+            pltpu.VMEM((NC + 1, 2 * D, C), BF16),
+            pltpu.VMEM((NC + 1, 2 * D, C), BF16),
+            pltpu.VMEM((NC, 1, C), F32),
+            pltpu.VMEM((NC + 1, 8, C), F32),
             pltpu.VMEM((NT, 2, 2, R, D), F32),
             pltpu.VMEM((NT, 2, 2, R, D), F32),
-            pltpu.VMEM((D, C), F32),
+            pltpu.VMEM((NC + 1, D, C), F32),
+            pltpu.SemaphoreType.DMA,
             pltpu.SemaphoreType.DMA,
         ],
         compiler_params=pltpu.CompilerParams(vmem_limit_bytes=48 << 20),

time: 140 us -> 134 us (0.957)
  Pallas kernels: 43.2 us -> 37.9 us
  waiting for transfers between devices: 28.7 us -> 31.4 us
  starting transfers between devices: 18.5 us -> 16.5 us
    pallas_call x1, Pallas kernels: 39.1 us -> 33.8 us  [body(): pl.pallas_call(attention_kernel, out_shape=[jax.ShapeDtypeStruct((16, QR,...]
    ppermute x8, waiting for transfers between devices: 20.3 us -> 22.9 us  [swap(): return lax.ppermute(array, 'y', [(i, i ^ distance) for i in range(4)])]
    ppermute x8, starting transfers between devices: 12.3 us -> 10.3 us  [swap(): return lax.ppermute(array, 'y', [(i, i ^ distance) for i in range(4)])]
where the time goes in v3:
time: 134 us; the launch traced here: 135 us
  blocking collectives  43.5 us (32%)
  Pallas kernels  37.9 us (28%)
  waiting for transfers between devices  31.4 us (23%)
  starting transfers between devices  16.5 us (12%)
  local copies, waits for them, and re-layouts  3.73 us (3%)
    all_to_all x3, blocking collectives, exchange(): return lax.all_to_all(array, axes, split_axis=0, concat_axis=0, tiled=True)  43.5 us
    pallas_call x1, Pallas kernels, body(): pl.pallas_call(attention_kernel, out_shape=[jax.ShapeDtypeStruct((16, QR,...  33.8 us
    ppermute x8, waiting for transfers between devices, swap(): return lax.ppermute(array, 'y', [(i, i ^ distance) for i in range(4)])  22.9 us
    ppermute x8, starting transfers between devices, swap(): return lax.ppermute(array, 'y', [(i, i ^ distance) for i in range(4)])  10.3 us
    ppermute x10, waiting for transfers between devices, flip(): return lax.ppermute(array, axis, [(0, 1), (1, 0)])  8.42 us
    all_to_all x1, starting transfers between devices, exchange(): return lax.all_to_all(array, axes, split_axis=0, concat_axis=0, tiled=True)  3.83 us
    pallas_call x3, Pallas kernels, on_vmem(): pl.pallas_call(kernel, out_shape=outs, compiler_params=pltpu.CompilerPara...  3.41 us
    unnamed x20, local copies, waits for them, and re-layouts  2.7 us
  transfers between devices with their start and end apart: 19, of which 8 were waited for; matrix products, arithmetic and copies ran while one was open for 1% of the time, Pallas kernels for 1%

profile of v3, /device:TPU:0, one launch (start us, length us, event | category | flops | bytes accessed | tf_op | source)
XLA Modules:
  0.0 134.5 jit_solution(14534477028331008311)
XLA Ops:
  0.7 1.0 copy-done.3
  1.7 0.9 copy-done.4
  2.6 0.8 copy-done.5
  3.3 0.7 shard_map.94
  4.1 16.4 %all_to_all.20 = bf16[8,128,128]{2,1,0:T(8,128)(2,1)S(1)} all-to-all(bf16[8,128,128]{2,1,0:T(8,128)(2,1)S(1)} %get-tuple-element.19), channel_id=1, replica_groups=mesh['z'=4,'core'=2,'xh'=2,'xl'=2,'y'=4] {'xh','z'}, dimensions={0} | all-to-all | bytes 524288 | tf_op jit(solution)/shard_map/all_to_all | solution.py:384
  20.5 0.6 collective-permute-start
  21.1 6.0 %collective-permute-done = bf16[8,128,128]{2,1,0:T(8,128)(2,1)S(1)} collective-permute-done((bf16[8,128,128]{2,1,0:T(8,128)(2,1)S(1)}, bf16[8,128,128]{2,1,0:T(8,128)(2,1)S(1)}, u32[]{:S(2)}, u32[]{:S(2)}) %collective-permute-start) | collective-permute-done | bytes 262176 | tf_op jit(solution)/shard_map/ppermute | solution.py:388
  27.1 0.1 pad_maximum_fusion.refs_0_
  27.1 0.0 copy-start.8
  27.1 3.1 %collective-permute-start.2 = (bf16[2,8,128,128]{3,2,1,0:T(8,128)(2,1)S(1)}, bf16[2,8,128,128]{3,2,1,0:T(8,128)(2,1)S(1)}, u32[]{:S(2)}, u32[]{:S(2)}) collective-permute-start(bf16[2,8,128,128]{3,2,1,0:T(8,128)(2,1)S(1)} %pad_maximum_fusion.refs_0_), channel_id=1, source_target_pairs={{0,3},{1,2},{2,1},{3,0},{4,7},{5,6},{6,5},{7,4},{8,11},{9,10},{10,... | collective-permute-start | bytes 1572872 | tf_op jit(solution)/shard_map/ppermute | solution.py:392
  30.2 0.1 collective-permute-start.1
  30.4 1.7 %shard_map.95 = bf16[16,272,128]{2,1,0:T(8,128)(2,1)} custom-call(bf16[64,4096]{1,0:T(8,128)(2,1)S(1)} %copy-done, bf16[64,4096]{1,0:T(8,128)(2,1)S(1)} %copy-done.1, bf16[64,4096]{1,0:T(8,128)(2,1)S(1)} %copy-done.2), custom_call_target="tpu_custom_call" | custom-call | tf_op jit(solution)/shard_map/pallas_call | solution.py:376
  32.0 3.8 %all-to-all-start = ((bf16[16,272,128]{2,1,0:T(8,128)(2,1)}), bf16[16,272,128]{2,1,0:T(8,128)(2,1)S(1)}, u32[]{:S(2)}, u32[]{:S(2)}) async-start(bf16[16,272,128]{2,1,0:T(8,128)(2,1)} %shard_map.95), calls=%async_computation | async-start | bytes 2228224 | tf_op jit(solution)/shard_map/all_to_all | solution.py:384
  35.9 0.1 collective-permute-start.5
  36.0 3.8 %collective-permute-done.2.refs_2_ = bf16[2,8,128,128]{3,2,1,0:T(8,128)(2,1)S(1)} collective-permute-done((bf16[2,8,128,128]{3,2,1,0:T(8,128)(2,1)S(1)}, bf16[2,8,128,128]{3,2,1,0:T(8,128)(2,1)S(1)}, u32[]{:S(2)}, u32[]{:S(2)}) %collective-permute-start.2) | collective-permute-done | bytes 524320 | tf_op jit(solution)/shard_map/ppermute | solution.py:392
  39.8 0.4 collective-permute-start.3
  40.2 3.0 %collective-permute-done.1.refs_1_ = bf16[2,8,128,128]{3,2,1,0:T(8,128)(2,1)} collective-permute-done((bf16[2,8,128,128]{3,2,1,0:T(8,128)(2,1)S(1)}, bf16[2,8,128,128]{3,2,1,0:T(8,128)(2,1)}, u32[]{:S(2)}, u32[]{:S(2)}) %collective-permute-start.1) | collective-permute-done | bytes 524320 | tf_op jit(solution)/shard_map/ppermute | solution.py:392
  43.2 1.0 slice_bitcast_fusion.2
  44.2 0.1 collective-permute-start.4
  44.3 0.1 collective-permute-start.7
  44.4 0.5 collective-permute-start.6
  44.9 2.0 %collective-permute-done.3.refs_3_ = bf16[8,128,128]{2,1,0:T(8,128)(2,1)S(1)} collective-permute-done((bf16[8,128,128]{2,1,0:T(8,128)(2,1)S(1)}, bf16[8,128,128]{2,1,0:T(8,128)(2,1)S(1)}, u32[]{:S(2)}, u32[]{:S(2)}) %collective-permute-start.3) | collective-permute-done | bytes 262176 | tf_op jit(solution)/shard_map/ppermute | solution.py:392
  46.9 0.0 collective-permute-start.8
  46.9 5.0 %collective-permute-done.4.refs_4_ = bf16[8,128,128]{2,1,0:T(8,128)(2,1)S(1)} collective-permute-done((bf16[8,128,128]{2,1,0:T(8,128)(2,1)S(1)}, bf16[8,128,128]{2,1,0:T(8,128)(2,1)S(1)}, u32[]{:S(2)}, u32[]{:S(2)}) %collective-permute-start.4) | collective-permute-done | bytes 262176 | tf_op jit(solution)/shard_map/ppermute | solution.py:392
  51.9 0.0 collective-permute-start.9
  51.9 0.0 collective-permute-done.5.refs_5_
  51.9 1.5 %collective-permute-done.9.refs_9_ = bf16[8,128,128]{2,1,0:T(8,128)(2,1)S(1)} collective-permute-done((bf16[8,128,128]{2,1,0:T(8,128)(2,1)S(1)}, bf16[8,128,128]{2,1,0:T(8,128)(2,1)S(1)}, u32[]{:S(2)}, u32[]{:S(2)}) %collective-permute-start.9) | collective-permute-done | bytes 262176 | tf_op jit(solution)/shard_map/ppermute | solution.py:388
  53.4 33.8 %shard_map.96 = (bf16[16,128,128]{2,1,0:T(8,128)(2,1)S(1)}, bf16[2,8,128,128]{3,2,1,0:T(8,128)(2,1)S(1)}, bf16[2,8,128,128]{3,2,1,0:T(8,128)(2,1)S(1)}, bf16[2,8...) custom-call(s32[32]{0:T(128)S(1)} %copy-done.6, ...), custom_call_target="tpu_custom_call" | custom-call | tf_op jit(solution)/shard_map/pallas_call | solution.py:455
  87.2 0.2 collective-permute-start.12
  87.5 0.4 collective-permute-start.11
  87.8 0.1 collective-permute-start.10
  88.0 0.4 collective-permute-start.15
  88.3 0.9 collective-permute-done.12
  89.2 0.1 add_convert_fusion
  89.4 6.1 %collective-permute-start.16 = (bf16[8,128,128]{2,1,0:T(8,128)(2,1)S(1)}, bf16[8,128,128]{2,1,0:T(8,128)(2,1)S(1)}, u32[]{:S(2)}, u32[]{:S(2)}) collective-permute-start(bf16[8,128,128]{2,1,0:T(8,128)(2,1)S(1)} %get-tuple-element.33), channel_id=1, source_target_pairs={{0,1},{1,0},{2,3},{3,2},{4,5},{5,4},{6,7},{7,6},{8,9},{9,8},{10,11... | collective-permute-start | bytes 786440 | tf_op jit(solution)/shard_map/ppermute | solution.py:392
  95.6 0.1 add_convert_fusion.2
  95.6 0.1 add_convert_fusion.1
  95.7 9.1 %collective-permute-done.13 = bf16[8,128,128]{2,1,0:T(8,128)(2,1)S(1)} collective-permute-done((bf16[8,128,128]{2,1,0:T(8,128)(2,1)S(1)}, bf16[8,128,128]{2,1,0:T(8,128)(2,1)S(1)}, u32[]{:S(2)}, u32[]{:S(2)}) %collective-permute-start.13) | collective-permute-done | bytes 262176 | tf_op jit(solution)/shard_map/ppermute | solution.py:392
  104.8 0.1 fusion.2
  104.9 0.1 pad_maximum_fusion.1
  105.0 0.1 collective-permute-start.14
  105.1 0.1 fusion.3
  105.2 0.1 pad_maximum_fusion.2
  105.3 0.4 collective-permute-start.17
  105.6 13.8 %all_to_all.21.dq = bf16[16,128,128]{2,1,0:T(8,128)(2,1)S(1)} all-to-all(bf16[16,128,128]{2,1,0:T(8,128)(2,1)S(1)} %get-tuple-element.28), channel_id=1, replica_groups=mesh['z'=4,'core'=2,'xh'=2,'xl'=2,'y'=4] {'xh','xl','z'}, dimensions={0} | all-to-all | bytes 1048576 | tf_op jit(solution)/shard_map/all_to_all | solution.py:384
  119.4 1.0 shard_map.97
  120.4 13.3 %all_to_all.22.got = bf16[16,128,128]{2,1,0:T(8,128)(2,1)S(1)} all-to-all(bf16[16,128,128]{2,1,0:T(8,128)(2,1)S(1)} %bitcast.28), channel_id=1, replica_groups=mesh['z'=4,'core'=2,'xh'=2,'xl'=2,'y'=4] {'xh','xl','z'}, dimensions={0} | all-to-all | bytes 1048576 | tf_op jit(solution)/shard_map/all_to_all | solution.py:384
  133.7 0.8 shard_map.98
  (29 shorter events, 0.1 us)
Async XLA Ops:
  0.6 29.7 %copy-start.2 = (bf16[64,4096]{1,0:T(8,128)(2,1)S(1)}, bf16[64,4096]{1,0:T(8,128)(2,1)}, u32[]{:S(2)}) copy-start(bf16[64,4096]{1,0:T(8,128)(2,1)} %grads.1) | copy-start | bytes 1572868
  0.6 29.7 %copy-start.1 = (bf16[64,4096]{1,0:T(8,128)(2,1)S(1)}, bf16[64,4096]{1,0:T(8,128)(2,1)}, u32[]{:S(2)}) copy-start(bf16[64,4096]{1,0:T(8,128)(2,1)} %saved.1) | copy-start | bytes 1572868
  0.7 29.7 %copy-start = (bf16[64,4096]{1,0:T(8,128)(2,1)S(1)}, bf16[64,4096]{1,0:T(8,128)(2,1)}, u32[]{:S(2)}) copy-start(bf16[64,4096]{1,0:T(8,128)(2,1)} %queries.1) | copy-start | bytes 1572868
  0.7 1.0 copy-start.3
  1.7 0.9 copy-start.4
  2.6 0.8 copy-start.5
  20.5 6.6 %collective-permute-start = (bf16[8,128,128]{2,1,0:T(8,128)(2,1)S(1)}, bf16[8,128,128]{2,1,0:T(8,128)(2,1)S(1)}, u32[]{:S(2)}, u32[]{:S(2)}) collective-permute-start(bf16[8,128,128]{2,1,0:T(8,128)(2,1)S(1)} %all_to_all.20), channel_id=1, source_target_pairs={{0,4},{4,0},{1,5},{5,1},{2,6},{6,2},{3,7},{7,3},{8,12},{12,8},{9,1... | collective-permute-start | bytes 786440 | tf_op jit(solution)/shard_map/ppermute | solution.py:388
  27.1 8.8 %copy-start.8 = (bf16[2,8,128,128]{3,2,1,0:T(8,128)(2,1)}, bf16[2,8,128,128]{3,2,1,0:T(8,128)(2,1)S(1)}, u32[]{:S(2)}) copy-start(bf16[2,8,128,128]{3,2,1,0:T(8,128)(2,1)S(1)} %pad_maximum_fusion.refs_0_) | copy-start | bytes 1572868
  27.1 12.7 %collective-permute-start.2 = (bf16[2,8,128,128]{3,2,1,0:T(8,128)(2,1)S(1)}, bf16[2,8,128,128]{3,2,1,0:T(8,128)(2,1)S(1)}, u32[]{:S(2)}, u32[]{:S(2)}) collective-permute-start(bf16[2,8,128,128]{3,2,1,0:T(8,128)(2,1)S(1)} %pad_maximum_fusion.refs_0_), channel_id=1, source_target_pairs={{0,3},{1,2},{2,1},{3,0},{4,7},{5,6},{6,5},{7,4},{8,11},{9,10},{10,... | collective-permute-start | bytes 1572872 | tf_op jit(solution)/shard_map/ppermute | solution.py:392
  30.2 13.0 %collective-permute-start.1 = (bf16[2,8,128,128]{3,2,1,0:T(8,128)(2,1)S(1)}, bf16[2,8,128,128]{3,2,1,0:T(8,128)(2,1)}, u32[]{:S(2)}, u32[]{:S(2)}) collective-permute-start(bf16[2,8,128,128]{3,2,1,0:T(8,128)(2,1)S(1)} %pad_maximum_fusion.refs_0_), channel_id=1, source_target_pairs={{0,1},{1,0},{2,3},{3,2},{4,5},{5,4},{6,7},{7,6},{8,9},{9,8},{10,11... | collective-permute-start | bytes 1572872 | tf_op jit(solution)/shard_map/ppermute | solution.py:392
  32.0 21.4 %copy-start.6 = (s32[32]{0:T(128)S(1)}, s32[32]{0:T(128)}, u32[]{:S(2)}) copy-start(s32[32]{0:T(128)} %order.1) | copy-start | bytes 388
  32.0 19.8 %all-to-all-start = ((bf16[16,272,128]{2,1,0:T(8,128)(2,1)}), bf16[16,272,128]{2,1,0:T(8,128)(2,1)S(1)}, u32[]{:S(2)}, u32[]{:S(2)}) async-start(bf16[16,272,128]{2,1,0:T(8,128)(2,1)} %shard_map.95), calls=%async_computation | async-start | bytes 2228224 | tf_op jit(solution)/shard_map/all_to_all | solution.py:384
  35.9 16.0 %collective-permute-start.5 = (bf16[2,8,128,128]{3,2,1,0:T(8,128)(2,1)S(1)}, bf16[2,8,128,128]{3,2,1,0:T(8,128)(2,1)}, u32[]{:S(2)}, u32[]{:S(2)}) collective-permute-start(bf16[2,8,128,128]{3,2,1,0:T(8,128)(2,1)S(1)} %pad_maximum_fusion.refs_0_), channel_id=1, source_target_pairs={{0,16},{16,0},{1,17},{17,1},{2,18},{18,2},{3,19},{19,3},{4,20},{20... | collective-permute-start | bytes 1572872 | tf_op jit(solution)/shard_map/ppermute | solution.py:388
  39.8 13.6 %copy-start.9 = (bf16[2,8,128,128]{3,2,1,0:T(8,128)(2,1)}, bf16[2,8,128,128]{3,2,1,0:T(8,128)(2,1)S(1)}, u32[]{:S(2)}) copy-start(bf16[2,8,128,128]{3,2,1,0:T(8,128)(2,1)S(1)} %collective-permute-done.2.refs_2_) | copy-start | bytes 1572868
  39.8 7.1 %collective-permute-start.3 = (bf16[8,128,128]{2,1,0:T(8,128)(2,1)S(1)}, bf16[8,128,128]{2,1,0:T(8,128)(2,1)S(1)}, u32[]{:S(2)}, u32[]{:S(2)}) collective-permute-start(bf16[8,128,128]{2,1,0:T(8,128)(2,1)S(1)} %slice_bitcast_fusion.3), channel_id=1, source_target_pairs={{0,1},{1,0},{2,3},{3,2},{4,5},{5,4},{6,7},{7,6},{8,9},{9,8},{10,11... | collective-permute-start | bytes 786440 | tf_op jit(solution)/shard_map/ppermute | solution.py:392
  44.2 7.7 %collective-permute-start.4 = (bf16[8,128,128]{2,1,0:T(8,128)(2,1)S(1)}, bf16[8,128,128]{2,1,0:T(8,128)(2,1)S(1)}, u32[]{:S(2)}, u32[]{:S(2)}) collective-permute-start(bf16[8,128,128]{2,1,0:T(8,128)(2,1)S(1)} %slice_bitcast_fusion.2), channel_id=1, source_target_pairs={{0,3},{1,2},{2,1},{3,0},{4,7},{5,6},{6,5},{7,4},{8,11},{9,10},{10,... | collective-permute-start | bytes 786440 | tf_op jit(solution)/shard_map/ppermute | solution.py:392
  44.3 7.6 %collective-permute-start.7 = (bf16[2,8,128,128]{3,2,1,0:T(8,128)(2,1)S(1)}, bf16[2,8,128,128]{3,2,1,0:T(8,128)(2,1)}, u32[]{:S(2)}, u32[]{:S(2)}) collective-permute-start(bf16[2,8,128,128]{3,2,1,0:T(8,128)(2,1)S(1)} %collective-permute-done.2.refs_2_), channel_id=1, source_target_pairs={{0,16},{16,0},{1,17},{17,1},{2,18},{18,2},{3,19},{19,3},{4,20},{20... | collective-permute-start | bytes 1572872 | tf_op jit(solution)/shard_map/ppermute | solution.py:388
  44.4 9.0 %collective-permute-start.6 = (bf16[2,8,128,128]{3,2,1,0:T(8,128)(2,1)}, bf16[2,8,128,128]{3,2,1,0:T(8,128)(2,1)}, u32[]{:S(2)}, u32[]{:S(2)}) collective-permute-start(bf16[2,8,128,128]{3,2,1,0:T(8,128)(2,1)} %collective-permute-done.1.refs_1_), channel_id=1, source_target_pairs={{0,16},{16,0},{1,17},{17,1},{2,18},{18,2},{3,19},{19,3},{4,20},{20... | collective-permute-start | bytes 1572872 | tf_op jit(solution)/shard_map/ppermute | solution.py:388
  46.9 5.0 %collective-permute-start.8 = (bf16[8,128,128]{2,1,0:T(8,128)(2,1)S(1)}, bf16[8,128,128]{2,1,0:T(8,128)(2,1)S(1)}, u32[]{:S(2)}, u32[]{:S(2)}) collective-permute-start(bf16[8,128,128]{2,1,0:T(8,128)(2,1)S(1)} %collective-permute-done.3.refs_3_), channel_id=1, source_target_pairs={{0,16},{16,0},{1,17},{17,1},{2,18},{18,2},{3,19},{19,3},{4,20},{20... | collective-permute-start | bytes 786440 | tf_op jit(solution)/shard_map/ppermute | solution.py:388
  51.9 1.5 %collective-permute-start.9 = (bf16[8,128,128]{2,1,0:T(8,128)(2,1)S(1)}, bf16[8,128,128]{2,1,0:T(8,128)(2,1)S(1)}, u32[]{:S(2)}, u32[]{:S(2)}) collective-permute-start(bf16[8,128,128]{2,1,0:T(8,128)(2,1)S(1)} %collective-permute-done.4.refs_4_), channel_id=1, source_target_pairs={{0,16},{16,0},{1,17},{17,1},{2,18},{18,2},{3,19},{19,3},{4,20},{20... | collective-permute-start | bytes 786440 | tf_op jit(solution)/shard_map/ppermute | solution.py:388
  51.9 1.5 %copy-start.7 = (bf16[16,272,128]{2,1,0:T(8,128)(2,1)}, bf16[16,272,128]{2,1,0:T(8,128)(2,1)S(1)}, u32[]{:S(2)}) copy-start(bf16[16,272,128]{2,1,0:T(8,128)(2,1)S(1)} %all-to-all-done.qpay) | copy-start | bytes 3342340
  87.2 2.0 %collective-permute-start.12 = (bf16[2,8,128,128]{3,2,1,0:T(8,128)(2,1)S(1)}, bf16[2,8,128,128]{3,2,1,0:T(8,128)(2,1)S(1)}, u32[]{:S(2)}, u32[]{:S(2)}) collective-permute-start(bf16[2,8,128,128]{3,2,1,0:T(8,128)(2,1)S(1)} %get-tuple-element.25), channel_id=1, source_target_pairs={{0,16},{16,0},{1,17},{17,1},{2,18},{18,2},{3,19},{19,3},{4,20},{20... | collective-permute-start | bytes 1572872 | tf_op jit(solution)/shard_map/ppermute | solution.py:388
  87.5 8.1 %collective-permute-start.11 = (bf16[2,8,128,128]{3,2,1,0:T(8,128)(2,1)S(1)}, bf16[2,8,128,128]{3,2,1,0:T(8,128)(2,1)S(1)}, u32[]{:S(2)}, u32[]{:S(2)}) collective-permute-start(bf16[2,8,128,128]{3,2,1,0:T(8,128)(2,1)S(1)} %get-tuple-element.23), channel_id=1, source_target_pairs={{0,16},{16,0},{1,17},{17,1},{2,18},{18,2},{3,19},{19,3},{4,20},{20... | collective-permute-start | bytes 1572872 | tf_op jit(solution)/shard_map/ppermute | solution.py:388
  87.8 31.6 %collective-permute-start.10 = (bf16[2,8,128,128]{3,2,1,0:T(8,128)(2,1)S(1)}, bf16[2,8,128,128]{3,2,1,0:T(8,128)(2,1)S(1)}, u32[]{:S(2)}, u32[]{:S(2)}) collective-permute-start(bf16[2,8,128,128]{3,2,1,0:T(8,128)(2,1)S(1)} %get-tuple-element.21), channel_id=1, source_target_pairs={{0,16},{16,0},{1,17},{17,1},{2,18},{18,2},{3,19},{19,3},{4,20},{20... | collective-permute-start | bytes 1572872 | tf_op jit(solution)/shard_map/ppermute | solution.py:388
  88.0 7.7 %collective-permute-start.15 = (bf16[2,8,128,128]{3,2,1,0:T(8,128)(2,1)S(1)}, bf16[2,8,128,128]{3,2,1,0:T(8,128)(2,1)S(1)}, u32[]{:S(2)}, u32[]{:S(2)}) collective-permute-start(bf16[2,8,128,128]{3,2,1,0:T(8,128)(2,1)S(1)} %get-tuple-element.27), channel_id=1, source_target_pairs={{0,16},{16,0},{1,17},{17,1},{2,18},{18,2},{3,19},{19,3},{4,20},{20... | collective-permute-start | bytes 1572872 | tf_op jit(solution)/shard_map/ppermute | solution.py:388
  89.4 15.7 %collective-permute-start.16 = (bf16[8,128,128]{2,1,0:T(8,128)(2,1)S(1)}, bf16[8,128,128]{2,1,0:T(8,128)(2,1)S(1)}, u32[]{:S(2)}, u32[]{:S(2)}) collective-permute-start(bf16[8,128,128]{2,1,0:T(8,128)(2,1)S(1)} %get-tuple-element.33), channel_id=1, source_target_pairs={{0,1},{1,0},{2,3},{3,2},{4,5},{5,4},{6,7},{7,6},{8,9},{9,8},{10,11... | collective-permute-start | bytes 786440 | tf_op jit(solution)/shard_map/ppermute | solution.py:392
  95.6 9.3 %collective-permute-start.13 = (bf16[8,128,128]{2,1,0:T(8,128)(2,1)S(1)}, bf16[8,128,128]{2,1,0:T(8,128)(2,1)S(1)}, u32[]{:S(2)}, u32[]{:S(2)}) collective-permute-start(bf16[8,128,128]{2,1,0:T(8,128)(2,1)S(1)} %get-tuple-element.34), channel_id=1, source_target_pairs={{0,3},{1,2},{2,1},{3,0},{4,7},{5,6},{6,5},{7,4},{8,11},{9,10},{10,... | collective-permute-start | bytes 786440 | tf_op jit(solution)/shard_map/ppermute | solution.py:392
  105.0 14.4 %collective-permute-start.14 = (bf16[2,8,128,128]{3,2,1,0:T(8,128)(2,1)S(1)}, bf16[2,8,128,128]{3,2,1,0:T(8,128)(2,1)S(1)}, u32[]{:S(2)}, u32[]{:S(2)}) collective-permute-start(bf16[2,8,128,128]{3,2,1,0:T(8,128)(2,1)S(1)} %pad_maximum_fusion.1), channel_id=1, source_target_pairs={{0,1},{1,0},{2,3},{3,2},{4,5},{5,4},{6,7},{7,6},{8,9},{9,8},{10,11... | collective-permute-start | bytes 1572872 | tf_op jit(solution)/shard_map/ppermute | solution.py:392
  105.3 14.2 %collective-permute-start.17 = (bf16[2,8,128,128]{3,2,1,0:T(8,128)(2,1)S(1)}, bf16[2,8,128,128]{3,2,1,0:T(8,128)(2,1)S(1)}, u32[]{:S(2)}, u32[]{:S(2)}) collective-permute-start(bf16[2,8,128,128]{3,2,1,0:T(8,128)(2,1)S(1)} %pad_maximum_fusion.2), channel_id=1, source_target_pairs={{0,3},{1,2},{2,1},{3,0},{4,7},{5,6},{6,5},{7,4},{8,11},{9,10},{10,... | collective-permute-start | bytes 1572872 | tf_op jit(solution)/shard_map/ppermute | solution.py:392

commit v4 on v3

--- a/solution.py
+++ b/solution.py
@@ -1,6 +1,3 @@
-import functools
-import math
-
 import jax
 import jax.numpy as jnp
 from jax import lax
@@ -11,45 +8,52 @@
 D = 128
 G = 4
 R = 64
+HR = R // 2
 SPAN = 256
+NT = 32
 KB = 2 * SPAN
-NT = 32
-HR = R // 2
 QR = G * HR
 C = 2 * QR
 NC = 8
 W = 4
 SCALE = D**-0.5
-LOG2E = math.log2(math.e)
-EXP_SCALE = SCALE * LOG2E
 HIDDEN = -1e30
 LARGE = 2.0**90
 F32 = jnp.float32
 BF16 = jnp.bfloat16
 AXES = ("z", "core", "xh", "xl", "y")
-HEADS = ("xh", "z")
 SPREAD = ("xh", "xl", "z")
 NT_DIMS = (((1,), (1,)), ((), ()))
+
+
+def spread_to(g, xl):
+    return (g // 4 * 2 + xl) * 4 + g % 4
+
+
+def head_columns(g, h):
+    return slice((g * G + h) * D, (g * G + h + 1) * D)
 
 
 def pack_kv_kernel(keys, values, segment, out, counts):
     counts[0] = jnp.sum((segment[...] == 0).astype(jnp.int32))
     counts[1] = jnp.sum((segment[...] != 2).astype(jnp.int32))
     for g in range(8):
-        out[g, :R] = keys[:, g * D : (g + 1) * D]
-        out[g, R:] = values[:, g * D : (g + 1) * D]
-
-
-def pack_q_kernel(queries, saved, grads, out):
+        for xl in range(2):
+            out[spread_to(g, xl), :R] = keys[:, g * D : (g + 1) * D]
+            out[spread_to(g, xl), R:] = values[:, g * D : (g + 1) * D]
+
+
+def pack_q_kernel(queries, saved, grads, after, out):
+    del after
     ones = jnp.ones((8, D), BF16)
     row = lax.broadcasted_iota(jnp.int32, (16, D), 0)
     for g in range(8):
         for half in range(2):
-            dest = (g // 4 * 2 + half) * 4 + g % 4
+            dest = spread_to(g, half)
             rows = slice(half * HR, (half + 1) * HR)
             prods = []
             for h in range(G):
-                cols = slice((g * G + h) * D, (g * G + h + 1) * D)
+                cols = head_columns(g, h)
                 grad = grads[rows, cols]
                 out[dest, h * HR : (h + 1) * HR] = queries[rows, cols]
                 out[dest, QR + h * HR : QR + (h + 1) * HR] = grad
@@ -70,17 +74,17 @@
 
 def attention_kernel(order, counts, qpay, *refs):
     pieces = refs[:10]
-    dq_out, outs = refs[10], (refs[11:15], refs[15:19])
-    (plain_c, plain_b, masked_c, masked_b, q_s, do_s, d_s, k_s, v_s, kt_s, qa_s, ga_s) = refs[19:31]
-    m_s, l_s, dk_s, dv_s, dq_s, sem, value_sem = refs[31:]
+    dq_out, keep_0, keep_1, keep_3, sum_a, sum_b, give_0, give_1, give_3, far_give = refs[10:20]
+    (plain_c, plain_b, masked_c, masked_b, q_s, do_s, d_s, k_s, v_s, kt_s, qa_s, ga_s) = refs[20:32]
+    m_s, l_s, dk_s, dv_s, dq_s, sem, value_sem = refs[32:]
     n0 = counts[0]
     n1 = counts[1]
     xl = lax.axis_index("xl")
     y = lax.axis_index("y")
     core = lax.axis_index("core")
 
-    def place(flip, dy, j):
-        return order[span_id(j // 2, xl ^ flip, y ^ dy, j % 2)]
+    def place(dy, xh, xl, zh):
+        return order[span_id(xh, xl, y ^ dy, zh)]
 
     copies = []
     value_copies = []
@@ -93,27 +97,22 @@
             )
     copies.append(pltpu.make_async_copy(qpay.at[:, pl.ds(2 * QR, 16)], d_s, sem))
     for number, piece in enumerate(pieces):
-        which = number % 5
         from_core = core if number < 5 else 1 - core
-        dy = (0, 1, 3, 2, 2)[which]
-        flips = ((0, 1), (0, 1), (0, 1), (0,), (1,))[which]
-        for at, flip in enumerate(flips):
-            source = piece.at[at] if len(flips) > 1 else piece
-            for j in range(4):
-                rank = place(flip, dy, j)
-                rows = source.at[pl.ds(2 * j, 2)]
-                copies.append(
-                    pltpu.make_async_copy(
-                        rows.at[:, pl.ds(0, R)], k_s.at[rank, :, from_core, :, pl.ds(0, D)], sem
-                    )
+        dy = (0, 1, 3, 2, 2)[number % 5]
+        halves = ((0, 1), (0, 1), (0, 1), (0,), (1,))[number % 5]
+        for at in range(4 * len(halves)):
+            rank = place(dy, halves[at // 4], at // 2 % 2, at % 2)
+            rows = piece.at[pl.ds(2 * at, 2)]
+            copies.append(
+                pltpu.make_async_copy(
+                    rows.at[:, pl.ds(0, R)], k_s.at[rank, :, from_core, :, pl.ds(0, D)], sem
                 )
-                value_copies.append(
-                    pltpu.make_async_copy(
-                        rows.at[:, pl.ds(R, R)],
-                        v_s.at[rank, :, from_core, :, pl.ds(0, D)],
-                        value_sem,
-                    )
+            )
+            value_copies.append(
+                pltpu.make_async_copy(
+                    rows.at[:, pl.ds(R, R)], v_s.at[rank, :, from_core, :, pl.ds(0, D)], value_sem
                 )
+            )
     for copy in copies + value_copies:
         copy.start()
 
@@ -229,7 +228,7 @@
         scores = jnp.dot(block_of(k_s, b), qa_s[c], preferred_element_type=F32)
         if masked:
             scores = jnp.where(seen(c, b), scores, HIDDEN)
-        return jnp.exp2(scores * EXP_SCALE)
+        return jnp.exp(scores * SCALE)
 
     def diagonal_step(i, carry):
         for c in [2 * i + k for k in range(2)]:
@@ -237,8 +236,8 @@
             scores = jnp.where(seen(c, b), raw_scores(c, b), HIDDEN)
             top = jnp.max(scores, axis=0, keepdims=True).astype(BF16).astype(F32)
             put_under(qa_s, c, -top)
-            m_s[c] = top * EXP_SCALE
-            l_s[c] = add_up(jnp.exp2((scores - top) * EXP_SCALE))
+            m_s[c] = top * SCALE
+            l_s[c] = add_up(jnp.exp((scores - top) * SCALE))
         return carry
 
     lax.fori_loop(0, NC // 2, diagonal_step, 0)
@@ -264,10 +263,10 @@
     @pl.when(jnp.logical_not(jnp.max(l_s[...]) < LARGE))
     def _():
         def careful(c, b):
-            scores = jnp.where(seen(c, b), raw_scores(c, b) * EXP_SCALE, HIDDEN)
+            scores = jnp.where(seen(c, b), raw_scores(c, b) * SCALE, HIDDEN)
             old = m_s[c]
             top = jnp.maximum(old, jnp.max(scores, axis=0, keepdims=True))
-            l_s[c] = l_s[c] * jnp.exp2(old - top) + add_up(jnp.exp2(scores - top))
+            l_s[c] = l_s[c] * jnp.exp(old - top) + add_up(jnp.exp(scores - top))
             m_s[c] = top
 
         def careful_masked(n, carry):
@@ -289,8 +288,8 @@
         lax.fori_loop(0, n_plain, careful_plain, 0)
 
     def put_logsum(c, carry):
-        logsum = m_s[c] + jnp.log2(jnp.sum(l_s[c], axis=0, keepdims=True))
-        rest = logsum * (1.0 / EXP_SCALE)
+        logsum = m_s[c] + jnp.log(jnp.sum(l_s[c], axis=0, keepdims=True))
+        rest = logsum * (1.0 / SCALE)
         rows = []
         for _ in range(3):
             part = rest.astype(BF16).astype(F32)
@@ -338,38 +337,56 @@
 
     lax.fori_loop(0, NC, finish, 0)
 
-    for from_core, group in ((core, outs[0]), (1 - core, outs[1])):
-        for dy, out in zip((0, 1, 3, 2), group):
-            for flip in range(2):
-                for j in range(4):
-                    rank = place(flip, dy, j)
-                    rows = slice(2 * j, 2 * j + 2)
-                    out[flip, rows, :R] = (dk_s[rank, :, from_core] * SCALE).astype(BF16)
-                    out[flip, rows, R:] = dv_s[rank, :, from_core].astype(BF16)
-
-
-def last_sum_kernel(mine, got, near_1, near_3, dq, sums, out):
-    for flip in range(2):
-        for xh in range(2):
-            rows = slice(xh * 4, xh * 4 + 4)
-            parts = [ref[flip, rows].astype(F32) for ref in (mine, got, near_1, near_3)]
-            total = (parts[0] + parts[1]) + (parts[2] + parts[3])
-            sums[xh, lax.axis_index("xl") ^ flip] = total.astype(BF16)
+    for from_core, group in (
+        (core, ((0, keep_0, 0), (1, keep_1, 0), (3, keep_3, 0), (2, sum_a, 0), (2, sum_b, 1))),
+        (1 - core, ((0, give_0, 0), (1, give_1, 0), (3, give_3, 0), (2, far_give, 0))),
+    ):
+        for dy, out, first_xh in group:
+            for at in range(out.shape[0] // 2):
+                rank = place(dy, first_xh + at // 4, at // 2 % 2, at % 2)
+                rows = slice(2 * at, 2 * at + 2)
+                out[rows, :R] = (dk_s[rank, :, from_core] * SCALE).astype(BF16)
+                out[rows, R:] = dv_s[rank, :, from_core].astype(BF16)
+
+
+def far_sum_kernel(sum_a, sum_b, got, out_a, out_b):
+    out_a[...] = (sum_a[...].astype(F32) + got[:8].astype(F32)).astype(BF16)
+    out_b[...] = (sum_b[...].astype(F32) + got[8:].astype(F32)).astype(BF16)
+
+
+def near_sum_kernel(sum_1, got_1, sum_3, got_3, from_1, from_3, out_1, out_3):
+    for rows, with_from in ((slice(0, 8), 3), (slice(8, 16), 1)):
+        for number, keep, got, came, out in (
+            (1, sum_1, got_1, from_3, out_1),
+            (3, sum_3, got_3, from_1, out_3),
+        ):
+            total = keep[rows].astype(F32) + got[rows].astype(F32)
+            if number == with_from:
+                total = total + came[...].astype(F32)
+            out[rows] = total.astype(BF16)
+
+
+def last_sum_kernel(keep, got, near_1, near_3, dq, sums, query_grad):
+    total = keep[...].astype(F32) + got[...].astype(F32)
+    total = total + (near_1[...].astype(F32) + near_3[...].astype(F32))
+    sums[...] = total.astype(BF16)
     for g in range(8):
         for half in range(2):
-            dest = (g // 4 * 2 + half) * 4 + g % 4
+            rows = slice(half * HR, (half + 1) * HR)
             for h in range(G):
-                cols = slice((g * G + h) * D, (g * G + h + 1) * D)
-                out[half * HR : (half + 1) * HR, cols] = dq[dest, h * HR : (h + 1) * HR]
-
-
-def unpack_kv_kernel(got, key_grad, value_grad):
+                query_grad[rows, head_columns(g, h)] = dq[spread_to(g, half), h * HR : (h + 1) * HR]
+
+
+def unpack_kernel(got, key_grad, value_grad):
     for g in range(8):
-        pair = [(g // 4 * 2 + xl) * 4 + g % 4 for xl in range(2)]
         for start, out in ((0, key_grad), (R, value_grad)):
-            rows = slice(start, start + R)
-            total = got[pair[0], rows].astype(F32) + got[pair[1], rows].astype(F32)
+            total = got[spread_to(g, 0), start : start + R].astype(F32)
+            total = total + got[spread_to(g, 1), start : start + R].astype(F32)
             out[:, g * D : (g + 1) * D] = total.astype(BF16)
+
+
+def bf16(*shape):
+    return jax.ShapeDtypeStruct(shape, BF16)
 
 
 def on_vmem(kernel, outs, *args):
@@ -380,83 +397,50 @@
     )(*args)
 
 
-def exchange(array, axes):
-    return lax.all_to_all(array, axes, split_axis=0, concat_axis=0, tiled=True)
-
-
-def flip(array, axis):
-    return lax.ppermute(array, axis, [(0, 1), (1, 0)])
+IN_SMEM = pl.BlockSpec(memory_space=pltpu.SMEM)
+IN_VMEM = pl.BlockSpec(memory_space=pltpu.VMEM)
+ANYWHERE = pl.BlockSpec(memory_space=pl.ANY)
+
+
+def exchange(array):
+    return lax.all_to_all(array, SPREAD, split_axis=0, concat_axis=0, tiled=True)
+
+
+def flip(array):
+    return lax.ppermute(array, "core", [(0, 1), (1, 0)])
 
 
 def swap(array, distance):
     return lax.ppermute(array, "y", [(i, i ^ distance) for i in range(4)])
-
-
-def gather_kv(own):
-    both = jnp.stack([own, flip(own, "xl")])
-    near_1 = swap(both, 1)
-    near_3 = swap(both, 3)
-    far_same = swap(near_3[0], 1)
-    far_flip = swap(near_1[1], 3)
-    mine = (both, near_1, near_3, far_same, far_flip)
-    return mine + tuple(flip(array, "core") for array in mine)
-
-
-def add(*terms):
-    total = terms[0].astype(F32)
-    for term in terms[1:]:
-        total = total + term.astype(F32)
-    return total
-
-
-def reduce_kv(mine, other, dq):
-    got_0, got_1, got_3, got_2 = [flip(array, "core") for array in other]
-    mine_0, mine_1, mine_3, mine_2 = mine
-    far = add(mine_2, got_2).astype(BF16)
-    from_1 = swap(far[0], 1)
-    from_3 = swap(far[1], 3)
-    to_3 = jnp.stack([add(mine_3[0], got_3[0], from_1), add(mine_3[1], got_3[1])])
-    to_1 = jnp.stack([add(mine_1[0], got_1[0]), add(mine_1[1], got_1[1], from_3)])
-    near_3 = swap(to_3.astype(BF16), 3)
-    near_1 = swap(to_1.astype(BF16), 1)
-    pair = (2, 2, 4, 2 * R, D)
-    sums, query_grad = on_vmem(
-        last_sum_kernel,
-        [jax.ShapeDtypeStruct(pair, BF16), jax.ShapeDtypeStruct((R, 8 * G * D), BF16)],
-        mine_0,
-        got_0,
-        near_1,
-        near_3,
-        dq,
-    )
-    return sums.reshape(16, 2 * R, D), query_grad
 
 
 def body(queries, keys, values, attn_out, out_grad, segment, span_order):
     kv_packed, counts = pl.pallas_call(
         pack_kv_kernel,
-        out_shape=[jax.ShapeDtypeStruct((8, 2 * R, D), BF16), jax.ShapeDtypeStruct((2,), jnp.int32)],
-        out_specs=[pl.BlockSpec(memory_space=pltpu.VMEM), pl.BlockSpec(memory_space=pltpu.SMEM)],
+        out_shape=[bf16(16, 2 * R, D), jax.ShapeDtypeStruct((2,), jnp.int32)],
+        out_specs=[IN_VMEM, IN_SMEM],
         compiler_params=pltpu.CompilerParams(vmem_limit_bytes=16 << 20),
     )(keys, values, segment.reshape(64, 128))
-    kv_own = exchange(kv_packed, HEADS)
-    q_own = exchange(
-        on_vmem(
-            pack_q_kernel,
-            jax.ShapeDtypeStruct((16, 2 * QR + 16, D), BF16),
-            queries,
-            attn_out,
-            out_grad,
-        ),
-        SPREAD,
-    )
-    pieces = gather_kv(kv_own)
-    group = jax.ShapeDtypeStruct((2, 8, 2 * R, D), BF16)
-    outs = pl.pallas_call(
+    own = exchange(kv_packed)
+    q_packed = pl.pallas_call(
+        pack_q_kernel,
+        out_shape=bf16(16, 2 * QR + 16, D),
+        in_specs=[IN_VMEM] * 3 + [ANYWHERE],
+        compiler_params=pltpu.CompilerParams(vmem_limit_bytes=16 << 20),
+    )(queries, attn_out, out_grad, own)
+    qpay = exchange(q_packed)
+
+    near_1 = swap(own, 1)
+    near_3 = swap(own, 3)
+    far_a = swap(near_3[:8], 1)
+    far_b = swap(near_1[8:], 3)
+    mine = (own, near_1, near_3, far_a, far_b)
+    group = bf16(16, 2 * R, D)
+    half = bf16(8, 2 * R, D)
+    dq, keep_0, keep_1, keep_3, sum_a, sum_b, give_0, give_1, give_3, far_give = pl.pallas_call(
         attention_kernel,
-        out_shape=[jax.ShapeDtypeStruct((16, QR, D), BF16)] + [group] * 8,
-        in_specs=[pl.BlockSpec(memory_space=pltpu.SMEM)] * 2
-        + [pl.BlockSpec(memory_space=pl.ANY)] * 11,
+        out_shape=[bf16(16, QR, D)] + [group] * 3 + [half] * 2 + [group] * 4,
+        in_specs=[IN_SMEM] * 2 + [ANYWHERE] * 11,
         scratch_shapes=[
             pltpu.SMEM((NC * NT // 2 + W,), jnp.int32),
             pltpu.SMEM((NC * NT // 2 + W,), jnp.int32),
@@ -479,11 +463,23 @@
             pltpu.SemaphoreType.DMA,
         ],
         compiler_params=pltpu.CompilerParams(vmem_limit_bytes=48 << 20),
-    )(span_order, counts, q_own, *pieces)
-    dkv, query_grad = reduce_kv(outs[1:5], outs[5:9], exchange(outs[0], SPREAD))
-    key_grad, value_grad = on_vmem(
-        unpack_kv_kernel, [jax.ShapeDtypeStruct((R, 8 * D), BF16)] * 2, exchange(dkv, SPREAD)
+    )(span_order, counts, qpay, *mine, *[flip(array) for array in mine])
+    far_sum_a, far_sum_b = on_vmem(far_sum_kernel, [half, half], sum_a, sum_b, flip(far_give))
+    from_1 = swap(far_sum_a, 1)
+    from_3 = swap(far_sum_b, 3)
+    to_1, to_3 = on_vmem(
+        near_sum_kernel, [group] * 2, keep_1, flip(give_1), keep_3, flip(give_3), from_1, from_3
     )
+    sums, query_grad = on_vmem(
+        last_sum_kernel,
+        [group, bf16(R, 8 * G * D)],
+        keep_0,
+        flip(give_0),
+        swap(to_1, 1),
+        swap(to_3, 3),
+        exchange(dq),
+    )
+    key_grad, value_grad = on_vmem(unpack_kernel, [bf16(R, 8 * D)] * 2, exchange(sums))
     return query_grad, key_grad, value_grad
 
 

time: 134 us -> 136 us (1.015)
  waiting for transfers between devices: 31.4 us -> 25.1 us
  starting transfers between devices: 16.5 us -> 22.7 us
  blocking collectives: 43.5 us -> 46.6 us
  local copies, waits for them, and re-layouts: 3.73 us -> 5.22 us
    ppermute x8, starting transfers between devices: 10.3 us -> 17.9 us  [swap(): return lax.ppermute(array, 'y', [(i, i ^ distance) for i in range(4)])]
    ppermute x10 -> x9, waiting for transfers between devices: 8.42 us -> 1.77 us  [flip(): return lax.ppermute(array, 'core', [(0, 1), (1, 0)])]
    all_to_all x3, blocking collectives: 43.5 us -> 46.6 us  [exchange(): lax.all_to_all(array, SPREAD, split_axis=0, concat_axis=0, tiled=True)]
    unnamed x20, local copies, waits for them, and re-layouts: 2.7 us -> 4.23 us
    ppermute x10 -> x9, starting transfers between devices: 2.37 us -> 0.98 us  [flip(): return lax.ppermute(array, 'core', [(0, 1), (1, 0)])]
    pallas_call x3 -> x4, Pallas kernels: 3.41 us -> 2.14 us  [on_vmem(): pl.pallas_call(kernel, out_shape=outs, compiler_params=pltpu.CompilerPara...]
    pallas_call x2 -> x3, Pallas kernels: 34.5 us -> 34.8 us  [the longest x1 32.4 us: body(): pl.pallas_call(attention_kernel, out_shape=[bf16(16, QR, D)] + [group] *...]
  transfers between devices with their start and end apart: 19 -> 18, of which waited for: 8 -> 9; matrix products, arithmetic and copies ran while one was open for 1% -> 1% of each run, Pallas kernels for 1% -> 2%
where the time goes in v4:
time: 136 us; the launch traced here: 137 us
  blocking collectives  46.6 us (34%)
  Pallas kernels  36.9 us (27%)
  waiting for transfers between devices  25.1 us (18%)
  starting transfers between devices  22.7 us (17%)
  local copies, waits for them, and re-layouts  5.22 us (4%)
    all_to_all x3, blocking collectives, exchange(): lax.all_to_all(array, SPREAD, split_axis=0, concat_axis=0, tiled=True)  46.6 us
    pallas_call x1, Pallas kernels, body(): pl.pallas_call(attention_kernel, out_shape=[bf16(16, QR, D)] + [group] *...  32.4 us
    ppermute x8, waiting for transfers between devices, swap(): return lax.ppermute(array, 'y', [(i, i ^ distance) for i in range(4)])  22.2 us
    ppermute x8, starting transfers between devices, swap(): return lax.ppermute(array, 'y', [(i, i ^ distance) for i in range(4)])  17.9 us
    unnamed x20, local copies, waits for them, and re-layouts  4.23 us
    all_to_all x1, starting transfers between devices, exchange(): lax.all_to_all(array, SPREAD, split_axis=0, concat_axis=0, tiled=True)  3.83 us
  transfers between devices with their start and end apart: 18, of which 9 were waited for; matrix products, arithmetic and copies ran while one was open for 1% of the time, Pallas kernels for 2%

profile of v4, /device:TPU:0, one launch (start us, length us, event | category | flops | bytes accessed | tf_op | source)
XLA Modules:
  0.0 137.4 jit_solution(14424060836273537612)
XLA Ops:
  0.7 1.0 copy-done.4
  1.6 0.9 copy-done.5
  2.5 0.8 copy-done.6
  3.3 0.7 shard_map.94
  4.0 19.3 %all_to_all.20.after.refs_0_ = bf16[16,128,128]{2,1,0:T(8,128)(2,1)S(1)} all-to-all(bf16[16,128,128]{2,1,0:T(8,128)(2,1)S(1)} %get-tuple-element.24), channel_id=1, replica_groups=mesh['z'=4,'core'=2,'xh'=2,'xl'=2,'y'=4] {'xh','xl','z'}, dimensions={0} | all-to-all | bytes 1048576 | tf_op jit(solution)/shard_map/all_to_all | solution.py:406
  23.3 3.0 %collective-permute-start.1 = (bf16[16,128,128]{2,1,0:T(8,128)(2,1)S(1)}, bf16[16,128,128]{2,1,0:T(8,128)(2,1)S(1)}, u32[]{:S(2)}, u32[]{:S(2)}) collective-permute-start(bf16[16,128,128]{2,1,0:T(8,128)(2,1)S(1)} %all_to_all.20.after.refs_0_), channel_id=1, source_target_pairs={{0,3},{1,2},{2,1},{3,0},{4,7},{5,6},{6,5},{7,4},{8,11},{9,10},{10,... | collective-permute-start | bytes 1572872 | tf_op jit(solution)/shard_map/ppermute | solution.py:414
  26.3 0.1 collective-permute-start
  26.4 1.0 copy-done.3
  27.5 1.7 %shard_map.95 = bf16[16,272,128]{2,1,0:T(8,128)(2,1)} custom-call(bf16[64,4096]{1,0:T(8,128)(2,1)S(1)} %copy-done.1, bf16[64,4096]{1,0:T(8,128)(2,1)S(1)} %copy-done.2, bf16[64,4096]{1,0:T(8,128)(2,1)S(1)} %copy-done.3, bf16[16,128,128]{2,1,0:T(8,128)(2,1)S(1)} %all_to_all.20.after.refs_0_), custom_call_target="tpu_custom_call" | custom-call | tf_op jit(solution)/shard_map/pallas_call | solution.py:425
  29.2 3.8 %all-to-all-start.1 = ((bf16[16,272,128]{2,1,0:T(8,128)(2,1)}), bf16[16,272,128]{2,1,0:T(8,128)(2,1)S(1)}, u32[]{:S(2)}, u32[]{:S(2)}) async-start(bf16[16,272,128]{2,1,0:T(8,128)(2,1)} %shard_map.95), calls=%async_computation.1 | async-start | bytes 2228224 | tf_op jit(solution)/shard_map/all_to_all | solution.py:406
  33.0 0.1 collective-permute-start.4
  33.1 3.7 %collective-permute-done.1.refs_2_ = bf16[16,128,128]{2,1,0:T(8,128)(2,1)S(1)} collective-permute-done((bf16[16,128,128]{2,1,0:T(8,128)(2,1)S(1)}, bf16[16,128,128]{2,1,0:T(8,128)(2,1)S(1)}, u32[]{:S(2)}, u32[]{:S(2)}) %collective-permute-start.1) | collective-permute-done | bytes 524320 | tf_op jit(solution)/shard_map/ppermute | solution.py:414
  36.8 0.4 collective-permute-start.2
  37.2 0.0 collective-permute-start.6
  37.2 2.4 %collective-permute-done.refs_1_ = bf16[16,128,128]{2,1,0:T(8,128)(2,1)} collective-permute-done((bf16[16,128,128]{2,1,0:T(8,128)(2,1)S(1)}, bf16[16,128,128]{2,1,0:T(8,128)(2,1)}, u32[]{:S(2)}, u32[]{:S(2)}) %collective-permute-start) | collective-permute-done | bytes 524320 | tf_op jit(solution)/shard_map/ppermute | solution.py:414
  39.5 1.0 slice.9
  40.5 0.5 collective-permute-start.3
  41.0 0.2 collective-permute-start.5
  41.2 2.6 %collective-permute-done.2.refs_3_ = bf16[8,128,128]{2,1,0:T(8,128)(2,1)S(1)} collective-permute-done((bf16[8,128,128]{2,1,0:T(8,128)(2,1)S(1)}, bf16[8,128,128]{2,1,0:T(8,128)(2,1)S(1)}, u32[]{:S(2)}, u32[]{:S(2)}) %collective-permute-start.2) | collective-permute-done | bytes 262176 | tf_op jit(solution)/shard_map/ppermute | solution.py:414
  43.8 0.0 collective-permute-start.7
  43.8 4.3 %collective-permute-done.3.refs_4_ = bf16[8,128,128]{2,1,0:T(8,128)(2,1)S(1)} collective-permute-done((bf16[8,128,128]{2,1,0:T(8,128)(2,1)S(1)}, bf16[8,128,128]{2,1,0:T(8,128)(2,1)S(1)}, u32[]{:S(2)}, u32[]{:S(2)}) %collective-permute-start.3) | collective-permute-done | bytes 262176 | tf_op jit(solution)/shard_map/ppermute | solution.py:414
  48.2 0.0 collective-permute-start.8
  48.2 0.0 collective-permute-done.4.refs_5_
  48.2 1.1 all-to-all-done.1.qpay
  49.2 0.0 collective-permute-done.7.refs_8_
  49.2 0.0 collective-permute-done.6.refs_7_
  49.2 0.4 collective-permute-done.8.refs_9_
  49.7 0.0 collective-permute-done.5.refs_6_
  49.7 0.5 copy-done.8
  50.2 32.4 %shard_map.96 = (bf16[16,128,128]{2,1,0:T(8,128)(2,1)S(1)}, bf16[16,128,128]{2,1,0:T(8,128)(2,1)S(1)}, bf16[16,128,128]{2,1,0:T(8,128)(2,1)S(1)}, bf16[16,128,12...) custom-call(s32[32]{0:T(128)S(1)} %copy-done.7, ...), custom_call_target="tpu_custom_call" | custom-call | tf_op jit(solution)/shard_map/pallas_call | solution.py:440
  82.7 0.1 collective-permute-start.12
  82.7 0.5 collective-permute-start.10
  83.2 0.1 collective-permute-start.11
  83.3 1.3 collective-permute-done.12.got
  84.6 0.1 shard_map.97
  84.8 13.4 %collective-permute-start.13 = (bf16[8,128,128]{2,1,0:T(8,128)(2,1)S(1)}, bf16[8,128,128]{2,1,0:T(8,128)(2,1)S(1)}, u32[]{:S(2)}, u32[]{:S(2)}) collective-permute-start(bf16[8,128,128]{2,1,0:T(8,128)(2,1)S(1)} %get-tuple-element.34), channel_id=1, source_target_pairs={{0,1},{1,0},{2,3},{3,2},{4,5},{5,4},{6,7},{7,6},{8,9},{9,8},{10,11... | collective-permute-start | bytes 786440 | tf_op jit(solution)/shard_map/ppermute | solution.py:414
  98.2 0.0 collective-permute-start.14
  98.2 0.0 collective-permute-start.9
  98.2 0.0 collective-permute-done.11.got_3
  98.2 6.6 %collective-permute-done.13.from_1 = bf16[8,128,128]{2,1,0:T(8,128)(2,1)S(1)} collective-permute-done((bf16[8,128,128]{2,1,0:T(8,128)(2,1)S(1)}, bf16[8,128,128]{2,1,0:T(8,128)(2,1)S(1)}, u32[]{:S(2)}, u32[]{:S(2)}) %collective-permute-start.13) | collective-permute-done | bytes 262176 | tf_op jit(solution)/shard_map/ppermute | solution.py:414
  104.8 2.7 %collective-permute-done.14.from_3 = bf16[8,128,128]{2,1,0:T(8,128)(2,1)S(1)} collective-permute-done((bf16[8,128,128]{2,1,0:T(8,128)(2,1)S(1)}, bf16[8,128,128]{2,1,0:T(8,128)(2,1)S(1)}, u32[]{:S(2)}, u32[]{:S(2)}) %collective-permute-start.14) | collective-permute-done | bytes 262176 | tf_op jit(solution)/shard_map/ppermute | solution.py:414
  107.5 0.3 shard_map.98
  107.8 0.1 collective-permute-start.15
  107.9 0.4 collective-permute-start.16
  108.2 14.1 %all_to_all.21.dq = bf16[16,128,128]{2,1,0:T(8,128)(2,1)S(1)} all-to-all(bf16[16,128,128]{2,1,0:T(8,128)(2,1)S(1)} %get-tuple-element.38), channel_id=1, replica_groups=mesh['z'=4,'core'=2,'xh'=2,'xl'=2,'y'=4] {'xh','xl','z'}, dimensions={0} | all-to-all | bytes 1048576 | tf_op jit(solution)/shard_map/all_to_all | solution.py:406
  122.3 0.9 shard_map.99
  123.3 13.3 %all_to_all.22.got = bf16[16,128,128]{2,1,0:T(8,128)(2,1)S(1)} all-to-all(bf16[16,128,128]{2,1,0:T(8,128)(2,1)S(1)} %get-tuple-element.40), channel_id=1, replica_groups=mesh['z'=4,'core'=2,'xh'=2,'xl'=2,'y'=4] {'xh','xl','z'}, dimensions={0} | all-to-all | bytes 1048576 | tf_op jit(solution)/shard_map/all_to_all | solution.py:406
  136.6 0.8 shard_map.100
  (20 shorter events, 0.1 us)
Async XLA Ops:
  0.6 25.8 %copy-start.2 = (bf16[64,4096]{1,0:T(8,128)(2,1)S(1)}, bf16[64,4096]{1,0:T(8,128)(2,1)}, u32[]{:S(2)}) copy-start(bf16[64,4096]{1,0:T(8,128)(2,1)} %saved.1) | copy-start | bytes 1572868
  0.6 25.8 %copy-start.1 = (bf16[64,4096]{1,0:T(8,128)(2,1)S(1)}, bf16[64,4096]{1,0:T(8,128)(2,1)}, u32[]{:S(2)}) copy-start(bf16[64,4096]{1,0:T(8,128)(2,1)} %queries.1) | copy-start | bytes 1572868
  0.7 1.0 copy-start.4
  1.6 0.9 copy-start.5
  2.5 0.8 copy-start.6
  23.3 9.7 %copy-start = (bf16[16,128,128]{2,1,0:T(8,128)(2,1)}, bf16[16,128,128]{2,1,0:T(8,128)(2,1)S(1)}, u32[]{:S(2)}) copy-start(bf16[16,128,128]{2,1,0:T(8,128)(2,1)S(1)} %all_to_all.20.after.refs_0_) | copy-start | bytes 1572868
  23.3 13.5 %collective-permute-start.1 = (bf16[16,128,128]{2,1,0:T(8,128)(2,1)S(1)}, bf16[16,128,128]{2,1,0:T(8,128)(2,1)S(1)}, u32[]{:S(2)}, u32[]{:S(2)}) collective-permute-start(bf16[16,128,128]{2,1,0:T(8,128)(2,1)S(1)} %all_to_all.20.after.refs_0_), channel_id=1, source_target_pairs={{0,3},{1,2},{2,1},{3,0},{4,7},{5,6},{6,5},{7,4},{8,11},{9,10},{10,... | collective-permute-start | bytes 1572872 | tf_op jit(solution)/shard_map/ppermute | solution.py:414
  26.3 13.2 %collective-permute-start = (bf16[16,128,128]{2,1,0:T(8,128)(2,1)S(1)}, bf16[16,128,128]{2,1,0:T(8,128)(2,1)}, u32[]{:S(2)}, u32[]{:S(2)}) collective-permute-start(bf16[16,128,128]{2,1,0:T(8,128)(2,1)S(1)} %all_to_all.20.after.refs_0_), channel_id=1, source_target_pairs={{0,1},{1,0},{2,3},{3,2},{4,5},{5,4},{6,7},{7,6},{8,9},{9,8},{10,11... | collective-permute-start | bytes 1572872 | tf_op jit(solution)/shard_map/ppermute | solution.py:414
  26.4 1.0 copy-start.3
  29.2 21.1 %copy-start.7 = (s32[32]{0:T(128)S(1)}, s32[32]{0:T(128)}, u32[]{:S(2)}) copy-start(s32[32]{0:T(128)} %order.1) | copy-start | bytes 388
  29.2 20.1 %all-to-all-start.1 = ((bf16[16,272,128]{2,1,0:T(8,128)(2,1)}), bf16[16,272,128]{2,1,0:T(8,128)(2,1)S(1)}, u32[]{:S(2)}, u32[]{:S(2)}) async-start(bf16[16,272,128]{2,1,0:T(8,128)(2,1)} %shard_map.95), calls=%async_computation.1 | async-start | bytes 2228224 | tf_op jit(solution)/shard_map/all_to_all | solution.py:406
  33.0 15.2 %collective-permute-start.4 = (bf16[16,128,128]{2,1,0:T(8,128)(2,1)S(1)}, bf16[16,128,128]{2,1,0:T(8,128)(2,1)}, u32[]{:S(2)}, u32[]{:S(2)}) collective-permute-start(bf16[16,128,128]{2,1,0:T(8,128)(2,1)S(1)} %all_to_all.20.after.refs_0_), channel_id=1, source_target_pairs={{0,16},{16,0},{1,17},{17,1},{2,18},{18,2},{3,19},{19,3},{4,20},{20... | collective-permute-start | bytes 1572872 | tf_op jit(solution)/shard_map/ppermute | solution.py:410
  36.8 12.9 %copy-start.9 = (bf16[16,128,128]{2,1,0:T(8,128)(2,1)}, bf16[16,128,128]{2,1,0:T(8,128)(2,1)S(1)}, u32[]{:S(2)}) copy-start(bf16[16,128,128]{2,1,0:T(8,128)(2,1)S(1)} %collective-permute-done.1.refs_2_) | copy-start | bytes 1572868
  36.8 7.1 %collective-permute-start.2 = (bf16[8,128,128]{2,1,0:T(8,128)(2,1)S(1)}, bf16[8,128,128]{2,1,0:T(8,128)(2,1)S(1)}, u32[]{:S(2)}, u32[]{:S(2)}) collective-permute-start(bf16[8,128,128]{2,1,0:T(8,128)(2,1)S(1)} %slice.8), channel_id=1, source_target_pairs={{0,1},{1,0},{2,3},{3,2},{4,5},{5,4},{6,7},{7,6},{8,9},{9,8},{10,11... | collective-permute-start | bytes 786440 | tf_op jit(solution)/shard_map/ppermute | solution.py:414
  37.2 12.1 %collective-permute-start.6 = (bf16[16,128,128]{2,1,0:T(8,128)(2,1)S(1)}, bf16[16,128,128]{2,1,0:T(8,128)(2,1)}, u32[]{:S(2)}, u32[]{:S(2)}) collective-permute-start(bf16[16,128,128]{2,1,0:T(8,128)(2,1)S(1)} %collective-permute-done.1.refs_2_), channel_id=1, source_target_pairs={{0,16},{16,0},{1,17},{17,1},{2,18},{18,2},{3,19},{19,3},{4,20},{20... | collective-permute-start | bytes 1572872 | tf_op jit(solution)/shard_map/ppermute | solution.py:410
  40.5 7.7 %collective-permute-start.3 = (bf16[8,128,128]{2,1,0:T(8,128)(2,1)S(1)}, bf16[8,128,128]{2,1,0:T(8,128)(2,1)S(1)}, u32[]{:S(2)}, u32[]{:S(2)}) collective-permute-start(bf16[8,128,128]{2,1,0:T(8,128)(2,1)S(1)} %slice.9), channel_id=1, source_target_pairs={{0,3},{1,2},{2,1},{3,0},{4,7},{5,6},{6,5},{7,4},{8,11},{9,10},{10,... | collective-permute-start | bytes 786440 | tf_op jit(solution)/shard_map/ppermute | solution.py:414
  41.0 8.7 %collective-permute-start.5 = (bf16[16,128,128]{2,1,0:T(8,128)(2,1)}, bf16[16,128,128]{2,1,0:T(8,128)(2,1)}, u32[]{:S(2)}, u32[]{:S(2)}) collective-permute-start(bf16[16,128,128]{2,1,0:T(8,128)(2,1)} %collective-permute-done.refs_1_), channel_id=1, source_target_pairs={{0,16},{16,0},{1,17},{17,1},{2,18},{18,2},{3,19},{19,3},{4,20},{20... | collective-permute-start | bytes 1572872 | tf_op jit(solution)/shard_map/ppermute | solution.py:410
  43.8 5.4 %collective-permute-start.7 = (bf16[8,128,128]{2,1,0:T(8,128)(2,1)S(1)}, bf16[8,128,128]{2,1,0:T(8,128)(2,1)S(1)}, u32[]{:S(2)}, u32[]{:S(2)}) collective-permute-start(bf16[8,128,128]{2,1,0:T(8,128)(2,1)S(1)} %collective-permute-done.2.refs_3_), channel_id=1, source_target_pairs={{0,16},{16,0},{1,17},{17,1},{2,18},{18,2},{3,19},{19,3},{4,20},{20... | collective-permute-start | bytes 786440 | tf_op jit(solution)/shard_map/ppermute | solution.py:410
  48.2 1.5 %collective-permute-start.8 = (bf16[8,128,128]{2,1,0:T(8,128)(2,1)S(1)}, bf16[8,128,128]{2,1,0:T(8,128)(2,1)S(1)}, u32[]{:S(2)}, u32[]{:S(2)}) collective-permute-start(bf16[8,128,128]{2,1,0:T(8,128)(2,1)S(1)} %collective-permute-done.3.refs_4_), channel_id=1, source_target_pairs={{0,16},{16,0},{1,17},{17,1},{2,18},{18,2},{3,19},{19,3},{4,20},{20... | collective-permute-start | bytes 786440 | tf_op jit(solution)/shard_map/ppermute | solution.py:410
  49.2 1.0 copy-start.8
  82.7 2.0 %collective-permute-start.12 = (bf16[16,128,128]{2,1,0:T(8,128)(2,1)S(1)}, bf16[16,128,128]{2,1,0:T(8,128)(2,1)S(1)}, u32[]{:S(2)}, u32[]{:S(2)}) collective-permute-start(bf16[16,128,128]{2,1,0:T(8,128)(2,1)S(1)} %get-tuple-element.33), channel_id=1, source_target_pairs={{0,16},{16,0},{1,17},{17,1},{2,18},{18,2},{3,19},{19,3},{4,20},{20... | collective-permute-start | bytes 1572872 | tf_op jit(solution)/shard_map/ppermute | solution.py:410
  82.7 15.5 %collective-permute-start.10 = (bf16[16,128,128]{2,1,0:T(8,128)(2,1)S(1)}, bf16[16,128,128]{2,1,0:T(8,128)(2,1)S(1)}, u32[]{:S(2)}, u32[]{:S(2)}) collective-permute-start(bf16[16,128,128]{2,1,0:T(8,128)(2,1)S(1)} %get-tuple-element.28), channel_id=1, source_target_pairs={{0,16},{16,0},{1,17},{17,1},{2,18},{18,2},{3,19},{19,3},{4,20},{20... | collective-permute-start | bytes 1572872 | tf_op jit(solution)/shard_map/ppermute | solution.py:410
  83.2 15.0 %collective-permute-start.11 = (bf16[16,128,128]{2,1,0:T(8,128)(2,1)S(1)}, bf16[16,128,128]{2,1,0:T(8,128)(2,1)S(1)}, u32[]{:S(2)}, u32[]{:S(2)}) collective-permute-start(bf16[16,128,128]{2,1,0:T(8,128)(2,1)S(1)} %get-tuple-element.30), channel_id=1, source_target_pairs={{0,16},{16,0},{1,17},{17,1},{2,18},{18,2},{3,19},{19,3},{4,20},{20... | collective-permute-start | bytes 1572872 | tf_op jit(solution)/shard_map/ppermute | solution.py:410
  84.8 20.0 %collective-permute-start.13 = (bf16[8,128,128]{2,1,0:T(8,128)(2,1)S(1)}, bf16[8,128,128]{2,1,0:T(8,128)(2,1)S(1)}, u32[]{:S(2)}, u32[]{:S(2)}) collective-permute-start(bf16[8,128,128]{2,1,0:T(8,128)(2,1)S(1)} %get-tuple-element.34), channel_id=1, source_target_pairs={{0,1},{1,0},{2,3},{3,2},{4,5},{5,4},{6,7},{7,6},{8,9},{9,8},{10,11... | collective-permute-start | bytes 786440 | tf_op jit(solution)/shard_map/ppermute | solution.py:414
  98.2 9.3 %collective-permute-start.14 = (bf16[8,128,128]{2,1,0:T(8,128)(2,1)S(1)}, bf16[8,128,128]{2,1,0:T(8,128)(2,1)S(1)}, u32[]{:S(2)}, u32[]{:S(2)}) collective-permute-start(bf16[8,128,128]{2,1,0:T(8,128)(2,1)S(1)} %get-tuple-element.35), channel_id=1, source_target_pairs={{0,3},{1,2},{2,1},{3,0},{4,7},{5,6},{6,5},{7,4},{8,11},{9,10},{10,... | collective-permute-start | bytes 786440 | tf_op jit(solution)/shard_map/ppermute | solution.py:414
  98.2 24.1 %collective-permute-start.9 = (bf16[16,128,128]{2,1,0:T(8,128)(2,1)S(1)}, bf16[16,128,128]{2,1,0:T(8,128)(2,1)S(1)}, u32[]{:S(2)}, u32[]{:S(2)}) collective-permute-start(bf16[16,128,128]{2,1,0:T(8,128)(2,1)S(1)} %get-tuple-element.26), channel_id=1, source_target_pairs={{0,16},{16,0},{1,17},{17,1},{2,18},{18,2},{3,19},{19,3},{4,20},{20... | collective-permute-start | bytes 1572872 | tf_op jit(solution)/shard_map/ppermute | solution.py:410
  107.8 14.5 %collective-permute-start.15 = (bf16[16,128,128]{2,1,0:T(8,128)(2,1)S(1)}, bf16[16,128,128]{2,1,0:T(8,128)(2,1)S(1)}, u32[]{:S(2)}, u32[]{:S(2)}) collective-permute-start(bf16[16,128,128]{2,1,0:T(8,128)(2,1)S(1)} %get-tuple-element.36), channel_id=1, source_target_pairs={{0,1},{1,0},{2,3},{3,2},{4,5},{5,4},{6,7},{7,6},{8,9},{9,8},{10,11... | collective-permute-start | bytes 1572872 | tf_op jit(solution)/shard_map/ppermute | solution.py:414
  107.9 14.4 %collective-permute-start.16 = (bf16[16,128,128]{2,1,0:T(8,128)(2,1)S(1)}, bf16[16,128,128]{2,1,0:T(8,128)(2,1)S(1)}, u32[]{:S(2)}, u32[]{:S(2)}) collective-permute-start(bf16[16,128,128]{2,1,0:T(8,128)(2,1)S(1)} %get-tuple-element.37), channel_id=1, source_target_pairs={{0,3},{1,2},{2,1},{3,0},{4,7},{5,6},{6,5},{7,4},{8,11},{9,10},{10,... | collective-permute-start | bytes 1572872 | tf_op jit(solution)/shard_map/ppermute | solution.py:414

commit v5 on v4

--- a/solution.py
+++ b/solution.py
@@ -15,7 +15,9 @@
 QR = G * HR
 C = 2 * QR
 NC = 8
+HC = 4
 W = 4
+WM = 2
 SCALE = D**-0.5
 HIDDEN = -1e30
 LARGE = 2.0**90
@@ -76,7 +78,7 @@
     pieces = refs[:10]
     dq_out, keep_0, keep_1, keep_3, sum_a, sum_b, give_0, give_1, give_3, far_give = refs[10:20]
     (plain_c, plain_b, masked_c, masked_b, q_s, do_s, d_s, k_s, v_s, kt_s, qa_s, ga_s) = refs[20:32]
-    m_s, l_s, dk_s, dv_s, dq_s, sem, value_sem = refs[32:]
+    stash, m_s, l_s, dk_s, dv_s, dq_s, sem, value_sem = refs[32:]
     n0 = counts[0]
     n1 = counts[1]
     xl = lax.axis_index("xl")
@@ -143,8 +145,8 @@
         lo = jnp.minimum(jnp.where(has_second, n0 // KB, 0), hi)
         skip_at = jnp.where(all_second, (n0 + (KB - 1)) // KB, hi)
         skip_to = jnp.where(all_second, n1 // KB, 0)
-        masked_c[c] = c
-        masked_b[c] = n_full
+        masked_c[c % HC] = c
+        masked_b[c % HC] = n_full
 
         def put_plain(b, n):
             plain_c[n] = c
@@ -160,13 +162,6 @@
         n_plain = lax.fori_loop(0, lo, put_plain, n_plain)
         n_plain = lax.fori_loop(hi, n_full, put_plain, n_plain)
         return n_plain, lax.fori_loop(lo, hi, put_masked, n_masked)
-
-    n_plain, n_masked = lax.fori_loop(0, NC, list_chunk, (jnp.int32(0), jnp.int32(NC)))
-    for i in range(W - 1):
-        plain_c[n_plain + i] = NC
-        plain_b[n_plain + i] = 0
-        masked_c[n_masked + i] = NC
-        masked_b[n_masked + i] = 0
 
     for copy in copies:
         copy.wait()
@@ -206,9 +201,7 @@
     qa_s[NC, :D] = jnp.zeros((D, C), BF16)
     put_under(qa_s, NC, jnp.full((1, C), HIDDEN, F32))
     ga_s[NC] = jnp.zeros((2 * D, C), BF16)
-    q_s[NC] = jnp.zeros((C, D), BF16)
-    do_s[NC] = jnp.zeros((C, D), BF16)
-    l_s[NC] = jnp.zeros((8, C), F32)
+    l_s[...] = jnp.zeros_like(l_s)
 
     def seen(c, b):
         lane = lax.broadcasted_iota(jnp.int32, (1, C), 1)
@@ -219,7 +212,8 @@
         return (key_pos <= query_pos) & ((key_pos < low) | (key_pos >= n1))
 
     def add_up(weights):
-        return jnp.sum(weights.reshape(KB // 8, 8, C), axis=0)
+        parts = jnp.sum(weights.reshape(8, KB // 8, C), axis=0)
+        return jnp.sum(parts.reshape(KB // 64, 8, C), axis=0)
 
     def raw_scores(c, b):
         return jnp.dot(keys_of(b), qa_s[c, :D], preferred_element_type=F32)
@@ -230,107 +224,138 @@
             scores = jnp.where(seen(c, b), scores, HIDDEN)
         return jnp.exp(scores * SCALE)
 
-    def diagonal_step(i, carry):
-        for c in [2 * i + k for k in range(2)]:
-            b = masked_b[c]
-            scores = jnp.where(seen(c, b), raw_scores(c, b), HIDDEN)
-            top = jnp.max(scores, axis=0, keepdims=True).astype(BF16).astype(F32)
-            put_under(qa_s, c, -top)
-            m_s[c] = top * SCALE
-            l_s[c] = add_up(jnp.exp((scores - top) * SCALE))
-        return carry
-
-    lax.fori_loop(0, NC // 2, diagonal_step, 0)
-
-    def add_weights(items, masked):
-        parts = [add_up(weights_of(c, b, masked)) for c, b in items]
-        for (c, b), part in zip(items, parts):
-            l_s[c] += part
-
-    def masked_stats(i, carry):
-        at = [NC + 2 * i + k for k in range(2)]
-        add_weights([(masked_c[n], masked_b[n]) for n in at], True)
-        return carry
-
-    def plain_stats(i, carry):
-        at = [W * i + k for k in range(W)]
-        add_weights([(plain_c[n], plain_b[n]) for n in at], False)
-        return carry
-
-    lax.fori_loop(0, (n_masked - NC + 1) // 2, masked_stats, 0)
-    lax.fori_loop(0, (n_plain + W - 1) // W, plain_stats, 0)
-
-    @pl.when(jnp.logical_not(jnp.max(l_s[...]) < LARGE))
-    def _():
-        def careful(c, b):
-            scores = jnp.where(seen(c, b), raw_scores(c, b) * SCALE, HIDDEN)
-            old = m_s[c]
-            top = jnp.maximum(old, jnp.max(scores, axis=0, keepdims=True))
-            l_s[c] = l_s[c] * jnp.exp(old - top) + add_up(jnp.exp(scores - top))
-            m_s[c] = top
-
-        def careful_masked(n, carry):
-            c = masked_c[n]
-
-            @pl.when(n < NC)
-            def _():
+    for copy in value_copies:
+        copy.wait()
+
+    def half_step(half, unused):
+        n_plain, n_masked = lax.fori_loop(
+            half * HC, half * HC + HC, list_chunk, (jnp.int32(0), jnp.int32(HC))
+        )
+        for i in range(W - 1):
+            plain_c[n_plain + i] = NC
+            plain_b[n_plain + i] = 0
+        for i in range(WM - 1):
+            masked_c[n_masked + i] = NC
+            masked_b[n_masked + i] = 0
+        n_plain = (n_plain + (W - 1)) // W * W
+        n_masked = (n_masked + (WM - 1)) // WM * WM
+
+        def masked_items(i):
+            at = [WM * i + k for k in range(WM)]
+            return [(n, masked_c[n], masked_b[n]) for n in at]
+
+        def plain_items(i):
+            at = [W * i + k for k in range(W)]
+            return [(n_masked + n, plain_c[n], plain_b[n]) for n in at]
+
+        def diagonal_step(i, carry):
+            for n, c, b in masked_items(i):
+                scores = jnp.where(seen(c, b), raw_scores(c, b), HIDDEN)
+                top = jnp.max(scores, axis=0, keepdims=True).astype(BF16).astype(F32)
+                put_under(qa_s, c, -top)
+                m_s[c] = top * SCALE
+                weights = jnp.exp((scores - top) * SCALE)
+                stash[n] = weights.astype(BF16)
+                l_s[c] = add_up(weights)
+            return carry
+
+        def weigh(items, masked):
+            for n, c, b in items:
+                weights = weights_of(c, b, masked)
+                stash[n] = weights.astype(BF16)
+                l_s[c] += add_up(weights)
+
+        def masked_stats(i, carry):
+            weigh(masked_items(i), True)
+            return carry
+
+        def plain_stats(i, carry):
+            weigh(plain_items(i), False)
+            return carry
+
+        lax.fori_loop(0, HC // WM, diagonal_step, 0)
+        lax.fori_loop(HC // WM, n_masked // WM, masked_stats, 0)
+        lax.fori_loop(0, n_plain // W, plain_stats, 0)
+
+        @pl.when(jnp.logical_not(jnp.max(l_s[...]) < LARGE))
+        def _():
+            def careful(c, b):
+                scores = jnp.where(seen(c, b), raw_scores(c, b) * SCALE, HIDDEN)
+                old = m_s[c]
+                top = jnp.maximum(old, jnp.max(scores, axis=0, keepdims=True))
+                l_s[c] = l_s[c] * jnp.exp(old - top) + add_up(jnp.exp(scores - top))
+                m_s[c] = top
+
+            def each(step):
+                def masked(n, carry):
+                    @pl.when(masked_c[n] < NC)
+                    def _():
+                        step(n, masked_c[n], masked_b[n])
+
+                    return carry
+
+                def plain(n, carry):
+                    @pl.when(plain_c[n] < NC)
+                    def _():
+                        step(n_masked + n, plain_c[n], plain_b[n])
+
+                    return carry
+
+                lax.fori_loop(0, n_masked, masked, 0)
+                lax.fori_loop(0, n_plain, plain, 0)
+
+            def keep(n, c, b):
+                scores = jnp.where(seen(c, b), raw_scores(c, b) * SCALE, HIDDEN)
+                stash[n] = jnp.exp(scores - m_s[c]).astype(BF16)
+
+            def start(c, carry):
                 m_s[c] = jnp.full((1, C), HIDDEN, F32)
                 l_s[c] = jnp.zeros((8, C), F32)
-
-            careful(c, masked_b[n])
+                return carry
+
+            lax.fori_loop(half * HC, half * HC + HC, start, 0)
+            each(lambda n, c, b: careful(c, b))
+            each(keep)
+
+        def divide(c, carry):
+            share = 1.0 / jnp.sum(l_s[c], axis=0, keepdims=True)
+            m_s[c] = share
+            column = jnp.broadcast_to(share, (8, C)).T[:, :1]
+            q_s[c] = (q_s[c].astype(F32) * column).astype(BF16)
+            do_s[c] = (do_s[c].astype(F32) * column).astype(BF16)
             return carry
 
-        def careful_plain(n, carry):
-            careful(plain_c[n], plain_b[n])
+        lax.fori_loop(half * HC, half * HC + HC, divide, 0)
+
+        def grad_step(items):
+            for n, c, b in items:
+                c = jnp.minimum(c, NC - 1)
+                weights = stash[n]
+                above = jnp.dot(block_of(v_s, b), ga_s[c], preferred_element_type=F32)
+                score_grad = (weights.astype(F32) * above).astype(BF16)
+                for ref, term in (
+                    (dv_s, jnp.dot(weights, do_s[c], preferred_element_type=F32)),
+                    (dk_s, jnp.dot(score_grad, q_s[c], preferred_element_type=F32)),
+                ):
+                    ref[pl.ds(2 * b, 2)] += term.reshape(2, 2, 2, R, D)
+                dq_s[c] += jnp.dot(kt_s[b], score_grad, preferred_element_type=F32)
+
+        def masked_grads(i, carry):
+            grad_step(masked_items(i))
             return carry
 
-        lax.fori_loop(0, n_masked, careful_masked, 0)
-        lax.fori_loop(0, n_plain, careful_plain, 0)
-
-    def put_logsum(c, carry):
-        logsum = m_s[c] + jnp.log(jnp.sum(l_s[c], axis=0, keepdims=True))
-        rest = logsum * (1.0 / SCALE)
-        rows = []
-        for _ in range(3):
-            part = rest.astype(BF16).astype(F32)
-            rows.append(-part)
-            rest = rest - part
-        put_under(qa_s, c, *rows)
-        return carry
-
-    lax.fori_loop(0, NC, put_logsum, 0)
-    for copy in value_copies:
-        copy.wait()
-
-    def grad_step(items, masked):
-        weights = [weights_of(c, b, masked) for c, b in items]
-        above = [
-            jnp.dot(block_of(v_s, b), ga_s[c], preferred_element_type=F32) for c, b in items
-        ]
-        score_grads = [(w * p).astype(BF16) for w, p in zip(weights, above)]
-        for (c, b), w, score_grad in zip(items, weights, score_grads):
-            for ref, term in (
-                (dv_s, jnp.dot(w.astype(BF16), do_s[c], preferred_element_type=F32)),
-                (dk_s, jnp.dot(score_grad, q_s[c], preferred_element_type=F32)),
-            ):
-                ref[pl.ds(2 * b, 2)] += term.reshape(2, 2, 2, R, D)
-            dq_s[c] += jnp.dot(kt_s[b], score_grad, preferred_element_type=F32)
-
-    def masked_grads(i, carry):
-        at = [2 * i + k for k in range(2)]
-        grad_step([(masked_c[n], masked_b[n]) for n in at], True)
-        return carry
-
-    def plain_grads(i, carry):
-        at = [W * i + k for k in range(W)]
-        grad_step([(plain_c[n], plain_b[n]) for n in at], False)
-        return carry
-
-    lax.fori_loop(0, (n_masked + 1) // 2, masked_grads, 0)
-    lax.fori_loop(0, (n_plain + W - 1) // W, plain_grads, 0)
+        def plain_grads(i, carry):
+            grad_step(plain_items(i))
+            return carry
+
+        lax.fori_loop(0, n_masked // WM, masked_grads, 0)
+        lax.fori_loop(0, n_plain // W, plain_grads, 0)
+        return unused
+
+    lax.fori_loop(0, NC // HC, half_step, 0)
 
     def finish(c, carry):
-        dq = (dq_s[c] * SCALE).T.astype(BF16)
+        dq = (dq_s[c] * (m_s[c] * SCALE)).T.astype(BF16)
         dq_out[2 * c] = dq[:QR]
         dq_out[2 * c + 1] = dq[QR:]
         return carry
@@ -442,27 +467,28 @@
         out_shape=[bf16(16, QR, D)] + [group] * 3 + [half] * 2 + [group] * 4,
         in_specs=[IN_SMEM] * 2 + [ANYWHERE] * 11,
         scratch_shapes=[
-            pltpu.SMEM((NC * NT // 2 + W,), jnp.int32),
-            pltpu.SMEM((NC * NT // 2 + W,), jnp.int32),
-            pltpu.SMEM((NC * NT // 2 + NC + W,), jnp.int32),
-            pltpu.SMEM((NC * NT // 2 + NC + W,), jnp.int32),
-            pltpu.VMEM((NC + 1, C, D), BF16),
-            pltpu.VMEM((NC + 1, C, D), BF16),
+            pltpu.SMEM((HC * NT // 2 + W,), jnp.int32),
+            pltpu.SMEM((HC * NT // 2 + W,), jnp.int32),
+            pltpu.SMEM((HC * NT // 2 + HC + W,), jnp.int32),
+            pltpu.SMEM((HC * NT // 2 + HC + W,), jnp.int32),
+            pltpu.VMEM((NC, C, D), BF16),
+            pltpu.VMEM((NC, C, D), BF16),
             pltpu.VMEM((16, 16, D), BF16),
             pltpu.VMEM((NT, 2, 2, R, 2 * D), BF16),
             pltpu.VMEM((NT, 2, 2, R, 2 * D), BF16),
             pltpu.VMEM((NT // 2, D, KB), BF16),
             pltpu.VMEM((NC + 1, 2 * D, C), BF16),
             pltpu.VMEM((NC + 1, 2 * D, C), BF16),
+            pltpu.VMEM((HC * NT // 2 + W + WM, KB, C), BF16),
             pltpu.VMEM((NC, 1, C), F32),
             pltpu.VMEM((NC + 1, 8, C), F32),
             pltpu.VMEM((NT, 2, 2, R, D), F32),
             pltpu.VMEM((NT, 2, 2, R, D), F32),
-            pltpu.VMEM((NC + 1, D, C), F32),
+            pltpu.VMEM((NC, D, C), F32),
             pltpu.SemaphoreType.DMA,
             pltpu.SemaphoreType.DMA,
         ],
-        compiler_params=pltpu.CompilerParams(vmem_limit_bytes=48 << 20),
+        compiler_params=pltpu.CompilerParams(vmem_limit_bytes=56 << 20),
     )(span_order, counts, qpay, *mine, *[flip(array) for array in mine])
     far_sum_a, far_sum_b = on_vmem(far_sum_kernel, [half, half], sum_a, sum_b, flip(far_give))
     from_1 = swap(far_sum_a, 1)

time: 136 us -> 140 us (1.029); the launches traced: 137 us -> 139 us
  starting transfers between devices: 22.7 us -> 12.1 us
  Pallas kernels: 36.9 us -> 47.1 us
  local copies, waits for them, and re-layouts: 5.22 us -> 6.89 us
    ppermute x8, starting transfers between devices: 17.9 us -> 7.49 us  [swap(): return lax.ppermute(array, 'y', [(i, i ^ distance) for i in range(4)])]
    pallas_call x1, Pallas kernels: 32.4 us -> 42.6 us  [body(): pl.pallas_call(attention_kernel, out_shape=[bf16(16, QR, D)] + [group] *...]
    unnamed x20 -> x38, local copies, waits for them, and re-layouts: 4.23 us -> 6.85 us
  transfers between devices with their start and end apart: 18 -> 18, of which waited for: 9 -> 8; matrix products, arithmetic and copies ran while one was open for 1% -> 0% of each run, Pallas kernels for 2% -> 2%
where the time goes in v5:
time: 140 us; the launch traced here: 139 us
  Pallas kernels  47.1 us (34%)
  blocking collectives  46.6 us (33%)
  waiting for transfers between devices  25.7 us (18%)
  starting transfers between devices  12.1 us (9%)
  local copies, waits for them, and re-layouts  6.89 us (5%)
    all_to_all x3, blocking collectives, exchange(): lax.all_to_all(array, SPREAD, split_axis=0, concat_axis=0, tiled=True)  46.6 us
    pallas_call x1, Pallas kernels, body(): pl.pallas_call(attention_kernel, out_shape=[bf16(16, QR, D)] + [group] *...  42.6 us
    ppermute x8, waiting for transfers between devices, swap(): return lax.ppermute(array, 'y', [(i, i ^ distance) for i in range(4)])  22.3 us
    ppermute x8, starting transfers between devices, swap(): return lax.ppermute(array, 'y', [(i, i ^ distance) for i in range(4)])  7.49 us
    unnamed x38, local copies, waits for them, and re-layouts  6.85 us
    all_to_all x1, starting transfers between devices, exchange(): lax.all_to_all(array, SPREAD, split_axis=0, concat_axis=0, tiled=True)  3.7 us
  transfers between devices with their start and end apart: 18, of which 8 were waited for; matrix products, arithmetic and copies ran while one was open for 0% of the time, Pallas kernels for 2%

profile of v5, /device:TPU:0, one launch (start us, length us, event | category | flops | bytes accessed | tf_op | source)
XLA Modules:
  0.0 139.3 jit_solution(15247383858110984455)
XLA Ops:
  0.7 1.0 copy-done.9
  1.6 0.9 copy-done.10
  2.5 0.8 copy-done.11
  3.3 0.7 shard_map.94
  4.0 0.0 copy-start.12
  4.0 19.3 %all_to_all.20.after.refs_0_ = bf16[16,128,128]{2,1,0:T(8,128)(2,1)S(1)} all-to-all(bf16[16,128,128]{2,1,0:T(8,128)(2,1)S(1)} %get-tuple-element.24), channel_id=1, replica_groups=mesh['z'=4,'core'=2,'xh'=2,'xl'=2,'y'=4] {'xh','xl','z'}, dimensions={0} | all-to-all | bytes 1048576 | tf_op jit(solution)/shard_map/all_to_all | solution.py:431
  23.3 3.0 %collective-permute-start.1 = (bf16[16,128,128]{2,1,0:T(8,128)(2,1)S(1)}, bf16[16,128,128]{2,1,0:T(8,128)(2,1)S(1)}, u32[]{:S(2)}, u32[]{:S(2)}) collective-permute-start(bf16[16,128,128]{2,1,0:T(8,128)(2,1)S(1)} %all_to_all.20.after.refs_0_), channel_id=1, source_target_pairs={{0,3},{1,2},{2,1},{3,0},{4,7},{5,6},{6,5},{7,4},{8,11},{9,10},{10,... | collective-permute-start | bytes 1572872 | tf_op jit(solution)/shard_map/ppermute | solution.py:439
  26.3 0.1 collective-permute-start
  26.5 1.0 copy-done.3
  27.5 1.7 %shard_map.95 = bf16[16,272,128]{2,1,0:T(8,128)(2,1)} custom-call(bf16[64,4096]{1,0:T(8,128)(2,1)S(1)} %copy-done.1, bf16[64,4096]{1,0:T(8,128)(2,1)S(1)} %copy-done.2, bf16[64,4096]{1,0:T(8,128)(2,1)S(1)} %copy-done.3, bf16[16,128,128]{2,1,0:T(8,128)(2,1)S(1)} %all_to_all.20.after.refs_0_), custom_call_target="tpu_custom_call" | custom-call | tf_op jit(solution)/shard_map/pallas_call | solution.py:450
  29.2 3.7 %all-to-all-start.1 = ((bf16[16,272,128]{2,1,0:T(8,128)(2,1)}), bf16[16,272,128]{2,1,0:T(8,128)(2,1)S(1)}, u32[]{:S(2)}, u32[]{:S(2)}) async-start(bf16[16,272,128]{2,1,0:T(8,128)(2,1)} %shard_map.95), calls=%async_computation.1 | async-start | bytes 2228224 | tf_op jit(solution)/shard_map/all_to_all | solution.py:431
  32.9 0.1 collective-permute-start.4
  33.0 3.8 %collective-permute-done.1.refs_2_ = bf16[16,128,128]{2,1,0:T(8,128)(2,1)S(1)} collective-permute-done((bf16[16,128,128]{2,1,0:T(8,128)(2,1)S(1)}, bf16[16,128,128]{2,1,0:T(8,128)(2,1)S(1)}, u32[]{:S(2)}, u32[]{:S(2)}) %collective-permute-start.1) | collective-permute-done | bytes 524320 | tf_op jit(solution)/shard_map/ppermute | solution.py:439
  36.8 0.4 collective-permute-start.2
  37.2 0.0 collective-permute-start.6
  37.2 2.2 %collective-permute-done.refs_1_ = bf16[16,128,128]{2,1,0:T(8,128)(2,1)S(1)} collective-permute-done((bf16[16,128,128]{2,1,0:T(8,128)(2,1)S(1)}, bf16[16,128,128]{2,1,0:T(8,128)(2,1)S(1)}, u32[]{:S(2)}, u32[]{:S(2)}) %collective-permute-start) | collective-permute-done | bytes 524320 | tf_op jit(solution)/shard_map/ppermute | solution.py:439
  39.5 0.6 collective-permute-start.3
  40.1 0.2 collective-permute-start.5
  40.3 3.6 %collective-permute-done.2.refs_3_ = bf16[8,128,128]{2,1,0:T(8,128)(2,1)S(1)} collective-permute-done((bf16[8,128,128]{2,1,0:T(8,128)(2,1)S(1)}, bf16[8,128,128]{2,1,0:T(8,128)(2,1)S(1)}, u32[]{:S(2)}, u32[]{:S(2)}) %collective-permute-start.2) | collective-permute-done | bytes 262176 | tf_op jit(solution)/shard_map/ppermute | solution.py:439
  43.9 0.0 collective-permute-start.7
  43.9 3.5 %collective-permute-done.3.refs_4_ = bf16[8,128,128]{2,1,0:T(8,128)(2,1)} collective-permute-done((bf16[8,128,128]{2,1,0:T(8,128)(2,1)S(1)}, bf16[8,128,128]{2,1,0:T(8,128)(2,1)}, u32[]{:S(2)}, u32[]{:S(2)}) %collective-permute-start.3) | collective-permute-done | bytes 262176 | tf_op jit(solution)/shard_map/ppermute | solution.py:439
  47.3 0.0 collective-permute-start.8
  47.3 0.0 collective-permute-done.4.refs_5_
  47.3 1.8 %all-to-all-done.1.qpay = bf16[16,272,128]{2,1,0:T(8,128)(2,1)S(1)} async-done(((bf16[16,272,128]{2,1,0:T(8,128)(2,1)}), bf16[16,272,128]{2,1,0:T(8,128)(2,1)S(1)}, u32[]{:S(2)}, u32[]{:S(2)}) %all-to-all-start.1) | async-done | bytes 1114144 | tf_op jit(solution)/shard_map/all_to_all | solution.py:431
  49.2 0.0 collective-permute-done.7.refs_8_
  49.2 0.0 collective-permute-done.8.refs_9_
  49.2 1.0 copy-done.13
  50.2 42.6 %shard_map.96 = (bf16[16,128,128]{2,1,0:T(8,128)(2,1)}, bf16[16,128,128]{2,1,0:T(8,128)(2,1)}, bf16[16,128,128]{2,1,0:T(8,128)(2,1)}, bf16[16,128,128]{2,1,0:T(8...) custom-call(s32[32]{0:T(128)} %order.1, ...), custom_call_target="tpu_custom_call" | custom-call | tf_op jit(solution)/shard_map/pallas_call | solution.py:465
  92.8 0.1 collective-permute-start.12
  92.9 0.5 collective-permute-start.10
  93.4 0.1 collective-permute-start.11
  93.5 1.5 %collective-permute-done.12.got = bf16[16,128,128]{2,1,0:T(8,128)(2,1)S(1)} collective-permute-done((bf16[16,128,128]{2,1,0:T(8,128)(2,1)}, bf16[16,128,128]{2,1,0:T(8,128)(2,1)S(1)}, u32[]{:S(2)}, u32[]{:S(2)}) %collective-permute-start.12) | collective-permute-done | bytes 524320 | tf_op jit(solution)/shard_map/ppermute | solution.py:435
  95.0 0.9 copy-done.7
  95.9 0.9 copy-done.8
  96.9 0.1 shard_map.97
  97.0 2.9 %collective-permute-start.13 = (bf16[8,128,128]{2,1,0:T(8,128)(2,1)S(1)}, bf16[8,128,128]{2,1,0:T(8,128)(2,1)S(1)}, u32[]{:S(2)}, u32[]{:S(2)}) collective-permute-start(bf16[8,128,128]{2,1,0:T(8,128)(2,1)S(1)} %get-tuple-element.34), channel_id=1, source_target_pairs={{0,1},{1,0},{2,3},{3,2},{4,5},{5,4},{6,7},{7,6},{8,9},{9,8},{10,11... | collective-permute-start | bytes 786440 | tf_op jit(solution)/shard_map/ppermute | solution.py:439
  99.9 0.0 collective-permute-done.10.got_1
  99.9 0.0 collective-permute-done.11.got_3
  99.9 6.6 %collective-permute-done.13.from_1 = bf16[8,128,128]{2,1,0:T(8,128)(2,1)S(1)} collective-permute-done((bf16[8,128,128]{2,1,0:T(8,128)(2,1)S(1)}, bf16[8,128,128]{2,1,0:T(8,128)(2,1)S(1)}, u32[]{:S(2)}, u32[]{:S(2)}) %collective-permute-start.13) | collective-permute-done | bytes 262176 | tf_op jit(solution)/shard_map/ppermute | solution.py:439
  106.5 2.7 %collective-permute-done.14.from_3 = bf16[8,128,128]{2,1,0:T(8,128)(2,1)S(1)} collective-permute-done((bf16[8,128,128]{2,1,0:T(8,128)(2,1)S(1)}, bf16[8,128,128]{2,1,0:T(8,128)(2,1)S(1)}, u32[]{:S(2)}, u32[]{:S(2)}) %collective-permute-start.14) | collective-permute-done | bytes 262176 | tf_op jit(solution)/shard_map/ppermute | solution.py:439
  109.2 0.3 shard_map.98
  109.5 0.1 collective-permute-start.15
  109.6 0.4 collective-permute-start.16
  110.0 0.3 copy-done.17
  110.2 14.0 %all_to_all.21.dq = bf16[16,128,128]{2,1,0:T(8,128)(2,1)S(1)} all-to-all(bf16[16,128,128]{2,1,0:T(8,128)(2,1)S(1)} %copy-done.17), channel_id=1, replica_groups=mesh['z'=4,'core'=2,'xh'=2,'xl'=2,'y'=4] {'xh','xl','z'}, dimensions={0} | all-to-all | bytes 1048576 | tf_op jit(solution)/shard_map/all_to_all | solution.py:431
  124.3 0.9 shard_map.99
  125.2 13.3 %all_to_all.22.got = bf16[16,128,128]{2,1,0:T(8,128)(2,1)S(1)} all-to-all(bf16[16,128,128]{2,1,0:T(8,128)(2,1)S(1)} %get-tuple-element.40), channel_id=1, replica_groups=mesh['z'=4,'core'=2,'xh'=2,'xl'=2,'y'=4] {'xh','xl','z'}, dimensions={0} | all-to-all | bytes 1048576 | tf_op jit(solution)/shard_map/all_to_all | solution.py:431
  138.5 0.8 shard_map.100
  (38 shorter events, 0.1 us)
Async XLA Ops:
  0.6 25.8 %copy-start.2 = (bf16[64,4096]{1,0:T(8,128)(2,1)S(1)}, bf16[64,4096]{1,0:T(8,128)(2,1)}, u32[]{:S(2)}) copy-start(bf16[64,4096]{1,0:T(8,128)(2,1)} %saved.1) | copy-start | bytes 1572868
  0.6 25.8 %copy-start.1 = (bf16[64,4096]{1,0:T(8,128)(2,1)S(1)}, bf16[64,4096]{1,0:T(8,128)(2,1)}, u32[]{:S(2)}) copy-start(bf16[64,4096]{1,0:T(8,128)(2,1)} %queries.1) | copy-start | bytes 1572868
  0.7 1.0 copy-start.9
  1.6 0.9 copy-start.10
  2.5 0.8 copy-start.11
  4.0 22.3 %copy-start.12 = (s32[2]{0:T(128)}, s32[2]{0:T(128)S(1)}, u32[]{:S(2)}) copy-start(s32[2]{0:T(128)S(1)} %get-tuple-element.23.counts) | copy-start | bytes 28
  23.3 9.6 %copy-start = (bf16[16,128,128]{2,1,0:T(8,128)(2,1)}, bf16[16,128,128]{2,1,0:T(8,128)(2,1)S(1)}, u32[]{:S(2)}) copy-start(bf16[16,128,128]{2,1,0:T(8,128)(2,1)S(1)} %all_to_all.20.after.refs_0_) | copy-start | bytes 1572868
  23.3 13.5 %collective-permute-start.1 = (bf16[16,128,128]{2,1,0:T(8,128)(2,1)S(1)}, bf16[16,128,128]{2,1,0:T(8,128)(2,1)S(1)}, u32[]{:S(2)}, u32[]{:S(2)}) collective-permute-start(bf16[16,128,128]{2,1,0:T(8,128)(2,1)S(1)} %all_to_all.20.after.refs_0_), channel_id=1, source_target_pairs={{0,3},{1,2},{2,1},{3,0},{4,7},{5,6},{6,5},{7,4},{8,11},{9,10},{10,... | collective-permute-start | bytes 1572872 | tf_op jit(solution)/shard_map/ppermute | solution.py:439
  26.3 13.1 %collective-permute-start = (bf16[16,128,128]{2,1,0:T(8,128)(2,1)S(1)}, bf16[16,128,128]{2,1,0:T(8,128)(2,1)S(1)}, u32[]{:S(2)}, u32[]{:S(2)}) collective-permute-start(bf16[16,128,128]{2,1,0:T(8,128)(2,1)S(1)} %all_to_all.20.after.refs_0_), channel_id=1, source_target_pairs={{0,1},{1,0},{2,3},{3,2},{4,5},{5,4},{6,7},{7,6},{8,9},{9,8},{10,11... | collective-permute-start | bytes 1572872 | tf_op jit(solution)/shard_map/ppermute | solution.py:439
  26.5 1.0 copy-start.3
  29.2 20.0 %all-to-all-start.1 = ((bf16[16,272,128]{2,1,0:T(8,128)(2,1)}), bf16[16,272,128]{2,1,0:T(8,128)(2,1)S(1)}, u32[]{:S(2)}, u32[]{:S(2)}) async-start(bf16[16,272,128]{2,1,0:T(8,128)(2,1)} %shard_map.95), calls=%async_computation.1 | async-start | bytes 2228224 | tf_op jit(solution)/shard_map/all_to_all | solution.py:431
  32.9 14.4 %collective-permute-start.4 = (bf16[16,128,128]{2,1,0:T(8,128)(2,1)S(1)}, bf16[16,128,128]{2,1,0:T(8,128)(2,1)S(1)}, u32[]{:S(2)}, u32[]{:S(2)}) collective-permute-start(bf16[16,128,128]{2,1,0:T(8,128)(2,1)S(1)} %all_to_all.20.after.refs_0_), channel_id=1, source_target_pairs={{0,16},{16,0},{1,17},{17,1},{2,18},{18,2},{3,19},{19,3},{4,20},{20... | collective-permute-start | bytes 1572872 | tf_op jit(solution)/shard_map/ppermute | solution.py:435
  36.8 12.4 %copy-start.14 = (bf16[16,128,128]{2,1,0:T(8,128)(2,1)}, bf16[16,128,128]{2,1,0:T(8,128)(2,1)S(1)}, u32[]{:S(2)}) copy-start(bf16[16,128,128]{2,1,0:T(8,128)(2,1)S(1)} %collective-permute-done.1.refs_2_) | copy-start | bytes 1572868
  36.8 7.1 %collective-permute-start.2 = (bf16[8,128,128]{2,1,0:T(8,128)(2,1)S(1)}, bf16[8,128,128]{2,1,0:T(8,128)(2,1)S(1)}, u32[]{:S(2)}, u32[]{:S(2)}) collective-permute-start(bf16[8,128,128]{2,1,0:T(8,128)(2,1)S(1)} %slice.8), channel_id=1, source_target_pairs={{0,1},{1,0},{2,3},{3,2},{4,5},{5,4},{6,7},{7,6},{8,9},{9,8},{10,11... | collective-permute-start | bytes 786440 | tf_op jit(solution)/shard_map/ppermute | solution.py:439
  37.2 12.0 %collective-permute-start.6 = (bf16[16,128,128]{2,1,0:T(8,128)(2,1)S(1)}, bf16[16,128,128]{2,1,0:T(8,128)(2,1)}, u32[]{:S(2)}, u32[]{:S(2)}) collective-permute-start(bf16[16,128,128]{2,1,0:T(8,128)(2,1)S(1)} %collective-permute-done.1.refs_2_), channel_id=1, source_target_pairs={{0,16},{16,0},{1,17},{17,1},{2,18},{18,2},{3,19},{19,3},{4,20},{20... | collective-permute-start | bytes 1572872 | tf_op jit(solution)/shard_map/ppermute | solution.py:435
  39.4 9.8 %copy-start.15 = (bf16[16,128,128]{2,1,0:T(8,128)(2,1)}, bf16[16,128,128]{2,1,0:T(8,128)(2,1)S(1)}, u32[]{:S(2)}) copy-start(bf16[16,128,128]{2,1,0:T(8,128)(2,1)S(1)} %collective-permute-done.refs_1_) | copy-start | bytes 1572868
  39.5 7.9 %collective-permute-start.3 = (bf16[8,128,128]{2,1,0:T(8,128)(2,1)S(1)}, bf16[8,128,128]{2,1,0:T(8,128)(2,1)}, u32[]{:S(2)}, u32[]{:S(2)}) collective-permute-start(bf16[8,128,128]{2,1,0:T(8,128)(2,1)S(1)} %slice.9), channel_id=1, source_target_pairs={{0,3},{1,2},{2,1},{3,0},{4,7},{5,6},{6,5},{7,4},{8,11},{9,10},{10,... | collective-permute-start | bytes 786440 | tf_op jit(solution)/shard_map/ppermute | solution.py:439
  40.1 9.1 %collective-permute-start.5 = (bf16[16,128,128]{2,1,0:T(8,128)(2,1)S(1)}, bf16[16,128,128]{2,1,0:T(8,128)(2,1)}, u32[]{:S(2)}, u32[]{:S(2)}) collective-permute-start(bf16[16,128,128]{2,1,0:T(8,128)(2,1)S(1)} %collective-permute-done.refs_1_), channel_id=1, source_target_pairs={{0,16},{16,0},{1,17},{17,1},{2,18},{18,2},{3,19},{19,3},{4,20},{20... | collective-permute-start | bytes 1572872 | tf_op jit(solution)/shard_map/ppermute | solution.py:435
  43.9 5.4 %copy-start.18 = (bf16[8,128,128]{2,1,0:T(8,128)(2,1)}, bf16[8,128,128]{2,1,0:T(8,128)(2,1)S(1)}, u32[]{:S(2)}) copy-start(bf16[8,128,128]{2,1,0:T(8,128)(2,1)S(1)} %collective-permute-done.2.refs_3_) | copy-start | bytes 786436
  43.9 5.3 %collective-permute-start.7 = (bf16[8,128,128]{2,1,0:T(8,128)(2,1)S(1)}, bf16[8,128,128]{2,1,0:T(8,128)(2,1)}, u32[]{:S(2)}, u32[]{:S(2)}) collective-permute-start(bf16[8,128,128]{2,1,0:T(8,128)(2,1)S(1)} %collective-permute-done.2.refs_3_), channel_id=1, source_target_pairs={{0,16},{16,0},{1,17},{17,1},{2,18},{18,2},{3,19},{19,3},{4,20},{20... | collective-permute-start | bytes 786440 | tf_op jit(solution)/shard_map/ppermute | solution.py:435
  47.3 1.9 %collective-permute-start.8 = (bf16[8,128,128]{2,1,0:T(8,128)(2,1)}, bf16[8,128,128]{2,1,0:T(8,128)(2,1)}, u32[]{:S(2)}, u32[]{:S(2)}) collective-permute-start(bf16[8,128,128]{2,1,0:T(8,128)(2,1)} %collective-permute-done.3.refs_4_), channel_id=1, source_target_pairs={{0,16},{16,0},{1,17},{17,1},{2,18},{18,2},{3,19},{19,3},{4,20},{20... | collective-permute-start | bytes 786440 | tf_op jit(solution)/shard_map/ppermute | solution.py:435
  47.3 1.9 %copy-start.16 = (bf16[16,128,128]{2,1,0:T(8,128)(2,1)}, bf16[16,128,128]{2,1,0:T(8,128)(2,1)S(1)}, u32[]{:S(2)}) copy-start(bf16[16,128,128]{2,1,0:T(8,128)(2,1)S(1)} %collective-permute-done.4.refs_5_) | copy-start | bytes 1572868
  49.2 1.0 copy-start.13
  92.8 16.4 %copy-start.5 = (bf16[16,128,128]{2,1,0:T(8,128)(2,1)S(1)}, bf16[16,128,128]{2,1,0:T(8,128)(2,1)}, u32[]{:S(2)}) copy-start(bf16[16,128,128]{2,1,0:T(8,128)(2,1)} %get-tuple-element.27.sum_1) | copy-start | bytes 1572868
  92.8 16.4 %copy-start.6 = (bf16[16,128,128]{2,1,0:T(8,128)(2,1)S(1)}, bf16[16,128,128]{2,1,0:T(8,128)(2,1)}, u32[]{:S(2)}) copy-start(bf16[16,128,128]{2,1,0:T(8,128)(2,1)} %get-tuple-element.29.sum_3) | copy-start | bytes 1572868
  92.8 2.2 %collective-permute-start.12 = (bf16[16,128,128]{2,1,0:T(8,128)(2,1)}, bf16[16,128,128]{2,1,0:T(8,128)(2,1)S(1)}, u32[]{:S(2)}, u32[]{:S(2)}) collective-permute-start(bf16[16,128,128]{2,1,0:T(8,128)(2,1)} %get-tuple-element.33), channel_id=1, source_target_pairs={{0,16},{16,0},{1,17},{17,1},{2,18},{18,2},{3,19},{19,3},{4,20},{20... | collective-permute-start | bytes 1572872 | tf_op jit(solution)/shard_map/ppermute | solution.py:435
  92.9 7.0 %collective-permute-start.10 = (bf16[16,128,128]{2,1,0:T(8,128)(2,1)}, bf16[16,128,128]{2,1,0:T(8,128)(2,1)S(1)}, u32[]{:S(2)}, u32[]{:S(2)}) collective-permute-start(bf16[16,128,128]{2,1,0:T(8,128)(2,1)} %get-tuple-element.28), channel_id=1, source_target_pairs={{0,16},{16,0},{1,17},{17,1},{2,18},{18,2},{3,19},{19,3},{4,20},{20... | collective-permute-start | bytes 1572872 | tf_op jit(solution)/shard_map/ppermute | solution.py:435
  93.4 6.5 %collective-permute-start.11 = (bf16[16,128,128]{2,1,0:T(8,128)(2,1)}, bf16[16,128,128]{2,1,0:T(8,128)(2,1)S(1)}, u32[]{:S(2)}, u32[]{:S(2)}) collective-permute-start(bf16[16,128,128]{2,1,0:T(8,128)(2,1)} %get-tuple-element.30), channel_id=1, source_target_pairs={{0,16},{16,0},{1,17},{17,1},{2,18},{18,2},{3,19},{19,3},{4,20},{20... | collective-permute-start | bytes 1572872 | tf_op jit(solution)/shard_map/ppermute | solution.py:435
  95.0 1.0 copy-start.7
  95.9 0.9 copy-start.8
  97.0 9.5 %collective-permute-start.13 = (bf16[8,128,128]{2,1,0:T(8,128)(2,1)S(1)}, bf16[8,128,128]{2,1,0:T(8,128)(2,1)S(1)}, u32[]{:S(2)}, u32[]{:S(2)}) collective-permute-start(bf16[8,128,128]{2,1,0:T(8,128)(2,1)S(1)} %get-tuple-element.34), channel_id=1, source_target_pairs={{0,1},{1,0},{2,3},{3,2},{4,5},{5,4},{6,7},{7,6},{8,9},{9,8},{10,11... | collective-permute-start | bytes 786440 | tf_op jit(solution)/shard_map/ppermute | solution.py:439
  99.9 9.3 %collective-permute-start.14 = (bf16[8,128,128]{2,1,0:T(8,128)(2,1)S(1)}, bf16[8,128,128]{2,1,0:T(8,128)(2,1)S(1)}, u32[]{:S(2)}, u32[]{:S(2)}) collective-permute-start(bf16[8,128,128]{2,1,0:T(8,128)(2,1)S(1)} %get-tuple-element.35), channel_id=1, source_target_pairs={{0,3},{1,2},{2,1},{3,0},{4,7},{5,6},{6,5},{7,4},{8,11},{9,10},{10,... | collective-permute-start | bytes 786440 | tf_op jit(solution)/shard_map/ppermute | solution.py:439
  99.9 24.3 %collective-permute-start.9 = (bf16[16,128,128]{2,1,0:T(8,128)(2,1)}, bf16[16,128,128]{2,1,0:T(8,128)(2,1)S(1)}, u32[]{:S(2)}, u32[]{:S(2)}) collective-permute-start(bf16[16,128,128]{2,1,0:T(8,128)(2,1)} %get-tuple-element.26), channel_id=1, source_target_pairs={{0,16},{16,0},{1,17},{17,1},{2,18},{18,2},{3,19},{19,3},{4,20},{20... | collective-permute-start | bytes 1572872 | tf_op jit(solution)/shard_map/ppermute | solution.py:435
  109.2 1.0 copy-start.17
  109.5 14.8 %copy-start.4 = (bf16[16,128,128]{2,1,0:T(8,128)(2,1)S(1)}, bf16[16,128,128]{2,1,0:T(8,128)(2,1)}, u32[]{:S(2)}) copy-start(bf16[16,128,128]{2,1,0:T(8,128)(2,1)} %get-tuple-element.25.keep) | copy-start | bytes 1572868
  109.5 14.7 %collective-permute-start.15 = (bf16[16,128,128]{2,1,0:T(8,128)(2,1)S(1)}, bf16[16,128,128]{2,1,0:T(8,128)(2,1)S(1)}, u32[]{:S(2)}, u32[]{:S(2)}) collective-permute-start(bf16[16,128,128]{2,1,0:T(8,128)(2,1)S(1)} %get-tuple-element.36), channel_id=1, source_target_pairs={{0,1},{1,0},{2,3},{3,2},{4,5},{5,4},{6,7},{7,6},{8,9},{9,8},{10,11... | collective-permute-start | bytes 1572872 | tf_op jit(solution)/shard_map/ppermute | solution.py:439
  109.6 14.7 %collective-permute-start.16 = (bf16[16,128,128]{2,1,0:T(8,128)(2,1)S(1)}, bf16[16,128,128]{2,1,0:T(8,128)(2,1)S(1)}, u32[]{:S(2)}, u32[]{:S(2)}) collective-permute-start(bf16[16,128,128]{2,1,0:T(8,128)(2,1)S(1)} %get-tuple-element.37), channel_id=1, source_target_pairs={{0,3},{1,2},{2,1},{3,0},{4,7},{5,6},{6,5},{7,4},{8,11},{9,10},{10,... | collective-permute-start | bytes 1572872 | tf_op jit(solution)/shard_map/ppermute | solution.py:439

commit v6 on v4

--- a/solution.py
+++ b/solution.py
@@ -12,10 +12,10 @@
 SPAN = 256
 NT = 32
 KB = 2 * SPAN
+KS = 2 * KB
 QR = G * HR
 C = 2 * QR
 NC = 8
-W = 4
 SCALE = D**-0.5
 HIDDEN = -1e30
 LARGE = 2.0**90
@@ -75,8 +75,8 @@
 def attention_kernel(order, counts, qpay, *refs):
     pieces = refs[:10]
     dq_out, keep_0, keep_1, keep_3, sum_a, sum_b, give_0, give_1, give_3, far_give = refs[10:20]
-    (plain_c, plain_b, masked_c, masked_b, q_s, do_s, d_s, k_s, v_s, kt_s, qa_s, ga_s) = refs[20:32]
-    m_s, l_s, dk_s, dv_s, dq_s, sem, value_sem = refs[32:]
+    (todo, plain_c, plain_0, plain_1, masked_c, masked_0, masked_1) = refs[20:27]
+    qg_s, kv_s, kt_s, ones_s, qa_s, ga_s, m_s, l_s, dk_s, dv_s, dq_s, sem = refs[27:]
     n0 = counts[0]
     n1 = counts[1]
     xl = lax.axis_index("xl")
@@ -86,48 +86,27 @@
     def place(dy, xh, xl, zh):
         return order[span_id(xh, xl, y ^ dy, zh)]
 
-    copies = []
-    value_copies = []
-    for s in range(16):
-        for part, dst in ((0, q_s), (1, do_s)):
-            copies.append(
-                pltpu.make_async_copy(
-                    qpay.at[s, pl.ds(part * QR, QR)], dst.at[s // 2, pl.ds((s % 2) * QR, QR)], sem
-                )
-            )
-    copies.append(pltpu.make_async_copy(qpay.at[:, pl.ds(2 * QR, 16)], d_s, sem))
+    copies = [pltpu.make_async_copy(qpay, qg_s, sem)]
     for number, piece in enumerate(pieces):
         from_core = core if number < 5 else 1 - core
         dy = (0, 1, 3, 2, 2)[number % 5]
         halves = ((0, 1), (0, 1), (0, 1), (0,), (1,))[number % 5]
         for at in range(4 * len(halves)):
             rank = place(dy, halves[at // 4], at // 2 % 2, at % 2)
-            rows = piece.at[pl.ds(2 * at, 2)]
             copies.append(
                 pltpu.make_async_copy(
-                    rows.at[:, pl.ds(0, R)], k_s.at[rank, :, from_core, :, pl.ds(0, D)], sem
+                    piece.at[pl.ds(2 * at, 2)], kv_s.at[rank, :, from_core], sem
                 )
             )
-            value_copies.append(
-                pltpu.make_async_copy(
-                    rows.at[:, pl.ds(R, R)], v_s.at[rank, :, from_core, :, pl.ds(0, D)], value_sem
-                )
-            )
-    for copy in copies + value_copies:
+    for copy in copies:
         copy.start()
 
-    beside = lax.broadcasted_iota(jnp.int32, (1, 1, 1, 1, D), 4) < 3
-    beside = jnp.broadcast_to(beside.astype(F32), (1, 2, 2, R, D)).astype(BF16)
-
-    def put_beside(i, carry):
-        k_s[pl.ds(i, 1), :, :, :, D:] = beside
-        v_s[pl.ds(i, 1), :, :, :, D:] = beside
-        return carry
-
-    lax.fori_loop(0, NT, put_beside, 0)
+    ones_s[...] = (lax.broadcasted_iota(jnp.int32, (KS, D), 1) < 3).astype(F32).astype(BF16)
     dk_s[...] = jnp.zeros_like(dk_s)
     dv_s[...] = jnp.zeros_like(dv_s)
     dq_s[...] = jnp.zeros_like(dq_s)
+    kv_s[NT:] = jnp.zeros((2, 2, 2, 2 * R, D), BF16)
+    kt_s[NT // 2] = jnp.zeros((D, KB), BF16)
 
     def span_of(c):
         return order[span_id(c // 4, c // 2 % 2, y, c % 2)]
@@ -143,42 +122,70 @@
         lo = jnp.minimum(jnp.where(has_second, n0 // KB, 0), hi)
         skip_at = jnp.where(all_second, (n0 + (KB - 1)) // KB, hi)
         skip_to = jnp.where(all_second, n1 // KB, 0)
+        all_plain = lo + n_full - hi
+
+        def plain_at(i):
+            return jnp.where(i < lo, i, i + (hi - lo))
+
+        def put_plain(i, n):
+            plain_c[n] = c
+            plain_0[n] = plain_at(2 * i)
+            plain_1[n] = plain_at(2 * i + 1)
+            return n + 1
+
+        def put_todo(b, n):
+            hidden = (b >= skip_at) & (b < skip_to)
+            todo[n] = b
+            return jnp.where(hidden, n, n + 1)
+
+        n_plain = lax.fori_loop(0, all_plain // 2, put_plain, n_plain)
+        todo[0] = n_full
+        n_todo = lax.fori_loop(lo, hi, put_todo, jnp.int32(1))
+        todo[n_todo] = plain_at(all_plain - 1)
+        n_todo = n_todo + all_plain % 2
+        todo[n_todo] = NT // 2
         masked_c[c] = c
-        masked_b[c] = n_full
-
-        def put_plain(b, n):
-            plain_c[n] = c
-            plain_b[n] = b
+        masked_0[c] = todo[0]
+        masked_1[c] = todo[1]
+
+        def put_masked(i, n):
+            masked_c[n] = c
+            masked_0[n] = todo[2 * i]
+            masked_1[n] = todo[2 * i + 1]
             return n + 1
 
-        def put_masked(b, n):
-            hidden = (b >= skip_at) & (b < skip_to)
-            masked_c[n] = c
-            masked_b[n] = b
-            return jnp.where(hidden, n, n + 1)
-
-        n_plain = lax.fori_loop(0, lo, put_plain, n_plain)
-        n_plain = lax.fori_loop(hi, n_full, put_plain, n_plain)
-        return n_plain, lax.fori_loop(lo, hi, put_masked, n_masked)
+        return n_plain, lax.fori_loop(1, (n_todo + 1) // 2, put_masked, n_masked)
 
     n_plain, n_masked = lax.fori_loop(0, NC, list_chunk, (jnp.int32(0), jnp.int32(NC)))
-    for i in range(W - 1):
-        plain_c[n_plain + i] = NC
-        plain_b[n_plain + i] = 0
-        masked_c[n_masked + i] = NC
-        masked_b[n_masked + i] = 0
+    plain_c[n_plain] = NC
+    plain_0[n_plain] = 0
+    plain_1[n_plain] = 0
+
+    def plain_item(n):
+        return plain_c[n], plain_0[n], plain_1[n]
+
+    def masked_item(n):
+        return masked_c[n], masked_0[n], masked_1[n]
 
     for copy in copies:
         copy.wait()
 
-    def block_of(ref, b):
-        return ref[pl.ds(2 * b, 2)].reshape(KB, 2 * D)
-
-    def keys_of(b):
-        return k_s[pl.ds(2 * b, 2), :, :, :, :D].reshape(KB, D)
+    def block_of(b, part):
+        return kv_s[pl.ds(2 * b, 2), :, :, part * R : (part + 1) * R].reshape(KB, D)
+
+    def rows_of(item, part):
+        _, b0, b1 = item
+        return jnp.concatenate([block_of(b0, part), block_of(b1, part)], axis=0)
+
+    def with_ones(rows):
+        return jnp.concatenate([rows, ones_s[...]], axis=1)
+
+    def query_rows(c, part):
+        rows = slice(part * QR, (part + 1) * QR)
+        return jnp.concatenate([qg_s[2 * c, rows], qg_s[2 * c + 1, rows]], axis=0)
 
     def turn_keys(b, carry):
-        kt_s[b] = keys_of(b).T
+        kt_s[b] = block_of(b, 0).T
         return carry
 
     lax.fori_loop(0, NT // 2, turn_keys, 0)
@@ -191,9 +198,9 @@
         ref[c, D:] = block.astype(BF16)
 
     def turn_rows(c, carry):
-        qa_s[c, :D] = q_s[c].T
-        ga_s[c, :D] = do_s[c].T
-        halves = [d_s[2 * c + half].astype(F32) for half in range(2)]
+        qa_s[c, :D] = query_rows(c, 0).T
+        ga_s[c, :D] = query_rows(c, 1).T
+        halves = [qg_s[2 * c + half, 2 * QR :].astype(F32) for half in range(2)]
         put_under(
             ga_s,
             c,
@@ -205,65 +212,68 @@
     lax.fori_loop(0, NC, turn_rows, 0)
     qa_s[NC, :D] = jnp.zeros((D, C), BF16)
     put_under(qa_s, NC, jnp.full((1, C), HIDDEN, F32))
-    ga_s[NC] = jnp.zeros((2 * D, C), BF16)
-    q_s[NC] = jnp.zeros((C, D), BF16)
-    do_s[NC] = jnp.zeros((C, D), BF16)
     l_s[NC] = jnp.zeros((8, C), F32)
 
-    def seen(c, b):
+    def seen(item):
+        c, b0, b1 = item
         lane = lax.broadcasted_iota(jnp.int32, (1, C), 1)
-        row = span_of(jnp.minimum(c, NC - 1)) * SPAN + core * R + xl * HR
-        query_pos = row + (lane // QR) * (2 * R) + lane % HR
-        key_pos = b * KB + lax.broadcasted_iota(jnp.int32, (KB, 1), 0)
+        start = span_of(c) * SPAN + core * R + xl * HR
+        query_pos = start + (lane // QR) * (2 * R) + lane % HR
+        row = lax.broadcasted_iota(jnp.int32, (KS, 1), 0)
+        key_pos = jnp.where(row < KB, b0 * KB, b1 * KB - KB) + row
         low = jnp.where(query_pos >= n1, n0, n1)
         return (key_pos <= query_pos) & ((key_pos < low) | (key_pos >= n1))
 
     def add_up(weights):
-        return jnp.sum(weights.reshape(KB // 8, 8, C), axis=0)
-
-    def raw_scores(c, b):
-        return jnp.dot(keys_of(b), qa_s[c, :D], preferred_element_type=F32)
-
-    def weights_of(c, b, masked):
-        scores = jnp.dot(block_of(k_s, b), qa_s[c], preferred_element_type=F32)
+        parts = jnp.sum(weights.reshape(16, KS // 16, C), axis=0)
+        return jnp.sum(parts.reshape(KS // 128, 8, C), axis=0)
+
+    def raw_scores(item):
+        scores = jnp.dot(rows_of(item, 0), qa_s[item[0], :D], preferred_element_type=F32)
+        return jnp.where(seen(item), scores, HIDDEN)
+
+    def weights_of(item, masked):
+        scores = jnp.dot(with_ones(rows_of(item, 0)), qa_s[item[0]], preferred_element_type=F32)
         if masked:
-            scores = jnp.where(seen(c, b), scores, HIDDEN)
+            scores = jnp.where(seen(item), scores, HIDDEN)
         return jnp.exp(scores * SCALE)
 
     def diagonal_step(i, carry):
-        for c in [2 * i + k for k in range(2)]:
-            b = masked_b[c]
-            scores = jnp.where(seen(c, b), raw_scores(c, b), HIDDEN)
+        items = [masked_item(2 * i + k) for k in range(2)]
+        found = []
+        for item in items:
+            scores = raw_scores(item)
             top = jnp.max(scores, axis=0, keepdims=True).astype(BF16).astype(F32)
+            found.append((top, add_up(jnp.exp((scores - top) * SCALE))))
+        for (c, _, _), (top, total) in zip(items, found):
             put_under(qa_s, c, -top)
             m_s[c] = top * SCALE
-            l_s[c] = add_up(jnp.exp((scores - top) * SCALE))
+            l_s[c] = total
         return carry
 
     lax.fori_loop(0, NC // 2, diagonal_step, 0)
 
     def add_weights(items, masked):
-        parts = [add_up(weights_of(c, b, masked)) for c, b in items]
-        for (c, b), part in zip(items, parts):
+        parts = [add_up(weights_of(item, masked)) for item in items]
+        for (c, _, _), part in zip(items, parts):
             l_s[c] += part
 
-    def masked_stats(i, carry):
-        at = [NC + 2 * i + k for k in range(2)]
-        add_weights([(masked_c[n], masked_b[n]) for n in at], True)
+    def masked_stats(n, carry):
+        add_weights([masked_item(n)], True)
         return carry
 
     def plain_stats(i, carry):
-        at = [W * i + k for k in range(W)]
-        add_weights([(plain_c[n], plain_b[n]) for n in at], False)
-        return carry
-
-    lax.fori_loop(0, (n_masked - NC + 1) // 2, masked_stats, 0)
-    lax.fori_loop(0, (n_plain + W - 1) // W, plain_stats, 0)
+        add_weights([plain_item(2 * i), plain_item(2 * i + 1)], False)
+        return carry
+
+    lax.fori_loop(NC, n_masked, masked_stats, 0)
+    lax.fori_loop(0, (n_plain + 1) // 2, plain_stats, 0)
 
     @pl.when(jnp.logical_not(jnp.max(l_s[...]) < LARGE))
     def _():
-        def careful(c, b):
-            scores = jnp.where(seen(c, b), raw_scores(c, b) * SCALE, HIDDEN)
+        def careful(item):
+            c = item[0]
+            scores = raw_scores(item) * SCALE
             old = m_s[c]
             top = jnp.maximum(old, jnp.max(scores, axis=0, keepdims=True))
             l_s[c] = l_s[c] * jnp.exp(old - top) + add_up(jnp.exp(scores - top))
@@ -277,11 +287,11 @@
                 m_s[c] = jnp.full((1, C), HIDDEN, F32)
                 l_s[c] = jnp.zeros((8, C), F32)
 
-            careful(c, masked_b[n])
+            careful(masked_item(n))
             return carry
 
         def careful_plain(n, carry):
-            careful(plain_c[n], plain_b[n])
+            careful(plain_item(n))
             return carry
 
         lax.fori_loop(0, n_masked, careful_masked, 0)
@@ -299,35 +309,36 @@
         return carry
 
     lax.fori_loop(0, NC, put_logsum, 0)
-    for copy in value_copies:
-        copy.wait()
-
-    def grad_step(items, masked):
-        weights = [weights_of(c, b, masked) for c, b in items]
-        above = [
-            jnp.dot(block_of(v_s, b), ga_s[c], preferred_element_type=F32) for c, b in items
-        ]
-        score_grads = [(w * p).astype(BF16) for w, p in zip(weights, above)]
-        for (c, b), w, score_grad in zip(items, weights, score_grads):
-            for ref, term in (
-                (dv_s, jnp.dot(w.astype(BF16), do_s[c], preferred_element_type=F32)),
-                (dk_s, jnp.dot(score_grad, q_s[c], preferred_element_type=F32)),
-            ):
-                ref[pl.ds(2 * b, 2)] += term.reshape(2, 2, 2, R, D)
-            dq_s[c] += jnp.dot(kt_s[b], score_grad, preferred_element_type=F32)
-
-    def masked_grads(i, carry):
-        at = [2 * i + k for k in range(2)]
-        grad_step([(masked_c[n], masked_b[n]) for n in at], True)
-        return carry
-
-    def plain_grads(i, carry):
-        at = [W * i + k for k in range(W)]
-        grad_step([(plain_c[n], plain_b[n]) for n in at], False)
-        return carry
-
-    lax.fori_loop(0, (n_masked + 1) // 2, masked_grads, 0)
-    lax.fori_loop(0, (n_plain + W - 1) // W, plain_grads, 0)
+
+    def grad_step(item, masked):
+        c, b0, b1 = item
+        above = jnp.dot(with_ones(rows_of(item, 1)), ga_s[c], preferred_element_type=F32)
+        weights = weights_of(item, masked)
+        score_grad = (weights * above).astype(BF16)
+        value_term = jnp.dot(weights.astype(BF16), query_rows(c, 1), preferred_element_type=F32)
+        key_term = jnp.dot(score_grad, query_rows(c, 0), preferred_element_type=F32)
+        keys_turned = jnp.concatenate([kt_s[b0], kt_s[b1]], axis=1)
+        query_term = jnp.dot(keys_turned, score_grad, preferred_element_type=F32)
+        sums = []
+        for ref, term in ((dv_s, value_term), (dk_s, key_term)):
+            for b, part in ((b0, term[:KB]), (b1, term[KB:])):
+                at = pl.ds(2 * b, 2)
+                sums.append((ref, at, ref[at] + part.reshape(2, 2, 2, R, D)))
+        query_sum = dq_s[c] + query_term
+        for ref, at, value in sums:
+            ref[at] = value
+        dq_s[c] = query_sum
+
+    def masked_grads(n, carry):
+        grad_step(masked_item(n), True)
+        return carry
+
+    def plain_grads(n, carry):
+        grad_step(plain_item(n), False)
+        return carry
+
+    lax.fori_loop(0, n_masked, masked_grads, 0)
+    lax.fori_loop(0, n_plain, plain_grads, 0)
 
     def finish(c, carry):
         dq = (dq_s[c] * SCALE).T.astype(BF16)
@@ -442,24 +453,20 @@
         out_shape=[bf16(16, QR, D)] + [group] * 3 + [half] * 2 + [group] * 4,
         in_specs=[IN_SMEM] * 2 + [ANYWHERE] * 11,
         scratch_shapes=[
-            pltpu.SMEM((NC * NT // 2 + W,), jnp.int32),
-            pltpu.SMEM((NC * NT // 2 + W,), jnp.int32),
-            pltpu.SMEM((NC * NT // 2 + NC + W,), jnp.int32),
-            pltpu.SMEM((NC * NT // 2 + NC + W,), jnp.int32),
-            pltpu.VMEM((NC + 1, C, D), BF16),
-            pltpu.VMEM((NC + 1, C, D), BF16),
-            pltpu.VMEM((16, 16, D), BF16),
-            pltpu.VMEM((NT, 2, 2, R, 2 * D), BF16),
-            pltpu.VMEM((NT, 2, 2, R, 2 * D), BF16),
-            pltpu.VMEM((NT // 2, D, KB), BF16),
+            pltpu.SMEM((NT // 2 + 3,), jnp.int32),
+            *[pltpu.SMEM((NC * NT // 4 + 1,), jnp.int32)] * 3,
+            *[pltpu.SMEM((NC * NT // 4 + NC,), jnp.int32)] * 3,
+            pltpu.VMEM((16, 2 * QR + 16, D), BF16),
+            pltpu.VMEM((NT + 2, 2, 2, 2 * R, D), BF16),
+            pltpu.VMEM((NT // 2 + 1, D, KB), BF16),
+            pltpu.VMEM((KS, D), BF16),
             pltpu.VMEM((NC + 1, 2 * D, C), BF16),
-            pltpu.VMEM((NC + 1, 2 * D, C), BF16),
+            pltpu.VMEM((NC, 2 * D, C), BF16),
             pltpu.VMEM((NC, 1, C), F32),
             pltpu.VMEM((NC + 1, 8, C), F32),
-            pltpu.VMEM((NT, 2, 2, R, D), F32),
-            pltpu.VMEM((NT, 2, 2, R, D), F32),
-            pltpu.VMEM((NC + 1, D, C), F32),
-            pltpu.SemaphoreType.DMA,
+            pltpu.VMEM((NT + 2, 2, 2, R, D), F32),
+            pltpu.VMEM((NT + 2, 2, 2, R, D), F32),
+            pltpu.VMEM((NC, D, C), F32),
             pltpu.SemaphoreType.DMA,
         ],
         compiler_params=pltpu.CompilerParams(vmem_limit_bytes=48 << 20),

time: 136 us -> 144 us (1.059); the launches traced: 137 us -> 143 us
  Pallas kernels: 36.9 us -> 54.1 us
  starting transfers between devices: 22.7 us -> 10.6 us
    pallas_call x1, Pallas kernels: 32.4 us -> 49.6 us  [body(): pl.pallas_call(attention_kernel, out_shape=[bf16(16, QR, D)] + [group] *...]
    ppermute x8, starting transfers between devices: 17.9 us -> 5.61 us  [swap(): return lax.ppermute(array, 'y', [(i, i ^ distance) for i in range(4)])]
  transfers between devices with their start and end apart: 18 -> 18, of which waited for: 9 -> 11; matrix products, arithmetic and copies ran while one was open for 1% -> 1% of each run, Pallas kernels for 2% -> 1%
where the time goes in v6:
time: 144 us; the launch traced here: 143 us
  Pallas kernels  54.1 us (38%)
  blocking collectives  47.4 us (33%)
  waiting for transfers between devices  25.1 us (17%)
  starting transfers between devices  10.6 us (7%)
  local copies, waits for them, and re-layouts  5.22 us (4%)
    pallas_call x1, Pallas kernels, body(): pl.pallas_call(attention_kernel, out_shape=[bf16(16, QR, D)] + [group] *...  49.6 us
    all_to_all x3, blocking collectives, exchange(): lax.all_to_all(array, SPREAD, split_axis=0, concat_axis=0, tiled=True)  47.4 us
    ppermute x8, waiting for transfers between devices, swap(): return lax.ppermute(array, 'y', [(i, i ^ distance) for i in range(4)])  21.3 us
    ppermute x8, starting transfers between devices, swap(): return lax.ppermute(array, 'y', [(i, i ^ distance) for i in range(4)])  5.61 us
    unnamed x20, local copies, waits for them, and re-layouts  4.23 us
    all_to_all x1, starting transfers between devices, exchange(): lax.all_to_all(array, SPREAD, split_axis=0, concat_axis=0, tiled=True)  3.83 us
  transfers between devices with their start and end apart: 18, of which 11 were waited for; matrix products, arithmetic and copies ran while one was open for 1% of the time, Pallas kernels for 1%

profile of v6, /device:TPU:0, one launch (start us, length us, event | category | flops | bytes accessed | tf_op | source)
XLA Modules:
  0.0 143.3 jit_solution(3120843755133949151)
XLA Ops:
  0.7 1.0 copy-done.4
  1.6 0.9 copy-done.5
  2.5 0.8 copy-done.6
  3.3 0.7 shard_map.94
  4.0 19.3 %all_to_all.20.after.refs_0_ = bf16[16,128,128]{2,1,0:T(8,128)(2,1)S(1)} all-to-all(bf16[16,128,128]{2,1,0:T(8,128)(2,1)S(1)} %get-tuple-element.24), channel_id=1, replica_groups=mesh['z'=4,'core'=2,'xh'=2,'xl'=2,'y'=4] {'xh','xl','z'}, dimensions={0} | all-to-all | bytes 1048576 | tf_op jit(solution)/shard_map/all_to_all | solution.py:417
  23.3 3.0 %collective-permute-start.1 = (bf16[16,128,128]{2,1,0:T(8,128)(2,1)S(1)}, bf16[16,128,128]{2,1,0:T(8,128)(2,1)S(1)}, u32[]{:S(2)}, u32[]{:S(2)}) collective-permute-start(bf16[16,128,128]{2,1,0:T(8,128)(2,1)S(1)} %all_to_all.20.after.refs_0_), channel_id=1, source_target_pairs={{0,3},{1,2},{2,1},{3,0},{4,7},{5,6},{6,5},{7,4},{8,11},{9,10},{10,... | collective-permute-start | bytes 1572872 | tf_op jit(solution)/shard_map/ppermute | solution.py:425
  26.3 0.1 collective-permute-start
  26.4 1.0 copy-done.3
  27.5 1.7 %shard_map.95 = bf16[16,272,128]{2,1,0:T(8,128)(2,1)} custom-call(bf16[64,4096]{1,0:T(8,128)(2,1)S(1)} %copy-done.1, bf16[64,4096]{1,0:T(8,128)(2,1)S(1)} %copy-done.2, bf16[64,4096]{1,0:T(8,128)(2,1)S(1)} %copy-done.3, bf16[16,128,128]{2,1,0:T(8,128)(2,1)S(1)} %all_to_all.20.after.refs_0_), custom_call_target="tpu_custom_call" | custom-call | tf_op jit(solution)/shard_map/pallas_call | solution.py:436
  29.2 3.8 %all-to-all-start.1 = ((bf16[16,272,128]{2,1,0:T(8,128)(2,1)}), bf16[16,272,128]{2,1,0:T(8,128)(2,1)S(1)}, u32[]{:S(2)}, u32[]{:S(2)}) async-start(bf16[16,272,128]{2,1,0:T(8,128)(2,1)} %shard_map.95), calls=%async_computation.1 | async-start | bytes 2228224 | tf_op jit(solution)/shard_map/all_to_all | solution.py:417
  33.0 0.1 collective-permute-start.4
  33.1 3.7 %collective-permute-done.1.refs_2_ = bf16[16,128,128]{2,1,0:T(8,128)(2,1)S(1)} collective-permute-done((bf16[16,128,128]{2,1,0:T(8,128)(2,1)S(1)}, bf16[16,128,128]{2,1,0:T(8,128)(2,1)S(1)}, u32[]{:S(2)}, u32[]{:S(2)}) %collective-permute-start.1) | collective-permute-done | bytes 524320 | tf_op jit(solution)/shard_map/ppermute | solution.py:425
  36.8 0.4 collective-permute-start.2
  37.2 0.0 collective-permute-start.6
  37.2 2.4 %collective-permute-done.refs_1_ = bf16[16,128,128]{2,1,0:T(8,128)(2,1)} collective-permute-done((bf16[16,128,128]{2,1,0:T(8,128)(2,1)S(1)}, bf16[16,128,128]{2,1,0:T(8,128)(2,1)}, u32[]{:S(2)}, u32[]{:S(2)}) %collective-permute-start) | collective-permute-done | bytes 524320 | tf_op jit(solution)/shard_map/ppermute | solution.py:425
  39.5 1.0 slice.9
  40.5 0.5 collective-permute-start.3
  41.0 0.2 collective-permute-start.5
  41.2 2.6 %collective-permute-done.2.refs_3_ = bf16[8,128,128]{2,1,0:T(8,128)(2,1)S(1)} collective-permute-done((bf16[8,128,128]{2,1,0:T(8,128)(2,1)S(1)}, bf16[8,128,128]{2,1,0:T(8,128)(2,1)S(1)}, u32[]{:S(2)}, u32[]{:S(2)}) %collective-permute-start.2) | collective-permute-done | bytes 262176 | tf_op jit(solution)/shard_map/ppermute | solution.py:425
  43.8 0.0 collective-permute-start.7
  43.8 4.3 %collective-permute-done.3.refs_4_ = bf16[8,128,128]{2,1,0:T(8,128)(2,1)S(1)} collective-permute-done((bf16[8,128,128]{2,1,0:T(8,128)(2,1)S(1)}, bf16[8,128,128]{2,1,0:T(8,128)(2,1)S(1)}, u32[]{:S(2)}, u32[]{:S(2)}) %collective-permute-start.3) | collective-permute-done | bytes 262176 | tf_op jit(solution)/shard_map/ppermute | solution.py:425
  48.2 0.0 collective-permute-start.8
  48.2 0.0 collective-permute-done.4.refs_5_
  48.2 1.1 all-to-all-done.1.qpay
  49.2 0.4 collective-permute-done.8.refs_9_
  49.7 0.5 copy-done.8
  50.2 49.6 %shard_map.96 = (bf16[16,128,128]{2,1,0:T(8,128)(2,1)S(1)}, bf16[16,128,128]{2,1,0:T(8,128)(2,1)S(1)}, bf16[16,128,128]{2,1,0:T(8,128)(2,1)S(1)}, bf16[16,128,12...) custom-call(s32[32]{0:T(128)S(1)} %copy-done.7, ...), custom_call_target="tpu_custom_call" | custom-call | tf_op jit(solution)/shard_map/pallas_call | solution.py:451
  99.9 0.1 collective-permute-start.12
  100.0 0.5 collective-permute-start.10
  100.5 0.1 collective-permute-start.11
  100.5 1.3 collective-permute-done.12.got
  101.9 0.1 shard_map.97
  102.0 0.1 collective-permute-start.13
  102.1 0.1 collective-permute-start.14
  102.2 0.2 collective-permute-start.9
  102.4 0.2 collective-permute-done.10.got_1
  102.6 0.7 collective-permute-done.11.got_3
  103.4 7.1 %collective-permute-done.13.from_1 = bf16[8,128,128]{2,1,0:T(8,128)(2,1)S(1)} collective-permute-done((bf16[8,128,128]{2,1,0:T(8,128)(2,1)S(1)}, bf16[8,128,128]{2,1,0:T(8,128)(2,1)S(1)}, u32[]{:S(2)}, u32[]{:S(2)}) %collective-permute-start.13) | collective-permute-done | bytes 262176 | tf_op jit(solution)/shard_map/ppermute | solution.py:425
  110.4 1.3 collective-permute-done.14.from_3
  111.7 0.3 shard_map.98
  112.0 0.5 collective-permute-start.15
  112.5 0.9 collective-permute-start.16
  113.4 14.8 %all_to_all.21.dq = bf16[16,128,128]{2,1,0:T(8,128)(2,1)S(1)} all-to-all(bf16[16,128,128]{2,1,0:T(8,128)(2,1)S(1)} %get-tuple-element.38), channel_id=1, replica_groups=mesh['z'=4,'core'=2,'xh'=2,'xl'=2,'y'=4] {'xh','xl','z'}, dimensions={0} | all-to-all | bytes 1048576 | tf_op jit(solution)/shard_map/all_to_all | solution.py:417
  128.2 0.0 collective-permute-done.15.near_1
  128.2 0.0 collective-permute-done.16.near_3
  128.2 0.9 shard_map.99
  129.2 13.3 %all_to_all.22.got = bf16[16,128,128]{2,1,0:T(8,128)(2,1)S(1)} all-to-all(bf16[16,128,128]{2,1,0:T(8,128)(2,1)S(1)} %get-tuple-element.40), channel_id=1, replica_groups=mesh['z'=4,'core'=2,'xh'=2,'xl'=2,'y'=4] {'xh','xl','z'}, dimensions={0} | all-to-all | bytes 1048576 | tf_op jit(solution)/shard_map/all_to_all | solution.py:417
  142.5 0.8 shard_map.100
  (20 shorter events, 0.1 us)
Async XLA Ops:
  0.6 25.8 %copy-start.2 = (bf16[64,4096]{1,0:T(8,128)(2,1)S(1)}, bf16[64,4096]{1,0:T(8,128)(2,1)}, u32[]{:S(2)}) copy-start(bf16[64,4096]{1,0:T(8,128)(2,1)} %saved.1) | copy-start | bytes 1572868
  0.6 25.8 %copy-start.1 = (bf16[64,4096]{1,0:T(8,128)(2,1)S(1)}, bf16[64,4096]{1,0:T(8,128)(2,1)}, u32[]{:S(2)}) copy-start(bf16[64,4096]{1,0:T(8,128)(2,1)} %queries.1) | copy-start | bytes 1572868
  0.7 1.0 copy-start.4
  1.6 0.9 copy-start.5
  2.5 0.8 copy-start.6
  23.3 9.7 %copy-start = (bf16[16,128,128]{2,1,0:T(8,128)(2,1)}, bf16[16,128,128]{2,1,0:T(8,128)(2,1)S(1)}, u32[]{:S(2)}) copy-start(bf16[16,128,128]{2,1,0:T(8,128)(2,1)S(1)} %all_to_all.20.after.refs_0_) | copy-start | bytes 1572868
  23.3 13.5 %collective-permute-start.1 = (bf16[16,128,128]{2,1,0:T(8,128)(2,1)S(1)}, bf16[16,128,128]{2,1,0:T(8,128)(2,1)S(1)}, u32[]{:S(2)}, u32[]{:S(2)}) collective-permute-start(bf16[16,128,128]{2,1,0:T(8,128)(2,1)S(1)} %all_to_all.20.after.refs_0_), channel_id=1, source_target_pairs={{0,3},{1,2},{2,1},{3,0},{4,7},{5,6},{6,5},{7,4},{8,11},{9,10},{10,... | collective-permute-start | bytes 1572872 | tf_op jit(solution)/shard_map/ppermute | solution.py:425
  26.3 13.2 %collective-permute-start = (bf16[16,128,128]{2,1,0:T(8,128)(2,1)S(1)}, bf16[16,128,128]{2,1,0:T(8,128)(2,1)}, u32[]{:S(2)}, u32[]{:S(2)}) collective-permute-start(bf16[16,128,128]{2,1,0:T(8,128)(2,1)S(1)} %all_to_all.20.after.refs_0_), channel_id=1, source_target_pairs={{0,1},{1,0},{2,3},{3,2},{4,5},{5,4},{6,7},{7,6},{8,9},{9,8},{10,11... | collective-permute-start | bytes 1572872 | tf_op jit(solution)/shard_map/ppermute | solution.py:425
  26.4 1.0 copy-start.3
  29.2 21.1 %copy-start.7 = (s32[32]{0:T(128)S(1)}, s32[32]{0:T(128)}, u32[]{:S(2)}) copy-start(s32[32]{0:T(128)} %order.1) | copy-start | bytes 388
  29.2 20.1 %all-to-all-start.1 = ((bf16[16,272,128]{2,1,0:T(8,128)(2,1)}), bf16[16,272,128]{2,1,0:T(8,128)(2,1)S(1)}, u32[]{:S(2)}, u32[]{:S(2)}) async-start(bf16[16,272,128]{2,1,0:T(8,128)(2,1)} %shard_map.95), calls=%async_computation.1 | async-start | bytes 2228224 | tf_op jit(solution)/shard_map/all_to_all | solution.py:417
  33.0 15.2 %collective-permute-start.4 = (bf16[16,128,128]{2,1,0:T(8,128)(2,1)S(1)}, bf16[16,128,128]{2,1,0:T(8,128)(2,1)}, u32[]{:S(2)}, u32[]{:S(2)}) collective-permute-start(bf16[16,128,128]{2,1,0:T(8,128)(2,1)S(1)} %all_to_all.20.after.refs_0_), channel_id=1, source_target_pairs={{0,16},{16,0},{1,17},{17,1},{2,18},{18,2},{3,19},{19,3},{4,20},{20... | collective-permute-start | bytes 1572872 | tf_op jit(solution)/shard_map/ppermute | solution.py:421
  36.8 12.9 %copy-start.9 = (bf16[16,128,128]{2,1,0:T(8,128)(2,1)}, bf16[16,128,128]{2,1,0:T(8,128)(2,1)S(1)}, u32[]{:S(2)}) copy-start(bf16[16,128,128]{2,1,0:T(8,128)(2,1)S(1)} %collective-permute-done.1.refs_2_) | copy-start | bytes 1572868
  36.8 7.1 %collective-permute-start.2 = (bf16[8,128,128]{2,1,0:T(8,128)(2,1)S(1)}, bf16[8,128,128]{2,1,0:T(8,128)(2,1)S(1)}, u32[]{:S(2)}, u32[]{:S(2)}) collective-permute-start(bf16[8,128,128]{2,1,0:T(8,128)(2,1)S(1)} %slice.8), channel_id=1, source_target_pairs={{0,1},{1,0},{2,3},{3,2},{4,5},{5,4},{6,7},{7,6},{8,9},{9,8},{10,11... | collective-permute-start | bytes 786440 | tf_op jit(solution)/shard_map/ppermute | solution.py:425
  37.2 12.1 %collective-permute-start.6 = (bf16[16,128,128]{2,1,0:T(8,128)(2,1)S(1)}, bf16[16,128,128]{2,1,0:T(8,128)(2,1)}, u32[]{:S(2)}, u32[]{:S(2)}) collective-permute-start(bf16[16,128,128]{2,1,0:T(8,128)(2,1)S(1)} %collective-permute-done.1.refs_2_), channel_id=1, source_target_pairs={{0,16},{16,0},{1,17},{17,1},{2,18},{18,2},{3,19},{19,3},{4,20},{20... | collective-permute-start | bytes 1572872 | tf_op jit(solution)/shard_map/ppermute | solution.py:421
  40.5 7.7 %collective-permute-start.3 = (bf16[8,128,128]{2,1,0:T(8,128)(2,1)S(1)}, bf16[8,128,128]{2,1,0:T(8,128)(2,1)S(1)}, u32[]{:S(2)}, u32[]{:S(2)}) collective-permute-start(bf16[8,128,128]{2,1,0:T(8,128)(2,1)S(1)} %slice.9), channel_id=1, source_target_pairs={{0,3},{1,2},{2,1},{3,0},{4,7},{5,6},{6,5},{7,4},{8,11},{9,10},{10,... | collective-permute-start | bytes 786440 | tf_op jit(solution)/shard_map/ppermute | solution.py:425
  41.0 8.7 %collective-permute-start.5 = (bf16[16,128,128]{2,1,0:T(8,128)(2,1)}, bf16[16,128,128]{2,1,0:T(8,128)(2,1)}, u32[]{:S(2)}, u32[]{:S(2)}) collective-permute-start(bf16[16,128,128]{2,1,0:T(8,128)(2,1)} %collective-permute-done.refs_1_), channel_id=1, source_target_pairs={{0,16},{16,0},{1,17},{17,1},{2,18},{18,2},{3,19},{19,3},{4,20},{20... | collective-permute-start | bytes 1572872 | tf_op jit(solution)/shard_map/ppermute | solution.py:421
  43.8 5.4 %collective-permute-start.7 = (bf16[8,128,128]{2,1,0:T(8,128)(2,1)S(1)}, bf16[8,128,128]{2,1,0:T(8,128)(2,1)S(1)}, u32[]{:S(2)}, u32[]{:S(2)}) collective-permute-start(bf16[8,128,128]{2,1,0:T(8,128)(2,1)S(1)} %collective-permute-done.2.refs_3_), channel_id=1, source_target_pairs={{0,16},{16,0},{1,17},{17,1},{2,18},{18,2},{3,19},{19,3},{4,20},{20... | collective-permute-start | bytes 786440 | tf_op jit(solution)/shard_map/ppermute | solution.py:421
  48.2 1.5 %collective-permute-start.8 = (bf16[8,128,128]{2,1,0:T(8,128)(2,1)S(1)}, bf16[8,128,128]{2,1,0:T(8,128)(2,1)S(1)}, u32[]{:S(2)}, u32[]{:S(2)}) collective-permute-start(bf16[8,128,128]{2,1,0:T(8,128)(2,1)S(1)} %collective-permute-done.3.refs_4_), channel_id=1, source_target_pairs={{0,16},{16,0},{1,17},{17,1},{2,18},{18,2},{3,19},{19,3},{4,20},{20... | collective-permute-start | bytes 786440 | tf_op jit(solution)/shard_map/ppermute | solution.py:421
  49.2 1.0 copy-start.8
  99.9 2.0 %collective-permute-start.12 = (bf16[16,128,128]{2,1,0:T(8,128)(2,1)S(1)}, bf16[16,128,128]{2,1,0:T(8,128)(2,1)S(1)}, u32[]{:S(2)}, u32[]{:S(2)}) collective-permute-start(bf16[16,128,128]{2,1,0:T(8,128)(2,1)S(1)} %get-tuple-element.33), channel_id=1, source_target_pairs={{0,16},{16,0},{1,17},{17,1},{2,18},{18,2},{3,19},{19,3},{4,20},{20... | collective-permute-start | bytes 1572872 | tf_op jit(solution)/shard_map/ppermute | solution.py:421
  100.0 2.6 %collective-permute-start.10 = (bf16[16,128,128]{2,1,0:T(8,128)(2,1)S(1)}, bf16[16,128,128]{2,1,0:T(8,128)(2,1)S(1)}, u32[]{:S(2)}, u32[]{:S(2)}) collective-permute-start(bf16[16,128,128]{2,1,0:T(8,128)(2,1)S(1)} %get-tuple-element.28), channel_id=1, source_target_pairs={{0,16},{16,0},{1,17},{17,1},{2,18},{18,2},{3,19},{19,3},{4,20},{20... | collective-permute-start | bytes 1572872 | tf_op jit(solution)/shard_map/ppermute | solution.py:421
  100.5 2.9 %collective-permute-start.11 = (bf16[16,128,128]{2,1,0:T(8,128)(2,1)S(1)}, bf16[16,128,128]{2,1,0:T(8,128)(2,1)S(1)}, u32[]{:S(2)}, u32[]{:S(2)}) collective-permute-start(bf16[16,128,128]{2,1,0:T(8,128)(2,1)S(1)} %get-tuple-element.30), channel_id=1, source_target_pairs={{0,16},{16,0},{1,17},{17,1},{2,18},{18,2},{3,19},{19,3},{4,20},{20... | collective-permute-start | bytes 1572872 | tf_op jit(solution)/shard_map/ppermute | solution.py:421
  102.0 8.4 %collective-permute-start.13 = (bf16[8,128,128]{2,1,0:T(8,128)(2,1)S(1)}, bf16[8,128,128]{2,1,0:T(8,128)(2,1)S(1)}, u32[]{:S(2)}, u32[]{:S(2)}) collective-permute-start(bf16[8,128,128]{2,1,0:T(8,128)(2,1)S(1)} %get-tuple-element.34), channel_id=1, source_target_pairs={{0,1},{1,0},{2,3},{3,2},{4,5},{5,4},{6,7},{7,6},{8,9},{9,8},{10,11... | collective-permute-start | bytes 786440 | tf_op jit(solution)/shard_map/ppermute | solution.py:425
  102.1 9.6 %collective-permute-start.14 = (bf16[8,128,128]{2,1,0:T(8,128)(2,1)S(1)}, bf16[8,128,128]{2,1,0:T(8,128)(2,1)S(1)}, u32[]{:S(2)}, u32[]{:S(2)}) collective-permute-start(bf16[8,128,128]{2,1,0:T(8,128)(2,1)S(1)} %get-tuple-element.35), channel_id=1, source_target_pairs={{0,3},{1,2},{2,1},{3,0},{4,7},{5,6},{6,5},{7,4},{8,11},{9,10},{10,... | collective-permute-start | bytes 786440 | tf_op jit(solution)/shard_map/ppermute | solution.py:425
  102.2 26.1 %collective-permute-start.9 = (bf16[16,128,128]{2,1,0:T(8,128)(2,1)S(1)}, bf16[16,128,128]{2,1,0:T(8,128)(2,1)S(1)}, u32[]{:S(2)}, u32[]{:S(2)}) collective-permute-start(bf16[16,128,128]{2,1,0:T(8,128)(2,1)S(1)} %get-tuple-element.26), channel_id=1, source_target_pairs={{0,16},{16,0},{1,17},{17,1},{2,18},{18,2},{3,19},{19,3},{4,20},{20... | collective-permute-start | bytes 1572872 | tf_op jit(solution)/shard_map/ppermute | solution.py:421
  112.0 16.2 %collective-permute-start.15 = (bf16[16,128,128]{2,1,0:T(8,128)(2,1)S(1)}, bf16[16,128,128]{2,1,0:T(8,128)(2,1)S(1)}, u32[]{:S(2)}, u32[]{:S(2)}) collective-permute-start(bf16[16,128,128]{2,1,0:T(8,128)(2,1)S(1)} %get-tuple-element.36), channel_id=1, source_target_pairs={{0,1},{1,0},{2,3},{3,2},{4,5},{5,4},{6,7},{7,6},{8,9},{9,8},{10,11... | collective-permute-start | bytes 1572872 | tf_op jit(solution)/shard_map/ppermute | solution.py:425
  112.5 15.7 %collective-permute-start.16 = (bf16[16,128,128]{2,1,0:T(8,128)(2,1)S(1)}, bf16[16,128,128]{2,1,0:T(8,128)(2,1)S(1)}, u32[]{:S(2)}, u32[]{:S(2)}) collective-permute-start(bf16[16,128,128]{2,1,0:T(8,128)(2,1)S(1)} %get-tuple-element.37), channel_id=1, source_target_pairs={{0,3},{1,2},{2,1},{3,0},{4,7},{5,6},{6,5},{7,4},{8,11},{9,10},{10,... | collective-permute-start | bytes 1572872 | tf_op jit(solution)/shard_map/ppermute | solution.py:425

commit v7 on v6

--- a/solution.py
+++ b/solution.py
@@ -1,3 +1,5 @@
+import math
+
 import jax
 import jax.numpy as jnp
 from jax import lax
@@ -17,11 +19,13 @@
 C = 2 * QR
 NC = 8
 SCALE = D**-0.5
+EXP_SCALE = SCALE * math.log2(math.e)
 HIDDEN = -1e30
 LARGE = 2.0**90
 F32 = jnp.float32
 BF16 = jnp.bfloat16
 AXES = ("z", "core", "xh", "xl", "y")
+HEADS = ("xh", "z")
 SPREAD = ("xh", "xl", "z")
 NT_DIMS = (((1,), (1,)), ((), ()))
 
@@ -34,17 +38,23 @@
     return slice((g * G + h) * D, (g * G + h + 1) * D)
 
 
-def pack_kv_kernel(keys, values, segment, out, counts):
+def pack_kv_kernel(keys, values, out, keys_s, values_s, sems):
+    copies = [
+        pltpu.make_async_copy(keys, keys_s, sems.at[0]),
+        pltpu.make_async_copy(values, values_s, sems.at[1]),
+    ]
+    for copy in copies:
+        copy.start()
+    for copy, held, start in zip(copies, (keys_s, values_s), (0, R)):
+        copy.wait()
+        for g in range(8):
+            out[g, start : start + R] = held[:, g * D : (g + 1) * D]
+
+
+def pack_q_kernel(queries, saved, grads, segment, after, out, counts):
+    del after
     counts[0] = jnp.sum((segment[...] == 0).astype(jnp.int32))
     counts[1] = jnp.sum((segment[...] != 2).astype(jnp.int32))
-    for g in range(8):
-        for xl in range(2):
-            out[spread_to(g, xl), :R] = keys[:, g * D : (g + 1) * D]
-            out[spread_to(g, xl), R:] = values[:, g * D : (g + 1) * D]
-
-
-def pack_q_kernel(queries, saved, grads, after, out):
-    del after
     ones = jnp.ones((8, D), BF16)
     row = lax.broadcasted_iota(jnp.int32, (16, D), 0)
     for g in range(8):
@@ -73,10 +83,11 @@
 
 
 def attention_kernel(order, counts, qpay, *refs):
-    pieces = refs[:10]
-    dq_out, keep_0, keep_1, keep_3, sum_a, sum_b, give_0, give_1, give_3, far_give = refs[10:20]
-    (todo, plain_c, plain_0, plain_1, masked_c, masked_0, masked_1) = refs[20:27]
-    qg_s, kv_s, kt_s, ones_s, qa_s, ga_s, m_s, l_s, dk_s, dv_s, dq_s, sem = refs[27:]
+    pieces = refs[:16]
+    dq_out, keep_0, far_a, far_b, near_1a, near_3b, near_1b, near_3a = refs[16:24]
+    give_0, give_far, give_early, give_late = refs[24:28]
+    (todo, plain_c, plain_0, plain_1, masked_c, masked_0, masked_1) = refs[28:35]
+    qg_s, kv_s, kt_s, ones_s, qa_s, ga_s, m_s, l_s, dk_s, dv_s, dq_s, sem = refs[35:]
     n0 = counts[0]
     n1 = counts[1]
     xl = lax.axis_index("xl")
@@ -88,11 +99,10 @@
 
     copies = [pltpu.make_async_copy(qpay, qg_s, sem)]
     for number, piece in enumerate(pieces):
-        from_core = core if number < 5 else 1 - core
-        dy = (0, 1, 3, 2, 2)[number % 5]
-        halves = ((0, 1), (0, 1), (0, 1), (0,), (1,))[number % 5]
-        for at in range(4 * len(halves)):
-            rank = place(dy, halves[at // 4], at // 2 % 2, at % 2)
+        from_core = core if number < 8 else 1 - core
+        from_xl = xl if number % 8 < 4 else 1 - xl
+        for at in range(4):
+            rank = place((0, 1, 3, 2)[number % 4], at // 2, from_xl, at % 2)
             copies.append(
                 pltpu.make_async_copy(
                     piece.at[pl.ds(2 * at, 2)], kv_s.at[rank, :, from_core], sem
@@ -236,7 +246,7 @@
         scores = jnp.dot(with_ones(rows_of(item, 0)), qa_s[item[0]], preferred_element_type=F32)
         if masked:
             scores = jnp.where(seen(item), scores, HIDDEN)
-        return jnp.exp(scores * SCALE)
+        return jnp.exp2(scores * EXP_SCALE)
 
     def diagonal_step(i, carry):
         items = [masked_item(2 * i + k) for k in range(2)]
@@ -244,10 +254,10 @@
         for item in items:
             scores = raw_scores(item)
             top = jnp.max(scores, axis=0, keepdims=True).astype(BF16).astype(F32)
-            found.append((top, add_up(jnp.exp((scores - top) * SCALE))))
+            found.append((top, add_up(jnp.exp2((scores - top) * EXP_SCALE))))
         for (c, _, _), (top, total) in zip(items, found):
             put_under(qa_s, c, -top)
-            m_s[c] = top * SCALE
+            m_s[c] = top * EXP_SCALE
             l_s[c] = total
         return carry
 
@@ -273,10 +283,10 @@
     def _():
         def careful(item):
             c = item[0]
-            scores = raw_scores(item) * SCALE
+            scores = raw_scores(item) * EXP_SCALE
             old = m_s[c]
             top = jnp.maximum(old, jnp.max(scores, axis=0, keepdims=True))
-            l_s[c] = l_s[c] * jnp.exp(old - top) + add_up(jnp.exp(scores - top))
+            l_s[c] = l_s[c] * jnp.exp2(old - top) + add_up(jnp.exp2(scores - top))
             m_s[c] = top
 
         def careful_masked(n, carry):
@@ -298,8 +308,8 @@
         lax.fori_loop(0, n_plain, careful_plain, 0)
 
     def put_logsum(c, carry):
-        logsum = m_s[c] + jnp.log(jnp.sum(l_s[c], axis=0, keepdims=True))
-        rest = logsum * (1.0 / SCALE)
+        logsum = m_s[c] + jnp.log2(jnp.sum(l_s[c], axis=0, keepdims=True))
+        rest = logsum * (1.0 / EXP_SCALE)
         rows = []
         for _ in range(3):
             part = rest.astype(BF16).astype(F32)
@@ -349,38 +359,42 @@
     lax.fori_loop(0, NC, finish, 0)
 
     for from_core, group in (
-        (core, ((0, keep_0, 0), (1, keep_1, 0), (3, keep_3, 0), (2, sum_a, 0), (2, sum_b, 1))),
-        (1 - core, ((0, give_0, 0), (1, give_1, 0), (3, give_3, 0), (2, far_give, 0))),
+        (core, (((2, 0), far_a), ((2, 1), far_b), ((1, 0), near_1a), ((3, 1), near_3b))),
+        (1 - core, (((2, 0), (2, 1), give_far), ((1, 0), (3, 1), give_early))),
+        (core, (((1, 1), near_1b), ((3, 0), near_3a), ((0, 0), (0, 1), keep_0))),
+        (1 - core, (((1, 1), (3, 0), give_late), ((0, 0), (0, 1), give_0))),
     ):
-        for dy, out, first_xh in group:
-            for at in range(out.shape[0] // 2):
-                rank = place(dy, first_xh + at // 4, at // 2 % 2, at % 2)
-                rows = slice(2 * at, 2 * at + 2)
-                out[rows, :R] = (dk_s[rank, :, from_core] * SCALE).astype(BF16)
-                out[rows, R:] = dv_s[rank, :, from_core].astype(BF16)
-
-
-def far_sum_kernel(sum_a, sum_b, got, out_a, out_b):
-    out_a[...] = (sum_a[...].astype(F32) + got[:8].astype(F32)).astype(BF16)
-    out_b[...] = (sum_b[...].astype(F32) + got[8:].astype(F32)).astype(BF16)
-
-
-def near_sum_kernel(sum_1, got_1, sum_3, got_3, from_1, from_3, out_1, out_3):
-    for rows, with_from in ((slice(0, 8), 3), (slice(8, 16), 1)):
-        for number, keep, got, came, out in (
-            (1, sum_1, got_1, from_3, out_1),
-            (3, sum_3, got_3, from_1, out_3),
-        ):
-            total = keep[rows].astype(F32) + got[rows].astype(F32)
-            if number == with_from:
-                total = total + came[...].astype(F32)
-            out[rows] = total.astype(BF16)
-
-
-def last_sum_kernel(keep, got, near_1, near_3, dq, sums, query_grad):
-    total = keep[...].astype(F32) + got[...].astype(F32)
-    total = total + (near_1[...].astype(F32) + near_3[...].astype(F32))
-    sums[...] = total.astype(BF16)
+        for *parts, out in group:
+            for number, (dy, xh) in enumerate(parts):
+                for at in range(4):
+                    rank = place(dy, xh, at // 2, at % 2)
+                    rows = slice(number * 8 + 2 * at, number * 8 + 2 * at + 2)
+                    out[rows, :R] = (dk_s[rank, :, from_core] * SCALE).astype(BF16)
+                    out[rows, R:] = dv_s[rank, :, from_core].astype(BF16)
+
+
+def add(*terms):
+    total = terms[0].astype(F32)
+    for term in terms[1:]:
+        total = total + term.astype(F32)
+    return total.astype(BF16)
+
+
+def first_sum_kernel(far_a, far_b, near_1a, near_3b, got_far, got_early, *outs):
+    outs[0][...] = add(far_a[...], got_far[:8])
+    outs[1][...] = add(far_b[...], got_far[8:])
+    outs[2][...] = add(near_1a[...], got_early[:8])
+    outs[3][...] = add(near_3b[...], got_early[8:])
+
+
+def second_sum_kernel(near_1b, near_3a, got_late, from_1, from_3, *outs):
+    outs[0][...] = add(near_1b[...], got_late[:8], from_3[...])
+    outs[1][...] = add(near_3a[...], got_late[8:], from_1[...])
+
+
+def last_sum_kernel(keep, got, at_1a, at_3a, at_1b, at_3b, dq, sums, query_grad):
+    sums[:8] = add(keep[:8], got[:8], at_1a[...], at_3a[...])
+    sums[8:] = add(keep[8:], got[8:], at_1b[...], at_3b[...])
     for g in range(8):
         for half in range(2):
             rows = slice(half * HR, (half + 1) * HR)
@@ -413,45 +427,64 @@
 ANYWHERE = pl.BlockSpec(memory_space=pl.ANY)
 
 
-def exchange(array):
-    return lax.all_to_all(array, SPREAD, split_axis=0, concat_axis=0, tiled=True)
-
-
-def flip(array):
-    return lax.ppermute(array, "core", [(0, 1), (1, 0)])
+def exchange(array, axes=SPREAD):
+    return lax.all_to_all(array, axes, split_axis=0, concat_axis=0, tiled=True)
+
+
+def flip(array, axis="core"):
+    return lax.ppermute(array, axis, [(0, 1), (1, 0)])
 
 
 def swap(array, distance):
     return lax.ppermute(array, "y", [(i, i ^ distance) for i in range(4)])
 
 
+def come_after(array, other):
+    def nothing(*refs):
+        del refs
+
+    return pl.pallas_call(
+        nothing,
+        out_shape=jax.ShapeDtypeStruct(array.shape, array.dtype),
+        in_specs=[ANYWHERE] * 2,
+        out_specs=ANYWHERE,
+        input_output_aliases={0: 0},
+    )(array, other)
+
+
 def body(queries, keys, values, attn_out, out_grad, segment, span_order):
-    kv_packed, counts = pl.pallas_call(
+    half = bf16(8, 2 * R, D)
+    kv_packed = pl.pallas_call(
         pack_kv_kernel,
-        out_shape=[bf16(16, 2 * R, D), jax.ShapeDtypeStruct((2,), jnp.int32)],
+        out_shape=half,
+        in_specs=[ANYWHERE] * 2,
+        scratch_shapes=[pltpu.VMEM((R, 8 * D), BF16)] * 2 + [pltpu.SemaphoreType.DMA((2,))],
+        compiler_params=pltpu.CompilerParams(vmem_limit_bytes=16 << 20),
+    )(keys, values)
+    q_packed, counts = pl.pallas_call(
+        pack_q_kernel,
+        out_shape=[bf16(16, 2 * QR + 16, D), jax.ShapeDtypeStruct((2,), jnp.int32)],
+        in_specs=[IN_VMEM] * 4 + [ANYWHERE],
         out_specs=[IN_VMEM, IN_SMEM],
         compiler_params=pltpu.CompilerParams(vmem_limit_bytes=16 << 20),
-    )(keys, values, segment.reshape(64, 128))
-    own = exchange(kv_packed)
-    q_packed = pl.pallas_call(
-        pack_q_kernel,
-        out_shape=bf16(16, 2 * QR + 16, D),
-        in_specs=[IN_VMEM] * 3 + [ANYWHERE],
-        compiler_params=pltpu.CompilerParams(vmem_limit_bytes=16 << 20),
-    )(queries, attn_out, out_grad, own)
-    qpay = exchange(q_packed)
-
-    near_1 = swap(own, 1)
-    near_3 = swap(own, 3)
-    far_a = swap(near_3[:8], 1)
-    far_b = swap(near_1[8:], 3)
-    mine = (own, near_1, near_3, far_a, far_b)
+    )(queries, attn_out, out_grad, segment.reshape(64, 128), kv_packed)
+    own = exchange(kv_packed, HEADS)
+    qpay = exchange(come_after(q_packed, own))
+
+    def round_y(array, way):
+        near_1, near_3 = swap(array, 1), swap(array, 3)
+        far = swap(near_3, 1) if way == 1 else swap(near_1, 3)
+        return [array, near_1, near_3, far]
+
+    mine = round_y(own, 1) + round_y(flip(own, "xl"), 3)
     group = bf16(16, 2 * R, D)
-    half = bf16(8, 2 * R, D)
-    dq, keep_0, keep_1, keep_3, sum_a, sum_b, give_0, give_1, give_3, far_give = pl.pallas_call(
+    (
+        dq, keep_0, far_a, far_b, near_1a, near_3b, near_1b, near_3a,
+        give_0, give_far, give_early, give_late,
+    ) = pl.pallas_call(
         attention_kernel,
-        out_shape=[bf16(16, QR, D)] + [group] * 3 + [half] * 2 + [group] * 4,
-        in_specs=[IN_SMEM] * 2 + [ANYWHERE] * 11,
+        out_shape=[bf16(16, QR, D), group] + [half] * 6 + [group] * 4,
+        in_specs=[IN_SMEM] * 2 + [ANYWHERE] * 17,
         scratch_shapes=[
             pltpu.SMEM((NT // 2 + 3,), jnp.int32),
             *[pltpu.SMEM((NC * NT // 4 + 1,), jnp.int32)] * 3,
@@ -471,19 +504,25 @@
         ],
         compiler_params=pltpu.CompilerParams(vmem_limit_bytes=48 << 20),
     )(span_order, counts, qpay, *mine, *[flip(array) for array in mine])
-    far_sum_a, far_sum_b = on_vmem(far_sum_kernel, [half, half], sum_a, sum_b, flip(far_give))
-    from_1 = swap(far_sum_a, 1)
-    from_3 = swap(far_sum_b, 3)
-    to_1, to_3 = on_vmem(
-        near_sum_kernel, [group] * 2, keep_1, flip(give_1), keep_3, flip(give_3), from_1, from_3
+    far_a, far_b, near_1a, near_3b = on_vmem(
+        first_sum_kernel, [half] * 4, far_a, far_b, near_1a, near_3b, flip(give_far), flip(give_early)
     )
+    from_1 = swap(far_a, 1)
+    from_3 = swap(far_b, 3)
+    at_1a, at_3b = swap(near_1a, 1), swap(near_3b, 3)
+    near_1b, near_3a = on_vmem(
+        second_sum_kernel, [half] * 2, near_1b, near_3a, flip(give_late), from_1, from_3
+    )
+    at_1b, at_3a = swap(near_1b, 1), swap(near_3a, 3)
     sums, query_grad = on_vmem(
         last_sum_kernel,
         [group, bf16(R, 8 * G * D)],
         keep_0,
         flip(give_0),
-        swap(to_1, 1),
-        swap(to_3, 3),
+        at_1a,
+        at_3a,
+        at_1b,
+        at_3b,
         exchange(dq),
     )
     key_grad, value_grad = on_vmem(unpack_kernel, [bf16(R, 8 * D)] * 2, exchange(sums))

time: 144 us -> 153 us (1.062)
  starting transfers between devices: 10.6 us -> 24.9 us
  blocking collectives: 47.4 us -> 33.5 us
  waiting for transfers between devices: 25.1 us -> 33 us
  local copies, waits for them, and re-layouts: 5.22 us -> 7.05 us
    all_to_all x3 -> x2, blocking collectives: 47.4 us -> 33.5 us  [exchange(): return lax.all_to_all(array, axes, split_axis=0, concat_axis=0, tiled=True)]
    all_to_all x1 -> x2, starting transfers between devices: 3.83 us -> 11.7 us  [exchange(): return lax.all_to_all(array, axes, split_axis=0, concat_axis=0, tiled=True)]
    ppermute x8 -> x12, starting transfers between devices: 5.61 us -> 10.9 us  [swap(): return lax.ppermute(array, 'y', [(i, i ^ distance) for i in range(4)])]
    pallas_call x3 -> x4, Pallas kernels: 52 us -> 47.9 us  [the longest x1 46.3 us: body(): pl.pallas_call(attention_kernel, out_shape=[bf16(16, QR, D), group] + [ha...]
    all_to_all x1 -> x2, waiting for transfers between devices: 1.07 us -> 4.9 us  [exchange(): return lax.all_to_all(array, axes, split_axis=0, concat_axis=0, tiled=True)]
    ppermute x8 -> x12, waiting for transfers between devices: 21.3 us -> 24.9 us  [swap(): return lax.ppermute(array, 'y', [(i, i ^ distance) for i in range(4)])]
    unnamed x20 -> x32, local copies, waits for them, and re-layouts: 4.23 us -> 7.05 us
    pallas_call x4, Pallas kernels: 2.14 us -> 4.69 us  [on_vmem(): pl.pallas_call(kernel, out_shape=outs, compiler_params=pltpu.CompilerPara...]
  transfers between devices with their start and end apart: 18 -> 27, of which waited for: 11 -> 11; matrix products, arithmetic and copies ran while one was open for 1% -> 0% of each run, Pallas kernels for 1% -> 3%
where the time goes in v7:
time: 153 us; the launch traced here: 152 us
  Pallas kernels  52.6 us (34%)
  blocking collectives  33.5 us (22%)
  waiting for transfers between devices  33 us (22%)
  starting transfers between devices  24.9 us (16%)
  local copies, waits for them, and re-layouts  7.05 us (5%)
    pallas_call x1, Pallas kernels, body(): pl.pallas_call(attention_kernel, out_shape=[bf16(16, QR, D), group] + [ha...  46.3 us
    all_to_all x2, blocking collectives, exchange(): return lax.all_to_all(array, axes, split_axis=0, concat_axis=0, tiled=True)  33.5 us
    ppermute x12, waiting for transfers between devices, swap(): return lax.ppermute(array, 'y', [(i, i ^ distance) for i in range(4)])  24.9 us
    all_to_all x2, starting transfers between devices, exchange(): return lax.all_to_all(array, axes, split_axis=0, concat_axis=0, tiled=True)  11.7 us
    ppermute x12, starting transfers between devices, swap(): return lax.ppermute(array, 'y', [(i, i ^ distance) for i in range(4)])  10.9 us
    unnamed x32, local copies, waits for them, and re-layouts  7.05 us
    all_to_all x2, waiting for transfers between devices, exchange(): return lax.all_to_all(array, axes, split_axis=0, concat_axis=0, tiled=True)  4.9 us
    pallas_call x4, Pallas kernels, on_vmem(): pl.pallas_call(kernel, out_shape=outs, compiler_params=pltpu.CompilerPara...  4.69 us
  transfers between devices with their start and end apart: 27, of which 11 were waited for; matrix products, arithmetic and copies ran while one was open for 0% of the time, Pallas kernels for 3%

profile of v7, /device:TPU:0, one launch (start us, length us, event | category | flops | bytes accessed | tf_op | source)
XLA Modules:
  0.0 151.9 jit_solution(11041871316798225031)
XLA Ops:
  0.7 1.0 copy-done.11
  1.6 0.9 copy-done.12
  2.5 0.4 shard_map.94.after
  2.9 16.5 %all_to_all.20.refs_1_.refs_0_ = bf16[8,128,128]{2,1,0:T(8,128)(2,1)} all-to-all(bf16[8,128,128]{2,1,0:T(8,128)(2,1)S(1)} %shard_map.94.after), channel_id=1, replica_groups=mesh['z'=4,'core'=2,'xh'=2,'xl'=2,'y'=4] {'xh','z'}, dimensions={0} | all-to-all | bytes 524288 | tf_op jit(solution)/shard_map/all_to_all | solution.py:431
  19.4 0.6 collective-permute-start.3
  20.0 1.0 copy-done.3
  21.1 0.8 copy-done.13
  21.8 1.2 shard_map.95
  23.1 1.0 copy-done
  24.1 4.5 %all-to-all-start.1 = ((bf16[16,272,128]{2,1,0:T(8,128)(2,1)}), bf16[16,272,128]{2,1,0:T(8,128)(2,1)}, u32[]{:S(2)}, u32[]{:S(2)}) async-start(bf16[16,272,128]{2,1,0:T(8,128)(2,1)} %shard_map.96), calls=%async_computation.1 | async-start | bytes 2228224 | tf_op jit(solution)/shard_map/all_to_all | solution.py:431
  28.6 0.1 collective-permute-start.7
  28.7 3.1 %collective-permute-start.1 = (bf16[8,128,128]{2,1,0:T(8,128)(2,1)}, bf16[8,128,128]{2,1,0:T(8,128)(2,1)S(1)}, u32[]{:S(2)}, u32[]{:S(2)}) collective-permute-start(bf16[8,128,128]{2,1,0:T(8,128)(2,1)} %all_to_all.20.refs_1_.refs_0_), channel_id=1, source_target_pairs={{0,3},{1,2},{2,1},{3,0},{4,7},{5,6},{6,5},{7,4},{8,11},{9,10},{10,... | collective-permute-start | bytes 786440 | tf_op jit(solution)/shard_map/ppermute | solution.py:439
  31.8 0.1 collective-permute-start
  31.9 1.9 %collective-permute-start.4 = (bf16[8,128,128]{2,1,0:T(8,128)(2,1)S(1)}, bf16[8,128,128]{2,1,0:T(8,128)(2,1)S(1)}, u32[]{:S(2)}, u32[]{:S(2)}) collective-permute-start(bf16[8,128,128]{2,1,0:T(8,128)(2,1)S(1)} %collective-permute-done.3.refs_4_), channel_id=1, source_target_pairs={{0,1},{1,0},{2,3},{3,2},{4,5},{5,4},{6,7},{7,6},{8,9},{9,8},{10,11... | collective-permute-start | bytes 786440 | tf_op jit(solution)/shard_map/ppermute | solution.py:439
  33.8 0.2 collective-permute-start.5
  34.0 5.3 %collective-permute-done.1.refs_2_ = bf16[8,128,128]{2,1,0:T(8,128)(2,1)S(1)} collective-permute-done((bf16[8,128,128]{2,1,0:T(8,128)(2,1)}, bf16[8,128,128]{2,1,0:T(8,128)(2,1)S(1)}, u32[]{:S(2)}, u32[]{:S(2)}) %collective-permute-start.1) | collective-permute-done | bytes 262176 | tf_op jit(solution)/shard_map/ppermute | solution.py:439
  39.3 1.8 %collective-permute-done.refs_1_ = bf16[8,128,128]{2,1,0:T(8,128)(2,1)S(1)} collective-permute-done((bf16[8,128,128]{2,1,0:T(8,128)(2,1)}, bf16[8,128,128]{2,1,0:T(8,128)(2,1)S(1)}, u32[]{:S(2)}, u32[]{:S(2)}) %collective-permute-start) | collective-permute-done | bytes 262176 | tf_op jit(solution)/shard_map/ppermute | solution.py:439
  41.1 0.1 collective-permute-start.2
  41.2 5.5 %collective-permute-done.4.refs_5_ = bf16[8,128,128]{2,1,0:T(8,128)(2,1)S(1)} collective-permute-done((bf16[8,128,128]{2,1,0:T(8,128)(2,1)S(1)}, bf16[8,128,128]{2,1,0:T(8,128)(2,1)S(1)}, u32[]{:S(2)}, u32[]{:S(2)}) %collective-permute-start.4) | collective-permute-done | bytes 262176 | tf_op jit(solution)/shard_map/ppermute | solution.py:439
  46.8 0.2 collective-permute-start.6
  47.0 0.5 collective-permute-start.12
  47.5 0.1 collective-permute-start.13
  47.6 4.0 %collective-permute-done.2.refs_3_ = bf16[8,128,128]{2,1,0:T(8,128)(2,1)S(1)} collective-permute-done((bf16[8,128,128]{2,1,0:T(8,128)(2,1)S(1)}, bf16[8,128,128]{2,1,0:T(8,128)(2,1)S(1)}, u32[]{:S(2)}, u32[]{:S(2)}) %collective-permute-start.2) | collective-permute-done | bytes 262176 | tf_op jit(solution)/shard_map/ppermute | solution.py:439
  51.6 3.1 %collective-permute-done.6.refs_7_ = bf16[8,128,128]{2,1,0:T(8,128)(2,1)S(1)} collective-permute-done((bf16[8,128,128]{2,1,0:T(8,128)(2,1)S(1)}, bf16[8,128,128]{2,1,0:T(8,128)(2,1)S(1)}, u32[]{:S(2)}, u32[]{:S(2)}) %collective-permute-start.6) | collective-permute-done | bytes 262176 | tf_op jit(solution)/shard_map/ppermute | solution.py:439
  54.7 0.0 copy-start.5
  54.8 0.7 copy-done.5
  55.5 0.9 collective-permute-done.14.refs_15_
  56.4 0.9 copy-done.6
  57.3 46.3 %shard_map.97 = (bf16[16,128,128]{2,1,0:T(8,128)(2,1)}, bf16[16,128,128]{2,1,0:T(8,128)(2,1)}, bf16[8,128,128]{2,1,0:T(8,128)(2,1)S(1)}, bf16[8,128,128]{2,1,0:T...) custom-call(s32[32]{0:T(128)S(1)} %copy-done.14, ...), custom_call_target="tpu_custom_call" | custom-call | tf_op jit(solution)/shard_map/pallas_call | solution.py:484
  103.7 0.4 collective-permute-start.16
  104.0 0.4 collective-permute-start.17
  104.4 0.1 collective-permute-start.19
  104.5 1.5 collective-permute-done.16.got_far
  106.0 0.7 collective-permute-done.17.got_early
  106.8 1.0 shard_map.98
  107.8 0.7 copy-done.15
  108.5 0.1 collective-permute-start.15
  108.6 7.2 %all-to-all-start.2 = ((bf16[16,128,128]{2,1,0:T(8,128)(2,1)}), bf16[16,128,128]{2,1,0:T(8,128)(2,1)S(1)}, u32[]{:S(2)}, u32[]{:S(2)}) async-start(bf16[16,128,128]{2,1,0:T(8,128)(2,1)} %get-tuple-element.46), calls=%async_computation.2 | async-start | bytes 1048576 | tf_op jit(solution)/shard_map/all_to_all | solution.py:431
  115.8 2.0 %collective-permute-start.18 = (bf16[8,128,128]{2,1,0:T(8,128)(2,1)}, bf16[8,128,128]{2,1,0:T(8,128)(2,1)S(1)}, u32[]{:S(2)}, u32[]{:S(2)}) collective-permute-start(bf16[8,128,128]{2,1,0:T(8,128)(2,1)} %get-tuple-element.37), channel_id=1, source_target_pairs={{0,1},{1,0},{2,3},{3,2},{4,5},{5,4},{6,7},{7,6},{8,9},{9,8},{10,11... | collective-permute-start | bytes 786440 | tf_op jit(solution)/shard_map/ppermute | solution.py:439
  117.8 2.6 %collective-permute-start.24 = (bf16[8,128,128]{2,1,0:T(8,128)(2,1)}, bf16[8,128,128]{2,1,0:T(8,128)(2,1)S(1)}, u32[]{:S(2)}, u32[]{:S(2)}) collective-permute-start(bf16[8,128,128]{2,1,0:T(8,128)(2,1)} %copy-done.15), channel_id=1, source_target_pairs={{0,3},{1,2},{2,1},{3,0},{4,7},{5,6},{6,5},{7,4},{8,11},{9,10},{10,... | collective-permute-start | bytes 786440 | tf_op jit(solution)/shard_map/ppermute | solution.py:439
  120.4 1.9 %shard_map.99 = (bf16[8,128,128]{2,1,0:T(8,128)(2,1)}, bf16[8,128,128]{2,1,0:T(8,128)(2,1)}) custom-call(bf16[8,128,128]{2,1,0:T(8,128)(2,1)S(1)} %copy-done.8, bf16[8,128,128]{2,1,0:T(8,128)(2,1)S(1)} %copy-done.10, bf16[16,128,128]{2,1,0:T(8,128)(2,1)S(1)} %collective-permute-done.19.got_late, bf16[8,128,128]{2,1,0:T(8,128)(2,1)S(1)} %collective-permute-done.20.from_1, ...), custom_call_target="tpu_custom_call" | custom-call | tf_op jit(solution)/shard_map/pallas_call | solution.py:418
  122.3 0.6 collective-permute-start.22
  122.9 4.9 %all-to-all-done.2.dq = bf16[16,128,128]{2,1,0:T(8,128)(2,1)S(1)} async-done(((bf16[16,128,128]{2,1,0:T(8,128)(2,1)}), bf16[16,128,128]{2,1,0:T(8,128)(2,1)S(1)}, u32[]{:S(2)}, u32[]{:S(2)}) %all-to-all-start.2) | async-done | bytes 524320 | tf_op jit(solution)/shard_map/all_to_all | solution.py:431
  127.8 0.6 collective-permute-done.24.at_3b
  128.4 4.6 %collective-permute-done.22.at_3a = bf16[8,128,128]{2,1,0:T(8,128)(2,1)S(1)} collective-permute-done((bf16[8,128,128]{2,1,0:T(8,128)(2,1)}, bf16[8,128,128]{2,1,0:T(8,128)(2,1)S(1)}, u32[]{:S(2)}, u32[]{:S(2)}) %collective-permute-start.22) | collective-permute-done | bytes 262176 | tf_op jit(solution)/shard_map/ppermute | solution.py:439
  133.0 1.1 shard_map.100
  134.0 17.0 %all_to_all.21.got = bf16[16,128,128]{2,1,0:T(8,128)(2,1)S(1)} all-to-all(bf16[16,128,128]{2,1,0:T(8,128)(2,1)S(1)} %get-tuple-element.48), channel_id=1, replica_groups=mesh['z'=4,'core'=2,'xh'=2,'xl'=2,'y'=4] {'xh','xl','z'}, dimensions={0} | all-to-all | bytes 1048576 | tf_op jit(solution)/shard_map/all_to_all | solution.py:431
  151.1 0.8 shard_map.101
  (48 shorter events, 0.1 us)
Async XLA Ops:
  0.6 19.4 %copy-start.2 = (bf16[64,4096]{1,0:T(8,128)(2,1)S(1)}, bf16[64,4096]{1,0:T(8,128)(2,1)}, u32[]{:S(2)}) copy-start(bf16[64,4096]{1,0:T(8,128)(2,1)} %saved.1) | copy-start | bytes 1572868
  0.6 19.4 %copy-start.1 = (bf16[64,4096]{1,0:T(8,128)(2,1)S(1)}, bf16[64,4096]{1,0:T(8,128)(2,1)}, u32[]{:S(2)}) copy-start(bf16[64,4096]{1,0:T(8,128)(2,1)} %queries.1) | copy-start | bytes 1572868
  0.7 1.0 copy-start.11
  1.6 0.9 copy-start.12
  19.4 12.5 %collective-permute-start.3 = (bf16[8,128,128]{2,1,0:T(8,128)(2,1)}, bf16[8,128,128]{2,1,0:T(8,128)(2,1)S(1)}, u32[]{:S(2)}, u32[]{:S(2)}) collective-permute-start(bf16[8,128,128]{2,1,0:T(8,128)(2,1)} %all_to_all.20.refs_1_.refs_0_), channel_id=1, source_target_pairs={{0,4},{4,0},{1,5},{5,1},{2,6},{6,2},{3,7},{7,3},{8,12},{12,8},{9,1... | collective-permute-start | bytes 786440 | tf_op jit(solution)/shard_map/ppermute | solution.py:435
  20.0 1.0 copy-start.3
  21.1 0.8 copy-start.13
  23.1 1.0 copy-start
  24.1 32.3 %copy-start.14 = (s32[32]{0:T(128)S(1)}, s32[32]{0:T(128)}, u32[]{:S(2)}) copy-start(s32[32]{0:T(128)} %order.1) | copy-start | bytes 388
  24.1 31.4 %all-to-all-start.1 = ((bf16[16,272,128]{2,1,0:T(8,128)(2,1)}), bf16[16,272,128]{2,1,0:T(8,128)(2,1)}, u32[]{:S(2)}, u32[]{:S(2)}) async-start(bf16[16,272,128]{2,1,0:T(8,128)(2,1)} %shard_map.96), calls=%async_computation.1 | async-start | bytes 2228224 | tf_op jit(solution)/shard_map/all_to_all | solution.py:431
  28.6 5.2 %collective-permute-start.7 = (bf16[8,128,128]{2,1,0:T(8,128)(2,1)}, bf16[8,128,128]{2,1,0:T(8,128)(2,1)S(1)}, u32[]{:S(2)}, u32[]{:S(2)}) collective-permute-start(bf16[8,128,128]{2,1,0:T(8,128)(2,1)} %all_to_all.20.refs_1_.refs_0_), channel_id=1, source_target_pairs={{0,16},{16,0},{1,17},{17,1},{2,18},{18,2},{3,19},{19,3},{4,20},{20... | collective-permute-start | bytes 786440 | tf_op jit(solution)/shard_map/ppermute | solution.py:435
  28.7 10.6 %collective-permute-start.1 = (bf16[8,128,128]{2,1,0:T(8,128)(2,1)}, bf16[8,128,128]{2,1,0:T(8,128)(2,1)S(1)}, u32[]{:S(2)}, u32[]{:S(2)}) collective-permute-start(bf16[8,128,128]{2,1,0:T(8,128)(2,1)} %all_to_all.20.refs_1_.refs_0_), channel_id=1, source_target_pairs={{0,3},{1,2},{2,1},{3,0},{4,7},{5,6},{6,5},{7,4},{8,11},{9,10},{10,... | collective-permute-start | bytes 786440 | tf_op jit(solution)/shard_map/ppermute | solution.py:439
  31.8 9.4 %collective-permute-start = (bf16[8,128,128]{2,1,0:T(8,128)(2,1)}, bf16[8,128,128]{2,1,0:T(8,128)(2,1)S(1)}, u32[]{:S(2)}, u32[]{:S(2)}) collective-permute-start(bf16[8,128,128]{2,1,0:T(8,128)(2,1)} %all_to_all.20.refs_1_.refs_0_), channel_id=1, source_target_pairs={{0,1},{1,0},{2,3},{3,2},{4,5},{5,4},{6,7},{7,6},{8,9},{9,8},{10,11... | collective-permute-start | bytes 786440 | tf_op jit(solution)/shard_map/ppermute | solution.py:439
  31.9 14.8 %collective-permute-start.4 = (bf16[8,128,128]{2,1,0:T(8,128)(2,1)S(1)}, bf16[8,128,128]{2,1,0:T(8,128)(2,1)S(1)}, u32[]{:S(2)}, u32[]{:S(2)}) collective-permute-start(bf16[8,128,128]{2,1,0:T(8,128)(2,1)S(1)} %collective-permute-done.3.refs_4_), channel_id=1, source_target_pairs={{0,1},{1,0},{2,3},{3,2},{4,5},{5,4},{6,7},{7,6},{8,9},{9,8},{10,11... | collective-permute-start | bytes 786440 | tf_op jit(solution)/shard_map/ppermute | solution.py:439
  33.8 13.2 %collective-permute-start.11 = (bf16[8,128,128]{2,1,0:T(8,128)(2,1)S(1)}, bf16[8,128,128]{2,1,0:T(8,128)(2,1)S(1)}, u32[]{:S(2)}, u32[]{:S(2)}) collective-permute-start(bf16[8,128,128]{2,1,0:T(8,128)(2,1)S(1)} %collective-permute-done.3.refs_4_), channel_id=1, source_target_pairs={{0,16},{16,0},{1,17},{17,1},{2,18},{18,2},{3,19},{19,3},{4,20},{20... | collective-permute-start | bytes 786440 | tf_op jit(solution)/shard_map/ppermute | solution.py:435
  33.8 13.2 %collective-permute-start.5 = (bf16[8,128,128]{2,1,0:T(8,128)(2,1)S(1)}, bf16[8,128,128]{2,1,0:T(8,128)(2,1)S(1)}, u32[]{:S(2)}, u32[]{:S(2)}) collective-permute-start(bf16[8,128,128]{2,1,0:T(8,128)(2,1)S(1)} %collective-permute-done.3.refs_4_), channel_id=1, source_target_pairs={{0,3},{1,2},{2,1},{3,0},{4,7},{5,6},{6,5},{7,4},{8,11},{9,10},{10,... | collective-permute-start | bytes 786440 | tf_op jit(solution)/shard_map/ppermute | solution.py:439
  39.3 8.2 %collective-permute-start.9 = (bf16[8,128,128]{2,1,0:T(8,128)(2,1)S(1)}, bf16[8,128,128]{2,1,0:T(8,128)(2,1)S(1)}, u32[]{:S(2)}, u32[]{:S(2)}) collective-permute-start(bf16[8,128,128]{2,1,0:T(8,128)(2,1)S(1)} %collective-permute-done.1.refs_2_), channel_id=1, source_target_pairs={{0,16},{16,0},{1,17},{17,1},{2,18},{18,2},{3,19},{19,3},{4,20},{20... | collective-permute-start | bytes 786440 | tf_op jit(solution)/shard_map/ppermute | solution.py:435
  41.1 10.4 %collective-permute-start.2 = (bf16[8,128,128]{2,1,0:T(8,128)(2,1)S(1)}, bf16[8,128,128]{2,1,0:T(8,128)(2,1)S(1)}, u32[]{:S(2)}, u32[]{:S(2)}) collective-permute-start(bf16[8,128,128]{2,1,0:T(8,128)(2,1)S(1)} %collective-permute-done.1.refs_2_), channel_id=1, source_target_pairs={{0,1},{1,0},{2,3},{3,2},{4,5},{5,4},{6,7},{7,6},{8,9},{9,8},{10,11... | collective-permute-start | bytes 786440 | tf_op jit(solution)/shard_map/ppermute | solution.py:439
  46.8 8.0 %collective-permute-start.6 = (bf16[8,128,128]{2,1,0:T(8,128)(2,1)S(1)}, bf16[8,128,128]{2,1,0:T(8,128)(2,1)S(1)}, u32[]{:S(2)}, u32[]{:S(2)}) collective-permute-start(bf16[8,128,128]{2,1,0:T(8,128)(2,1)S(1)} %collective-permute-done.4.refs_5_), channel_id=1, source_target_pairs={{0,3},{1,2},{2,1},{3,0},{4,7},{5,6},{6,5},{7,4},{8,11},{9,10},{10,... | collective-permute-start | bytes 786440 | tf_op jit(solution)/shard_map/ppermute | solution.py:439
  47.0 7.7 %collective-permute-start.8 = (bf16[8,128,128]{2,1,0:T(8,128)(2,1)S(1)}, bf16[8,128,128]{2,1,0:T(8,128)(2,1)S(1)}, u32[]{:S(2)}, u32[]{:S(2)}) collective-permute-start(bf16[8,128,128]{2,1,0:T(8,128)(2,1)S(1)} %collective-permute-done.refs_1_), channel_id=1, source_target_pairs={{0,16},{16,0},{1,17},{17,1},{2,18},{18,2},{3,19},{19,3},{4,20},{20... | collective-permute-start | bytes 786440 | tf_op jit(solution)/shard_map/ppermute | solution.py:435
  47.0 7.7 %collective-permute-start.12 = (bf16[8,128,128]{2,1,0:T(8,128)(2,1)S(1)}, bf16[8,128,128]{2,1,0:T(8,128)(2,1)S(1)}, u32[]{:S(2)}, u32[]{:S(2)}) collective-permute-start(bf16[8,128,128]{2,1,0:T(8,128)(2,1)S(1)} %collective-permute-done.4.refs_5_), channel_id=1, source_target_pairs={{0,16},{16,0},{1,17},{17,1},{2,18},{18,2},{3,19},{19,3},{4,20},{20... | collective-permute-start | bytes 786440 | tf_op jit(solution)/shard_map/ppermute | solution.py:435
  47.5 7.2 %collective-permute-start.13 = (bf16[8,128,128]{2,1,0:T(8,128)(2,1)S(1)}, bf16[8,128,128]{2,1,0:T(8,128)(2,1)S(1)}, u32[]{:S(2)}, u32[]{:S(2)}) collective-permute-start(bf16[8,128,128]{2,1,0:T(8,128)(2,1)S(1)} %collective-permute-done.5.refs_6_), channel_id=1, source_target_pairs={{0,16},{16,0},{1,17},{17,1},{2,18},{18,2},{3,19},{19,3},{4,20},{20... | collective-permute-start | bytes 786440 | tf_op jit(solution)/shard_map/ppermute | solution.py:435
  51.6 3.1 %collective-permute-start.10 = (bf16[8,128,128]{2,1,0:T(8,128)(2,1)S(1)}, bf16[8,128,128]{2,1,0:T(8,128)(2,1)S(1)}, u32[]{:S(2)}, u32[]{:S(2)}) collective-permute-start(bf16[8,128,128]{2,1,0:T(8,128)(2,1)S(1)} %collective-permute-done.2.refs_3_), channel_id=1, source_target_pairs={{0,16},{16,0},{1,17},{17,1},{2,18},{18,2},{3,19},{19,3},{4,20},{20... | collective-permute-start | bytes 786440 | tf_op jit(solution)/shard_map/ppermute | solution.py:435
  54.7 1.7 %collective-permute-start.14 = (bf16[8,128,128]{2,1,0:T(8,128)(2,1)S(1)}, bf16[8,128,128]{2,1,0:T(8,128)(2,1)}, u32[]{:S(2)}, u32[]{:S(2)}) collective-permute-start(bf16[8,128,128]{2,1,0:T(8,128)(2,1)S(1)} %collective-permute-done.6.refs_7_), channel_id=1, source_target_pairs={{0,16},{16,0},{1,17},{17,1},{2,18},{18,2},{3,19},{19,3},{4,20},{20... | collective-permute-start | bytes 786440 | tf_op jit(solution)/shard_map/ppermute | solution.py:435
  54.7 0.7 copy-start.5
  56.4 1.0 copy-start.6
  103.6 5.0 %copy-start.7 = (bf16[8,128,128]{2,1,0:T(8,128)(2,1)}, bf16[8,128,128]{2,1,0:T(8,128)(2,1)S(1)}, u32[]{:S(2)}) copy-start(bf16[8,128,128]{2,1,0:T(8,128)(2,1)S(1)} %get-tuple-element.38.near_1b) | copy-start | bytes 786436
  103.6 5.0 %copy-start.9 = (bf16[8,128,128]{2,1,0:T(8,128)(2,1)}, bf16[8,128,128]{2,1,0:T(8,128)(2,1)S(1)}, u32[]{:S(2)}) copy-start(bf16[8,128,128]{2,1,0:T(8,128)(2,1)S(1)} %get-tuple-element.39.near_3a) | copy-start | bytes 786436
  103.7 2.4 %collective-permute-start.16 = (bf16[16,128,128]{2,1,0:T(8,128)(2,1)}, bf16[16,128,128]{2,1,0:T(8,128)(2,1)S(1)}, u32[]{:S(2)}, u32[]{:S(2)}) collective-permute-start(bf16[16,128,128]{2,1,0:T(8,128)(2,1)} %get-tuple-element.35), channel_id=1, source_target_pairs={{0,16},{16,0},{1,17},{17,1},{2,18},{18,2},{3,19},{19,3},{4,20},{20... | collective-permute-start | bytes 1572872 | tf_op jit(solution)/shard_map/ppermute | solution.py:435
  104.0 2.8 %collective-permute-start.17 = (bf16[16,128,128]{2,1,0:T(8,128)(2,1)}, bf16[16,128,128]{2,1,0:T(8,128)(2,1)S(1)}, u32[]{:S(2)}, u32[]{:S(2)}) collective-permute-start(bf16[16,128,128]{2,1,0:T(8,128)(2,1)} %get-tuple-element.36), channel_id=1, source_target_pairs={{0,16},{16,0},{1,17},{17,1},{2,18},{18,2},{3,19},{19,3},{4,20},{20... | collective-permute-start | bytes 1572872 | tf_op jit(solution)/shard_map/ppermute | solution.py:435
  104.4 13.4 %collective-permute-start.19 = (bf16[16,128,128]{2,1,0:T(8,128)(2,1)}, bf16[16,128,128]{2,1,0:T(8,128)(2,1)S(1)}, u32[]{:S(2)}, u32[]{:S(2)}) collective-permute-start(bf16[16,128,128]{2,1,0:T(8,128)(2,1)} %get-tuple-element.40), channel_id=1, source_target_pairs={{0,16},{16,0},{1,17},{17,1},{2,18},{18,2},{3,19},{19,3},{4,20},{20... | collective-permute-start | bytes 1572872 | tf_op jit(solution)/shard_map/ppermute | solution.py:435
  107.8 0.7 copy-start.15
  108.5 11.9 %collective-permute-start.20 = (bf16[8,128,128]{2,1,0:T(8,128)(2,1)}, bf16[8,128,128]{2,1,0:T(8,128)(2,1)S(1)}, u32[]{:S(2)}, u32[]{:S(2)}) collective-permute-start(bf16[8,128,128]{2,1,0:T(8,128)(2,1)} %get-tuple-element.41), channel_id=1, source_target_pairs={{0,1},{1,0},{2,3},{3,2},{4,5},{5,4},{6,7},{7,6},{8,9},{9,8},{10,11... | collective-permute-start | bytes 786440 | tf_op jit(solution)/shard_map/ppermute | solution.py:439
  108.5 11.9 %collective-permute-start.21 = (bf16[8,128,128]{2,1,0:T(8,128)(2,1)}, bf16[8,128,128]{2,1,0:T(8,128)(2,1)}, u32[]{:S(2)}, u32[]{:S(2)}) collective-permute-start(bf16[8,128,128]{2,1,0:T(8,128)(2,1)} %get-tuple-element.42), channel_id=1, source_target_pairs={{0,3},{1,2},{2,1},{3,0},{4,7},{5,6},{6,5},{7,4},{8,11},{9,10},{10,... | collective-permute-start | bytes 786440 | tf_op jit(solution)/shard_map/ppermute | solution.py:439
  108.5 19.4 %collective-permute-start.15 = (bf16[16,128,128]{2,1,0:T(8,128)(2,1)}, bf16[16,128,128]{2,1,0:T(8,128)(2,1)S(1)}, u32[]{:S(2)}, u32[]{:S(2)}) collective-permute-start(bf16[16,128,128]{2,1,0:T(8,128)(2,1)} %get-tuple-element.30), channel_id=1, source_target_pairs={{0,16},{16,0},{1,17},{17,1},{2,18},{18,2},{3,19},{19,3},{4,20},{20... | collective-permute-start | bytes 1572872 | tf_op jit(solution)/shard_map/ppermute | solution.py:435
  108.6 11.8 %copy-start.8 = (bf16[8,128,128]{2,1,0:T(8,128)(2,1)S(1)}, bf16[8,128,128]{2,1,0:T(8,128)(2,1)}, u32[]{:S(2)}) copy-start(bf16[8,128,128]{2,1,0:T(8,128)(2,1)} %copy-done.7) | copy-start | bytes 786436
  108.6 11.8 %copy-start.10 = (bf16[8,128,128]{2,1,0:T(8,128)(2,1)S(1)}, bf16[8,128,128]{2,1,0:T(8,128)(2,1)}, u32[]{:S(2)}) copy-start(bf16[8,128,128]{2,1,0:T(8,128)(2,1)} %copy-done.9) | copy-start | bytes 786436
  108.6 24.3 %copy-start.4 = (bf16[16,128,128]{2,1,0:T(8,128)(2,1)S(1)}, bf16[16,128,128]{2,1,0:T(8,128)(2,1)}, u32[]{:S(2)}) copy-start(bf16[16,128,128]{2,1,0:T(8,128)(2,1)} %get-tuple-element.29.keep) | copy-start | bytes 1572868
  108.6 19.2 %all-to-all-start.2 = ((bf16[16,128,128]{2,1,0:T(8,128)(2,1)}), bf16[16,128,128]{2,1,0:T(8,128)(2,1)S(1)}, u32[]{:S(2)}, u32[]{:S(2)}) async-start(bf16[16,128,128]{2,1,0:T(8,128)(2,1)} %get-tuple-element.46), calls=%async_computation.2 | async-start | bytes 1048576 | tf_op jit(solution)/shard_map/all_to_all | solution.py:431
  115.8 12.0 %collective-permute-start.18 = (bf16[8,128,128]{2,1,0:T(8,128)(2,1)}, bf16[8,128,128]{2,1,0:T(8,128)(2,1)S(1)}, u32[]{:S(2)}, u32[]{:S(2)}) collective-permute-start(bf16[8,128,128]{2,1,0:T(8,128)(2,1)} %get-tuple-element.37), channel_id=1, source_target_pairs={{0,1},{1,0},{2,3},{3,2},{4,5},{5,4},{6,7},{7,6},{8,9},{9,8},{10,11... | collective-permute-start | bytes 786440 | tf_op jit(solution)/shard_map/ppermute | solution.py:439
  117.8 10.6 %collective-permute-start.24 = (bf16[8,128,128]{2,1,0:T(8,128)(2,1)}, bf16[8,128,128]{2,1,0:T(8,128)(2,1)S(1)}, u32[]{:S(2)}, u32[]{:S(2)}) collective-permute-start(bf16[8,128,128]{2,1,0:T(8,128)(2,1)} %copy-done.15), channel_id=1, source_target_pairs={{0,3},{1,2},{2,1},{3,0},{4,7},{5,6},{6,5},{7,4},{8,11},{9,10},{10,... | collective-permute-start | bytes 786440 | tf_op jit(solution)/shard_map/ppermute | solution.py:439
  122.3 10.7 %collective-permute-start.22 = (bf16[8,128,128]{2,1,0:T(8,128)(2,1)}, bf16[8,128,128]{2,1,0:T(8,128)(2,1)S(1)}, u32[]{:S(2)}, u32[]{:S(2)}) collective-permute-start(bf16[8,128,128]{2,1,0:T(8,128)(2,1)} %get-tuple-element.43), channel_id=1, source_target_pairs={{0,3},{1,2},{2,1},{3,0},{4,7},{5,6},{6,5},{7,4},{8,11},{9,10},{10,... | collective-permute-start | bytes 786440 | tf_op jit(solution)/shard_map/ppermute | solution.py:439
  122.9 10.1 %collective-permute-start.23 = (bf16[8,128,128]{2,1,0:T(8,128)(2,1)}, bf16[8,128,128]{2,1,0:T(8,128)(2,1)S(1)}, u32[]{:S(2)}, u32[]{:S(2)}) collective-permute-start(bf16[8,128,128]{2,1,0:T(8,128)(2,1)} %get-tuple-element.44), channel_id=1, source_target_pairs={{0,1},{1,0},{2,3},{3,2},{4,5},{5,4},{6,7},{7,6},{8,9},{9,8},{10,11... | collective-permute-start | bytes 786440 | tf_op jit(solution)/shard_map/ppermute | solution.py:439

commit v8 on v6

--- a/solution.py
+++ b/solution.py
@@ -1,3 +1,5 @@
+import math
+
 import jax
 import jax.numpy as jnp
 from jax import lax
@@ -12,11 +14,13 @@
 SPAN = 256
 NT = 32
 KB = 2 * SPAN
-KS = 2 * KB
 QR = G * HR
 C = 2 * QR
 NC = 8
+W = 4
+WM = 2
 SCALE = D**-0.5
+EXP_SCALE = SCALE * math.log2(math.e)
 HIDDEN = -1e30
 LARGE = 2.0**90
 F32 = jnp.float32
@@ -24,6 +28,7 @@
 AXES = ("z", "core", "xh", "xl", "y")
 SPREAD = ("xh", "xl", "z")
 NT_DIMS = (((1,), (1,)), ((), ()))
+TN_DIMS = (((0,), (0,)), ((), ()))
 
 
 def spread_to(g, xl):
@@ -75,8 +80,8 @@
 def attention_kernel(order, counts, qpay, *refs):
     pieces = refs[:10]
     dq_out, keep_0, keep_1, keep_3, sum_a, sum_b, give_0, give_1, give_3, far_give = refs[10:20]
-    (todo, plain_c, plain_0, plain_1, masked_c, masked_0, masked_1) = refs[20:27]
-    qg_s, kv_s, kt_s, ones_s, qa_s, ga_s, m_s, l_s, dk_s, dv_s, dq_s, sem = refs[27:]
+    plain_c, plain_b, masked_c, masked_b = refs[20:24]
+    qg_s, kv_s, ones_s, qa_s, ga_s, m_s, l_s, dk_s, dv_s, dq_s, sem = refs[24:]
     n0 = counts[0]
     n1 = counts[1]
     xl = lax.axis_index("xl")
@@ -101,12 +106,10 @@
     for copy in copies:
         copy.start()
 
-    ones_s[...] = (lax.broadcasted_iota(jnp.int32, (KS, D), 1) < 3).astype(F32).astype(BF16)
+    ones_s[...] = (lax.broadcasted_iota(jnp.int32, (KB, D), 1) < 3).astype(F32).astype(BF16)
     dk_s[...] = jnp.zeros_like(dk_s)
     dv_s[...] = jnp.zeros_like(dv_s)
     dq_s[...] = jnp.zeros_like(dq_s)
-    kv_s[NT:] = jnp.zeros((2, 2, 2, 2 * R, D), BF16)
-    kt_s[NT // 2] = jnp.zeros((D, KB), BF16)
 
     def span_of(c):
         return order[span_id(c // 4, c // 2 % 2, y, c % 2)]
@@ -122,60 +125,55 @@
         lo = jnp.minimum(jnp.where(has_second, n0 // KB, 0), hi)
         skip_at = jnp.where(all_second, (n0 + (KB - 1)) // KB, hi)
         skip_to = jnp.where(all_second, n1 // KB, 0)
-        all_plain = lo + n_full - hi
-
-        def plain_at(i):
-            return jnp.where(i < lo, i, i + (hi - lo))
-
-        def put_plain(i, n):
+        masked_c[c] = c
+        masked_b[c] = n_full
+
+        def put_plain(b, n):
             plain_c[n] = c
-            plain_0[n] = plain_at(2 * i)
-            plain_1[n] = plain_at(2 * i + 1)
+            plain_b[n] = b
             return n + 1
 
-        def put_todo(b, n):
+        def put_masked(b, n):
             hidden = (b >= skip_at) & (b < skip_to)
-            todo[n] = b
+            masked_c[n] = c
+            masked_b[n] = b
             return jnp.where(hidden, n, n + 1)
 
-        n_plain = lax.fori_loop(0, all_plain // 2, put_plain, n_plain)
-        todo[0] = n_full
-        n_todo = lax.fori_loop(lo, hi, put_todo, jnp.int32(1))
-        todo[n_todo] = plain_at(all_plain - 1)
-        n_todo = n_todo + all_plain % 2
-        todo[n_todo] = NT // 2
-        masked_c[c] = c
-        masked_0[c] = todo[0]
-        masked_1[c] = todo[1]
-
-        def put_masked(i, n):
-            masked_c[n] = c
-            masked_0[n] = todo[2 * i]
-            masked_1[n] = todo[2 * i + 1]
-            return n + 1
-
-        return n_plain, lax.fori_loop(1, (n_todo + 1) // 2, put_masked, n_masked)
+        n_plain = lax.fori_loop(0, lo, put_plain, n_plain)
+        n_plain = lax.fori_loop(hi, n_full, put_plain, n_plain)
+        return n_plain, lax.fori_loop(lo, hi, put_masked, n_masked)
 
     n_plain, n_masked = lax.fori_loop(0, NC, list_chunk, (jnp.int32(0), jnp.int32(NC)))
-    plain_c[n_plain] = NC
-    plain_0[n_plain] = 0
-    plain_1[n_plain] = 0
+    for i in range(W - 1):
+        plain_c[n_plain + i] = NC
+        plain_b[n_plain + i] = 0
+    for i in range(WM - 1):
+        masked_c[n_masked + i] = NC
+        masked_b[n_masked + i] = 0
 
     def plain_item(n):
-        return plain_c[n], plain_0[n], plain_1[n]
+        return plain_c[n], plain_b[n]
 
     def masked_item(n):
-        return masked_c[n], masked_0[n], masked_1[n]
+        return masked_c[n], masked_b[n]
+
+    def each_step(step, first_masked):
+        def masked(i, carry):
+            step([masked_item(WM * i + k) for k in range(WM)], True)
+            return carry
+
+        def plain(i, carry):
+            step([plain_item(W * i + k) for k in range(W)], False)
+            return carry
+
+        lax.fori_loop(first_masked // WM, (n_masked + (WM - 1)) // WM, masked, 0)
+        lax.fori_loop(0, (n_plain + (W - 1)) // W, plain, 0)
 
     for copy in copies:
         copy.wait()
 
     def block_of(b, part):
         return kv_s[pl.ds(2 * b, 2), :, :, part * R : (part + 1) * R].reshape(KB, D)
-
-    def rows_of(item, part):
-        _, b0, b1 = item
-        return jnp.concatenate([block_of(b0, part), block_of(b1, part)], axis=0)
 
     def with_ones(rows):
         return jnp.concatenate([rows, ones_s[...]], axis=1)
@@ -183,12 +181,6 @@
     def query_rows(c, part):
         rows = slice(part * QR, (part + 1) * QR)
         return jnp.concatenate([qg_s[2 * c, rows], qg_s[2 * c + 1, rows]], axis=0)
-
-    def turn_keys(b, carry):
-        kt_s[b] = block_of(b, 0).T
-        return carry
-
-    lax.fori_loop(0, NT // 2, turn_keys, 0)
 
     def put_under(ref, c, *rows):
         number = lax.broadcasted_iota(jnp.int32, (D, C), 0)
@@ -215,28 +207,27 @@
     l_s[NC] = jnp.zeros((8, C), F32)
 
     def seen(item):
-        c, b0, b1 = item
+        c, b = item
         lane = lax.broadcasted_iota(jnp.int32, (1, C), 1)
-        start = span_of(c) * SPAN + core * R + xl * HR
+        start = span_of(jnp.minimum(c, NC - 1)) * SPAN + core * R + xl * HR
         query_pos = start + (lane // QR) * (2 * R) + lane % HR
-        row = lax.broadcasted_iota(jnp.int32, (KS, 1), 0)
-        key_pos = jnp.where(row < KB, b0 * KB, b1 * KB - KB) + row
+        key_pos = b * KB + lax.broadcasted_iota(jnp.int32, (KB, 1), 0)
         low = jnp.where(query_pos >= n1, n0, n1)
         return (key_pos <= query_pos) & ((key_pos < low) | (key_pos >= n1))
 
     def add_up(weights):
-        parts = jnp.sum(weights.reshape(16, KS // 16, C), axis=0)
-        return jnp.sum(parts.reshape(KS // 128, 8, C), axis=0)
+        parts = jnp.sum(weights.reshape(8, KB // 8, C), axis=0)
+        return jnp.sum(parts.reshape(KB // 64, 8, C), axis=0)
 
     def raw_scores(item):
-        scores = jnp.dot(rows_of(item, 0), qa_s[item[0], :D], preferred_element_type=F32)
+        scores = jnp.dot(block_of(item[1], 0), qa_s[item[0], :D], preferred_element_type=F32)
         return jnp.where(seen(item), scores, HIDDEN)
 
     def weights_of(item, masked):
-        scores = jnp.dot(with_ones(rows_of(item, 0)), qa_s[item[0]], preferred_element_type=F32)
+        scores = jnp.dot(with_ones(block_of(item[1], 0)), qa_s[item[0]], preferred_element_type=F32)
         if masked:
             scores = jnp.where(seen(item), scores, HIDDEN)
-        return jnp.exp(scores * SCALE)
+        return jnp.exp2(scores * EXP_SCALE)
 
     def diagonal_step(i, carry):
         items = [masked_item(2 * i + k) for k in range(2)]
@@ -244,10 +235,10 @@
         for item in items:
             scores = raw_scores(item)
             top = jnp.max(scores, axis=0, keepdims=True).astype(BF16).astype(F32)
-            found.append((top, add_up(jnp.exp((scores - top) * SCALE))))
-        for (c, _, _), (top, total) in zip(items, found):
+            found.append((top, add_up(jnp.exp2((scores - top) * EXP_SCALE))))
+        for (c, _), (top, total) in zip(items, found):
             put_under(qa_s, c, -top)
-            m_s[c] = top * SCALE
+            m_s[c] = top * EXP_SCALE
             l_s[c] = total
         return carry
 
@@ -255,28 +246,19 @@
 
     def add_weights(items, masked):
         parts = [add_up(weights_of(item, masked)) for item in items]
-        for (c, _, _), part in zip(items, parts):
+        for (c, _), part in zip(items, parts):
             l_s[c] += part
 
-    def masked_stats(n, carry):
-        add_weights([masked_item(n)], True)
-        return carry
-
-    def plain_stats(i, carry):
-        add_weights([plain_item(2 * i), plain_item(2 * i + 1)], False)
-        return carry
-
-    lax.fori_loop(NC, n_masked, masked_stats, 0)
-    lax.fori_loop(0, (n_plain + 1) // 2, plain_stats, 0)
+    each_step(add_weights, NC)
 
     @pl.when(jnp.logical_not(jnp.max(l_s[...]) < LARGE))
     def _():
         def careful(item):
             c = item[0]
-            scores = raw_scores(item) * SCALE
+            scores = raw_scores(item) * EXP_SCALE
             old = m_s[c]
             top = jnp.maximum(old, jnp.max(scores, axis=0, keepdims=True))
-            l_s[c] = l_s[c] * jnp.exp(old - top) + add_up(jnp.exp(scores - top))
+            l_s[c] = l_s[c] * jnp.exp2(old - top) + add_up(jnp.exp2(scores - top))
             m_s[c] = top
 
         def careful_masked(n, carry):
@@ -298,8 +280,8 @@
         lax.fori_loop(0, n_plain, careful_plain, 0)
 
     def put_logsum(c, carry):
-        logsum = m_s[c] + jnp.log(jnp.sum(l_s[c], axis=0, keepdims=True))
-        rest = logsum * (1.0 / SCALE)
+        logsum = m_s[c] + jnp.log2(jnp.sum(l_s[c], axis=0, keepdims=True))
+        rest = logsum * (1.0 / EXP_SCALE)
         rows = []
         for _ in range(3):
             part = rest.astype(BF16).astype(F32)
@@ -310,38 +292,28 @@
 
     lax.fori_loop(0, NC, put_logsum, 0)
 
-    def grad_step(item, masked):
-        c, b0, b1 = item
-        above = jnp.dot(with_ones(rows_of(item, 1)), ga_s[c], preferred_element_type=F32)
-        weights = weights_of(item, masked)
-        score_grad = (weights * above).astype(BF16)
-        value_term = jnp.dot(weights.astype(BF16), query_rows(c, 1), preferred_element_type=F32)
-        key_term = jnp.dot(score_grad, query_rows(c, 0), preferred_element_type=F32)
-        keys_turned = jnp.concatenate([kt_s[b0], kt_s[b1]], axis=1)
-        query_term = jnp.dot(keys_turned, score_grad, preferred_element_type=F32)
-        sums = []
-        for ref, term in ((dv_s, value_term), (dk_s, key_term)):
-            for b, part in ((b0, term[:KB]), (b1, term[KB:])):
-                at = pl.ds(2 * b, 2)
-                sums.append((ref, at, ref[at] + part.reshape(2, 2, 2, R, D)))
-        query_sum = dq_s[c] + query_term
-        for ref, at, value in sums:
-            ref[at] = value
-        dq_s[c] = query_sum
-
-    def masked_grads(n, carry):
-        grad_step(masked_item(n), True)
-        return carry
-
-    def plain_grads(n, carry):
-        grad_step(plain_item(n), False)
-        return carry
-
-    lax.fori_loop(0, n_masked, masked_grads, 0)
-    lax.fori_loop(0, n_plain, plain_grads, 0)
+    def grad_step(items, masked):
+        weights = [weights_of(item, masked) for item in items]
+        of = [jnp.minimum(c, NC - 1) for c, _ in items]
+        above = [
+            jnp.dot(with_ones(block_of(b, 1)), ga_s[c], preferred_element_type=F32)
+            for c, (_, b) in zip(of, items)
+        ]
+        score_grads = [(w * p).astype(BF16) for w, p in zip(weights, above)]
+        for c, (_, b), w, score_grad in zip(of, items, weights, score_grads):
+            for ref, term in (
+                (dv_s, jnp.dot(w.astype(BF16), query_rows(c, 1), preferred_element_type=F32)),
+                (dk_s, jnp.dot(score_grad, query_rows(c, 0), preferred_element_type=F32)),
+            ):
+                ref[pl.ds(2 * b, 2)] += term.reshape(2, 2, 2, R, D)
+            dq_s[c] += lax.dot_general(
+                score_grad, block_of(b, 0), TN_DIMS, preferred_element_type=F32
+            )
+
+    each_step(grad_step, 0)
 
     def finish(c, carry):
-        dq = (dq_s[c] * SCALE).T.astype(BF16)
+        dq = (dq_s[c] * SCALE).astype(BF16)
         dq_out[2 * c] = dq[:QR]
         dq_out[2 * c + 1] = dq[QR:]
         return carry
@@ -453,20 +425,18 @@
         out_shape=[bf16(16, QR, D)] + [group] * 3 + [half] * 2 + [group] * 4,
         in_specs=[IN_SMEM] * 2 + [ANYWHERE] * 11,
         scratch_shapes=[
-            pltpu.SMEM((NT // 2 + 3,), jnp.int32),
-            *[pltpu.SMEM((NC * NT // 4 + 1,), jnp.int32)] * 3,
-            *[pltpu.SMEM((NC * NT // 4 + NC,), jnp.int32)] * 3,
+            *[pltpu.SMEM((NC * NT // 2 + W,), jnp.int32)] * 2,
+            *[pltpu.SMEM((NC * NT // 2 + NC + W,), jnp.int32)] * 2,
             pltpu.VMEM((16, 2 * QR + 16, D), BF16),
-            pltpu.VMEM((NT + 2, 2, 2, 2 * R, D), BF16),
-            pltpu.VMEM((NT // 2 + 1, D, KB), BF16),
-            pltpu.VMEM((KS, D), BF16),
+            pltpu.VMEM((NT, 2, 2, 2 * R, D), BF16),
+            pltpu.VMEM((KB, D), BF16),
             pltpu.VMEM((NC + 1, 2 * D, C), BF16),
             pltpu.VMEM((NC, 2 * D, C), BF16),
             pltpu.VMEM((NC, 1, C), F32),
             pltpu.VMEM((NC + 1, 8, C), F32),
-            pltpu.VMEM((NT + 2, 2, 2, R, D), F32),
-            pltpu.VMEM((NT + 2, 2, 2, R, D), F32),
-            pltpu.VMEM((NC, D, C), F32),
+            pltpu.VMEM((NT, 2, 2, R, D), F32),
+            pltpu.VMEM((NT, 2, 2, R, D), F32),
+            pltpu.VMEM((NC, C, D), F32),
             pltpu.SemaphoreType.DMA,
         ],
         compiler_params=pltpu.CompilerParams(vmem_limit_bytes=48 << 20),

time: 144 us -> 132 us (0.917); the launches traced: 143 us -> 134 us
  Pallas kernels: 54.1 us -> 40.4 us
  starting transfers between devices: 10.6 us -> 18.6 us
  waiting for transfers between devices: 25.1 us -> 22.1 us
    pallas_call x1, Pallas kernels: 49.6 us -> 35.9 us  [body(): pl.pallas_call(attention_kernel, out_shape=[bf16(16, QR, D)] + [group] *...]
    ppermute x8, starting transfers between devices: 5.61 us -> 13.8 us  [swap(): return lax.ppermute(array, 'y', [(i, i ^ distance) for i in range(4)])]
    ppermute x8, waiting for transfers between devices: 21.3 us -> 19.3 us  [swap(): return lax.ppermute(array, 'y', [(i, i ^ distance) for i in range(4)])]
  transfers between devices with their start and end apart: 18 -> 18, of which waited for: 11 -> 9; matrix products, arithmetic and copies ran while one was open for 1% -> 1% of each run, Pallas kernels for 1% -> 2%
where the time goes in v8:
time: 132 us; the launch traced here: 134 us
  blocking collectives  46.5 us (35%)
  Pallas kernels  40.4 us (31%)
  waiting for transfers between devices  22.1 us (17%)
  starting transfers between devices  18.6 us (14%)
  local copies, waits for them, and re-layouts  5.22 us (4%)
    all_to_all x3, blocking collectives, exchange(): lax.all_to_all(array, SPREAD, split_axis=0, concat_axis=0, tiled=True)  46.5 us
    pallas_call x1, Pallas kernels, body(): pl.pallas_call(attention_kernel, out_shape=[bf16(16, QR, D)] + [group] *...  35.9 us
    ppermute x8, waiting for transfers between devices, swap(): return lax.ppermute(array, 'y', [(i, i ^ distance) for i in range(4)])  19.3 us
    ppermute x8, starting transfers between devices, swap(): return lax.ppermute(array, 'y', [(i, i ^ distance) for i in range(4)])  13.8 us
    unnamed x20, local copies, waits for them, and re-layouts  4.23 us
    all_to_all x1, starting transfers between devices, exchange(): lax.all_to_all(array, SPREAD, split_axis=0, concat_axis=0, tiled=True)  3.83 us
  transfers between devices with their start and end apart: 18, of which 9 were waited for; matrix products, arithmetic and copies ran while one was open for 1% of the time, Pallas kernels for 2%

profile of v8, /device:TPU:0, one launch (start us, length us, event | category | flops | bytes accessed | tf_op | source)
XLA Modules:
  0.0 133.7 jit_solution(2587926449275886869)
XLA Ops:
  0.7 1.0 copy-done.4
  1.6 0.9 copy-done.5
  2.5 0.8 copy-done.6
  3.3 0.7 shard_map.94
  4.0 19.3 %all_to_all.20.after.refs_0_ = bf16[16,128,128]{2,1,0:T(8,128)(2,1)S(1)} all-to-all(bf16[16,128,128]{2,1,0:T(8,128)(2,1)S(1)} %get-tuple-element.24), channel_id=1, replica_groups=mesh['z'=4,'core'=2,'xh'=2,'xl'=2,'y'=4] {'xh','xl','z'}, dimensions={0} | all-to-all | bytes 1048576 | tf_op jit(solution)/shard_map/all_to_all | solution.py:389
  23.3 3.0 %collective-permute-start.1 = (bf16[16,128,128]{2,1,0:T(8,128)(2,1)S(1)}, bf16[16,128,128]{2,1,0:T(8,128)(2,1)S(1)}, u32[]{:S(2)}, u32[]{:S(2)}) collective-permute-start(bf16[16,128,128]{2,1,0:T(8,128)(2,1)S(1)} %all_to_all.20.after.refs_0_), channel_id=1, source_target_pairs={{0,3},{1,2},{2,1},{3,0},{4,7},{5,6},{6,5},{7,4},{8,11},{9,10},{10,... | collective-permute-start | bytes 1572872 | tf_op jit(solution)/shard_map/ppermute | solution.py:397
  26.3 0.1 collective-permute-start
  26.4 1.0 copy-done.3
  27.5 1.7 %shard_map.95 = bf16[16,272,128]{2,1,0:T(8,128)(2,1)} custom-call(bf16[64,4096]{1,0:T(8,128)(2,1)S(1)} %copy-done.1, bf16[64,4096]{1,0:T(8,128)(2,1)S(1)} %copy-done.2, bf16[64,4096]{1,0:T(8,128)(2,1)S(1)} %copy-done.3, bf16[16,128,128]{2,1,0:T(8,128)(2,1)S(1)} %all_to_all.20.after.refs_0_), custom_call_target="tpu_custom_call" | custom-call | tf_op jit(solution)/shard_map/pallas_call | solution.py:408
  29.2 3.8 %all-to-all-start.1 = ((bf16[16,272,128]{2,1,0:T(8,128)(2,1)}), bf16[16,272,128]{2,1,0:T(8,128)(2,1)S(1)}, u32[]{:S(2)}, u32[]{:S(2)}) async-start(bf16[16,272,128]{2,1,0:T(8,128)(2,1)} %shard_map.95), calls=%async_computation.1 | async-start | bytes 2228224 | tf_op jit(solution)/shard_map/all_to_all | solution.py:389
  33.0 0.1 collective-permute-start.4
  33.1 3.7 %collective-permute-done.1.refs_2_ = bf16[16,128,128]{2,1,0:T(8,128)(2,1)S(1)} collective-permute-done((bf16[16,128,128]{2,1,0:T(8,128)(2,1)S(1)}, bf16[16,128,128]{2,1,0:T(8,128)(2,1)S(1)}, u32[]{:S(2)}, u32[]{:S(2)}) %collective-permute-start.1) | collective-permute-done | bytes 524320 | tf_op jit(solution)/shard_map/ppermute | solution.py:397
  36.8 0.4 collective-permute-start.2
  37.2 0.0 collective-permute-start.6
  37.2 2.4 %collective-permute-done.refs_1_ = bf16[16,128,128]{2,1,0:T(8,128)(2,1)} collective-permute-done((bf16[16,128,128]{2,1,0:T(8,128)(2,1)S(1)}, bf16[16,128,128]{2,1,0:T(8,128)(2,1)}, u32[]{:S(2)}, u32[]{:S(2)}) %collective-permute-start) | collective-permute-done | bytes 524320 | tf_op jit(solution)/shard_map/ppermute | solution.py:397
  39.5 1.0 slice.9
  40.5 0.5 collective-permute-start.3
  41.0 0.2 collective-permute-start.5
  41.2 2.6 %collective-permute-done.2.refs_3_ = bf16[8,128,128]{2,1,0:T(8,128)(2,1)S(1)} collective-permute-done((bf16[8,128,128]{2,1,0:T(8,128)(2,1)S(1)}, bf16[8,128,128]{2,1,0:T(8,128)(2,1)S(1)}, u32[]{:S(2)}, u32[]{:S(2)}) %collective-permute-start.2) | collective-permute-done | bytes 262176 | tf_op jit(solution)/shard_map/ppermute | solution.py:397
  43.8 0.0 collective-permute-start.7
  43.8 4.3 %collective-permute-done.3.refs_4_ = bf16[8,128,128]{2,1,0:T(8,128)(2,1)S(1)} collective-permute-done((bf16[8,128,128]{2,1,0:T(8,128)(2,1)S(1)}, bf16[8,128,128]{2,1,0:T(8,128)(2,1)S(1)}, u32[]{:S(2)}, u32[]{:S(2)}) %collective-permute-start.3) | collective-permute-done | bytes 262176 | tf_op jit(solution)/shard_map/ppermute | solution.py:397
  48.2 0.0 collective-permute-start.8
  48.2 0.0 collective-permute-done.4.refs_5_
  48.2 1.1 all-to-all-done.1.qpay
  49.2 0.0 collective-permute-done.7.refs_8_
  49.2 0.0 collective-permute-done.6.refs_7_
  49.2 0.4 collective-permute-done.8.refs_9_
  49.7 0.5 copy-done.8
  50.2 35.9 %shard_map.96 = (bf16[16,128,128]{2,1,0:T(8,128)(2,1)S(1)}, bf16[16,128,128]{2,1,0:T(8,128)(2,1)S(1)}, bf16[16,128,128]{2,1,0:T(8,128)(2,1)S(1)}, bf16[16,128,12...) custom-call(s32[32]{0:T(128)S(1)} %copy-done.7, ...), custom_call_target="tpu_custom_call" | custom-call | tf_op jit(solution)/shard_map/pallas_call | solution.py:423
  86.1 0.1 collective-permute-start.12
  86.2 0.5 collective-permute-start.10
  86.7 0.1 collective-permute-start.11
  86.8 1.3 collective-permute-done.12.got
  88.1 0.1 shard_map.97
  88.3 0.1 collective-permute-start.13
  88.4 6.5 %collective-permute-start.14 = (bf16[8,128,128]{2,1,0:T(8,128)(2,1)S(1)}, bf16[8,128,128]{2,1,0:T(8,128)(2,1)S(1)}, u32[]{:S(2)}, u32[]{:S(2)}) collective-permute-start(bf16[8,128,128]{2,1,0:T(8,128)(2,1)S(1)} %get-tuple-element.35), channel_id=1, source_target_pairs={{0,3},{1,2},{2,1},{3,0},{4,7},{5,6},{6,5},{7,4},{8,11},{9,10},{10,... | collective-permute-start | bytes 786440 | tf_op jit(solution)/shard_map/ppermute | solution.py:397
  94.9 0.0 collective-permute-start.9
  94.9 0.0 collective-permute-done.10.got_1
  94.9 1.8 %collective-permute-done.13.from_1 = bf16[8,128,128]{2,1,0:T(8,128)(2,1)S(1)} collective-permute-done((bf16[8,128,128]{2,1,0:T(8,128)(2,1)S(1)}, bf16[8,128,128]{2,1,0:T(8,128)(2,1)S(1)}, u32[]{:S(2)}, u32[]{:S(2)}) %collective-permute-start.13) | collective-permute-done | bytes 262176 | tf_op jit(solution)/shard_map/ppermute | solution.py:397
  96.7 4.5 %collective-permute-done.14.from_3 = bf16[8,128,128]{2,1,0:T(8,128)(2,1)S(1)} collective-permute-done((bf16[8,128,128]{2,1,0:T(8,128)(2,1)S(1)}, bf16[8,128,128]{2,1,0:T(8,128)(2,1)S(1)}, u32[]{:S(2)}, u32[]{:S(2)}) %collective-permute-start.14) | collective-permute-done | bytes 262176 | tf_op jit(solution)/shard_map/ppermute | solution.py:397
  101.2 0.3 shard_map.98
  101.5 0.1 collective-permute-start.15
  101.6 3.0 %collective-permute-start.16 = (bf16[16,128,128]{2,1,0:T(8,128)(2,1)S(1)}, bf16[16,128,128]{2,1,0:T(8,128)(2,1)S(1)}, u32[]{:S(2)}, u32[]{:S(2)}) collective-permute-start(bf16[16,128,128]{2,1,0:T(8,128)(2,1)S(1)} %get-tuple-element.37), channel_id=1, source_target_pairs={{0,3},{1,2},{2,1},{3,0},{4,7},{5,6},{6,5},{7,4},{8,11},{9,10},{10,... | collective-permute-start | bytes 1572872 | tf_op jit(solution)/shard_map/ppermute | solution.py:397
  104.7 13.9 %all_to_all.21.dq = bf16[16,128,128]{2,1,0:T(8,128)(2,1)S(1)} all-to-all(bf16[16,128,128]{2,1,0:T(8,128)(2,1)S(1)} %get-tuple-element.38), channel_id=1, replica_groups=mesh['z'=4,'core'=2,'xh'=2,'xl'=2,'y'=4] {'xh','xl','z'}, dimensions={0} | all-to-all | bytes 1048576 | tf_op jit(solution)/shard_map/all_to_all | solution.py:389
  118.6 0.0 collective-permute-done.9.got
  118.6 0.9 shard_map.99
  119.5 13.3 %all_to_all.22.got = bf16[16,128,128]{2,1,0:T(8,128)(2,1)S(1)} all-to-all(bf16[16,128,128]{2,1,0:T(8,128)(2,1)S(1)} %get-tuple-element.40), channel_id=1, replica_groups=mesh['z'=4,'core'=2,'xh'=2,'xl'=2,'y'=4] {'xh','xl','z'}, dimensions={0} | all-to-all | bytes 1048576 | tf_op jit(solution)/shard_map/all_to_all | solution.py:389
  132.9 0.8 shard_map.100
  (20 shorter events, 0.1 us)
Async XLA Ops:
  0.6 25.8 %copy-start.2 = (bf16[64,4096]{1,0:T(8,128)(2,1)S(1)}, bf16[64,4096]{1,0:T(8,128)(2,1)}, u32[]{:S(2)}) copy-start(bf16[64,4096]{1,0:T(8,128)(2,1)} %saved.1) | copy-start | bytes 1572868
  0.6 25.8 %copy-start.1 = (bf16[64,4096]{1,0:T(8,128)(2,1)S(1)}, bf16[64,4096]{1,0:T(8,128)(2,1)}, u32[]{:S(2)}) copy-start(bf16[64,4096]{1,0:T(8,128)(2,1)} %queries.1) | copy-start | bytes 1572868
  0.7 1.0 copy-start.4
  1.6 0.9 copy-start.5
  2.5 0.8 copy-start.6
  23.3 9.7 %copy-start = (bf16[16,128,128]{2,1,0:T(8,128)(2,1)}, bf16[16,128,128]{2,1,0:T(8,128)(2,1)S(1)}, u32[]{:S(2)}) copy-start(bf16[16,128,128]{2,1,0:T(8,128)(2,1)S(1)} %all_to_all.20.after.refs_0_) | copy-start | bytes 1572868
  23.3 13.5 %collective-permute-start.1 = (bf16[16,128,128]{2,1,0:T(8,128)(2,1)S(1)}, bf16[16,128,128]{2,1,0:T(8,128)(2,1)S(1)}, u32[]{:S(2)}, u32[]{:S(2)}) collective-permute-start(bf16[16,128,128]{2,1,0:T(8,128)(2,1)S(1)} %all_to_all.20.after.refs_0_), channel_id=1, source_target_pairs={{0,3},{1,2},{2,1},{3,0},{4,7},{5,6},{6,5},{7,4},{8,11},{9,10},{10,... | collective-permute-start | bytes 1572872 | tf_op jit(solution)/shard_map/ppermute | solution.py:397
  26.3 13.2 %collective-permute-start = (bf16[16,128,128]{2,1,0:T(8,128)(2,1)S(1)}, bf16[16,128,128]{2,1,0:T(8,128)(2,1)}, u32[]{:S(2)}, u32[]{:S(2)}) collective-permute-start(bf16[16,128,128]{2,1,0:T(8,128)(2,1)S(1)} %all_to_all.20.after.refs_0_), channel_id=1, source_target_pairs={{0,1},{1,0},{2,3},{3,2},{4,5},{5,4},{6,7},{7,6},{8,9},{9,8},{10,11... | collective-permute-start | bytes 1572872 | tf_op jit(solution)/shard_map/ppermute | solution.py:397
  26.4 1.0 copy-start.3
  29.2 21.1 %copy-start.7 = (s32[32]{0:T(128)S(1)}, s32[32]{0:T(128)}, u32[]{:S(2)}) copy-start(s32[32]{0:T(128)} %order.1) | copy-start | bytes 388
  29.2 20.1 %all-to-all-start.1 = ((bf16[16,272,128]{2,1,0:T(8,128)(2,1)}), bf16[16,272,128]{2,1,0:T(8,128)(2,1)S(1)}, u32[]{:S(2)}, u32[]{:S(2)}) async-start(bf16[16,272,128]{2,1,0:T(8,128)(2,1)} %shard_map.95), calls=%async_computation.1 | async-start | bytes 2228224 | tf_op jit(solution)/shard_map/all_to_all | solution.py:389
  33.0 15.2 %collective-permute-start.4 = (bf16[16,128,128]{2,1,0:T(8,128)(2,1)S(1)}, bf16[16,128,128]{2,1,0:T(8,128)(2,1)}, u32[]{:S(2)}, u32[]{:S(2)}) collective-permute-start(bf16[16,128,128]{2,1,0:T(8,128)(2,1)S(1)} %all_to_all.20.after.refs_0_), channel_id=1, source_target_pairs={{0,16},{16,0},{1,17},{17,1},{2,18},{18,2},{3,19},{19,3},{4,20},{20... | collective-permute-start | bytes 1572872 | tf_op jit(solution)/shard_map/ppermute | solution.py:393
  36.8 12.9 %copy-start.9 = (bf16[16,128,128]{2,1,0:T(8,128)(2,1)}, bf16[16,128,128]{2,1,0:T(8,128)(2,1)S(1)}, u32[]{:S(2)}) copy-start(bf16[16,128,128]{2,1,0:T(8,128)(2,1)S(1)} %collective-permute-done.1.refs_2_) | copy-start | bytes 1572868
  36.8 7.1 %collective-permute-start.2 = (bf16[8,128,128]{2,1,0:T(8,128)(2,1)S(1)}, bf16[8,128,128]{2,1,0:T(8,128)(2,1)S(1)}, u32[]{:S(2)}, u32[]{:S(2)}) collective-permute-start(bf16[8,128,128]{2,1,0:T(8,128)(2,1)S(1)} %slice.8), channel_id=1, source_target_pairs={{0,1},{1,0},{2,3},{3,2},{4,5},{5,4},{6,7},{7,6},{8,9},{9,8},{10,11... | collective-permute-start | bytes 786440 | tf_op jit(solution)/shard_map/ppermute | solution.py:397
  37.2 12.1 %collective-permute-start.6 = (bf16[16,128,128]{2,1,0:T(8,128)(2,1)S(1)}, bf16[16,128,128]{2,1,0:T(8,128)(2,1)}, u32[]{:S(2)}, u32[]{:S(2)}) collective-permute-start(bf16[16,128,128]{2,1,0:T(8,128)(2,1)S(1)} %collective-permute-done.1.refs_2_), channel_id=1, source_target_pairs={{0,16},{16,0},{1,17},{17,1},{2,18},{18,2},{3,19},{19,3},{4,20},{20... | collective-permute-start | bytes 1572872 | tf_op jit(solution)/shard_map/ppermute | solution.py:393
  40.5 7.7 %collective-permute-start.3 = (bf16[8,128,128]{2,1,0:T(8,128)(2,1)S(1)}, bf16[8,128,128]{2,1,0:T(8,128)(2,1)S(1)}, u32[]{:S(2)}, u32[]{:S(2)}) collective-permute-start(bf16[8,128,128]{2,1,0:T(8,128)(2,1)S(1)} %slice.9), channel_id=1, source_target_pairs={{0,3},{1,2},{2,1},{3,0},{4,7},{5,6},{6,5},{7,4},{8,11},{9,10},{10,... | collective-permute-start | bytes 786440 | tf_op jit(solution)/shard_map/ppermute | solution.py:397
  41.0 8.7 %collective-permute-start.5 = (bf16[16,128,128]{2,1,0:T(8,128)(2,1)}, bf16[16,128,128]{2,1,0:T(8,128)(2,1)}, u32[]{:S(2)}, u32[]{:S(2)}) collective-permute-start(bf16[16,128,128]{2,1,0:T(8,128)(2,1)} %collective-permute-done.refs_1_), channel_id=1, source_target_pairs={{0,16},{16,0},{1,17},{17,1},{2,18},{18,2},{3,19},{19,3},{4,20},{20... | collective-permute-start | bytes 1572872 | tf_op jit(solution)/shard_map/ppermute | solution.py:393
  43.8 5.4 %collective-permute-start.7 = (bf16[8,128,128]{2,1,0:T(8,128)(2,1)S(1)}, bf16[8,128,128]{2,1,0:T(8,128)(2,1)S(1)}, u32[]{:S(2)}, u32[]{:S(2)}) collective-permute-start(bf16[8,128,128]{2,1,0:T(8,128)(2,1)S(1)} %collective-permute-done.2.refs_3_), channel_id=1, source_target_pairs={{0,16},{16,0},{1,17},{17,1},{2,18},{18,2},{3,19},{19,3},{4,20},{20... | collective-permute-start | bytes 786440 | tf_op jit(solution)/shard_map/ppermute | solution.py:393
  48.2 1.5 %collective-permute-start.8 = (bf16[8,128,128]{2,1,0:T(8,128)(2,1)S(1)}, bf16[8,128,128]{2,1,0:T(8,128)(2,1)S(1)}, u32[]{:S(2)}, u32[]{:S(2)}) collective-permute-start(bf16[8,128,128]{2,1,0:T(8,128)(2,1)S(1)} %collective-permute-done.3.refs_4_), channel_id=1, source_target_pairs={{0,16},{16,0},{1,17},{17,1},{2,18},{18,2},{3,19},{19,3},{4,20},{20... | collective-permute-start | bytes 786440 | tf_op jit(solution)/shard_map/ppermute | solution.py:393
  49.2 1.0 copy-start.8
  86.1 2.0 %collective-permute-start.12 = (bf16[16,128,128]{2,1,0:T(8,128)(2,1)S(1)}, bf16[16,128,128]{2,1,0:T(8,128)(2,1)S(1)}, u32[]{:S(2)}, u32[]{:S(2)}) collective-permute-start(bf16[16,128,128]{2,1,0:T(8,128)(2,1)S(1)} %get-tuple-element.33), channel_id=1, source_target_pairs={{0,16},{16,0},{1,17},{17,1},{2,18},{18,2},{3,19},{19,3},{4,20},{20... | collective-permute-start | bytes 1572872 | tf_op jit(solution)/shard_map/ppermute | solution.py:393
  86.2 8.7 %collective-permute-start.10 = (bf16[16,128,128]{2,1,0:T(8,128)(2,1)S(1)}, bf16[16,128,128]{2,1,0:T(8,128)(2,1)S(1)}, u32[]{:S(2)}, u32[]{:S(2)}) collective-permute-start(bf16[16,128,128]{2,1,0:T(8,128)(2,1)S(1)} %get-tuple-element.28), channel_id=1, source_target_pairs={{0,16},{16,0},{1,17},{17,1},{2,18},{18,2},{3,19},{19,3},{4,20},{20... | collective-permute-start | bytes 1572872 | tf_op jit(solution)/shard_map/ppermute | solution.py:393
  86.7 8.2 %collective-permute-start.11 = (bf16[16,128,128]{2,1,0:T(8,128)(2,1)S(1)}, bf16[16,128,128]{2,1,0:T(8,128)(2,1)S(1)}, u32[]{:S(2)}, u32[]{:S(2)}) collective-permute-start(bf16[16,128,128]{2,1,0:T(8,128)(2,1)S(1)} %get-tuple-element.30), channel_id=1, source_target_pairs={{0,16},{16,0},{1,17},{17,1},{2,18},{18,2},{3,19},{19,3},{4,20},{20... | collective-permute-start | bytes 1572872 | tf_op jit(solution)/shard_map/ppermute | solution.py:393
  88.3 8.4 %collective-permute-start.13 = (bf16[8,128,128]{2,1,0:T(8,128)(2,1)S(1)}, bf16[8,128,128]{2,1,0:T(8,128)(2,1)S(1)}, u32[]{:S(2)}, u32[]{:S(2)}) collective-permute-start(bf16[8,128,128]{2,1,0:T(8,128)(2,1)S(1)} %get-tuple-element.34), channel_id=1, source_target_pairs={{0,1},{1,0},{2,3},{3,2},{4,5},{5,4},{6,7},{7,6},{8,9},{9,8},{10,11... | collective-permute-start | bytes 786440 | tf_op jit(solution)/shard_map/ppermute | solution.py:397
  88.4 12.9 %collective-permute-start.14 = (bf16[8,128,128]{2,1,0:T(8,128)(2,1)S(1)}, bf16[8,128,128]{2,1,0:T(8,128)(2,1)S(1)}, u32[]{:S(2)}, u32[]{:S(2)}) collective-permute-start(bf16[8,128,128]{2,1,0:T(8,128)(2,1)S(1)} %get-tuple-element.35), channel_id=1, source_target_pairs={{0,3},{1,2},{2,1},{3,0},{4,7},{5,6},{6,5},{7,4},{8,11},{9,10},{10,... | collective-permute-start | bytes 786440 | tf_op jit(solution)/shard_map/ppermute | solution.py:397
  94.9 23.7 %collective-permute-start.9 = (bf16[16,128,128]{2,1,0:T(8,128)(2,1)S(1)}, bf16[16,128,128]{2,1,0:T(8,128)(2,1)S(1)}, u32[]{:S(2)}, u32[]{:S(2)}) collective-permute-start(bf16[16,128,128]{2,1,0:T(8,128)(2,1)S(1)} %get-tuple-element.26), channel_id=1, source_target_pairs={{0,16},{16,0},{1,17},{17,1},{2,18},{18,2},{3,19},{19,3},{4,20},{20... | collective-permute-start | bytes 1572872 | tf_op jit(solution)/shard_map/ppermute | solution.py:393
  101.5 17.1 %collective-permute-start.15 = (bf16[16,128,128]{2,1,0:T(8,128)(2,1)S(1)}, bf16[16,128,128]{2,1,0:T(8,128)(2,1)S(1)}, u32[]{:S(2)}, u32[]{:S(2)}) collective-permute-start(bf16[16,128,128]{2,1,0:T(8,128)(2,1)S(1)} %get-tuple-element.36), channel_id=1, source_target_pairs={{0,1},{1,0},{2,3},{3,2},{4,5},{5,4},{6,7},{7,6},{8,9},{9,8},{10,11... | collective-permute-start | bytes 1572872 | tf_op jit(solution)/shard_map/ppermute | solution.py:397
  101.6 17.0 %collective-permute-start.16 = (bf16[16,128,128]{2,1,0:T(8,128)(2,1)S(1)}, bf16[16,128,128]{2,1,0:T(8,128)(2,1)S(1)}, u32[]{:S(2)}, u32[]{:S(2)}) collective-permute-start(bf16[16,128,128]{2,1,0:T(8,128)(2,1)S(1)} %get-tuple-element.37), channel_id=1, source_target_pairs={{0,3},{1,2},{2,1},{3,0},{4,7},{5,6},{6,5},{7,4},{8,11},{9,10},{10,... | collective-permute-start | bytes 1572872 | tf_op jit(solution)/shard_map/ppermute | solution.py:397

commit v9 on v4

--- a/solution.py
+++ b/solution.py
@@ -1,3 +1,5 @@
+import math
+
 import jax
 import jax.numpy as jnp
 from jax import lax
@@ -17,6 +19,7 @@
 NC = 8
 W = 4
 SCALE = D**-0.5
+EXP_SCALE = SCALE * math.log2(math.e)
 HIDDEN = -1e30
 LARGE = 2.0**90
 F32 = jnp.float32
@@ -34,17 +37,17 @@
     return slice((g * G + h) * D, (g * G + h + 1) * D)
 
 
-def pack_kv_kernel(keys, values, segment, out, counts):
-    counts[0] = jnp.sum((segment[...] == 0).astype(jnp.int32))
-    counts[1] = jnp.sum((segment[...] != 2).astype(jnp.int32))
+def pack_kv_kernel(keys, values, out):
     for g in range(8):
         for xl in range(2):
             out[spread_to(g, xl), :R] = keys[:, g * D : (g + 1) * D]
             out[spread_to(g, xl), R:] = values[:, g * D : (g + 1) * D]
 
 
-def pack_q_kernel(queries, saved, grads, after, out):
+def pack_q_kernel(queries, saved, grads, segment, after, out, counts):
     del after
+    counts[0] = jnp.sum((segment[...] == 0).astype(jnp.int32))
+    counts[1] = jnp.sum((segment[...] != 2).astype(jnp.int32))
     ones = jnp.ones((8, D), BF16)
     row = lax.broadcasted_iota(jnp.int32, (16, D), 0)
     for g in range(8):
@@ -75,8 +78,8 @@
 def attention_kernel(order, counts, qpay, *refs):
     pieces = refs[:10]
     dq_out, keep_0, keep_1, keep_3, sum_a, sum_b, give_0, give_1, give_3, far_give = refs[10:20]
-    (plain_c, plain_b, masked_c, masked_b, q_s, do_s, d_s, k_s, v_s, kt_s, qa_s, ga_s) = refs[20:32]
-    m_s, l_s, dk_s, dv_s, dq_s, sem, value_sem = refs[32:]
+    plain_c, plain_b, q_s, do_s, d_s, k_s, v_s, kt_s, qa_s, ga_s = refs[20:30]
+    m_s, l_s, dk_s, dv_s, dq_s, sem, value_sem = refs[30:]
     n0 = counts[0]
     n1 = counts[1]
     xl = lax.axis_index("xl")
@@ -116,10 +119,13 @@
     for copy in copies + value_copies:
         copy.start()
 
-    beside = lax.broadcasted_iota(jnp.int32, (1, 1, 1, 1, D), 4) < 3
-    beside = jnp.broadcast_to(beside.astype(F32), (1, 2, 2, R, D)).astype(BF16)
+    column = lax.broadcasted_iota(jnp.int32, (SPAN, D), 1)
+    row = lax.broadcasted_iota(jnp.int32, (SPAN, D), 0)
 
     def put_beside(i, carry):
+        chosen = (i * SPAN + row >= n0) & (i * SPAN + row < n1)
+        beside = jnp.where((column < 3) | ((column == 3) & chosen), 1.0, 0.0).astype(BF16)
+        beside = beside.reshape(1, 2, 2, R, D)
         k_s[pl.ds(i, 1), :, :, :, D:] = beside
         v_s[pl.ds(i, 1), :, :, :, D:] = beside
         return carry
@@ -132,41 +138,26 @@
     def span_of(c):
         return order[span_id(c // 4, c // 2 % 2, y, c % 2)]
 
-    def list_chunk(c, sizes):
-        n_plain, n_masked = sizes
-        span_q = span_of(c)
-        first = span_q * SPAN
-        has_second = first + (SPAN - 1) >= n1
-        all_second = first >= n1
-        n_full = span_q // 2
-        hi = jnp.minimum(jnp.where(has_second, (n1 + (KB - 1)) // KB, 0), n_full)
-        lo = jnp.minimum(jnp.where(has_second, n0 // KB, 0), hi)
-        skip_at = jnp.where(all_second, (n0 + (KB - 1)) // KB, hi)
+    def full_blocks(c):
+        return span_of(c) // 2
+
+    def list_chunk(c, size):
+        all_second = span_of(c) * SPAN >= n1
+        skip_at = (n0 + (KB - 1)) // KB
         skip_to = jnp.where(all_second, n1 // KB, 0)
-        masked_c[c] = c
-        masked_b[c] = n_full
-
-        def put_plain(b, n):
+
+        def put(b, n):
+            hidden = (b >= skip_at) & (b < skip_to)
             plain_c[n] = c
             plain_b[n] = b
-            return n + 1
-
-        def put_masked(b, n):
-            hidden = (b >= skip_at) & (b < skip_to)
-            masked_c[n] = c
-            masked_b[n] = b
             return jnp.where(hidden, n, n + 1)
 
-        n_plain = lax.fori_loop(0, lo, put_plain, n_plain)
-        n_plain = lax.fori_loop(hi, n_full, put_plain, n_plain)
-        return n_plain, lax.fori_loop(lo, hi, put_masked, n_masked)
-
-    n_plain, n_masked = lax.fori_loop(0, NC, list_chunk, (jnp.int32(0), jnp.int32(NC)))
+        return lax.fori_loop(0, full_blocks(c), put, size)
+
+    n_plain = lax.fori_loop(0, NC, list_chunk, jnp.int32(0))
     for i in range(W - 1):
         plain_c[n_plain + i] = NC
         plain_b[n_plain + i] = 0
-        masked_c[n_masked + i] = NC
-        masked_b[n_masked + i] = 0
 
     for copy in copies:
         copy.wait()
@@ -210,11 +201,16 @@
     do_s[NC] = jnp.zeros((C, D), BF16)
     l_s[NC] = jnp.zeros((8, C), F32)
 
+    def query_positions(c):
+        lane = lax.broadcasted_iota(jnp.int32, (1, C), 1)
+        start = span_of(c) * SPAN + core * R + xl * HR
+        return start + (lane // QR) * (2 * R) + lane % HR
+
+    def key_positions(b):
+        return b * KB + lax.broadcasted_iota(jnp.int32, (KB, 1), 0)
+
     def seen(c, b):
-        lane = lax.broadcasted_iota(jnp.int32, (1, C), 1)
-        row = span_of(jnp.minimum(c, NC - 1)) * SPAN + core * R + xl * HR
-        query_pos = row + (lane // QR) * (2 * R) + lane % HR
-        key_pos = b * KB + lax.broadcasted_iota(jnp.int32, (KB, 1), 0)
+        query_pos, key_pos = query_positions(c), key_positions(b)
         low = jnp.where(query_pos >= n1, n0, n1)
         return (key_pos <= query_pos) & ((key_pos < low) | (key_pos >= n1))
 
@@ -223,21 +219,26 @@
 
     def raw_scores(c, b):
         return jnp.dot(keys_of(b), qa_s[c, :D], preferred_element_type=F32)
+
+    def put_shift(c, *rows):
+        rows = (rows + (jnp.zeros((1, C), F32),) * 3)[:3]
+        hide = jnp.where(query_positions(c) >= n1, HIDDEN, 0.0)
+        put_under(qa_s, c, *rows, hide)
 
     def weights_of(c, b, masked):
         scores = jnp.dot(block_of(k_s, b), qa_s[c], preferred_element_type=F32)
         if masked:
-            scores = jnp.where(seen(c, b), scores, HIDDEN)
-        return jnp.exp(scores * SCALE)
+            scores = jnp.where(key_positions(b) <= query_positions(c), scores, HIDDEN)
+        return jnp.exp2(scores * EXP_SCALE)
 
     def diagonal_step(i, carry):
         for c in [2 * i + k for k in range(2)]:
-            b = masked_b[c]
+            b = full_blocks(c)
             scores = jnp.where(seen(c, b), raw_scores(c, b), HIDDEN)
             top = jnp.max(scores, axis=0, keepdims=True).astype(BF16).astype(F32)
-            put_under(qa_s, c, -top)
-            m_s[c] = top * SCALE
-            l_s[c] = add_up(jnp.exp((scores - top) * SCALE))
+            put_shift(c, -top)
+            m_s[c] = top * EXP_SCALE
+            l_s[c] = add_up(jnp.exp2((scores - top) * EXP_SCALE))
         return carry
 
     lax.fori_loop(0, NC // 2, diagonal_step, 0)
@@ -247,55 +248,46 @@
         for (c, b), part in zip(items, parts):
             l_s[c] += part
 
-    def masked_stats(i, carry):
-        at = [NC + 2 * i + k for k in range(2)]
-        add_weights([(masked_c[n], masked_b[n]) for n in at], True)
-        return carry
+    def plain_items(i):
+        return [(plain_c[n], plain_b[n]) for n in [W * i + k for k in range(W)]]
 
     def plain_stats(i, carry):
-        at = [W * i + k for k in range(W)]
-        add_weights([(plain_c[n], plain_b[n]) for n in at], False)
-        return carry
-
-    lax.fori_loop(0, (n_masked - NC + 1) // 2, masked_stats, 0)
+        add_weights(plain_items(i), False)
+        return carry
+
     lax.fori_loop(0, (n_plain + W - 1) // W, plain_stats, 0)
 
     @pl.when(jnp.logical_not(jnp.max(l_s[...]) < LARGE))
     def _():
         def careful(c, b):
-            scores = jnp.where(seen(c, b), raw_scores(c, b) * SCALE, HIDDEN)
+            scores = jnp.where(seen(c, b), raw_scores(c, b) * EXP_SCALE, HIDDEN)
             old = m_s[c]
             top = jnp.maximum(old, jnp.max(scores, axis=0, keepdims=True))
-            l_s[c] = l_s[c] * jnp.exp(old - top) + add_up(jnp.exp(scores - top))
+            l_s[c] = l_s[c] * jnp.exp2(old - top) + add_up(jnp.exp2(scores - top))
             m_s[c] = top
 
-        def careful_masked(n, carry):
-            c = masked_c[n]
-
-            @pl.when(n < NC)
-            def _():
-                m_s[c] = jnp.full((1, C), HIDDEN, F32)
-                l_s[c] = jnp.zeros((8, C), F32)
-
-            careful(c, masked_b[n])
+        def careful_diagonal(c, carry):
+            m_s[c] = jnp.full((1, C), HIDDEN, F32)
+            l_s[c] = jnp.zeros((8, C), F32)
+            careful(c, full_blocks(c))
             return carry
 
         def careful_plain(n, carry):
             careful(plain_c[n], plain_b[n])
             return carry
 
-        lax.fori_loop(0, n_masked, careful_masked, 0)
+        lax.fori_loop(0, NC, careful_diagonal, 0)
         lax.fori_loop(0, n_plain, careful_plain, 0)
 
     def put_logsum(c, carry):
-        logsum = m_s[c] + jnp.log(jnp.sum(l_s[c], axis=0, keepdims=True))
-        rest = logsum * (1.0 / SCALE)
+        logsum = m_s[c] + jnp.log2(jnp.sum(l_s[c], axis=0, keepdims=True))
+        rest = logsum * (1.0 / EXP_SCALE)
         rows = []
         for _ in range(3):
             part = rest.astype(BF16).astype(F32)
             rows.append(-part)
             rest = rest - part
-        put_under(qa_s, c, *rows)
+        put_shift(c, *rows)
         return carry
 
     lax.fori_loop(0, NC, put_logsum, 0)
@@ -316,17 +308,15 @@
                 ref[pl.ds(2 * b, 2)] += term.reshape(2, 2, 2, R, D)
             dq_s[c] += jnp.dot(kt_s[b], score_grad, preferred_element_type=F32)
 
-    def masked_grads(i, carry):
-        at = [2 * i + k for k in range(2)]
-        grad_step([(masked_c[n], masked_b[n]) for n in at], True)
+    def diagonal_grads(i, carry):
+        grad_step([(c, full_blocks(c)) for c in [2 * i + k for k in range(2)]], True)
         return carry
 
     def plain_grads(i, carry):
-        at = [W * i + k for k in range(W)]
-        grad_step([(plain_c[n], plain_b[n]) for n in at], False)
-        return carry
-
-    lax.fori_loop(0, (n_masked + 1) // 2, masked_grads, 0)
+        grad_step(plain_items(i), False)
+        return carry
+
+    lax.fori_loop(0, NC // 2, diagonal_grads, 0)
     lax.fori_loop(0, (n_plain + W - 1) // W, plain_grads, 0)
 
     def finish(c, carry):
@@ -415,19 +405,14 @@
 
 
 def body(queries, keys, values, attn_out, out_grad, segment, span_order):
-    kv_packed, counts = pl.pallas_call(
-        pack_kv_kernel,
-        out_shape=[bf16(16, 2 * R, D), jax.ShapeDtypeStruct((2,), jnp.int32)],
+    own = exchange(on_vmem(pack_kv_kernel, bf16(16, 2 * R, D), keys, values))
+    q_packed, counts = pl.pallas_call(
+        pack_q_kernel,
+        out_shape=[bf16(16, 2 * QR + 16, D), jax.ShapeDtypeStruct((2,), jnp.int32)],
+        in_specs=[IN_VMEM] * 4 + [ANYWHERE],
         out_specs=[IN_VMEM, IN_SMEM],
         compiler_params=pltpu.CompilerParams(vmem_limit_bytes=16 << 20),
-    )(keys, values, segment.reshape(64, 128))
-    own = exchange(kv_packed)
-    q_packed = pl.pallas_call(
-        pack_q_kernel,
-        out_shape=bf16(16, 2 * QR + 16, D),
-        in_specs=[IN_VMEM] * 3 + [ANYWHERE],
-        compiler_params=pltpu.CompilerParams(vmem_limit_bytes=16 << 20),
-    )(queries, attn_out, out_grad, own)
+    )(queries, attn_out, out_grad, segment.reshape(64, 128), own)
     qpay = exchange(q_packed)
 
     near_1 = swap(own, 1)
@@ -444,8 +429,6 @@
         scratch_shapes=[
             pltpu.SMEM((NC * NT // 2 + W,), jnp.int32),
             pltpu.SMEM((NC * NT // 2 + W,), jnp.int32),
-            pltpu.SMEM((NC * NT // 2 + NC + W,), jnp.int32),
-            pltpu.SMEM((NC * NT // 2 + NC + W,), jnp.int32),
             pltpu.VMEM((NC + 1, C, D), BF16),
             pltpu.VMEM((NC + 1, C, D), BF16),
             pltpu.VMEM((16, 16, D), BF16),

time: 136 us -> 131 us (0.963)
  starting transfers between devices: 22.7 us -> 18.9 us
  Pallas kernels: 36.9 us -> 40.3 us
  local copies, waits for them, and re-layouts: 5.22 us -> 2.93 us
  waiting for transfers between devices: 25.1 us -> 23.5 us
    pallas_call x1, Pallas kernels: 32.4 us -> 36.4 us  [body(): pl.pallas_call(attention_kernel, out_shape=[bf16(16, QR, D)] + [group] *...]
    ppermute x8, starting transfers between devices: 17.9 us -> 14.2 us  [swap(): return lax.ppermute(array, 'y', [(i, i ^ distance) for i in range(4)])]
    unnamed x20, local copies, waits for them, and re-layouts: 4.23 us -> 1.95 us
    ppermute x8, waiting for transfers between devices: 22.2 us -> 20.7 us  [swap(): return lax.ppermute(array, 'y', [(i, i ^ distance) for i in range(4)])]
  transfers between devices with their start and end apart: 18 -> 18, of which waited for: 9 -> 8; matrix products, arithmetic and copies ran while one was open for 1% -> 1% of each run, Pallas kernels for 2% -> 2%
where the time goes in v9:
time: 131 us; the launch traced here: 133 us
  blocking collectives  46.5 us (35%)
  Pallas kernels  40.3 us (31%)
  waiting for transfers between devices  23.5 us (18%)
  starting transfers between devices  18.9 us (14%)
  local copies, waits for them, and re-layouts  2.93 us (2%)
    all_to_all x3, blocking collectives, exchange(): lax.all_to_all(array, SPREAD, split_axis=0, concat_axis=0, tiled=True)  46.5 us
    pallas_call x1, Pallas kernels, body(): pl.pallas_call(attention_kernel, out_shape=[bf16(16, QR, D)] + [group] *...  36.4 us
    ppermute x8, waiting for transfers between devices, swap(): return lax.ppermute(array, 'y', [(i, i ^ distance) for i in range(4)])  20.7 us
    ppermute x8, starting transfers between devices, swap(): return lax.ppermute(array, 'y', [(i, i ^ distance) for i in range(4)])  14.2 us
    all_to_all x1, starting transfers between devices, exchange(): lax.all_to_all(array, SPREAD, split_axis=0, concat_axis=0, tiled=True)  3.71 us
    ppermute x9, waiting for transfers between devices, flip(): return lax.ppermute(array, 'core', [(0, 1), (1, 0)])  2.78 us
  transfers between devices with their start and end apart: 18, of which 8 were waited for; matrix products, arithmetic and copies ran while one was open for 1% of the time, Pallas kernels for 2%

profile of v9, /device:TPU:0, one launch (start us, length us, event | category | flops | bytes accessed | tf_op | source)
XLA Modules:
  0.0 132.9 jit_solution(10790059049419276489)
XLA Ops:
  0.7 1.0 copy-done.4
  1.7 0.9 copy-done.5
  2.6 0.1 shard_map.94
  2.7 19.3 %all_to_all.20.after.refs_0_ = bf16[16,128,128]{2,1,0:T(8,128)(2,1)S(1)} all-to-all(bf16[16,128,128]{2,1,0:T(8,128)(2,1)S(1)} %shard_map.94), channel_id=1, replica_groups=mesh['z'=4,'core'=2,'xh'=2,'xl'=2,'y'=4] {'xh','xl','z'}, dimensions={0} | all-to-all | bytes 1048576 | tf_op jit(solution)/shard_map/all_to_all | solution.py:396
  21.9 3.0 %collective-permute-start.1 = (bf16[16,128,128]{2,1,0:T(8,128)(2,1)S(1)}, bf16[16,128,128]{2,1,0:T(8,128)(2,1)S(1)}, u32[]{:S(2)}, u32[]{:S(2)}) collective-permute-start(bf16[16,128,128]{2,1,0:T(8,128)(2,1)S(1)} %all_to_all.20.after.refs_0_), channel_id=1, source_target_pairs={{0,3},{1,2},{2,1},{3,0},{4,7},{5,6},{6,5},{7,4},{8,11},{9,10},{10,... | collective-permute-start | bytes 1572872 | tf_op jit(solution)/shard_map/ppermute | solution.py:404
  24.9 0.1 collective-permute-start
  25.1 1.7 %shard_map.95 = (bf16[16,272,128]{2,1,0:T(8,128)(2,1)}, s32[2]{0:T(128)S(1)}) custom-call(bf16[64,4096]{1,0:T(8,128)(2,1)S(1)} %copy-done.1, bf16[64,4096]{1,0:T(8,128)(2,1)S(1)} %copy-done.2, bf16[64,4096]{1,0:T(8,128)(2,1)S(1)} %copy-done.3, s32[64,128]{1,0:T(8,128)S(1)} %bitcast.1, bf16[16,128,128]{2,1,0:T(8,128)(2,1)S(1)} %all_to_all.20.after.refs_0_), custom_call_target="tpu_custom_call" | custom-call | tf_op jit(solution)/shard_map/pallas_call | solution.py:409
  26.8 0.0 copy-start.7
  26.8 3.7 %all-to-all-start.1 = ((bf16[16,272,128]{2,1,0:T(8,128)(2,1)}), bf16[16,272,128]{2,1,0:T(8,128)(2,1)S(1)}, u32[]{:S(2)}, u32[]{:S(2)}) async-start(bf16[16,272,128]{2,1,0:T(8,128)(2,1)} %get-tuple-element.24), calls=%async_computation.1 | async-start | bytes 2228224 | tf_op jit(solution)/shard_map/all_to_all | solution.py:396
  30.5 0.1 collective-permute-start.4
  30.6 4.8 %collective-permute-done.1.refs_2_ = bf16[16,128,128]{2,1,0:T(8,128)(2,1)S(1)} collective-permute-done((bf16[16,128,128]{2,1,0:T(8,128)(2,1)S(1)}, bf16[16,128,128]{2,1,0:T(8,128)(2,1)S(1)}, u32[]{:S(2)}, u32[]{:S(2)}) %collective-permute-start.1) | collective-permute-done | bytes 524320 | tf_op jit(solution)/shard_map/ppermute | solution.py:404
  35.4 0.4 collective-permute-start.2
  35.8 0.0 collective-permute-start.6
  35.8 2.4 %collective-permute-done.refs_1_ = bf16[16,128,128]{2,1,0:T(8,128)(2,1)} collective-permute-done((bf16[16,128,128]{2,1,0:T(8,128)(2,1)S(1)}, bf16[16,128,128]{2,1,0:T(8,128)(2,1)}, u32[]{:S(2)}, u32[]{:S(2)}) %collective-permute-start) | collective-permute-done | bytes 524320 | tf_op jit(solution)/shard_map/ppermute | solution.py:404
  38.1 1.0 slice.9
  39.1 0.5 collective-permute-start.3
  39.6 0.2 collective-permute-start.5
  39.8 2.6 %collective-permute-done.2.refs_3_ = bf16[8,128,128]{2,1,0:T(8,128)(2,1)S(1)} collective-permute-done((bf16[8,128,128]{2,1,0:T(8,128)(2,1)S(1)}, bf16[8,128,128]{2,1,0:T(8,128)(2,1)S(1)}, u32[]{:S(2)}, u32[]{:S(2)}) %collective-permute-start.2) | collective-permute-done | bytes 262176 | tf_op jit(solution)/shard_map/ppermute | solution.py:404
  42.5 0.0 collective-permute-start.7
  42.5 4.3 %collective-permute-done.3.refs_4_ = bf16[8,128,128]{2,1,0:T(8,128)(2,1)S(1)} collective-permute-done((bf16[8,128,128]{2,1,0:T(8,128)(2,1)S(1)}, bf16[8,128,128]{2,1,0:T(8,128)(2,1)S(1)}, u32[]{:S(2)}, u32[]{:S(2)}) %collective-permute-start.3) | collective-permute-done | bytes 262176 | tf_op jit(solution)/shard_map/ppermute | solution.py:404
  46.8 0.0 collective-permute-start.8
  46.8 0.0 collective-permute-done.4.refs_5_
  46.8 0.0 all-to-all-done.1.qpay
  46.8 0.0 collective-permute-done.7.refs_8_
  46.8 0.0 collective-permute-done.6.refs_7_
  46.8 1.5 %collective-permute-done.8.refs_9_ = bf16[8,128,128]{2,1,0:T(8,128)(2,1)S(1)} collective-permute-done((bf16[8,128,128]{2,1,0:T(8,128)(2,1)S(1)}, bf16[8,128,128]{2,1,0:T(8,128)(2,1)S(1)}, u32[]{:S(2)}, u32[]{:S(2)}) %collective-permute-start.8) | collective-permute-done | bytes 262176 | tf_op jit(solution)/shard_map/ppermute | solution.py:400
  48.3 0.0 collective-permute-done.5.refs_6_
  48.3 36.4 %shard_map.96 = (bf16[16,128,128]{2,1,0:T(8,128)(2,1)S(1)}, bf16[16,128,128]{2,1,0:T(8,128)(2,1)S(1)}, bf16[16,128,128]{2,1,0:T(8,128)(2,1)S(1)}, bf16[16,128,12...) custom-call(s32[32]{0:T(128)S(1)} %copy-done.7, ...), custom_call_target="tpu_custom_call" | custom-call | tf_op jit(solution)/shard_map/pallas_call | solution.py:425
  84.7 0.2 collective-permute-start.12
  85.0 0.4 collective-permute-start.10
  85.3 0.1 collective-permute-start.11
  85.5 1.3 collective-permute-done.12.got
  86.7 0.1 shard_map.97
  86.9 0.1 collective-permute-start.13
  86.9 6.6 %collective-permute-start.14 = (bf16[8,128,128]{2,1,0:T(8,128)(2,1)S(1)}, bf16[8,128,128]{2,1,0:T(8,128)(2,1)S(1)}, u32[]{:S(2)}, u32[]{:S(2)}) collective-permute-start(bf16[8,128,128]{2,1,0:T(8,128)(2,1)S(1)} %get-tuple-element.35), channel_id=1, source_target_pairs={{0,3},{1,2},{2,1},{3,0},{4,7},{5,6},{6,5},{7,4},{8,11},{9,10},{10,... | collective-permute-start | bytes 786440 | tf_op jit(solution)/shard_map/ppermute | solution.py:404
  93.5 0.0 collective-permute-start.9
  93.5 0.0 collective-permute-done.10.got_1
  93.5 0.0 collective-permute-done.11.got_3
  93.5 1.7 %collective-permute-done.13.from_1 = bf16[8,128,128]{2,1,0:T(8,128)(2,1)S(1)} collective-permute-done((bf16[8,128,128]{2,1,0:T(8,128)(2,1)S(1)}, bf16[8,128,128]{2,1,0:T(8,128)(2,1)S(1)}, u32[]{:S(2)}, u32[]{:S(2)}) %collective-permute-start.13) | collective-permute-done | bytes 262176 | tf_op jit(solution)/shard_map/ppermute | solution.py:404
  95.3 4.9 %collective-permute-done.14.from_3 = bf16[8,128,128]{2,1,0:T(8,128)(2,1)S(1)} collective-permute-done((bf16[8,128,128]{2,1,0:T(8,128)(2,1)S(1)}, bf16[8,128,128]{2,1,0:T(8,128)(2,1)S(1)}, u32[]{:S(2)}, u32[]{:S(2)}) %collective-permute-start.14) | collective-permute-done | bytes 262176 | tf_op jit(solution)/shard_map/ppermute | solution.py:404
  100.1 0.3 shard_map.98
  100.4 1.1 collective-permute-start.15
  101.6 2.3 %collective-permute-start.16 = (bf16[16,128,128]{2,1,0:T(8,128)(2,1)S(1)}, bf16[16,128,128]{2,1,0:T(8,128)(2,1)S(1)}, u32[]{:S(2)}, u32[]{:S(2)}) collective-permute-start(bf16[16,128,128]{2,1,0:T(8,128)(2,1)S(1)} %get-tuple-element.37), channel_id=1, source_target_pairs={{0,3},{1,2},{2,1},{3,0},{4,7},{5,6},{6,5},{7,4},{8,11},{9,10},{10,... | collective-permute-start | bytes 1572872 | tf_op jit(solution)/shard_map/ppermute | solution.py:404
  103.9 13.9 %all_to_all.21.dq = bf16[16,128,128]{2,1,0:T(8,128)(2,1)S(1)} all-to-all(bf16[16,128,128]{2,1,0:T(8,128)(2,1)S(1)} %get-tuple-element.38), channel_id=1, replica_groups=mesh['z'=4,'core'=2,'xh'=2,'xl'=2,'y'=4] {'xh','xl','z'}, dimensions={0} | all-to-all | bytes 1048576 | tf_op jit(solution)/shard_map/all_to_all | solution.py:396
  117.8 0.0 collective-permute-done.9.got
  117.8 0.9 shard_map.99
  118.8 13.3 %all_to_all.22.got = bf16[16,128,128]{2,1,0:T(8,128)(2,1)S(1)} all-to-all(bf16[16,128,128]{2,1,0:T(8,128)(2,1)S(1)} %get-tuple-element.40), channel_id=1, replica_groups=mesh['z'=4,'core'=2,'xh'=2,'xl'=2,'y'=4] {'xh','xl','z'}, dimensions={0} | all-to-all | bytes 1048576 | tf_op jit(solution)/shard_map/all_to_all | solution.py:396
  132.1 0.8 shard_map.100
  (20 shorter events, 0.1 us)
Async XLA Ops:
  0.6 24.4 %copy-start.3 = (bf16[64,4096]{1,0:T(8,128)(2,1)S(1)}, bf16[64,4096]{1,0:T(8,128)(2,1)}, u32[]{:S(2)}) copy-start(bf16[64,4096]{1,0:T(8,128)(2,1)} %grads.1) | copy-start | bytes 1572868
  0.6 24.4 %copy-start.2 = (bf16[64,4096]{1,0:T(8,128)(2,1)S(1)}, bf16[64,4096]{1,0:T(8,128)(2,1)}, u32[]{:S(2)}) copy-start(bf16[64,4096]{1,0:T(8,128)(2,1)} %saved.1) | copy-start | bytes 1572868
  0.7 24.4 %copy-start.1 = (bf16[64,4096]{1,0:T(8,128)(2,1)S(1)}, bf16[64,4096]{1,0:T(8,128)(2,1)}, u32[]{:S(2)}) copy-start(bf16[64,4096]{1,0:T(8,128)(2,1)} %queries.1) | copy-start | bytes 1572868
  0.7 1.0 copy-start.4
  1.7 0.9 copy-start.5
  2.6 22.5 %copy-start.6 = (s32[8192]{0:T(1024)S(1)}, s32[8192]{0:T(1024)}, u32[]{:S(2)}) copy-start(s32[8192]{0:T(1024)} %param.12) | copy-start | bytes 98308
  21.9 8.6 %copy-start = (bf16[16,128,128]{2,1,0:T(8,128)(2,1)}, bf16[16,128,128]{2,1,0:T(8,128)(2,1)S(1)}, u32[]{:S(2)}) copy-start(bf16[16,128,128]{2,1,0:T(8,128)(2,1)S(1)} %all_to_all.20.after.refs_0_) | copy-start | bytes 1572868
  21.9 13.5 %collective-permute-start.1 = (bf16[16,128,128]{2,1,0:T(8,128)(2,1)S(1)}, bf16[16,128,128]{2,1,0:T(8,128)(2,1)S(1)}, u32[]{:S(2)}, u32[]{:S(2)}) collective-permute-start(bf16[16,128,128]{2,1,0:T(8,128)(2,1)S(1)} %all_to_all.20.after.refs_0_), channel_id=1, source_target_pairs={{0,3},{1,2},{2,1},{3,0},{4,7},{5,6},{6,5},{7,4},{8,11},{9,10},{10,... | collective-permute-start | bytes 1572872 | tf_op jit(solution)/shard_map/ppermute | solution.py:404
  24.9 13.2 %collective-permute-start = (bf16[16,128,128]{2,1,0:T(8,128)(2,1)S(1)}, bf16[16,128,128]{2,1,0:T(8,128)(2,1)}, u32[]{:S(2)}, u32[]{:S(2)}) collective-permute-start(bf16[16,128,128]{2,1,0:T(8,128)(2,1)S(1)} %all_to_all.20.after.refs_0_), channel_id=1, source_target_pairs={{0,1},{1,0},{2,3},{3,2},{4,5},{5,4},{6,7},{7,6},{8,9},{9,8},{10,11... | collective-permute-start | bytes 1572872 | tf_op jit(solution)/shard_map/ppermute | solution.py:404
  26.8 21.6 %copy-start.7 = (s32[32]{0:T(128)S(1)}, s32[32]{0:T(128)}, u32[]{:S(2)}) copy-start(s32[32]{0:T(128)} %order.1) | copy-start | bytes 388
  26.8 20.0 %all-to-all-start.1 = ((bf16[16,272,128]{2,1,0:T(8,128)(2,1)}), bf16[16,272,128]{2,1,0:T(8,128)(2,1)S(1)}, u32[]{:S(2)}, u32[]{:S(2)}) async-start(bf16[16,272,128]{2,1,0:T(8,128)(2,1)} %get-tuple-element.24), calls=%async_computation.1 | async-start | bytes 2228224 | tf_op jit(solution)/shard_map/all_to_all | solution.py:396
  30.5 16.3 %collective-permute-start.4 = (bf16[16,128,128]{2,1,0:T(8,128)(2,1)S(1)}, bf16[16,128,128]{2,1,0:T(8,128)(2,1)}, u32[]{:S(2)}, u32[]{:S(2)}) collective-permute-start(bf16[16,128,128]{2,1,0:T(8,128)(2,1)S(1)} %all_to_all.20.after.refs_0_), channel_id=1, source_target_pairs={{0,16},{16,0},{1,17},{17,1},{2,18},{18,2},{3,19},{19,3},{4,20},{20... | collective-permute-start | bytes 1572872 | tf_op jit(solution)/shard_map/ppermute | solution.py:400
  35.4 12.9 %copy-start.9 = (bf16[16,128,128]{2,1,0:T(8,128)(2,1)}, bf16[16,128,128]{2,1,0:T(8,128)(2,1)S(1)}, u32[]{:S(2)}) copy-start(bf16[16,128,128]{2,1,0:T(8,128)(2,1)S(1)} %collective-permute-done.1.refs_2_) | copy-start | bytes 1572868
  35.4 7.1 %collective-permute-start.2 = (bf16[8,128,128]{2,1,0:T(8,128)(2,1)S(1)}, bf16[8,128,128]{2,1,0:T(8,128)(2,1)S(1)}, u32[]{:S(2)}, u32[]{:S(2)}) collective-permute-start(bf16[8,128,128]{2,1,0:T(8,128)(2,1)S(1)} %slice.8), channel_id=1, source_target_pairs={{0,1},{1,0},{2,3},{3,2},{4,5},{5,4},{6,7},{7,6},{8,9},{9,8},{10,11... | collective-permute-start | bytes 786440 | tf_op jit(solution)/shard_map/ppermute | solution.py:404
  35.8 11.0 %collective-permute-start.6 = (bf16[16,128,128]{2,1,0:T(8,128)(2,1)S(1)}, bf16[16,128,128]{2,1,0:T(8,128)(2,1)}, u32[]{:S(2)}, u32[]{:S(2)}) collective-permute-start(bf16[16,128,128]{2,1,0:T(8,128)(2,1)S(1)} %collective-permute-done.1.refs_2_), channel_id=1, source_target_pairs={{0,16},{16,0},{1,17},{17,1},{2,18},{18,2},{3,19},{19,3},{4,20},{20... | collective-permute-start | bytes 1572872 | tf_op jit(solution)/shard_map/ppermute | solution.py:400
  39.1 7.7 %collective-permute-start.3 = (bf16[8,128,128]{2,1,0:T(8,128)(2,1)S(1)}, bf16[8,128,128]{2,1,0:T(8,128)(2,1)S(1)}, u32[]{:S(2)}, u32[]{:S(2)}) collective-permute-start(bf16[8,128,128]{2,1,0:T(8,128)(2,1)S(1)} %slice.9), channel_id=1, source_target_pairs={{0,3},{1,2},{2,1},{3,0},{4,7},{5,6},{6,5},{7,4},{8,11},{9,10},{10,... | collective-permute-start | bytes 786440 | tf_op jit(solution)/shard_map/ppermute | solution.py:404
  39.6 8.7 %collective-permute-start.5 = (bf16[16,128,128]{2,1,0:T(8,128)(2,1)}, bf16[16,128,128]{2,1,0:T(8,128)(2,1)}, u32[]{:S(2)}, u32[]{:S(2)}) collective-permute-start(bf16[16,128,128]{2,1,0:T(8,128)(2,1)} %collective-permute-done.refs_1_), channel_id=1, source_target_pairs={{0,16},{16,0},{1,17},{17,1},{2,18},{18,2},{3,19},{19,3},{4,20},{20... | collective-permute-start | bytes 1572872 | tf_op jit(solution)/shard_map/ppermute | solution.py:400
  42.5 4.3 %collective-permute-start.7 = (bf16[8,128,128]{2,1,0:T(8,128)(2,1)S(1)}, bf16[8,128,128]{2,1,0:T(8,128)(2,1)S(1)}, u32[]{:S(2)}, u32[]{:S(2)}) collective-permute-start(bf16[8,128,128]{2,1,0:T(8,128)(2,1)S(1)} %collective-permute-done.2.refs_3_), channel_id=1, source_target_pairs={{0,16},{16,0},{1,17},{17,1},{2,18},{18,2},{3,19},{19,3},{4,20},{20... | collective-permute-start | bytes 786440 | tf_op jit(solution)/shard_map/ppermute | solution.py:400
  46.8 1.5 %collective-permute-start.8 = (bf16[8,128,128]{2,1,0:T(8,128)(2,1)S(1)}, bf16[8,128,128]{2,1,0:T(8,128)(2,1)S(1)}, u32[]{:S(2)}, u32[]{:S(2)}) collective-permute-start(bf16[8,128,128]{2,1,0:T(8,128)(2,1)S(1)} %collective-permute-done.3.refs_4_), channel_id=1, source_target_pairs={{0,16},{16,0},{1,17},{17,1},{2,18},{18,2},{3,19},{19,3},{4,20},{20... | collective-permute-start | bytes 786440 | tf_op jit(solution)/shard_map/ppermute | solution.py:400
  46.8 1.5 %copy-start.8 = (bf16[16,272,128]{2,1,0:T(8,128)(2,1)}, bf16[16,272,128]{2,1,0:T(8,128)(2,1)S(1)}, u32[]{:S(2)}) copy-start(bf16[16,272,128]{2,1,0:T(8,128)(2,1)S(1)} %all-to-all-done.1.qpay) | copy-start | bytes 3342340
  84.7 2.0 %collective-permute-start.12 = (bf16[16,128,128]{2,1,0:T(8,128)(2,1)S(1)}, bf16[16,128,128]{2,1,0:T(8,128)(2,1)S(1)}, u32[]{:S(2)}, u32[]{:S(2)}) collective-permute-start(bf16[16,128,128]{2,1,0:T(8,128)(2,1)S(1)} %get-tuple-element.33), channel_id=1, source_target_pairs={{0,16},{16,0},{1,17},{17,1},{2,18},{18,2},{3,19},{19,3},{4,20},{20... | collective-permute-start | bytes 1572872 | tf_op jit(solution)/shard_map/ppermute | solution.py:400
  85.0 8.6 %collective-permute-start.10 = (bf16[16,128,128]{2,1,0:T(8,128)(2,1)S(1)}, bf16[16,128,128]{2,1,0:T(8,128)(2,1)S(1)}, u32[]{:S(2)}, u32[]{:S(2)}) collective-permute-start(bf16[16,128,128]{2,1,0:T(8,128)(2,1)S(1)} %get-tuple-element.28), channel_id=1, source_target_pairs={{0,16},{16,0},{1,17},{17,1},{2,18},{18,2},{3,19},{19,3},{4,20},{20... | collective-permute-start | bytes 1572872 | tf_op jit(solution)/shard_map/ppermute | solution.py:400
  85.3 8.2 %collective-permute-start.11 = (bf16[16,128,128]{2,1,0:T(8,128)(2,1)S(1)}, bf16[16,128,128]{2,1,0:T(8,128)(2,1)S(1)}, u32[]{:S(2)}, u32[]{:S(2)}) collective-permute-start(bf16[16,128,128]{2,1,0:T(8,128)(2,1)S(1)} %get-tuple-element.30), channel_id=1, source_target_pairs={{0,16},{16,0},{1,17},{17,1},{2,18},{18,2},{3,19},{19,3},{4,20},{20... | collective-permute-start | bytes 1572872 | tf_op jit(solution)/shard_map/ppermute | solution.py:400
  86.9 8.4 %collective-permute-start.13 = (bf16[8,128,128]{2,1,0:T(8,128)(2,1)S(1)}, bf16[8,128,128]{2,1,0:T(8,128)(2,1)S(1)}, u32[]{:S(2)}, u32[]{:S(2)}) collective-permute-start(bf16[8,128,128]{2,1,0:T(8,128)(2,1)S(1)} %get-tuple-element.34), channel_id=1, source_target_pairs={{0,1},{1,0},{2,3},{3,2},{4,5},{5,4},{6,7},{7,6},{8,9},{9,8},{10,11... | collective-permute-start | bytes 786440 | tf_op jit(solution)/shard_map/ppermute | solution.py:404
  86.9 13.2 %collective-permute-start.14 = (bf16[8,128,128]{2,1,0:T(8,128)(2,1)S(1)}, bf16[8,128,128]{2,1,0:T(8,128)(2,1)S(1)}, u32[]{:S(2)}, u32[]{:S(2)}) collective-permute-start(bf16[8,128,128]{2,1,0:T(8,128)(2,1)S(1)} %get-tuple-element.35), channel_id=1, source_target_pairs={{0,3},{1,2},{2,1},{3,0},{4,7},{5,6},{6,5},{7,4},{8,11},{9,10},{10,... | collective-permute-start | bytes 786440 | tf_op jit(solution)/shard_map/ppermute | solution.py:404
  93.5 24.3 %collective-permute-start.9 = (bf16[16,128,128]{2,1,0:T(8,128)(2,1)S(1)}, bf16[16,128,128]{2,1,0:T(8,128)(2,1)S(1)}, u32[]{:S(2)}, u32[]{:S(2)}) collective-permute-start(bf16[16,128,128]{2,1,0:T(8,128)(2,1)S(1)} %get-tuple-element.26), channel_id=1, source_target_pairs={{0,16},{16,0},{1,17},{17,1},{2,18},{18,2},{3,19},{19,3},{4,20},{20... | collective-permute-start | bytes 1572872 | tf_op jit(solution)/shard_map/ppermute | solution.py:400
  100.4 17.4 %collective-permute-start.15 = (bf16[16,128,128]{2,1,0:T(8,128)(2,1)S(1)}, bf16[16,128,128]{2,1,0:T(8,128)(2,1)S(1)}, u32[]{:S(2)}, u32[]{:S(2)}) collective-permute-start(bf16[16,128,128]{2,1,0:T(8,128)(2,1)S(1)} %get-tuple-element.36), channel_id=1, source_target_pairs={{0,1},{1,0},{2,3},{3,2},{4,5},{5,4},{6,7},{7,6},{8,9},{9,8},{10,11... | collective-permute-start | bytes 1572872 | tf_op jit(solution)/shard_map/ppermute | solution.py:404
  101.6 16.3 %collective-permute-start.16 = (bf16[16,128,128]{2,1,0:T(8,128)(2,1)S(1)}, bf16[16,128,128]{2,1,0:T(8,128)(2,1)S(1)}, u32[]{:S(2)}, u32[]{:S(2)}) collective-permute-start(bf16[16,128,128]{2,1,0:T(8,128)(2,1)S(1)} %get-tuple-element.37), channel_id=1, source_target_pairs={{0,3},{1,2},{2,1},{3,0},{4,7},{5,6},{6,5},{7,4},{8,11},{9,10},{10,... | collective-permute-start | bytes 1572872 | tf_op jit(solution)/shard_map/ppermute | solution.py:404

commit v10 on v9

--- a/solution.py
+++ b/solution.py
@@ -37,11 +37,22 @@
     return slice((g * G + h) * D, (g * G + h + 1) * D)
 
 
-def pack_kv_kernel(keys, values, out):
+def pack_kv_kernel(keys, values, out, sem):
+    copies = []
     for g in range(8):
         for xl in range(2):
-            out[spread_to(g, xl), :R] = keys[:, g * D : (g + 1) * D]
-            out[spread_to(g, xl), R:] = values[:, g * D : (g + 1) * D]
+            for part, array in enumerate((keys, values)):
+                copies.append(
+                    pltpu.make_async_copy(
+                        array.at[:, pl.ds(g * D, D)],
+                        out.at[spread_to(g, xl), pl.ds(part * R, R)],
+                        sem,
+                    )
+                )
+    for copy in copies:
+        copy.start()
+    for copy in copies:
+        copy.wait()
 
 
 def pack_q_kernel(queries, saved, grads, segment, after, out, counts):
@@ -130,7 +141,7 @@
         v_s[pl.ds(i, 1), :, :, :, D:] = beside
         return carry
 
-    lax.fori_loop(0, NT, put_beside, 0)
+    lax.fori_loop(0, NT, put_beside, 0, unroll=4)
     dk_s[...] = jnp.zeros_like(dk_s)
     dv_s[...] = jnp.zeros_like(dv_s)
     dq_s[...] = jnp.zeros_like(dq_s)
@@ -172,7 +183,7 @@
         kt_s[b] = keys_of(b).T
         return carry
 
-    lax.fori_loop(0, NT // 2, turn_keys, 0)
+    lax.fori_loop(0, NT // 2, turn_keys, 0, unroll=4)
 
     def put_under(ref, c, *rows):
         number = lax.broadcasted_iota(jnp.int32, (D, C), 0)
@@ -193,7 +204,7 @@
         )
         return carry
 
-    lax.fori_loop(0, NC, turn_rows, 0)
+    lax.fori_loop(0, NC, turn_rows, 0, unroll=4)
     qa_s[NC, :D] = jnp.zeros((D, C), BF16)
     put_under(qa_s, NC, jnp.full((1, C), HIDDEN, F32))
     ga_s[NC] = jnp.zeros((2 * D, C), BF16)
@@ -232,16 +243,20 @@
         return jnp.exp2(scores * EXP_SCALE)
 
     def diagonal_step(i, carry):
-        for c in [2 * i + k for k in range(2)]:
+        chunks = [W * i + k for k in range(W)]
+        found = []
+        for c in chunks:
             b = full_blocks(c)
             scores = jnp.where(seen(c, b), raw_scores(c, b), HIDDEN)
             top = jnp.max(scores, axis=0, keepdims=True).astype(BF16).astype(F32)
+            found.append((top, add_up(jnp.exp2((scores - top) * EXP_SCALE))))
+        for c, (top, total) in zip(chunks, found):
             put_shift(c, -top)
             m_s[c] = top * EXP_SCALE
-            l_s[c] = add_up(jnp.exp2((scores - top) * EXP_SCALE))
-        return carry
-
-    lax.fori_loop(0, NC // 2, diagonal_step, 0)
+            l_s[c] = total
+        return carry
+
+    lax.fori_loop(0, NC // W, diagonal_step, 0)
 
     def add_weights(items, masked):
         parts = [add_up(weights_of(c, b, masked)) for c, b in items]
@@ -290,33 +305,33 @@
         put_shift(c, *rows)
         return carry
 
-    lax.fori_loop(0, NC, put_logsum, 0)
+    lax.fori_loop(0, NC, put_logsum, 0, unroll=4)
     for copy in value_copies:
         copy.wait()
 
     def grad_step(items, masked):
-        weights = [weights_of(c, b, masked) for c, b in items]
-        above = [
-            jnp.dot(block_of(v_s, b), ga_s[c], preferred_element_type=F32) for c, b in items
-        ]
-        score_grads = [(w * p).astype(BF16) for w, p in zip(weights, above)]
-        for (c, b), w, score_grad in zip(items, weights, score_grads):
+        made = []
+        for c, b in items:
+            weights = weights_of(c, b, masked)
+            above = jnp.dot(block_of(v_s, b), ga_s[c], preferred_element_type=F32)
+            made.append((weights.astype(BF16), (weights * above).astype(BF16)))
+        for (c, b), (weights, score_grad) in zip(items, made):
             for ref, term in (
-                (dv_s, jnp.dot(w.astype(BF16), do_s[c], preferred_element_type=F32)),
+                (dv_s, jnp.dot(weights, do_s[c], preferred_element_type=F32)),
                 (dk_s, jnp.dot(score_grad, q_s[c], preferred_element_type=F32)),
             ):
                 ref[pl.ds(2 * b, 2)] += term.reshape(2, 2, 2, R, D)
             dq_s[c] += jnp.dot(kt_s[b], score_grad, preferred_element_type=F32)
 
     def diagonal_grads(i, carry):
-        grad_step([(c, full_blocks(c)) for c in [2 * i + k for k in range(2)]], True)
+        grad_step([(c, full_blocks(c)) for c in [W * i + k for k in range(W)]], True)
         return carry
 
     def plain_grads(i, carry):
         grad_step(plain_items(i), False)
         return carry
 
-    lax.fori_loop(0, NC // 2, diagonal_grads, 0)
+    lax.fori_loop(0, NC // W, diagonal_grads, 0)
     lax.fori_loop(0, (n_plain + W - 1) // W, plain_grads, 0)
 
     def finish(c, carry):
@@ -325,7 +340,7 @@
         dq_out[2 * c + 1] = dq[QR:]
         return carry
 
-    lax.fori_loop(0, NC, finish, 0)
+    lax.fori_loop(0, NC, finish, 0, unroll=4)
 
     for from_core, group in (
         (core, ((0, keep_0, 0), (1, keep_1, 0), (3, keep_3, 0), (2, sum_a, 0), (2, sum_b, 1))),
@@ -405,7 +420,14 @@
 
 
 def body(queries, keys, values, attn_out, out_grad, segment, span_order):
-    own = exchange(on_vmem(pack_kv_kernel, bf16(16, 2 * R, D), keys, values))
+    kv_packed = pl.pallas_call(
+        pack_kv_kernel,
+        out_shape=bf16(16, 2 * R, D),
+        in_specs=[pl.BlockSpec(memory_space=pltpu.HBM)] * 2,
+        scratch_shapes=[pltpu.SemaphoreType.DMA],
+        compiler_params=pltpu.CompilerParams(vmem_limit_bytes=16 << 20),
+    )(keys, values)
+    own = exchange(kv_packed)
     q_packed, counts = pl.pallas_call(
         pack_q_kernel,
         out_shape=[bf16(16, 2 * QR + 16, D), jax.ShapeDtypeStruct((2,), jnp.int32)],

time: 131 us -> 128 us (0.977)
  starting transfers between devices: 18.9 us -> 10.7 us
  waiting for transfers between devices: 23.5 us -> 26.1 us
  Pallas kernels: 40.3 us -> 41.7 us
    ppermute x8, starting transfers between devices: 14.2 us -> 5.61 us  [swap(): return lax.ppermute(array, 'y', [(i, i ^ distance) for i in range(4)])]
    ppermute x8, waiting for transfers between devices: 20.7 us -> 22.5 us  [swap(): return lax.ppermute(array, 'y', [(i, i ^ distance) for i in range(4)])]
    pallas_call x1, Pallas kernels: 36.4 us -> 37.7 us  [body(): pl.pallas_call(attention_kernel, out_shape=[bf16(16, QR, D)] + [group] *...]
  transfers between devices with their start and end apart: 18 -> 18, of which waited for: 8 -> 10; matrix products, arithmetic and copies ran while one was open for 1% -> 1% of each run, Pallas kernels for 2% -> 2%
where the time goes in v10:
time: 128 us; the launch traced here: 129 us
  blocking collectives  46.7 us (36%)
  Pallas kernels  41.7 us (33%)
  waiting for transfers between devices  26.1 us (20%)
  starting transfers between devices  10.7 us (8%)
  local copies, waits for them, and re-layouts  2.93 us (2%)
    all_to_all x3, blocking collectives, exchange(): lax.all_to_all(array, SPREAD, split_axis=0, concat_axis=0, tiled=True)  46.7 us
    pallas_call x1, Pallas kernels, body(): pl.pallas_call(attention_kernel, out_shape=[bf16(16, QR, D)] + [group] *...  37.7 us
    ppermute x8, waiting for transfers between devices, swap(): return lax.ppermute(array, 'y', [(i, i ^ distance) for i in range(4)])  22.5 us
    ppermute x8, starting transfers between devices, swap(): return lax.ppermute(array, 'y', [(i, i ^ distance) for i in range(4)])  5.61 us
    all_to_all x1, starting transfers between devices, exchange(): lax.all_to_all(array, SPREAD, split_axis=0, concat_axis=0, tiled=True)  3.71 us
    ppermute x9, waiting for transfers between devices, flip(): return lax.ppermute(array, 'core', [(0, 1), (1, 0)])  3.6 us
  transfers between devices with their start and end apart: 18, of which 10 were waited for; matrix products, arithmetic and copies ran while one was open for 1% of the time, Pallas kernels for 2%

profile of v10, /device:TPU:0, one launch (start us, length us, event | category | flops | bytes accessed | tf_op | source)
XLA Modules:
  0.0 129.0 jit_solution(17245376445434274972)
XLA Ops:
  0.7 1.0 copy-done.4
  1.7 0.9 copy-done.5
  2.6 0.2 shard_map.94
  2.8 19.3 %all_to_all.20.after.refs_0_ = bf16[16,128,128]{2,1,0:T(8,128)(2,1)S(1)} all-to-all(bf16[16,128,128]{2,1,0:T(8,128)(2,1)S(1)} %shard_map.94), channel_id=1, replica_groups=mesh['z'=4,'core'=2,'xh'=2,'xl'=2,'y'=4] {'xh','xl','z'}, dimensions={0} | all-to-all | bytes 1048576 | tf_op jit(solution)/shard_map/all_to_all | solution.py:411
  22.0 3.0 %collective-permute-start.1 = (bf16[16,128,128]{2,1,0:T(8,128)(2,1)S(1)}, bf16[16,128,128]{2,1,0:T(8,128)(2,1)S(1)}, u32[]{:S(2)}, u32[]{:S(2)}) collective-permute-start(bf16[16,128,128]{2,1,0:T(8,128)(2,1)S(1)} %all_to_all.20.after.refs_0_), channel_id=1, source_target_pairs={{0,3},{1,2},{2,1},{3,0},{4,7},{5,6},{6,5},{7,4},{8,11},{9,10},{10,... | collective-permute-start | bytes 1572872 | tf_op jit(solution)/shard_map/ppermute | solution.py:419
  25.0 0.1 collective-permute-start
  25.2 1.7 %shard_map.95 = (bf16[16,272,128]{2,1,0:T(8,128)(2,1)}, s32[2]{0:T(128)S(1)}) custom-call(bf16[64,4096]{1,0:T(8,128)(2,1)S(1)} %copy-done.1, bf16[64,4096]{1,0:T(8,128)(2,1)S(1)} %copy-done.2, bf16[64,4096]{1,0:T(8,128)(2,1)S(1)} %copy-done.3, s32[64,128]{1,0:T(8,128)S(1)} %bitcast.1, bf16[16,128,128]{2,1,0:T(8,128)(2,1)S(1)} %all_to_all.20.after.refs_0_), custom_call_target="tpu_custom_call" | custom-call | tf_op jit(solution)/shard_map/pallas_call | solution.py:431
  26.9 0.0 copy-start.7
  26.9 3.7 %all-to-all-start.1 = ((bf16[16,272,128]{2,1,0:T(8,128)(2,1)}), bf16[16,272,128]{2,1,0:T(8,128)(2,1)S(1)}, u32[]{:S(2)}, u32[]{:S(2)}) async-start(bf16[16,272,128]{2,1,0:T(8,128)(2,1)} %get-tuple-element.24), calls=%async_computation.1 | async-start | bytes 2228224 | tf_op jit(solution)/shard_map/all_to_all | solution.py:411
  30.6 0.1 collective-permute-start.4
  30.7 4.8 %collective-permute-done.1.refs_2_ = bf16[16,128,128]{2,1,0:T(8,128)(2,1)S(1)} collective-permute-done((bf16[16,128,128]{2,1,0:T(8,128)(2,1)S(1)}, bf16[16,128,128]{2,1,0:T(8,128)(2,1)S(1)}, u32[]{:S(2)}, u32[]{:S(2)}) %collective-permute-start.1) | collective-permute-done | bytes 524320 | tf_op jit(solution)/shard_map/ppermute | solution.py:419
  35.5 0.4 collective-permute-start.2
  35.9 0.0 collective-permute-start.6
  35.9 2.4 %collective-permute-done.refs_1_ = bf16[16,128,128]{2,1,0:T(8,128)(2,1)} collective-permute-done((bf16[16,128,128]{2,1,0:T(8,128)(2,1)S(1)}, bf16[16,128,128]{2,1,0:T(8,128)(2,1)}, u32[]{:S(2)}, u32[]{:S(2)}) %collective-permute-start) | collective-permute-done | bytes 524320 | tf_op jit(solution)/shard_map/ppermute | solution.py:419
  38.2 1.0 slice.9
  39.2 0.5 collective-permute-start.3
  39.7 0.2 collective-permute-start.5
  39.9 2.6 %collective-permute-done.2.refs_3_ = bf16[8,128,128]{2,1,0:T(8,128)(2,1)S(1)} collective-permute-done((bf16[8,128,128]{2,1,0:T(8,128)(2,1)S(1)}, bf16[8,128,128]{2,1,0:T(8,128)(2,1)S(1)}, u32[]{:S(2)}, u32[]{:S(2)}) %collective-permute-start.2) | collective-permute-done | bytes 262176 | tf_op jit(solution)/shard_map/ppermute | solution.py:419
  42.6 0.0 collective-permute-start.7
  42.6 4.3 %collective-permute-done.3.refs_4_ = bf16[8,128,128]{2,1,0:T(8,128)(2,1)S(1)} collective-permute-done((bf16[8,128,128]{2,1,0:T(8,128)(2,1)S(1)}, bf16[8,128,128]{2,1,0:T(8,128)(2,1)S(1)}, u32[]{:S(2)}, u32[]{:S(2)}) %collective-permute-start.3) | collective-permute-done | bytes 262176 | tf_op jit(solution)/shard_map/ppermute | solution.py:419
  46.9 0.0 collective-permute-start.8
  46.9 0.0 collective-permute-done.4.refs_5_
  46.9 0.0 all-to-all-done.1.qpay
  46.9 0.0 collective-permute-done.7.refs_8_
  46.9 0.0 collective-permute-done.6.refs_7_
  46.9 1.5 %collective-permute-done.8.refs_9_ = bf16[8,128,128]{2,1,0:T(8,128)(2,1)S(1)} collective-permute-done((bf16[8,128,128]{2,1,0:T(8,128)(2,1)S(1)}, bf16[8,128,128]{2,1,0:T(8,128)(2,1)S(1)}, u32[]{:S(2)}, u32[]{:S(2)}) %collective-permute-start.8) | collective-permute-done | bytes 262176 | tf_op jit(solution)/shard_map/ppermute | solution.py:415
  48.4 0.0 collective-permute-done.5.refs_6_
  48.4 37.7 %shard_map.96 = (bf16[16,128,128]{2,1,0:T(8,128)(2,1)S(1)}, bf16[16,128,128]{2,1,0:T(8,128)(2,1)S(1)}, bf16[16,128,128]{2,1,0:T(8,128)(2,1)S(1)}, bf16[16,128,12...) custom-call(s32[32]{0:T(128)S(1)} %copy-done.7, ...), custom_call_target="tpu_custom_call" | custom-call | tf_op jit(solution)/shard_map/pallas_call | solution.py:447
  86.2 0.2 collective-permute-start.12
  86.4 0.4 collective-permute-start.10
  86.8 0.3 collective-permute-start.11
  87.1 1.1 collective-permute-done.12.got
  88.2 0.1 shard_map.97
  88.3 0.1 collective-permute-start.13
  88.4 0.1 collective-permute-start.14
  88.5 0.2 collective-permute-start.9
  88.7 0.2 collective-permute-done.10.got_1
  88.9 0.7 collective-permute-done.11.got_3
  89.7 7.1 %collective-permute-done.13.from_1 = bf16[8,128,128]{2,1,0:T(8,128)(2,1)S(1)} collective-permute-done((bf16[8,128,128]{2,1,0:T(8,128)(2,1)S(1)}, bf16[8,128,128]{2,1,0:T(8,128)(2,1)S(1)}, u32[]{:S(2)}, u32[]{:S(2)}) %collective-permute-start.13) | collective-permute-done | bytes 262176 | tf_op jit(solution)/shard_map/ppermute | solution.py:419
  96.7 1.3 %collective-permute-done.14.from_3 = bf16[8,128,128]{2,1,0:T(8,128)(2,1)S(1)} collective-permute-done((bf16[8,128,128]{2,1,0:T(8,128)(2,1)S(1)}, bf16[8,128,128]{2,1,0:T(8,128)(2,1)S(1)}, u32[]{:S(2)}, u32[]{:S(2)}) %collective-permute-start.14) | collective-permute-done | bytes 262176 | tf_op jit(solution)/shard_map/ppermute | solution.py:419
  98.0 0.3 shard_map.98
  98.3 0.5 collective-permute-start.15
  98.9 0.9 collective-permute-start.16
  99.8 14.1 %all_to_all.21.dq = bf16[16,128,128]{2,1,0:T(8,128)(2,1)S(1)} all-to-all(bf16[16,128,128]{2,1,0:T(8,128)(2,1)S(1)} %get-tuple-element.38), channel_id=1, replica_groups=mesh['z'=4,'core'=2,'xh'=2,'xl'=2,'y'=4] {'xh','xl','z'}, dimensions={0} | all-to-all | bytes 1048576 | tf_op jit(solution)/shard_map/all_to_all | solution.py:411
  113.9 0.0 collective-permute-done.16.near_3
  113.9 0.9 shard_map.99
  114.8 13.3 %all_to_all.22.got = bf16[16,128,128]{2,1,0:T(8,128)(2,1)S(1)} all-to-all(bf16[16,128,128]{2,1,0:T(8,128)(2,1)S(1)} %get-tuple-element.40), channel_id=1, replica_groups=mesh['z'=4,'core'=2,'xh'=2,'xl'=2,'y'=4] {'xh','xl','z'}, dimensions={0} | all-to-all | bytes 1048576 | tf_op jit(solution)/shard_map/all_to_all | solution.py:411
  128.2 0.8 shard_map.100
  (20 shorter events, 0.1 us)
Async XLA Ops:
  0.6 24.5 %copy-start.3 = (bf16[64,4096]{1,0:T(8,128)(2,1)S(1)}, bf16[64,4096]{1,0:T(8,128)(2,1)}, u32[]{:S(2)}) copy-start(bf16[64,4096]{1,0:T(8,128)(2,1)} %grads.1) | copy-start | bytes 1572868
  0.6 24.5 %copy-start.2 = (bf16[64,4096]{1,0:T(8,128)(2,1)S(1)}, bf16[64,4096]{1,0:T(8,128)(2,1)}, u32[]{:S(2)}) copy-start(bf16[64,4096]{1,0:T(8,128)(2,1)} %saved.1) | copy-start | bytes 1572868
  0.7 24.5 %copy-start.1 = (bf16[64,4096]{1,0:T(8,128)(2,1)S(1)}, bf16[64,4096]{1,0:T(8,128)(2,1)}, u32[]{:S(2)}) copy-start(bf16[64,4096]{1,0:T(8,128)(2,1)} %queries.1) | copy-start | bytes 1572868
  0.7 1.0 copy-start.4
  1.7 0.9 copy-start.5
  2.6 22.6 %copy-start.6 = (s32[8192]{0:T(1024)S(1)}, s32[8192]{0:T(1024)}, u32[]{:S(2)}) copy-start(s32[8192]{0:T(1024)} %param.12) | copy-start | bytes 98308
  22.0 8.6 %copy-start = (bf16[16,128,128]{2,1,0:T(8,128)(2,1)}, bf16[16,128,128]{2,1,0:T(8,128)(2,1)S(1)}, u32[]{:S(2)}) copy-start(bf16[16,128,128]{2,1,0:T(8,128)(2,1)S(1)} %all_to_all.20.after.refs_0_) | copy-start | bytes 1572868
  22.0 13.5 %collective-permute-start.1 = (bf16[16,128,128]{2,1,0:T(8,128)(2,1)S(1)}, bf16[16,128,128]{2,1,0:T(8,128)(2,1)S(1)}, u32[]{:S(2)}, u32[]{:S(2)}) collective-permute-start(bf16[16,128,128]{2,1,0:T(8,128)(2,1)S(1)} %all_to_all.20.after.refs_0_), channel_id=1, source_target_pairs={{0,3},{1,2},{2,1},{3,0},{4,7},{5,6},{6,5},{7,4},{8,11},{9,10},{10,... | collective-permute-start | bytes 1572872 | tf_op jit(solution)/shard_map/ppermute | solution.py:419
  25.0 13.2 %collective-permute-start = (bf16[16,128,128]{2,1,0:T(8,128)(2,1)S(1)}, bf16[16,128,128]{2,1,0:T(8,128)(2,1)}, u32[]{:S(2)}, u32[]{:S(2)}) collective-permute-start(bf16[16,128,128]{2,1,0:T(8,128)(2,1)S(1)} %all_to_all.20.after.refs_0_), channel_id=1, source_target_pairs={{0,1},{1,0},{2,3},{3,2},{4,5},{5,4},{6,7},{7,6},{8,9},{9,8},{10,11... | collective-permute-start | bytes 1572872 | tf_op jit(solution)/shard_map/ppermute | solution.py:419
  26.9 21.6 %copy-start.7 = (s32[32]{0:T(128)S(1)}, s32[32]{0:T(128)}, u32[]{:S(2)}) copy-start(s32[32]{0:T(128)} %order.1) | copy-start | bytes 388
  26.9 20.0 %all-to-all-start.1 = ((bf16[16,272,128]{2,1,0:T(8,128)(2,1)}), bf16[16,272,128]{2,1,0:T(8,128)(2,1)S(1)}, u32[]{:S(2)}, u32[]{:S(2)}) async-start(bf16[16,272,128]{2,1,0:T(8,128)(2,1)} %get-tuple-element.24), calls=%async_computation.1 | async-start | bytes 2228224 | tf_op jit(solution)/shard_map/all_to_all | solution.py:411
  30.6 16.3 %collective-permute-start.4 = (bf16[16,128,128]{2,1,0:T(8,128)(2,1)S(1)}, bf16[16,128,128]{2,1,0:T(8,128)(2,1)}, u32[]{:S(2)}, u32[]{:S(2)}) collective-permute-start(bf16[16,128,128]{2,1,0:T(8,128)(2,1)S(1)} %all_to_all.20.after.refs_0_), channel_id=1, source_target_pairs={{0,16},{16,0},{1,17},{17,1},{2,18},{18,2},{3,19},{19,3},{4,20},{20... | collective-permute-start | bytes 1572872 | tf_op jit(solution)/shard_map/ppermute | solution.py:415
  35.5 12.9 %copy-start.9 = (bf16[16,128,128]{2,1,0:T(8,128)(2,1)}, bf16[16,128,128]{2,1,0:T(8,128)(2,1)S(1)}, u32[]{:S(2)}) copy-start(bf16[16,128,128]{2,1,0:T(8,128)(2,1)S(1)} %collective-permute-done.1.refs_2_) | copy-start | bytes 1572868
  35.5 7.1 %collective-permute-start.2 = (bf16[8,128,128]{2,1,0:T(8,128)(2,1)S(1)}, bf16[8,128,128]{2,1,0:T(8,128)(2,1)S(1)}, u32[]{:S(2)}, u32[]{:S(2)}) collective-permute-start(bf16[8,128,128]{2,1,0:T(8,128)(2,1)S(1)} %slice.8), channel_id=1, source_target_pairs={{0,1},{1,0},{2,3},{3,2},{4,5},{5,4},{6,7},{7,6},{8,9},{9,8},{10,11... | collective-permute-start | bytes 786440 | tf_op jit(solution)/shard_map/ppermute | solution.py:419
  35.9 11.0 %collective-permute-start.6 = (bf16[16,128,128]{2,1,0:T(8,128)(2,1)S(1)}, bf16[16,128,128]{2,1,0:T(8,128)(2,1)}, u32[]{:S(2)}, u32[]{:S(2)}) collective-permute-start(bf16[16,128,128]{2,1,0:T(8,128)(2,1)S(1)} %collective-permute-done.1.refs_2_), channel_id=1, source_target_pairs={{0,16},{16,0},{1,17},{17,1},{2,18},{18,2},{3,19},{19,3},{4,20},{20... | collective-permute-start | bytes 1572872 | tf_op jit(solution)/shard_map/ppermute | solution.py:415
  39.2 7.7 %collective-permute-start.3 = (bf16[8,128,128]{2,1,0:T(8,128)(2,1)S(1)}, bf16[8,128,128]{2,1,0:T(8,128)(2,1)S(1)}, u32[]{:S(2)}, u32[]{:S(2)}) collective-permute-start(bf16[8,128,128]{2,1,0:T(8,128)(2,1)S(1)} %slice.9), channel_id=1, source_target_pairs={{0,3},{1,2},{2,1},{3,0},{4,7},{5,6},{6,5},{7,4},{8,11},{9,10},{10,... | collective-permute-start | bytes 786440 | tf_op jit(solution)/shard_map/ppermute | solution.py:419
  39.7 8.7 %collective-permute-start.5 = (bf16[16,128,128]{2,1,0:T(8,128)(2,1)}, bf16[16,128,128]{2,1,0:T(8,128)(2,1)}, u32[]{:S(2)}, u32[]{:S(2)}) collective-permute-start(bf16[16,128,128]{2,1,0:T(8,128)(2,1)} %collective-permute-done.refs_1_), channel_id=1, source_target_pairs={{0,16},{16,0},{1,17},{17,1},{2,18},{18,2},{3,19},{19,3},{4,20},{20... | collective-permute-start | bytes 1572872 | tf_op jit(solution)/shard_map/ppermute | solution.py:415
  42.6 4.3 %collective-permute-start.7 = (bf16[8,128,128]{2,1,0:T(8,128)(2,1)S(1)}, bf16[8,128,128]{2,1,0:T(8,128)(2,1)S(1)}, u32[]{:S(2)}, u32[]{:S(2)}) collective-permute-start(bf16[8,128,128]{2,1,0:T(8,128)(2,1)S(1)} %collective-permute-done.2.refs_3_), channel_id=1, source_target_pairs={{0,16},{16,0},{1,17},{17,1},{2,18},{18,2},{3,19},{19,3},{4,20},{20... | collective-permute-start | bytes 786440 | tf_op jit(solution)/shard_map/ppermute | solution.py:415
  46.9 1.5 %collective-permute-start.8 = (bf16[8,128,128]{2,1,0:T(8,128)(2,1)S(1)}, bf16[8,128,128]{2,1,0:T(8,128)(2,1)S(1)}, u32[]{:S(2)}, u32[]{:S(2)}) collective-permute-start(bf16[8,128,128]{2,1,0:T(8,128)(2,1)S(1)} %collective-permute-done.3.refs_4_), channel_id=1, source_target_pairs={{0,16},{16,0},{1,17},{17,1},{2,18},{18,2},{3,19},{19,3},{4,20},{20... | collective-permute-start | bytes 786440 | tf_op jit(solution)/shard_map/ppermute | solution.py:415
  46.9 1.5 %copy-start.8 = (bf16[16,272,128]{2,1,0:T(8,128)(2,1)}, bf16[16,272,128]{2,1,0:T(8,128)(2,1)S(1)}, u32[]{:S(2)}) copy-start(bf16[16,272,128]{2,1,0:T(8,128)(2,1)S(1)} %all-to-all-done.1.qpay) | copy-start | bytes 3342340
  86.2 2.0 %collective-permute-start.12 = (bf16[16,128,128]{2,1,0:T(8,128)(2,1)S(1)}, bf16[16,128,128]{2,1,0:T(8,128)(2,1)S(1)}, u32[]{:S(2)}, u32[]{:S(2)}) collective-permute-start(bf16[16,128,128]{2,1,0:T(8,128)(2,1)S(1)} %get-tuple-element.33), channel_id=1, source_target_pairs={{0,16},{16,0},{1,17},{17,1},{2,18},{18,2},{3,19},{19,3},{4,20},{20... | collective-permute-start | bytes 1572872 | tf_op jit(solution)/shard_map/ppermute | solution.py:415
  86.4 2.6 %collective-permute-start.10 = (bf16[16,128,128]{2,1,0:T(8,128)(2,1)S(1)}, bf16[16,128,128]{2,1,0:T(8,128)(2,1)S(1)}, u32[]{:S(2)}, u32[]{:S(2)}) collective-permute-start(bf16[16,128,128]{2,1,0:T(8,128)(2,1)S(1)} %get-tuple-element.28), channel_id=1, source_target_pairs={{0,16},{16,0},{1,17},{17,1},{2,18},{18,2},{3,19},{19,3},{4,20},{20... | collective-permute-start | bytes 1572872 | tf_op jit(solution)/shard_map/ppermute | solution.py:415
  86.8 2.9 %collective-permute-start.11 = (bf16[16,128,128]{2,1,0:T(8,128)(2,1)S(1)}, bf16[16,128,128]{2,1,0:T(8,128)(2,1)S(1)}, u32[]{:S(2)}, u32[]{:S(2)}) collective-permute-start(bf16[16,128,128]{2,1,0:T(8,128)(2,1)S(1)} %get-tuple-element.30), channel_id=1, source_target_pairs={{0,16},{16,0},{1,17},{17,1},{2,18},{18,2},{3,19},{19,3},{4,20},{20... | collective-permute-start | bytes 1572872 | tf_op jit(solution)/shard_map/ppermute | solution.py:415
  88.3 8.4 %collective-permute-start.13 = (bf16[8,128,128]{2,1,0:T(8,128)(2,1)S(1)}, bf16[8,128,128]{2,1,0:T(8,128)(2,1)S(1)}, u32[]{:S(2)}, u32[]{:S(2)}) collective-permute-start(bf16[8,128,128]{2,1,0:T(8,128)(2,1)S(1)} %get-tuple-element.34), channel_id=1, source_target_pairs={{0,1},{1,0},{2,3},{3,2},{4,5},{5,4},{6,7},{7,6},{8,9},{9,8},{10,11... | collective-permute-start | bytes 786440 | tf_op jit(solution)/shard_map/ppermute | solution.py:419
  88.4 9.6 %collective-permute-start.14 = (bf16[8,128,128]{2,1,0:T(8,128)(2,1)S(1)}, bf16[8,128,128]{2,1,0:T(8,128)(2,1)S(1)}, u32[]{:S(2)}, u32[]{:S(2)}) collective-permute-start(bf16[8,128,128]{2,1,0:T(8,128)(2,1)S(1)} %get-tuple-element.35), channel_id=1, source_target_pairs={{0,3},{1,2},{2,1},{3,0},{4,7},{5,6},{6,5},{7,4},{8,11},{9,10},{10,... | collective-permute-start | bytes 786440 | tf_op jit(solution)/shard_map/ppermute | solution.py:419
  88.5 25.4 %collective-permute-start.9 = (bf16[16,128,128]{2,1,0:T(8,128)(2,1)S(1)}, bf16[16,128,128]{2,1,0:T(8,128)(2,1)S(1)}, u32[]{:S(2)}, u32[]{:S(2)}) collective-permute-start(bf16[16,128,128]{2,1,0:T(8,128)(2,1)S(1)} %get-tuple-element.26), channel_id=1, source_target_pairs={{0,16},{16,0},{1,17},{17,1},{2,18},{18,2},{3,19},{19,3},{4,20},{20... | collective-permute-start | bytes 1572872 | tf_op jit(solution)/shard_map/ppermute | solution.py:415
  98.3 15.6 %collective-permute-start.15 = (bf16[16,128,128]{2,1,0:T(8,128)(2,1)S(1)}, bf16[16,128,128]{2,1,0:T(8,128)(2,1)S(1)}, u32[]{:S(2)}, u32[]{:S(2)}) collective-permute-start(bf16[16,128,128]{2,1,0:T(8,128)(2,1)S(1)} %get-tuple-element.36), channel_id=1, source_target_pairs={{0,1},{1,0},{2,3},{3,2},{4,5},{5,4},{6,7},{7,6},{8,9},{9,8},{10,11... | collective-permute-start | bytes 1572872 | tf_op jit(solution)/shard_map/ppermute | solution.py:419
  98.9 15.0 %collective-permute-start.16 = (bf16[16,128,128]{2,1,0:T(8,128)(2,1)S(1)}, bf16[16,128,128]{2,1,0:T(8,128)(2,1)S(1)}, u32[]{:S(2)}, u32[]{:S(2)}) collective-permute-start(bf16[16,128,128]{2,1,0:T(8,128)(2,1)S(1)} %get-tuple-element.37), channel_id=1, source_target_pairs={{0,3},{1,2},{2,1},{3,0},{4,7},{5,6},{6,5},{7,4},{8,11},{9,10},{10,... | collective-permute-start | bytes 1572872 | tf_op jit(solution)/shard_map/ppermute | solution.py:419

commit v11 on v10

--- a/solution.py
+++ b/solution.py
@@ -18,6 +18,7 @@
 C = 2 * QR
 NC = 8
 W = 4
+WG = 2
 SCALE = D**-0.5
 EXP_SCALE = SCALE * math.log2(math.e)
 HIDDEN = -1e30
@@ -263,11 +264,11 @@
         for (c, b), part in zip(items, parts):
             l_s[c] += part
 
-    def plain_items(i):
-        return [(plain_c[n], plain_b[n]) for n in [W * i + k for k in range(W)]]
+    def plain_items(i, width):
+        return [(plain_c[n], plain_b[n]) for n in [width * i + k for k in range(width)]]
 
     def plain_stats(i, carry):
-        add_weights(plain_items(i), False)
+        add_weights(plain_items(i, W), False)
         return carry
 
     lax.fori_loop(0, (n_plain + W - 1) // W, plain_stats, 0)
@@ -324,15 +325,15 @@
             dq_s[c] += jnp.dot(kt_s[b], score_grad, preferred_element_type=F32)
 
     def diagonal_grads(i, carry):
-        grad_step([(c, full_blocks(c)) for c in [W * i + k for k in range(W)]], True)
+        grad_step([(c, full_blocks(c)) for c in [WG * i + k for k in range(WG)]], True)
         return carry
 
     def plain_grads(i, carry):
-        grad_step(plain_items(i), False)
-        return carry
-
-    lax.fori_loop(0, NC // W, diagonal_grads, 0)
-    lax.fori_loop(0, (n_plain + W - 1) // W, plain_grads, 0)
+        grad_step(plain_items(i, WG), False)
+        return carry
+
+    lax.fori_loop(0, NC // WG, diagonal_grads, 0)
+    lax.fori_loop(0, (n_plain + WG - 1) // WG, plain_grads, 0)
 
     def finish(c, carry):
         dq = (dq_s[c] * SCALE).T.astype(BF16)
@@ -425,7 +426,7 @@
         out_shape=bf16(16, 2 * R, D),
         in_specs=[pl.BlockSpec(memory_space=pltpu.HBM)] * 2,
         scratch_shapes=[pltpu.SemaphoreType.DMA],
-        compiler_params=pltpu.CompilerParams(vmem_limit_bytes=16 << 20),
+        compiler_params=pltpu.CompilerParams(vmem_limit_bytes=60 << 20),
     )(keys, values)
     own = exchange(kv_packed)
     q_packed, counts = pl.pallas_call(
@@ -467,7 +468,7 @@
             pltpu.SemaphoreType.DMA,
             pltpu.SemaphoreType.DMA,
         ],
-        compiler_params=pltpu.CompilerParams(vmem_limit_bytes=48 << 20),
+        compiler_params=pltpu.CompilerParams(vmem_limit_bytes=34 << 20),
     )(span_order, counts, qpay, *mine, *[flip(array) for array in mine])
     far_sum_a, far_sum_b = on_vmem(far_sum_kernel, [half, half], sum_a, sum_b, flip(far_give))
     from_1 = swap(far_sum_a, 1)

time: 128 us -> 134 us (1.047)
  starting transfers between devices: 10.7 us -> 21.9 us
  waiting for transfers between devices: 26.1 us -> 22.9 us
  local copies, waits for them, and re-layouts: 2.93 us -> 1.07 us
    ppermute x8, starting transfers between devices: 5.61 us -> 17.1 us  [swap(): return lax.ppermute(array, 'y', [(i, i ^ distance) for i in range(4)])]
    ppermute x8, waiting for transfers between devices: 22.5 us -> 19.7 us  [swap(): return lax.ppermute(array, 'y', [(i, i ^ distance) for i in range(4)])]
    ppermute x9, waiting for transfers between devices: 3.6 us -> 1.63 us  [flip(): return lax.ppermute(array, 'core', [(0, 1), (1, 0)])]
    pallas_call x1, Pallas kernels: 0.16 us -> 1.87 us  [body(): pl.pallas_call(pack_kv_kernel, out_shape=bf16(16, 2 * R, D), in_specs=[pl...]
    pallas_call x1, Pallas kernels: 37.7 us -> 36.1 us  [body(): pl.pallas_call(attention_kernel, out_shape=[bf16(16, QR, D)] + [group] *...]
    all_to_all x1, waiting for transfers between devices: 0.01 us -> 1.52 us  [exchange(): lax.all_to_all(array, SPREAD, split_axis=0, concat_axis=0, tiled=True)]
  transfers between devices with their start and end apart: 18 -> 18, of which waited for: 10 -> 8; matrix products, arithmetic and copies ran while one was open for 1% -> 0% of each run, Pallas kernels for 2% -> 1%
where the time goes in v11:
time: 134 us; the launch traced here: 135 us
  blocking collectives  46.7 us (35%)
  Pallas kernels  41.3 us (31%)
  waiting for transfers between devices  22.9 us (17%)
  starting transfers between devices  21.9 us (16%)
    all_to_all x3, blocking collectives, exchange(): lax.all_to_all(array, SPREAD, split_axis=0, concat_axis=0, tiled=True)  46.7 us
    pallas_call x1, Pallas kernels, body(): pl.pallas_call(attention_kernel, out_shape=[bf16(16, QR, D)] + [group] *...  36.1 us
    ppermute x8, waiting for transfers between devices, swap(): return lax.ppermute(array, 'y', [(i, i ^ distance) for i in range(4)])  19.7 us
    ppermute x8, starting transfers between devices, swap(): return lax.ppermute(array, 'y', [(i, i ^ distance) for i in range(4)])  17.1 us
    all_to_all x1, starting transfers between devices, exchange(): lax.all_to_all(array, SPREAD, split_axis=0, concat_axis=0, tiled=True)  3.83 us
  transfers between devices with their start and end apart: 18, of which 8 were waited for; matrix products, arithmetic and copies ran while one was open for 0% of the time, Pallas kernels for 1%

profile of v11, /device:TPU:0, one launch (start us, length us, event | category | flops | bytes accessed | tf_op | source)
XLA Modules:
  0.0 134.7 jit_solution(11362481302744829910)
XLA Ops:
  0.7 1.9 %shard_map.94 = bf16[16,128,128]{2,1,0:T(8,128)(2,1)} custom-call(bf16[64,1024]{1,0:T(8,128)(2,1)} %keys.1, bf16[64,1024]{1,0:T(8,128)(2,1)} %values.1), custom_call_target="tpu_custom_call" | custom-call | tf_op jit(solution)/shard_map/pallas_call | solution.py:424
  2.5 19.5 %all_to_all.20.after.refs_0_ = bf16[16,128,128]{2,1,0:T(8,128)(2,1)S(1)} all-to-all(bf16[16,128,128]{2,1,0:T(8,128)(2,1)} %shard_map.94), channel_id=1, replica_groups=mesh['z'=4,'core'=2,'xh'=2,'xl'=2,'y'=4] {'xh','xl','z'}, dimensions={0} | all-to-all | bytes 1048576 | tf_op jit(solution)/shard_map/all_to_all | solution.py:412
  22.0 3.0 %collective-permute-start.1 = (bf16[16,128,128]{2,1,0:T(8,128)(2,1)S(1)}, bf16[16,128,128]{2,1,0:T(8,128)(2,1)S(1)}, u32[]{:S(2)}, u32[]{:S(2)}) collective-permute-start(bf16[16,128,128]{2,1,0:T(8,128)(2,1)S(1)} %all_to_all.20.after.refs_0_), channel_id=1, source_target_pairs={{0,3},{1,2},{2,1},{3,0},{4,7},{5,6},{6,5},{7,4},{8,11},{9,10},{10,... | collective-permute-start | bytes 1572872 | tf_op jit(solution)/shard_map/ppermute | solution.py:420
  25.0 0.1 collective-permute-start
  25.2 0.0 copy-done.3
  25.2 1.3 shard_map.95
  26.4 1.0 copy-done
  27.5 3.8 %all-to-all-start.1 = ((bf16[16,272,128]{2,1,0:T(8,128)(2,1)}), bf16[16,272,128]{2,1,0:T(8,128)(2,1)S(1)}, u32[]{:S(2)}, u32[]{:S(2)}) async-start(bf16[16,272,128]{2,1,0:T(8,128)(2,1)} %copy-done), calls=%async_computation.1 | async-start | bytes 2228224 | tf_op jit(solution)/shard_map/all_to_all | solution.py:412
  31.3 0.1 collective-permute-start.4
  31.4 4.1 %collective-permute-done.1.refs_2_ = bf16[16,128,128]{2,1,0:T(8,128)(2,1)S(1)} collective-permute-done((bf16[16,128,128]{2,1,0:T(8,128)(2,1)S(1)}, bf16[16,128,128]{2,1,0:T(8,128)(2,1)S(1)}, u32[]{:S(2)}, u32[]{:S(2)}) %collective-permute-start.1) | collective-permute-done | bytes 524320 | tf_op jit(solution)/shard_map/ppermute | solution.py:420
  35.5 0.4 collective-permute-start.2
  35.9 0.0 collective-permute-start.6
  35.9 2.2 %collective-permute-done.refs_1_ = bf16[16,128,128]{2,1,0:T(8,128)(2,1)S(1)} collective-permute-done((bf16[16,128,128]{2,1,0:T(8,128)(2,1)S(1)}, bf16[16,128,128]{2,1,0:T(8,128)(2,1)S(1)}, u32[]{:S(2)}, u32[]{:S(2)}) %collective-permute-start) | collective-permute-done | bytes 524320 | tf_op jit(solution)/shard_map/ppermute | solution.py:420
  38.2 0.6 collective-permute-start.3
  38.8 0.2 collective-permute-start.5
  39.0 3.6 %collective-permute-done.2.refs_3_ = bf16[8,128,128]{2,1,0:T(8,128)(2,1)S(1)} collective-permute-done((bf16[8,128,128]{2,1,0:T(8,128)(2,1)S(1)}, bf16[8,128,128]{2,1,0:T(8,128)(2,1)S(1)}, u32[]{:S(2)}, u32[]{:S(2)}) %collective-permute-start.2) | collective-permute-done | bytes 262176 | tf_op jit(solution)/shard_map/ppermute | solution.py:420
  42.6 0.0 collective-permute-start.7
  42.6 3.5 %collective-permute-done.3.refs_4_ = bf16[8,128,128]{2,1,0:T(8,128)(2,1)} collective-permute-done((bf16[8,128,128]{2,1,0:T(8,128)(2,1)S(1)}, bf16[8,128,128]{2,1,0:T(8,128)(2,1)}, u32[]{:S(2)}, u32[]{:S(2)}) %collective-permute-start.3) | collective-permute-done | bytes 262176 | tf_op jit(solution)/shard_map/ppermute | solution.py:420
  46.0 0.0 collective-permute-start.8
  46.0 0.0 collective-permute-done.4.refs_5_
  46.0 1.5 %all-to-all-done.1.qpay = bf16[16,272,128]{2,1,0:T(8,128)(2,1)S(1)} async-done(((bf16[16,272,128]{2,1,0:T(8,128)(2,1)}), bf16[16,272,128]{2,1,0:T(8,128)(2,1)S(1)}, u32[]{:S(2)}, u32[]{:S(2)}) %all-to-all-start.1) | async-done | bytes 1114144 | tf_op jit(solution)/shard_map/all_to_all | solution.py:412
  47.6 0.0 collective-permute-done.7.refs_8_
  47.6 0.0 collective-permute-done.6.refs_7_
  47.6 0.3 collective-permute-done.8.refs_9_
  47.9 0.0 collective-permute-done.5.refs_6_
  47.9 36.1 %shard_map.96 = (bf16[16,128,128]{2,1,0:T(8,128)(2,1)S(1)}, bf16[16,128,128]{2,1,0:T(8,128)(2,1)S(1)}, bf16[16,128,128]{2,1,0:T(8,128)(2,1)S(1)}, bf16[16,128,12...) custom-call(s32[32]{0:T(128)S(1)} %copy-done.5, ...), custom_call_target="tpu_custom_call" | custom-call | tf_op jit(solution)/shard_map/pallas_call | solution.py:448
  84.0 0.2 collective-permute-start.12
  84.2 0.4 collective-permute-start.10
  84.6 0.1 collective-permute-start.11
  84.7 1.3 collective-permute-done.12.got
  86.0 0.1 shard_map.97
  86.1 0.1 collective-permute-start.13
  86.2 9.7 %collective-permute-start.14 = (bf16[8,128,128]{2,1,0:T(8,128)(2,1)S(1)}, bf16[8,128,128]{2,1,0:T(8,128)(2,1)S(1)}, u32[]{:S(2)}, u32[]{:S(2)}) collective-permute-start(bf16[8,128,128]{2,1,0:T(8,128)(2,1)S(1)} %get-tuple-element.35), channel_id=1, source_target_pairs={{0,3},{1,2},{2,1},{3,0},{4,7},{5,6},{6,5},{7,4},{8,11},{9,10},{10,... | collective-permute-start | bytes 786440 | tf_op jit(solution)/shard_map/ppermute | solution.py:420
  95.9 0.0 collective-permute-start.9
  95.9 0.0 collective-permute-done.10.got_1
  95.9 0.0 collective-permute-done.11.got_3
  95.9 0.0 collective-permute-done.13.from_1
  95.9 6.3 %collective-permute-done.14.from_3 = bf16[8,128,128]{2,1,0:T(8,128)(2,1)S(1)} collective-permute-done((bf16[8,128,128]{2,1,0:T(8,128)(2,1)S(1)}, bf16[8,128,128]{2,1,0:T(8,128)(2,1)S(1)}, u32[]{:S(2)}, u32[]{:S(2)}) %collective-permute-start.14) | collective-permute-done | bytes 262176 | tf_op jit(solution)/shard_map/ppermute | solution.py:420
  102.2 0.3 shard_map.98
  102.6 0.1 collective-permute-start.15
  102.6 3.0 %collective-permute-start.16 = (bf16[16,128,128]{2,1,0:T(8,128)(2,1)S(1)}, bf16[16,128,128]{2,1,0:T(8,128)(2,1)S(1)}, u32[]{:S(2)}, u32[]{:S(2)}) collective-permute-start(bf16[16,128,128]{2,1,0:T(8,128)(2,1)S(1)} %get-tuple-element.37), channel_id=1, source_target_pairs={{0,3},{1,2},{2,1},{3,0},{4,7},{5,6},{6,5},{7,4},{8,11},{9,10},{10,... | collective-permute-start | bytes 1572872 | tf_op jit(solution)/shard_map/ppermute | solution.py:420
  105.7 13.9 %all_to_all.21.dq = bf16[16,128,128]{2,1,0:T(8,128)(2,1)S(1)} all-to-all(bf16[16,128,128]{2,1,0:T(8,128)(2,1)S(1)} %get-tuple-element.38), channel_id=1, replica_groups=mesh['z'=4,'core'=2,'xh'=2,'xl'=2,'y'=4] {'xh','xl','z'}, dimensions={0} | all-to-all | bytes 1048576 | tf_op jit(solution)/shard_map/all_to_all | solution.py:412
  119.6 0.0 collective-permute-done.9.got
  119.6 0.0 collective-permute-done.15.near_1
  119.6 0.0 collective-permute-done.16.near_3
  119.6 0.9 shard_map.99
  120.6 13.3 %all_to_all.22.got = bf16[16,128,128]{2,1,0:T(8,128)(2,1)S(1)} all-to-all(bf16[16,128,128]{2,1,0:T(8,128)(2,1)S(1)} %get-tuple-element.40), channel_id=1, replica_groups=mesh['z'=4,'core'=2,'xh'=2,'xl'=2,'y'=4] {'xh','xl','z'}, dimensions={0} | all-to-all | bytes 1048576 | tf_op jit(solution)/shard_map/all_to_all | solution.py:412
  133.9 0.8 shard_map.100
  (12 shorter events, 0.1 us)
Async XLA Ops:
  0.6 24.5 %copy-start.4 = (s32[8192]{0:T(1024)S(1)}, s32[8192]{0:T(1024)}, u32[]{:S(2)}) copy-start(s32[8192]{0:T(1024)} %param.12) | copy-start | bytes 98308
  0.6 24.5 %copy-start.3 = (bf16[64,4096]{1,0:T(8,128)(2,1)S(1)}, bf16[64,4096]{1,0:T(8,128)(2,1)}, u32[]{:S(2)}) copy-start(bf16[64,4096]{1,0:T(8,128)(2,1)} %grads.1) | copy-start | bytes 1572868
  0.7 24.5 %copy-start.2 = (bf16[64,4096]{1,0:T(8,128)(2,1)S(1)}, bf16[64,4096]{1,0:T(8,128)(2,1)}, u32[]{:S(2)}) copy-start(bf16[64,4096]{1,0:T(8,128)(2,1)} %saved.1) | copy-start | bytes 1572868
  0.7 24.5 %copy-start.1 = (bf16[64,4096]{1,0:T(8,128)(2,1)S(1)}, bf16[64,4096]{1,0:T(8,128)(2,1)}, u32[]{:S(2)}) copy-start(bf16[64,4096]{1,0:T(8,128)(2,1)} %queries.1) | copy-start | bytes 1572868
  22.0 13.5 %collective-permute-start.1 = (bf16[16,128,128]{2,1,0:T(8,128)(2,1)S(1)}, bf16[16,128,128]{2,1,0:T(8,128)(2,1)S(1)}, u32[]{:S(2)}, u32[]{:S(2)}) collective-permute-start(bf16[16,128,128]{2,1,0:T(8,128)(2,1)S(1)} %all_to_all.20.after.refs_0_), channel_id=1, source_target_pairs={{0,3},{1,2},{2,1},{3,0},{4,7},{5,6},{6,5},{7,4},{8,11},{9,10},{10,... | collective-permute-start | bytes 1572872 | tf_op jit(solution)/shard_map/ppermute | solution.py:420
  25.0 13.1 %collective-permute-start = (bf16[16,128,128]{2,1,0:T(8,128)(2,1)S(1)}, bf16[16,128,128]{2,1,0:T(8,128)(2,1)S(1)}, u32[]{:S(2)}, u32[]{:S(2)}) collective-permute-start(bf16[16,128,128]{2,1,0:T(8,128)(2,1)S(1)} %all_to_all.20.after.refs_0_), channel_id=1, source_target_pairs={{0,1},{1,0},{2,3},{3,2},{4,5},{5,4},{6,7},{7,6},{8,9},{9,8},{10,11... | collective-permute-start | bytes 1572872 | tf_op jit(solution)/shard_map/ppermute | solution.py:420
  26.4 1.0 copy-start
  27.5 20.4 %copy-start.5 = (s32[32]{0:T(128)S(1)}, s32[32]{0:T(128)}, u32[]{:S(2)}) copy-start(s32[32]{0:T(128)} %order.1) | copy-start | bytes 388
  27.5 20.1 %all-to-all-start.1 = ((bf16[16,272,128]{2,1,0:T(8,128)(2,1)}), bf16[16,272,128]{2,1,0:T(8,128)(2,1)S(1)}, u32[]{:S(2)}, u32[]{:S(2)}) async-start(bf16[16,272,128]{2,1,0:T(8,128)(2,1)} %copy-done), calls=%async_computation.1 | async-start | bytes 2228224 | tf_op jit(solution)/shard_map/all_to_all | solution.py:412
  31.3 14.7 %collective-permute-start.4 = (bf16[16,128,128]{2,1,0:T(8,128)(2,1)S(1)}, bf16[16,128,128]{2,1,0:T(8,128)(2,1)S(1)}, u32[]{:S(2)}, u32[]{:S(2)}) collective-permute-start(bf16[16,128,128]{2,1,0:T(8,128)(2,1)S(1)} %all_to_all.20.after.refs_0_), channel_id=1, source_target_pairs={{0,16},{16,0},{1,17},{17,1},{2,18},{18,2},{3,19},{19,3},{4,20},{20... | collective-permute-start | bytes 1572872 | tf_op jit(solution)/shard_map/ppermute | solution.py:416
  35.5 7.1 %collective-permute-start.2 = (bf16[8,128,128]{2,1,0:T(8,128)(2,1)S(1)}, bf16[8,128,128]{2,1,0:T(8,128)(2,1)S(1)}, u32[]{:S(2)}, u32[]{:S(2)}) collective-permute-start(bf16[8,128,128]{2,1,0:T(8,128)(2,1)S(1)} %slice.8), channel_id=1, source_target_pairs={{0,1},{1,0},{2,3},{3,2},{4,5},{5,4},{6,7},{7,6},{8,9},{9,8},{10,11... | collective-permute-start | bytes 786440 | tf_op jit(solution)/shard_map/ppermute | solution.py:420
  35.9 11.7 %collective-permute-start.6 = (bf16[16,128,128]{2,1,0:T(8,128)(2,1)S(1)}, bf16[16,128,128]{2,1,0:T(8,128)(2,1)}, u32[]{:S(2)}, u32[]{:S(2)}) collective-permute-start(bf16[16,128,128]{2,1,0:T(8,128)(2,1)S(1)} %collective-permute-done.1.refs_2_), channel_id=1, source_target_pairs={{0,16},{16,0},{1,17},{17,1},{2,18},{18,2},{3,19},{19,3},{4,20},{20... | collective-permute-start | bytes 1572872 | tf_op jit(solution)/shard_map/ppermute | solution.py:416
  38.2 7.9 %collective-permute-start.3 = (bf16[8,128,128]{2,1,0:T(8,128)(2,1)S(1)}, bf16[8,128,128]{2,1,0:T(8,128)(2,1)}, u32[]{:S(2)}, u32[]{:S(2)}) collective-permute-start(bf16[8,128,128]{2,1,0:T(8,128)(2,1)S(1)} %slice.9), channel_id=1, source_target_pairs={{0,3},{1,2},{2,1},{3,0},{4,7},{5,6},{6,5},{7,4},{8,11},{9,10},{10,... | collective-permute-start | bytes 786440 | tf_op jit(solution)/shard_map/ppermute | solution.py:420
  38.8 9.2 %collective-permute-start.5 = (bf16[16,128,128]{2,1,0:T(8,128)(2,1)S(1)}, bf16[16,128,128]{2,1,0:T(8,128)(2,1)}, u32[]{:S(2)}, u32[]{:S(2)}) collective-permute-start(bf16[16,128,128]{2,1,0:T(8,128)(2,1)S(1)} %collective-permute-done.refs_1_), channel_id=1, source_target_pairs={{0,16},{16,0},{1,17},{17,1},{2,18},{18,2},{3,19},{19,3},{4,20},{20... | collective-permute-start | bytes 1572872 | tf_op jit(solution)/shard_map/ppermute | solution.py:416
  42.6 5.0 %collective-permute-start.7 = (bf16[8,128,128]{2,1,0:T(8,128)(2,1)S(1)}, bf16[8,128,128]{2,1,0:T(8,128)(2,1)}, u32[]{:S(2)}, u32[]{:S(2)}) collective-permute-start(bf16[8,128,128]{2,1,0:T(8,128)(2,1)S(1)} %collective-permute-done.2.refs_3_), channel_id=1, source_target_pairs={{0,16},{16,0},{1,17},{17,1},{2,18},{18,2},{3,19},{19,3},{4,20},{20... | collective-permute-start | bytes 786440 | tf_op jit(solution)/shard_map/ppermute | solution.py:416
  46.0 1.9 %collective-permute-start.8 = (bf16[8,128,128]{2,1,0:T(8,128)(2,1)}, bf16[8,128,128]{2,1,0:T(8,128)(2,1)}, u32[]{:S(2)}, u32[]{:S(2)}) collective-permute-start(bf16[8,128,128]{2,1,0:T(8,128)(2,1)} %collective-permute-done.3.refs_4_), channel_id=1, source_target_pairs={{0,16},{16,0},{1,17},{17,1},{2,18},{18,2},{3,19},{19,3},{4,20},{20... | collective-permute-start | bytes 786440 | tf_op jit(solution)/shard_map/ppermute | solution.py:416
  84.0 2.0 %collective-permute-start.12 = (bf16[16,128,128]{2,1,0:T(8,128)(2,1)S(1)}, bf16[16,128,128]{2,1,0:T(8,128)(2,1)S(1)}, u32[]{:S(2)}, u32[]{:S(2)}) collective-permute-start(bf16[16,128,128]{2,1,0:T(8,128)(2,1)S(1)} %get-tuple-element.33), channel_id=1, source_target_pairs={{0,16},{16,0},{1,17},{17,1},{2,18},{18,2},{3,19},{19,3},{4,20},{20... | collective-permute-start | bytes 1572872 | tf_op jit(solution)/shard_map/ppermute | solution.py:416
  84.2 11.7 %collective-permute-start.10 = (bf16[16,128,128]{2,1,0:T(8,128)(2,1)S(1)}, bf16[16,128,128]{2,1,0:T(8,128)(2,1)S(1)}, u32[]{:S(2)}, u32[]{:S(2)}) collective-permute-start(bf16[16,128,128]{2,1,0:T(8,128)(2,1)S(1)} %get-tuple-element.28), channel_id=1, source_target_pairs={{0,16},{16,0},{1,17},{17,1},{2,18},{18,2},{3,19},{19,3},{4,20},{20... | collective-permute-start | bytes 1572872 | tf_op jit(solution)/shard_map/ppermute | solution.py:416
  84.6 11.4 %collective-permute-start.11 = (bf16[16,128,128]{2,1,0:T(8,128)(2,1)S(1)}, bf16[16,128,128]{2,1,0:T(8,128)(2,1)S(1)}, u32[]{:S(2)}, u32[]{:S(2)}) collective-permute-start(bf16[16,128,128]{2,1,0:T(8,128)(2,1)S(1)} %get-tuple-element.30), channel_id=1, source_target_pairs={{0,16},{16,0},{1,17},{17,1},{2,18},{18,2},{3,19},{19,3},{4,20},{20... | collective-permute-start | bytes 1572872 | tf_op jit(solution)/shard_map/ppermute | solution.py:416
  86.1 9.8 %collective-permute-start.13 = (bf16[8,128,128]{2,1,0:T(8,128)(2,1)S(1)}, bf16[8,128,128]{2,1,0:T(8,128)(2,1)S(1)}, u32[]{:S(2)}, u32[]{:S(2)}) collective-permute-start(bf16[8,128,128]{2,1,0:T(8,128)(2,1)S(1)} %get-tuple-element.34), channel_id=1, source_target_pairs={{0,1},{1,0},{2,3},{3,2},{4,5},{5,4},{6,7},{7,6},{8,9},{9,8},{10,11... | collective-permute-start | bytes 786440 | tf_op jit(solution)/shard_map/ppermute | solution.py:420
  86.2 16.1 %collective-permute-start.14 = (bf16[8,128,128]{2,1,0:T(8,128)(2,1)S(1)}, bf16[8,128,128]{2,1,0:T(8,128)(2,1)S(1)}, u32[]{:S(2)}, u32[]{:S(2)}) collective-permute-start(bf16[8,128,128]{2,1,0:T(8,128)(2,1)S(1)} %get-tuple-element.35), channel_id=1, source_target_pairs={{0,3},{1,2},{2,1},{3,0},{4,7},{5,6},{6,5},{7,4},{8,11},{9,10},{10,... | collective-permute-start | bytes 786440 | tf_op jit(solution)/shard_map/ppermute | solution.py:420
  95.9 23.7 %collective-permute-start.9 = (bf16[16,128,128]{2,1,0:T(8,128)(2,1)S(1)}, bf16[16,128,128]{2,1,0:T(8,128)(2,1)S(1)}, u32[]{:S(2)}, u32[]{:S(2)}) collective-permute-start(bf16[16,128,128]{2,1,0:T(8,128)(2,1)S(1)} %get-tuple-element.26), channel_id=1, source_target_pairs={{0,16},{16,0},{1,17},{17,1},{2,18},{18,2},{3,19},{19,3},{4,20},{20... | collective-permute-start | bytes 1572872 | tf_op jit(solution)/shard_map/ppermute | solution.py:416
  102.6 17.1 %collective-permute-start.15 = (bf16[16,128,128]{2,1,0:T(8,128)(2,1)S(1)}, bf16[16,128,128]{2,1,0:T(8,128)(2,1)S(1)}, u32[]{:S(2)}, u32[]{:S(2)}) collective-permute-start(bf16[16,128,128]{2,1,0:T(8,128)(2,1)S(1)} %get-tuple-element.36), channel_id=1, source_target_pairs={{0,1},{1,0},{2,3},{3,2},{4,5},{5,4},{6,7},{7,6},{8,9},{9,8},{10,11... | collective-permute-start | bytes 1572872 | tf_op jit(solution)/shard_map/ppermute | solution.py:420
  102.6 17.0 %collective-permute-start.16 = (bf16[16,128,128]{2,1,0:T(8,128)(2,1)S(1)}, bf16[16,128,128]{2,1,0:T(8,128)(2,1)S(1)}, u32[]{:S(2)}, u32[]{:S(2)}) collective-permute-start(bf16[16,128,128]{2,1,0:T(8,128)(2,1)S(1)} %get-tuple-element.37), channel_id=1, source_target_pairs={{0,3},{1,2},{2,1},{3,0},{4,7},{5,6},{6,5},{7,4},{8,11},{9,10},{10,... | collective-permute-start | bytes 1572872 | tf_op jit(solution)/shard_map/ppermute | solution.py:420

commit v12 on v11

--- a/solution.py
+++ b/solution.py
@@ -17,8 +17,8 @@
 QR = G * HR
 C = 2 * QR
 NC = 8
-W = 4
-WG = 2
+W = 8
+REST = 2
 SCALE = D**-0.5
 EXP_SCALE = SCALE * math.log2(math.e)
 HIDDEN = -1e30
@@ -167,7 +167,7 @@
         return lax.fori_loop(0, full_blocks(c), put, size)
 
     n_plain = lax.fori_loop(0, NC, list_chunk, jnp.int32(0))
-    for i in range(W - 1):
+    for i in range(REST - 1):
         plain_c[n_plain + i] = NC
         plain_b[n_plain + i] = 0
 
@@ -244,7 +244,7 @@
         return jnp.exp2(scores * EXP_SCALE)
 
     def diagonal_step(i, carry):
-        chunks = [W * i + k for k in range(W)]
+        chunks = [4 * i + k for k in range(4)]
         found = []
         for c in chunks:
             b = full_blocks(c)
@@ -257,21 +257,27 @@
             l_s[c] = total
         return carry
 
-    lax.fori_loop(0, NC // W, diagonal_step, 0)
+    lax.fori_loop(0, NC // 4, diagonal_step, 0)
 
     def add_weights(items, masked):
         parts = [add_up(weights_of(c, b, masked)) for c, b in items]
         for (c, b), part in zip(items, parts):
             l_s[c] += part
 
-    def plain_items(i, width):
-        return [(plain_c[n], plain_b[n]) for n in [width * i + k for k in range(width)]]
-
-    def plain_stats(i, carry):
-        add_weights(plain_items(i, W), False)
-        return carry
-
-    lax.fori_loop(0, (n_plain + W - 1) // W, plain_stats, 0)
+    def each_plain(step):
+        def wide(i, carry):
+            step([(plain_c[n], plain_b[n]) for n in [W * i + k for k in range(W)]], False)
+            return carry
+
+        def narrow(i, carry):
+            step([(plain_c[n], plain_b[n]) for n in [REST * i + k for k in range(REST)]], False)
+            return carry
+
+        n_wide = n_plain // W
+        lax.fori_loop(0, n_wide, wide, 0)
+        lax.fori_loop(n_wide * (W // REST), (n_plain + (REST - 1)) // REST, narrow, 0)
+
+    each_plain(add_weights)
 
     @pl.when(jnp.logical_not(jnp.max(l_s[...]) < LARGE))
     def _():
@@ -325,15 +331,11 @@
             dq_s[c] += jnp.dot(kt_s[b], score_grad, preferred_element_type=F32)
 
     def diagonal_grads(i, carry):
-        grad_step([(c, full_blocks(c)) for c in [WG * i + k for k in range(WG)]], True)
-        return carry
-
-    def plain_grads(i, carry):
-        grad_step(plain_items(i, WG), False)
-        return carry
-
-    lax.fori_loop(0, NC // WG, diagonal_grads, 0)
-    lax.fori_loop(0, (n_plain + WG - 1) // WG, plain_grads, 0)
+        grad_step([(c, full_blocks(c)) for c in [4 * i + k for k in range(4)]], True)
+        return carry
+
+    lax.fori_loop(0, NC // 4, diagonal_grads, 0)
+    each_plain(grad_step)
 
     def finish(c, carry):
         dq = (dq_s[c] * SCALE).T.astype(BF16)

time: 134 us -> 130 us (0.970); the launches traced: 135 us -> 128 us
  Pallas kernels: 41.3 us -> 32.2 us
  starting transfers between devices: 21.9 us -> 24.7 us
    pallas_call x1, Pallas kernels: 36.1 us -> 27 us  [body(): pl.pallas_call(attention_kernel, out_shape=[bf16(16, QR, D)] + [group] *...]
    ppermute x8, starting transfers between devices: 17.1 us -> 19.8 us  [swap(): return lax.ppermute(array, 'y', [(i, i ^ distance) for i in range(4)])]
where the time goes in v12:
time: 130 us; the launch traced here: 128 us
  blocking collectives  46.7 us (36%)
  Pallas kernels  32.2 us (25%)
  starting transfers between devices  24.7 us (19%)
  waiting for transfers between devices  22.8 us (18%)
    all_to_all x3, blocking collectives, exchange(): lax.all_to_all(array, SPREAD, split_axis=0, concat_axis=0, tiled=True)  46.7 us
    pallas_call x1, Pallas kernels, body(): pl.pallas_call(attention_kernel, out_shape=[bf16(16, QR, D)] + [group] *...  27 us
    ppermute x8, starting transfers between devices, swap(): return lax.ppermute(array, 'y', [(i, i ^ distance) for i in range(4)])  19.8 us
    ppermute x8, waiting for transfers between devices, swap(): return lax.ppermute(array, 'y', [(i, i ^ distance) for i in range(4)])  19.7 us
    all_to_all x1, starting transfers between devices, exchange(): lax.all_to_all(array, SPREAD, split_axis=0, concat_axis=0, tiled=True)  3.83 us
  transfers between devices with their start and end apart: 18, of which 8 were waited for; matrix products, arithmetic and copies ran while one was open for 0% of the time, Pallas kernels for 1%

profile of v12, /device:TPU:0, one launch (start us, length us, event | category | flops | bytes accessed | tf_op | source)
XLA Modules:
  0.0 128.4 jit_solution(10230500850064524696)
XLA Ops:
  0.7 1.9 %shard_map.94 = bf16[16,128,128]{2,1,0:T(8,128)(2,1)} custom-call(bf16[64,1024]{1,0:T(8,128)(2,1)} %keys.1, bf16[64,1024]{1,0:T(8,128)(2,1)} %values.1), custom_call_target="tpu_custom_call" | custom-call | tf_op jit(solution)/shard_map/pallas_call | solution.py:426
  2.5 19.5 %all_to_all.20.after.refs_0_ = bf16[16,128,128]{2,1,0:T(8,128)(2,1)S(1)} all-to-all(bf16[16,128,128]{2,1,0:T(8,128)(2,1)} %shard_map.94), channel_id=1, replica_groups=mesh['z'=4,'core'=2,'xh'=2,'xl'=2,'y'=4] {'xh','xl','z'}, dimensions={0} | all-to-all | bytes 1048576 | tf_op jit(solution)/shard_map/all_to_all | solution.py:414
  22.0 3.0 %collective-permute-start.1 = (bf16[16,128,128]{2,1,0:T(8,128)(2,1)S(1)}, bf16[16,128,128]{2,1,0:T(8,128)(2,1)S(1)}, u32[]{:S(2)}, u32[]{:S(2)}) collective-permute-start(bf16[16,128,128]{2,1,0:T(8,128)(2,1)S(1)} %all_to_all.20.after.refs_0_), channel_id=1, source_target_pairs={{0,3},{1,2},{2,1},{3,0},{4,7},{5,6},{6,5},{7,4},{8,11},{9,10},{10,... | collective-permute-start | bytes 1572872 | tf_op jit(solution)/shard_map/ppermute | solution.py:422
  25.0 0.1 collective-permute-start
  25.2 0.0 copy-done.2
  25.2 1.3 shard_map.95
  26.4 1.0 copy-done
  27.5 3.8 %all-to-all-start.1 = ((bf16[16,272,128]{2,1,0:T(8,128)(2,1)}), bf16[16,272,128]{2,1,0:T(8,128)(2,1)S(1)}, u32[]{:S(2)}, u32[]{:S(2)}) async-start(bf16[16,272,128]{2,1,0:T(8,128)(2,1)} %copy-done), calls=%async_computation.1 | async-start | bytes 2228224 | tf_op jit(solution)/shard_map/all_to_all | solution.py:414
  31.3 0.1 collective-permute-start.4
  31.4 4.1 %collective-permute-done.1.refs_2_ = bf16[16,128,128]{2,1,0:T(8,128)(2,1)S(1)} collective-permute-done((bf16[16,128,128]{2,1,0:T(8,128)(2,1)S(1)}, bf16[16,128,128]{2,1,0:T(8,128)(2,1)S(1)}, u32[]{:S(2)}, u32[]{:S(2)}) %collective-permute-start.1) | collective-permute-done | bytes 524320 | tf_op jit(solution)/shard_map/ppermute | solution.py:422
  35.5 0.4 collective-permute-start.2
  35.9 0.0 collective-permute-start.6
  35.9 2.2 %collective-permute-done.refs_1_ = bf16[16,128,128]{2,1,0:T(8,128)(2,1)S(1)} collective-permute-done((bf16[16,128,128]{2,1,0:T(8,128)(2,1)S(1)}, bf16[16,128,128]{2,1,0:T(8,128)(2,1)S(1)}, u32[]{:S(2)}, u32[]{:S(2)}) %collective-permute-start) | collective-permute-done | bytes 524320 | tf_op jit(solution)/shard_map/ppermute | solution.py:422
  38.2 0.6 collective-permute-start.3
  38.8 0.2 collective-permute-start.5
  39.0 3.6 %collective-permute-done.2.refs_3_ = bf16[8,128,128]{2,1,0:T(8,128)(2,1)S(1)} collective-permute-done((bf16[8,128,128]{2,1,0:T(8,128)(2,1)S(1)}, bf16[8,128,128]{2,1,0:T(8,128)(2,1)S(1)}, u32[]{:S(2)}, u32[]{:S(2)}) %collective-permute-start.2) | collective-permute-done | bytes 262176 | tf_op jit(solution)/shard_map/ppermute | solution.py:422
  42.6 0.0 collective-permute-start.7
  42.6 3.5 %collective-permute-done.3.refs_4_ = bf16[8,128,128]{2,1,0:T(8,128)(2,1)} collective-permute-done((bf16[8,128,128]{2,1,0:T(8,128)(2,1)S(1)}, bf16[8,128,128]{2,1,0:T(8,128)(2,1)}, u32[]{:S(2)}, u32[]{:S(2)}) %collective-permute-start.3) | collective-permute-done | bytes 262176 | tf_op jit(solution)/shard_map/ppermute | solution.py:422
  46.0 0.0 collective-permute-start.8
  46.0 0.0 collective-permute-done.4.refs_5_
  46.0 1.5 %all-to-all-done.1.qpay = bf16[16,272,128]{2,1,0:T(8,128)(2,1)S(1)} async-done(((bf16[16,272,128]{2,1,0:T(8,128)(2,1)}), bf16[16,272,128]{2,1,0:T(8,128)(2,1)S(1)}, u32[]{:S(2)}, u32[]{:S(2)}) %all-to-all-start.1) | async-done | bytes 1114144 | tf_op jit(solution)/shard_map/all_to_all | solution.py:414
  47.6 0.0 collective-permute-done.7.refs_8_
  47.6 0.0 collective-permute-done.6.refs_7_
  47.6 0.3 collective-permute-done.8.refs_9_
  47.9 0.0 collective-permute-done.5.refs_6_
  47.9 27.0 %shard_map.96 = (bf16[16,128,128]{2,1,0:T(8,128)(2,1)S(1)}, bf16[16,128,128]{2,1,0:T(8,128)(2,1)S(1)}, bf16[16,128,128]{2,1,0:T(8,128)(2,1)S(1)}, bf16[16,128,12...) custom-call(s32[32]{0:T(128)S(1)} %copy-done.5, ...), custom_call_target="tpu_custom_call" | custom-call | tf_op jit(solution)/shard_map/pallas_call | solution.py:450
  74.9 0.2 collective-permute-start.12
  75.1 0.4 collective-permute-start.10
  75.5 0.1 collective-permute-start.11
  75.6 1.3 collective-permute-done.12.got
  76.9 0.1 shard_map.97
  77.0 4.8 %collective-permute-start.13 = (bf16[8,128,128]{2,1,0:T(8,128)(2,1)S(1)}, bf16[8,128,128]{2,1,0:T(8,128)(2,1)S(1)}, u32[]{:S(2)}, u32[]{:S(2)}) collective-permute-start(bf16[8,128,128]{2,1,0:T(8,128)(2,1)S(1)} %get-tuple-element.34), channel_id=1, source_target_pairs={{0,1},{1,0},{2,3},{3,2},{4,5},{5,4},{6,7},{7,6},{8,9},{9,8},{10,11... | collective-permute-start | bytes 786440 | tf_op jit(solution)/shard_map/ppermute | solution.py:422
  81.8 7.8 %collective-permute-start.14 = (bf16[8,128,128]{2,1,0:T(8,128)(2,1)S(1)}, bf16[8,128,128]{2,1,0:T(8,128)(2,1)S(1)}, u32[]{:S(2)}, u32[]{:S(2)}) collective-permute-start(bf16[8,128,128]{2,1,0:T(8,128)(2,1)S(1)} %get-tuple-element.35), channel_id=1, source_target_pairs={{0,3},{1,2},{2,1},{3,0},{4,7},{5,6},{6,5},{7,4},{8,11},{9,10},{10,... | collective-permute-start | bytes 786440 | tf_op jit(solution)/shard_map/ppermute | solution.py:422
  89.6 0.0 collective-permute-start.9
  89.6 0.0 collective-permute-done.10.got_1
  89.6 0.0 collective-permute-done.11.got_3
  89.6 0.0 collective-permute-done.13.from_1
  89.6 6.3 %collective-permute-done.14.from_3 = bf16[8,128,128]{2,1,0:T(8,128)(2,1)S(1)} collective-permute-done((bf16[8,128,128]{2,1,0:T(8,128)(2,1)S(1)}, bf16[8,128,128]{2,1,0:T(8,128)(2,1)S(1)}, u32[]{:S(2)}, u32[]{:S(2)}) %collective-permute-start.14) | collective-permute-done | bytes 262176 | tf_op jit(solution)/shard_map/ppermute | solution.py:422
  95.9 0.3 shard_map.98
  96.2 0.1 collective-permute-start.15
  96.3 3.0 %collective-permute-start.16 = (bf16[16,128,128]{2,1,0:T(8,128)(2,1)S(1)}, bf16[16,128,128]{2,1,0:T(8,128)(2,1)S(1)}, u32[]{:S(2)}, u32[]{:S(2)}) collective-permute-start(bf16[16,128,128]{2,1,0:T(8,128)(2,1)S(1)} %get-tuple-element.37), channel_id=1, source_target_pairs={{0,3},{1,2},{2,1},{3,0},{4,7},{5,6},{6,5},{7,4},{8,11},{9,10},{10,... | collective-permute-start | bytes 1572872 | tf_op jit(solution)/shard_map/ppermute | solution.py:422
  99.4 13.9 %all_to_all.21.dq = bf16[16,128,128]{2,1,0:T(8,128)(2,1)S(1)} all-to-all(bf16[16,128,128]{2,1,0:T(8,128)(2,1)S(1)} %get-tuple-element.38), channel_id=1, replica_groups=mesh['z'=4,'core'=2,'xh'=2,'xl'=2,'y'=4] {'xh','xl','z'}, dimensions={0} | all-to-all | bytes 1048576 | tf_op jit(solution)/shard_map/all_to_all | solution.py:414
  113.3 0.0 collective-permute-done.9.got
  113.3 0.0 collective-permute-done.15.near_1
  113.3 0.0 collective-permute-done.16.near_3
  113.3 0.9 shard_map.99
  114.3 13.3 %all_to_all.22.got = bf16[16,128,128]{2,1,0:T(8,128)(2,1)S(1)} all-to-all(bf16[16,128,128]{2,1,0:T(8,128)(2,1)S(1)} %get-tuple-element.40), channel_id=1, replica_groups=mesh['z'=4,'core'=2,'xh'=2,'xl'=2,'y'=4] {'xh','xl','z'}, dimensions={0} | all-to-all | bytes 1048576 | tf_op jit(solution)/shard_map/all_to_all | solution.py:414
  127.6 0.8 shard_map.100
  (12 shorter events, 0.1 us)
Async XLA Ops:
  0.6 24.5 %copy-start.4 = (s32[8192]{0:T(1024)S(1)}, s32[8192]{0:T(1024)}, u32[]{:S(2)}) copy-start(s32[8192]{0:T(1024)} %param.12) | copy-start | bytes 98308
  0.6 24.5 %copy-start.3 = (bf16[64,4096]{1,0:T(8,128)(2,1)S(1)}, bf16[64,4096]{1,0:T(8,128)(2,1)}, u32[]{:S(2)}) copy-start(bf16[64,4096]{1,0:T(8,128)(2,1)} %grads.1) | copy-start | bytes 1572868
  0.7 24.5 %copy-start.2 = (bf16[64,4096]{1,0:T(8,128)(2,1)S(1)}, bf16[64,4096]{1,0:T(8,128)(2,1)}, u32[]{:S(2)}) copy-start(bf16[64,4096]{1,0:T(8,128)(2,1)} %saved.1) | copy-start | bytes 1572868
  0.7 24.5 %copy-start.1 = (bf16[64,4096]{1,0:T(8,128)(2,1)S(1)}, bf16[64,4096]{1,0:T(8,128)(2,1)}, u32[]{:S(2)}) copy-start(bf16[64,4096]{1,0:T(8,128)(2,1)} %queries.1) | copy-start | bytes 1572868
  22.0 13.5 %collective-permute-start.1 = (bf16[16,128,128]{2,1,0:T(8,128)(2,1)S(1)}, bf16[16,128,128]{2,1,0:T(8,128)(2,1)S(1)}, u32[]{:S(2)}, u32[]{:S(2)}) collective-permute-start(bf16[16,128,128]{2,1,0:T(8,128)(2,1)S(1)} %all_to_all.20.after.refs_0_), channel_id=1, source_target_pairs={{0,3},{1,2},{2,1},{3,0},{4,7},{5,6},{6,5},{7,4},{8,11},{9,10},{10,... | collective-permute-start | bytes 1572872 | tf_op jit(solution)/shard_map/ppermute | solution.py:422
  25.0 13.1 %collective-permute-start = (bf16[16,128,128]{2,1,0:T(8,128)(2,1)S(1)}, bf16[16,128,128]{2,1,0:T(8,128)(2,1)S(1)}, u32[]{:S(2)}, u32[]{:S(2)}) collective-permute-start(bf16[16,128,128]{2,1,0:T(8,128)(2,1)S(1)} %all_to_all.20.after.refs_0_), channel_id=1, source_target_pairs={{0,1},{1,0},{2,3},{3,2},{4,5},{5,4},{6,7},{7,6},{8,9},{9,8},{10,11... | collective-permute-start | bytes 1572872 | tf_op jit(solution)/shard_map/ppermute | solution.py:422
  26.4 1.0 copy-start
  27.5 20.4 %copy-start.5 = (s32[32]{0:T(128)S(1)}, s32[32]{0:T(128)}, u32[]{:S(2)}) copy-start(s32[32]{0:T(128)} %order.1) | copy-start | bytes 388
  27.5 20.1 %all-to-all-start.1 = ((bf16[16,272,128]{2,1,0:T(8,128)(2,1)}), bf16[16,272,128]{2,1,0:T(8,128)(2,1)S(1)}, u32[]{:S(2)}, u32[]{:S(2)}) async-start(bf16[16,272,128]{2,1,0:T(8,128)(2,1)} %copy-done), calls=%async_computation.1 | async-start | bytes 2228224 | tf_op jit(solution)/shard_map/all_to_all | solution.py:414
  31.3 14.7 %collective-permute-start.4 = (bf16[16,128,128]{2,1,0:T(8,128)(2,1)S(1)}, bf16[16,128,128]{2,1,0:T(8,128)(2,1)S(1)}, u32[]{:S(2)}, u32[]{:S(2)}) collective-permute-start(bf16[16,128,128]{2,1,0:T(8,128)(2,1)S(1)} %all_to_all.20.after.refs_0_), channel_id=1, source_target_pairs={{0,16},{16,0},{1,17},{17,1},{2,18},{18,2},{3,19},{19,3},{4,20},{20... | collective-permute-start | bytes 1572872 | tf_op jit(solution)/shard_map/ppermute | solution.py:418
  35.5 7.1 %collective-permute-start.2 = (bf16[8,128,128]{2,1,0:T(8,128)(2,1)S(1)}, bf16[8,128,128]{2,1,0:T(8,128)(2,1)S(1)}, u32[]{:S(2)}, u32[]{:S(2)}) collective-permute-start(bf16[8,128,128]{2,1,0:T(8,128)(2,1)S(1)} %slice.8), channel_id=1, source_target_pairs={{0,1},{1,0},{2,3},{3,2},{4,5},{5,4},{6,7},{7,6},{8,9},{9,8},{10,11... | collective-permute-start | bytes 786440 | tf_op jit(solution)/shard_map/ppermute | solution.py:422
  35.9 11.7 %collective-permute-start.6 = (bf16[16,128,128]{2,1,0:T(8,128)(2,1)S(1)}, bf16[16,128,128]{2,1,0:T(8,128)(2,1)}, u32[]{:S(2)}, u32[]{:S(2)}) collective-permute-start(bf16[16,128,128]{2,1,0:T(8,128)(2,1)S(1)} %collective-permute-done.1.refs_2_), channel_id=1, source_target_pairs={{0,16},{16,0},{1,17},{17,1},{2,18},{18,2},{3,19},{19,3},{4,20},{20... | collective-permute-start | bytes 1572872 | tf_op jit(solution)/shard_map/ppermute | solution.py:418
  38.2 7.9 %collective-permute-start.3 = (bf16[8,128,128]{2,1,0:T(8,128)(2,1)S(1)}, bf16[8,128,128]{2,1,0:T(8,128)(2,1)}, u32[]{:S(2)}, u32[]{:S(2)}) collective-permute-start(bf16[8,128,128]{2,1,0:T(8,128)(2,1)S(1)} %slice.9), channel_id=1, source_target_pairs={{0,3},{1,2},{2,1},{3,0},{4,7},{5,6},{6,5},{7,4},{8,11},{9,10},{10,... | collective-permute-start | bytes 786440 | tf_op jit(solution)/shard_map/ppermute | solution.py:422
  38.8 9.2 %collective-permute-start.5 = (bf16[16,128,128]{2,1,0:T(8,128)(2,1)S(1)}, bf16[16,128,128]{2,1,0:T(8,128)(2,1)}, u32[]{:S(2)}, u32[]{:S(2)}) collective-permute-start(bf16[16,128,128]{2,1,0:T(8,128)(2,1)S(1)} %collective-permute-done.refs_1_), channel_id=1, source_target_pairs={{0,16},{16,0},{1,17},{17,1},{2,18},{18,2},{3,19},{19,3},{4,20},{20... | collective-permute-start | bytes 1572872 | tf_op jit(solution)/shard_map/ppermute | solution.py:418
  42.6 5.0 %collective-permute-start.7 = (bf16[8,128,128]{2,1,0:T(8,128)(2,1)S(1)}, bf16[8,128,128]{2,1,0:T(8,128)(2,1)}, u32[]{:S(2)}, u32[]{:S(2)}) collective-permute-start(bf16[8,128,128]{2,1,0:T(8,128)(2,1)S(1)} %collective-permute-done.2.refs_3_), channel_id=1, source_target_pairs={{0,16},{16,0},{1,17},{17,1},{2,18},{18,2},{3,19},{19,3},{4,20},{20... | collective-permute-start | bytes 786440 | tf_op jit(solution)/shard_map/ppermute | solution.py:418
  46.0 1.9 %collective-permute-start.8 = (bf16[8,128,128]{2,1,0:T(8,128)(2,1)}, bf16[8,128,128]{2,1,0:T(8,128)(2,1)}, u32[]{:S(2)}, u32[]{:S(2)}) collective-permute-start(bf16[8,128,128]{2,1,0:T(8,128)(2,1)} %collective-permute-done.3.refs_4_), channel_id=1, source_target_pairs={{0,16},{16,0},{1,17},{17,1},{2,18},{18,2},{3,19},{19,3},{4,20},{20... | collective-permute-start | bytes 786440 | tf_op jit(solution)/shard_map/ppermute | solution.py:418
  74.9 2.0 %collective-permute-start.12 = (bf16[16,128,128]{2,1,0:T(8,128)(2,1)S(1)}, bf16[16,128,128]{2,1,0:T(8,128)(2,1)S(1)}, u32[]{:S(2)}, u32[]{:S(2)}) collective-permute-start(bf16[16,128,128]{2,1,0:T(8,128)(2,1)S(1)} %get-tuple-element.33), channel_id=1, source_target_pairs={{0,16},{16,0},{1,17},{17,1},{2,18},{18,2},{3,19},{19,3},{4,20},{20... | collective-permute-start | bytes 1572872 | tf_op jit(solution)/shard_map/ppermute | solution.py:418
  75.1 14.5 %collective-permute-start.10 = (bf16[16,128,128]{2,1,0:T(8,128)(2,1)S(1)}, bf16[16,128,128]{2,1,0:T(8,128)(2,1)S(1)}, u32[]{:S(2)}, u32[]{:S(2)}) collective-permute-start(bf16[16,128,128]{2,1,0:T(8,128)(2,1)S(1)} %get-tuple-element.28), channel_id=1, source_target_pairs={{0,16},{16,0},{1,17},{17,1},{2,18},{18,2},{3,19},{19,3},{4,20},{20... | collective-permute-start | bytes 1572872 | tf_op jit(solution)/shard_map/ppermute | solution.py:418
  75.5 14.1 %collective-permute-start.11 = (bf16[16,128,128]{2,1,0:T(8,128)(2,1)S(1)}, bf16[16,128,128]{2,1,0:T(8,128)(2,1)S(1)}, u32[]{:S(2)}, u32[]{:S(2)}) collective-permute-start(bf16[16,128,128]{2,1,0:T(8,128)(2,1)S(1)} %get-tuple-element.30), channel_id=1, source_target_pairs={{0,16},{16,0},{1,17},{17,1},{2,18},{18,2},{3,19},{19,3},{4,20},{20... | collective-permute-start | bytes 1572872 | tf_op jit(solution)/shard_map/ppermute | solution.py:418
  77.0 12.6 %collective-permute-start.13 = (bf16[8,128,128]{2,1,0:T(8,128)(2,1)S(1)}, bf16[8,128,128]{2,1,0:T(8,128)(2,1)S(1)}, u32[]{:S(2)}, u32[]{:S(2)}) collective-permute-start(bf16[8,128,128]{2,1,0:T(8,128)(2,1)S(1)} %get-tuple-element.34), channel_id=1, source_target_pairs={{0,1},{1,0},{2,3},{3,2},{4,5},{5,4},{6,7},{7,6},{8,9},{9,8},{10,11... | collective-permute-start | bytes 786440 | tf_op jit(solution)/shard_map/ppermute | solution.py:422
  81.8 14.1 %collective-permute-start.14 = (bf16[8,128,128]{2,1,0:T(8,128)(2,1)S(1)}, bf16[8,128,128]{2,1,0:T(8,128)(2,1)S(1)}, u32[]{:S(2)}, u32[]{:S(2)}) collective-permute-start(bf16[8,128,128]{2,1,0:T(8,128)(2,1)S(1)} %get-tuple-element.35), channel_id=1, source_target_pairs={{0,3},{1,2},{2,1},{3,0},{4,7},{5,6},{6,5},{7,4},{8,11},{9,10},{10,... | collective-permute-start | bytes 786440 | tf_op jit(solution)/shard_map/ppermute | solution.py:422
  89.6 23.7 %collective-permute-start.9 = (bf16[16,128,128]{2,1,0:T(8,128)(2,1)S(1)}, bf16[16,128,128]{2,1,0:T(8,128)(2,1)S(1)}, u32[]{:S(2)}, u32[]{:S(2)}) collective-permute-start(bf16[16,128,128]{2,1,0:T(8,128)(2,1)S(1)} %get-tuple-element.26), channel_id=1, source_target_pairs={{0,16},{16,0},{1,17},{17,1},{2,18},{18,2},{3,19},{19,3},{4,20},{20... | collective-permute-start | bytes 1572872 | tf_op jit(solution)/shard_map/ppermute | solution.py:418
  96.2 17.1 %collective-permute-start.15 = (bf16[16,128,128]{2,1,0:T(8,128)(2,1)S(1)}, bf16[16,128,128]{2,1,0:T(8,128)(2,1)S(1)}, u32[]{:S(2)}, u32[]{:S(2)}) collective-permute-start(bf16[16,128,128]{2,1,0:T(8,128)(2,1)S(1)} %get-tuple-element.36), channel_id=1, source_target_pairs={{0,1},{1,0},{2,3},{3,2},{4,5},{5,4},{6,7},{7,6},{8,9},{9,8},{10,11... | collective-permute-start | bytes 1572872 | tf_op jit(solution)/shard_map/ppermute | solution.py:422
  96.3 17.0 %collective-permute-start.16 = (bf16[16,128,128]{2,1,0:T(8,128)(2,1)S(1)}, bf16[16,128,128]{2,1,0:T(8,128)(2,1)S(1)}, u32[]{:S(2)}, u32[]{:S(2)}) collective-permute-start(bf16[16,128,128]{2,1,0:T(8,128)(2,1)S(1)} %get-tuple-element.37), channel_id=1, source_target_pairs={{0,3},{1,2},{2,1},{3,0},{4,7},{5,6},{6,5},{7,4},{8,11},{9,10},{10,... | collective-permute-start | bytes 1572872 | tf_op jit(solution)/shard_map/ppermute | solution.py:422

commit v13 on v12

--- a/solution.py
+++ b/solution.py
@@ -17,8 +17,8 @@
 QR = G * HR
 C = 2 * QR
 NC = 8
-W = 8
-REST = 2
+WIDTHS = (8, 2)
+REST = WIDTHS[-1]
 SCALE = D**-0.5
 EXP_SCALE = SCALE * math.log2(math.e)
 HIDDEN = -1e30
@@ -243,21 +243,16 @@
             scores = jnp.where(key_positions(b) <= query_positions(c), scores, HIDDEN)
         return jnp.exp2(scores * EXP_SCALE)
 
-    def diagonal_step(i, carry):
-        chunks = [4 * i + k for k in range(4)]
-        found = []
-        for c in chunks:
-            b = full_blocks(c)
-            scores = jnp.where(seen(c, b), raw_scores(c, b), HIDDEN)
-            top = jnp.max(scores, axis=0, keepdims=True).astype(BF16).astype(F32)
-            found.append((top, add_up(jnp.exp2((scores - top) * EXP_SCALE))))
-        for c, (top, total) in zip(chunks, found):
-            put_shift(c, -top)
-            m_s[c] = top * EXP_SCALE
-            l_s[c] = total
-        return carry
-
-    lax.fori_loop(0, NC // 4, diagonal_step, 0)
+    found = []
+    for c in range(NC):
+        b = full_blocks(c)
+        scores = jnp.where(seen(c, b), raw_scores(c, b), HIDDEN)
+        top = jnp.max(scores, axis=0, keepdims=True).astype(BF16).astype(F32)
+        found.append((top, add_up(jnp.exp2((scores - top) * EXP_SCALE))))
+    for c, (top, total) in enumerate(found):
+        put_shift(c, -top)
+        m_s[c] = top * EXP_SCALE
+        l_s[c] = total
 
     def add_weights(items, masked):
         parts = [add_up(weights_of(c, b, masked)) for c, b in items]
@@ -265,17 +260,18 @@
             l_s[c] += part
 
     def each_plain(step):
-        def wide(i, carry):
-            step([(plain_c[n], plain_b[n]) for n in [W * i + k for k in range(W)]], False)
-            return carry
-
-        def narrow(i, carry):
-            step([(plain_c[n], plain_b[n]) for n in [REST * i + k for k in range(REST)]], False)
-            return carry
-
-        n_wide = n_plain // W
-        lax.fori_loop(0, n_wide, wide, 0)
-        lax.fori_loop(n_wide * (W // REST), (n_plain + (REST - 1)) // REST, narrow, 0)
+        done = jnp.int32(0)
+        for width in WIDTHS:
+
+            def some(i, carry, width=width, done=done):
+                at = [done + width * i + k for k in range(width)]
+                step([(plain_c[n], plain_b[n]) for n in at], False)
+                return carry
+
+            left = n_plain - done
+            count = (left + (REST - 1)) // width if width == REST else left // width
+            lax.fori_loop(0, count, some, 0)
+            done = done + count * width
 
     each_plain(add_weights)
 
@@ -330,11 +326,7 @@
                 ref[pl.ds(2 * b, 2)] += term.reshape(2, 2, 2, R, D)
             dq_s[c] += jnp.dot(kt_s[b], score_grad, preferred_element_type=F32)
 
-    def diagonal_grads(i, carry):
-        grad_step([(c, full_blocks(c)) for c in [4 * i + k for k in range(4)]], True)
-        return carry
-
-    lax.fori_loop(0, NC // 4, diagonal_grads, 0)
+    grad_step([(c, full_blocks(c)) for c in range(NC)], True)
     each_plain(grad_step)
 
     def finish(c, carry):
@@ -452,8 +444,8 @@
         out_shape=[bf16(16, QR, D)] + [group] * 3 + [half] * 2 + [group] * 4,
         in_specs=[IN_SMEM] * 2 + [ANYWHERE] * 11,
         scratch_shapes=[
-            pltpu.SMEM((NC * NT // 2 + W,), jnp.int32),
-            pltpu.SMEM((NC * NT // 2 + W,), jnp.int32),
+            pltpu.SMEM((NC * NT // 2 + REST,), jnp.int32),
+            pltpu.SMEM((NC * NT // 2 + REST,), jnp.int32),
             pltpu.VMEM((NC + 1, C, D), BF16),
             pltpu.VMEM((NC + 1, C, D), BF16),
             pltpu.VMEM((16, 16, D), BF16),
@@ -470,7 +462,7 @@
             pltpu.SemaphoreType.DMA,
             pltpu.SemaphoreType.DMA,
         ],
-        compiler_params=pltpu.CompilerParams(vmem_limit_bytes=34 << 20),
+        compiler_params=pltpu.CompilerParams(vmem_limit_bytes=40 << 20),
     )(span_order, counts, qpay, *mine, *[flip(array) for array in mine])
     far_sum_a, far_sum_b = on_vmem(far_sum_kernel, [half, half], sum_a, sum_b, flip(far_give))
     from_1 = swap(far_sum_a, 1)

time: 130 us -> 125 us (0.962)
  starting transfers between devices: 24.7 us -> 11.8 us
  Pallas kernels: 32.2 us -> 37.8 us
  waiting for transfers between devices: 22.8 us -> 25.8 us
    ppermute x8, starting transfers between devices: 19.8 us -> 6.91 us  [swap(): return lax.ppermute(array, 'y', [(i, i ^ distance) for i in range(4)])]
    pallas_call x1, Pallas kernels: 27 us -> 32.5 us  [body(): pl.pallas_call(attention_kernel, out_shape=[bf16(16, QR, D)] + [group] *...]
    ppermute x8, waiting for transfers between devices: 19.7 us -> 22.7 us  [swap(): return lax.ppermute(array, 'y', [(i, i ^ distance) for i in range(4)])]
  transfers between devices with their start and end apart: 18 -> 18, of which waited for: 8 -> 9; matrix products, arithmetic and copies ran while one was open for 0% -> 0% of each run, Pallas kernels for 1% -> 1%
where the time goes in v13:
time: 125 us; the launch traced here: 124 us
  blocking collectives  46.9 us (38%)
  Pallas kernels  37.8 us (30%)
  waiting for transfers between devices  25.8 us (21%)
  starting transfers between devices  11.8 us (9%)
    all_to_all x3, blocking collectives, exchange(): lax.all_to_all(array, SPREAD, split_axis=0, concat_axis=0, tiled=True)  46.9 us
    pallas_call x1, Pallas kernels, body(): pl.pallas_call(attention_kernel, out_shape=[bf16(16, QR, D)] + [group] *...  32.5 us
    ppermute x8, waiting for transfers between devices, swap(): return lax.ppermute(array, 'y', [(i, i ^ distance) for i in range(4)])  22.7 us
    ppermute x8, starting transfers between devices, swap(): return lax.ppermute(array, 'y', [(i, i ^ distance) for i in range(4)])  6.91 us
    all_to_all x1, starting transfers between devices, exchange(): lax.all_to_all(array, SPREAD, split_axis=0, concat_axis=0, tiled=True)  3.83 us
  transfers between devices with their start and end apart: 18, of which 9 were waited for; matrix products, arithmetic and copies ran while one was open for 0% of the time, Pallas kernels for 1%

profile of v13, /device:TPU:0, one launch (start us, length us, event | category | flops | bytes accessed | tf_op | source)
XLA Modules:
  0.0 124.1 jit_solution(5891654296680291633)
XLA Ops:
  0.7 1.9 %shard_map.94 = bf16[16,128,128]{2,1,0:T(8,128)(2,1)} custom-call(bf16[64,1024]{1,0:T(8,128)(2,1)} %keys.1, bf16[64,1024]{1,0:T(8,128)(2,1)} %values.1), custom_call_target="tpu_custom_call" | custom-call | tf_op jit(solution)/shard_map/pallas_call | solution.py:418
  2.5 19.5 %all_to_all.20.after.refs_0_ = bf16[16,128,128]{2,1,0:T(8,128)(2,1)S(1)} all-to-all(bf16[16,128,128]{2,1,0:T(8,128)(2,1)} %shard_map.94), channel_id=1, replica_groups=mesh['z'=4,'core'=2,'xh'=2,'xl'=2,'y'=4] {'xh','xl','z'}, dimensions={0} | all-to-all | bytes 1048576 | tf_op jit(solution)/shard_map/all_to_all | solution.py:406
  22.0 3.0 %collective-permute-start.1 = (bf16[16,128,128]{2,1,0:T(8,128)(2,1)S(1)}, bf16[16,128,128]{2,1,0:T(8,128)(2,1)S(1)}, u32[]{:S(2)}, u32[]{:S(2)}) collective-permute-start(bf16[16,128,128]{2,1,0:T(8,128)(2,1)S(1)} %all_to_all.20.after.refs_0_), channel_id=1, source_target_pairs={{0,3},{1,2},{2,1},{3,0},{4,7},{5,6},{6,5},{7,4},{8,11},{9,10},{10,... | collective-permute-start | bytes 1572872 | tf_op jit(solution)/shard_map/ppermute | solution.py:414
  25.0 0.1 collective-permute-start
  25.2 0.0 copy-done.3
  25.2 1.3 %shard_map.95 = (bf16[16,272,128]{2,1,0:T(8,128)(2,1)S(1)}, s32[2]{0:T(128)S(1)}) custom-call(bf16[64,4096]{1,0:T(8,128)(2,1)S(1)} %copy-done.1, bf16[64,4096]{1,0:T(8,128)(2,1)S(1)} %copy-done.2, bf16[64,4096]{1,0:T(8,128)(2,1)S(1)} %copy-done.3, s32[64,128]{1,0:T(8,128)S(1)} %bitcast.1, bf16[16,128,128]{2,1,0:T(8,128)(2,1)S(1)} %all_to_all.20.after.refs_0_), custom_call_target="tpu_custom_call" | custom-call | tf_op jit(solution)/shard_map/pallas_call | solution.py:426
  26.4 1.0 copy-done
  27.5 3.8 %all-to-all-start.1 = ((bf16[16,272,128]{2,1,0:T(8,128)(2,1)}), bf16[16,272,128]{2,1,0:T(8,128)(2,1)S(1)}, u32[]{:S(2)}, u32[]{:S(2)}) async-start(bf16[16,272,128]{2,1,0:T(8,128)(2,1)} %copy-done), calls=%async_computation.1 | async-start | bytes 2228224 | tf_op jit(solution)/shard_map/all_to_all | solution.py:406
  31.3 0.1 collective-permute-start.4
  31.4 4.1 %collective-permute-done.1.refs_2_ = bf16[16,128,128]{2,1,0:T(8,128)(2,1)S(1)} collective-permute-done((bf16[16,128,128]{2,1,0:T(8,128)(2,1)S(1)}, bf16[16,128,128]{2,1,0:T(8,128)(2,1)S(1)}, u32[]{:S(2)}, u32[]{:S(2)}) %collective-permute-start.1) | collective-permute-done | bytes 524320 | tf_op jit(solution)/shard_map/ppermute | solution.py:414
  35.5 0.4 collective-permute-start.2
  35.9 0.0 collective-permute-start.6
  35.9 2.2 %collective-permute-done.refs_1_ = bf16[16,128,128]{2,1,0:T(8,128)(2,1)S(1)} collective-permute-done((bf16[16,128,128]{2,1,0:T(8,128)(2,1)S(1)}, bf16[16,128,128]{2,1,0:T(8,128)(2,1)S(1)}, u32[]{:S(2)}, u32[]{:S(2)}) %collective-permute-start) | collective-permute-done | bytes 524320 | tf_op jit(solution)/shard_map/ppermute | solution.py:414
  38.2 0.6 collective-permute-start.3
  38.8 0.2 collective-permute-start.5
  39.0 3.6 %collective-permute-done.2.refs_3_ = bf16[8,128,128]{2,1,0:T(8,128)(2,1)S(1)} collective-permute-done((bf16[8,128,128]{2,1,0:T(8,128)(2,1)S(1)}, bf16[8,128,128]{2,1,0:T(8,128)(2,1)S(1)}, u32[]{:S(2)}, u32[]{:S(2)}) %collective-permute-start.2) | collective-permute-done | bytes 262176 | tf_op jit(solution)/shard_map/ppermute | solution.py:414
  42.6 0.0 collective-permute-start.7
  42.6 3.5 %collective-permute-done.3.refs_4_ = bf16[8,128,128]{2,1,0:T(8,128)(2,1)} collective-permute-done((bf16[8,128,128]{2,1,0:T(8,128)(2,1)S(1)}, bf16[8,128,128]{2,1,0:T(8,128)(2,1)}, u32[]{:S(2)}, u32[]{:S(2)}) %collective-permute-start.3) | collective-permute-done | bytes 262176 | tf_op jit(solution)/shard_map/ppermute | solution.py:414
  46.0 0.0 collective-permute-start.8
  46.0 0.0 collective-permute-done.4.refs_5_
  46.0 1.5 %all-to-all-done.1.qpay = bf16[16,272,128]{2,1,0:T(8,128)(2,1)S(1)} async-done(((bf16[16,272,128]{2,1,0:T(8,128)(2,1)}), bf16[16,272,128]{2,1,0:T(8,128)(2,1)S(1)}, u32[]{:S(2)}, u32[]{:S(2)}) %all-to-all-start.1) | async-done | bytes 1114144 | tf_op jit(solution)/shard_map/all_to_all | solution.py:406
  47.6 0.0 collective-permute-done.7.refs_8_
  47.6 0.0 collective-permute-done.6.refs_7_
  47.6 0.3 collective-permute-done.8.refs_9_
  47.9 0.0 collective-permute-done.5.refs_6_
  47.9 32.5 %shard_map.96 = (bf16[16,128,128]{2,1,0:T(8,128)(2,1)S(1)}, bf16[16,128,128]{2,1,0:T(8,128)(2,1)S(1)}, bf16[16,128,128]{2,1,0:T(8,128)(2,1)S(1)}, bf16[16,128,12...) custom-call(s32[32]{0:T(128)S(1)} %copy-done.5, ...), custom_call_target="tpu_custom_call" | custom-call | tf_op jit(solution)/shard_map/pallas_call | solution.py:442
  80.5 0.2 collective-permute-start.12
  80.7 0.4 collective-permute-start.10
  81.0 0.1 collective-permute-start.11
  81.2 1.3 %collective-permute-done.12.got = bf16[16,128,128]{2,1,0:T(8,128)(2,1)S(1)} collective-permute-done((bf16[16,128,128]{2,1,0:T(8,128)(2,1)S(1)}, bf16[16,128,128]{2,1,0:T(8,128)(2,1)S(1)}, u32[]{:S(2)}, u32[]{:S(2)}) %collective-permute-start.12) | collective-permute-done | bytes 524320 | tf_op jit(solution)/shard_map/ppermute | solution.py:410
  82.4 0.1 shard_map.97
  82.6 2.3 %collective-permute-start.13 = (bf16[8,128,128]{2,1,0:T(8,128)(2,1)S(1)}, bf16[8,128,128]{2,1,0:T(8,128)(2,1)S(1)}, u32[]{:S(2)}, u32[]{:S(2)}) collective-permute-start(bf16[8,128,128]{2,1,0:T(8,128)(2,1)S(1)} %get-tuple-element.34), channel_id=1, source_target_pairs={{0,1},{1,0},{2,3},{3,2},{4,5},{5,4},{6,7},{7,6},{8,9},{9,8},{10,11... | collective-permute-start | bytes 786440 | tf_op jit(solution)/shard_map/ppermute | solution.py:414
  84.9 0.0 collective-permute-start.14
  84.9 0.0 collective-permute-start.9
  84.9 0.0 collective-permute-done.10.got_1
  84.9 0.0 collective-permute-done.11.got_3
  84.9 6.6 %collective-permute-done.13.from_1 = bf16[8,128,128]{2,1,0:T(8,128)(2,1)S(1)} collective-permute-done((bf16[8,128,128]{2,1,0:T(8,128)(2,1)S(1)}, bf16[8,128,128]{2,1,0:T(8,128)(2,1)S(1)}, u32[]{:S(2)}, u32[]{:S(2)}) %collective-permute-start.13) | collective-permute-done | bytes 262176 | tf_op jit(solution)/shard_map/ppermute | solution.py:414
  91.5 2.7 %collective-permute-done.14.from_3 = bf16[8,128,128]{2,1,0:T(8,128)(2,1)S(1)} collective-permute-done((bf16[8,128,128]{2,1,0:T(8,128)(2,1)S(1)}, bf16[8,128,128]{2,1,0:T(8,128)(2,1)S(1)}, u32[]{:S(2)}, u32[]{:S(2)}) %collective-permute-start.14) | collective-permute-done | bytes 262176 | tf_op jit(solution)/shard_map/ppermute | solution.py:414
  94.2 0.3 shard_map.98
  94.5 0.1 collective-permute-start.15
  94.6 0.4 collective-permute-start.16
  94.9 14.1 %all_to_all.21.dq = bf16[16,128,128]{2,1,0:T(8,128)(2,1)S(1)} all-to-all(bf16[16,128,128]{2,1,0:T(8,128)(2,1)S(1)} %get-tuple-element.38), channel_id=1, replica_groups=mesh['z'=4,'core'=2,'xh'=2,'xl'=2,'y'=4] {'xh','xl','z'}, dimensions={0} | all-to-all | bytes 1048576 | tf_op jit(solution)/shard_map/all_to_all | solution.py:406
  109.0 0.0 collective-permute-done.9.got
  109.0 0.0 collective-permute-done.15.near_1
  109.0 0.0 collective-permute-done.16.near_3
  109.0 0.9 shard_map.99
  109.9 13.3 %all_to_all.22.got = bf16[16,128,128]{2,1,0:T(8,128)(2,1)S(1)} all-to-all(bf16[16,128,128]{2,1,0:T(8,128)(2,1)S(1)} %get-tuple-element.40), channel_id=1, replica_groups=mesh['z'=4,'core'=2,'xh'=2,'xl'=2,'y'=4] {'xh','xl','z'}, dimensions={0} | all-to-all | bytes 1048576 | tf_op jit(solution)/shard_map/all_to_all | solution.py:406
  123.3 0.8 shard_map.100
  (12 shorter events, 0.1 us)
Async XLA Ops:
  0.6 24.5 %copy-start.4 = (s32[8192]{0:T(1024)S(1)}, s32[8192]{0:T(1024)}, u32[]{:S(2)}) copy-start(s32[8192]{0:T(1024)} %param.12) | copy-start | bytes 98308
  0.6 24.5 %copy-start.3 = (bf16[64,4096]{1,0:T(8,128)(2,1)S(1)}, bf16[64,4096]{1,0:T(8,128)(2,1)}, u32[]{:S(2)}) copy-start(bf16[64,4096]{1,0:T(8,128)(2,1)} %grads.1) | copy-start | bytes 1572868
  0.7 24.5 %copy-start.2 = (bf16[64,4096]{1,0:T(8,128)(2,1)S(1)}, bf16[64,4096]{1,0:T(8,128)(2,1)}, u32[]{:S(2)}) copy-start(bf16[64,4096]{1,0:T(8,128)(2,1)} %saved.1) | copy-start | bytes 1572868
  0.7 24.5 %copy-start.1 = (bf16[64,4096]{1,0:T(8,128)(2,1)S(1)}, bf16[64,4096]{1,0:T(8,128)(2,1)}, u32[]{:S(2)}) copy-start(bf16[64,4096]{1,0:T(8,128)(2,1)} %queries.1) | copy-start | bytes 1572868
  22.0 13.5 %collective-permute-start.1 = (bf16[16,128,128]{2,1,0:T(8,128)(2,1)S(1)}, bf16[16,128,128]{2,1,0:T(8,128)(2,1)S(1)}, u32[]{:S(2)}, u32[]{:S(2)}) collective-permute-start(bf16[16,128,128]{2,1,0:T(8,128)(2,1)S(1)} %all_to_all.20.after.refs_0_), channel_id=1, source_target_pairs={{0,3},{1,2},{2,1},{3,0},{4,7},{5,6},{6,5},{7,4},{8,11},{9,10},{10,... | collective-permute-start | bytes 1572872 | tf_op jit(solution)/shard_map/ppermute | solution.py:414
  25.0 13.1 %collective-permute-start = (bf16[16,128,128]{2,1,0:T(8,128)(2,1)S(1)}, bf16[16,128,128]{2,1,0:T(8,128)(2,1)S(1)}, u32[]{:S(2)}, u32[]{:S(2)}) collective-permute-start(bf16[16,128,128]{2,1,0:T(8,128)(2,1)S(1)} %all_to_all.20.after.refs_0_), channel_id=1, source_target_pairs={{0,1},{1,0},{2,3},{3,2},{4,5},{5,4},{6,7},{7,6},{8,9},{9,8},{10,11... | collective-permute-start | bytes 1572872 | tf_op jit(solution)/shard_map/ppermute | solution.py:414
  26.4 1.0 copy-start
  27.5 20.4 %copy-start.5 = (s32[32]{0:T(128)S(1)}, s32[32]{0:T(128)}, u32[]{:S(2)}) copy-start(s32[32]{0:T(128)} %order.1) | copy-start | bytes 388
  27.5 20.1 %all-to-all-start.1 = ((bf16[16,272,128]{2,1,0:T(8,128)(2,1)}), bf16[16,272,128]{2,1,0:T(8,128)(2,1)S(1)}, u32[]{:S(2)}, u32[]{:S(2)}) async-start(bf16[16,272,128]{2,1,0:T(8,128)(2,1)} %copy-done), calls=%async_computation.1 | async-start | bytes 2228224 | tf_op jit(solution)/shard_map/all_to_all | solution.py:406
  31.3 14.7 %collective-permute-start.4 = (bf16[16,128,128]{2,1,0:T(8,128)(2,1)S(1)}, bf16[16,128,128]{2,1,0:T(8,128)(2,1)S(1)}, u32[]{:S(2)}, u32[]{:S(2)}) collective-permute-start(bf16[16,128,128]{2,1,0:T(8,128)(2,1)S(1)} %all_to_all.20.after.refs_0_), channel_id=1, source_target_pairs={{0,16},{16,0},{1,17},{17,1},{2,18},{18,2},{3,19},{19,3},{4,20},{20... | collective-permute-start | bytes 1572872 | tf_op jit(solution)/shard_map/ppermute | solution.py:410
  35.5 7.1 %collective-permute-start.2 = (bf16[8,128,128]{2,1,0:T(8,128)(2,1)S(1)}, bf16[8,128,128]{2,1,0:T(8,128)(2,1)S(1)}, u32[]{:S(2)}, u32[]{:S(2)}) collective-permute-start(bf16[8,128,128]{2,1,0:T(8,128)(2,1)S(1)} %slice.8), channel_id=1, source_target_pairs={{0,1},{1,0},{2,3},{3,2},{4,5},{5,4},{6,7},{7,6},{8,9},{9,8},{10,11... | collective-permute-start | bytes 786440 | tf_op jit(solution)/shard_map/ppermute | solution.py:414
  35.9 11.7 %collective-permute-start.6 = (bf16[16,128,128]{2,1,0:T(8,128)(2,1)S(1)}, bf16[16,128,128]{2,1,0:T(8,128)(2,1)}, u32[]{:S(2)}, u32[]{:S(2)}) collective-permute-start(bf16[16,128,128]{2,1,0:T(8,128)(2,1)S(1)} %collective-permute-done.1.refs_2_), channel_id=1, source_target_pairs={{0,16},{16,0},{1,17},{17,1},{2,18},{18,2},{3,19},{19,3},{4,20},{20... | collective-permute-start | bytes 1572872 | tf_op jit(solution)/shard_map/ppermute | solution.py:410
  38.2 7.9 %collective-permute-start.3 = (bf16[8,128,128]{2,1,0:T(8,128)(2,1)S(1)}, bf16[8,128,128]{2,1,0:T(8,128)(2,1)}, u32[]{:S(2)}, u32[]{:S(2)}) collective-permute-start(bf16[8,128,128]{2,1,0:T(8,128)(2,1)S(1)} %slice.9), channel_id=1, source_target_pairs={{0,3},{1,2},{2,1},{3,0},{4,7},{5,6},{6,5},{7,4},{8,11},{9,10},{10,... | collective-permute-start | bytes 786440 | tf_op jit(solution)/shard_map/ppermute | solution.py:414
  38.8 9.2 %collective-permute-start.5 = (bf16[16,128,128]{2,1,0:T(8,128)(2,1)S(1)}, bf16[16,128,128]{2,1,0:T(8,128)(2,1)}, u32[]{:S(2)}, u32[]{:S(2)}) collective-permute-start(bf16[16,128,128]{2,1,0:T(8,128)(2,1)S(1)} %collective-permute-done.refs_1_), channel_id=1, source_target_pairs={{0,16},{16,0},{1,17},{17,1},{2,18},{18,2},{3,19},{19,3},{4,20},{20... | collective-permute-start | bytes 1572872 | tf_op jit(solution)/shard_map/ppermute | solution.py:410
  42.6 5.0 %collective-permute-start.7 = (bf16[8,128,128]{2,1,0:T(8,128)(2,1)S(1)}, bf16[8,128,128]{2,1,0:T(8,128)(2,1)}, u32[]{:S(2)}, u32[]{:S(2)}) collective-permute-start(bf16[8,128,128]{2,1,0:T(8,128)(2,1)S(1)} %collective-permute-done.2.refs_3_), channel_id=1, source_target_pairs={{0,16},{16,0},{1,17},{17,1},{2,18},{18,2},{3,19},{19,3},{4,20},{20... | collective-permute-start | bytes 786440 | tf_op jit(solution)/shard_map/ppermute | solution.py:410
  46.0 1.9 %collective-permute-start.8 = (bf16[8,128,128]{2,1,0:T(8,128)(2,1)}, bf16[8,128,128]{2,1,0:T(8,128)(2,1)}, u32[]{:S(2)}, u32[]{:S(2)}) collective-permute-start(bf16[8,128,128]{2,1,0:T(8,128)(2,1)} %collective-permute-done.3.refs_4_), channel_id=1, source_target_pairs={{0,16},{16,0},{1,17},{17,1},{2,18},{18,2},{3,19},{19,3},{4,20},{20... | collective-permute-start | bytes 786440 | tf_op jit(solution)/shard_map/ppermute | solution.py:410
  80.5 2.0 %collective-permute-start.12 = (bf16[16,128,128]{2,1,0:T(8,128)(2,1)S(1)}, bf16[16,128,128]{2,1,0:T(8,128)(2,1)S(1)}, u32[]{:S(2)}, u32[]{:S(2)}) collective-permute-start(bf16[16,128,128]{2,1,0:T(8,128)(2,1)S(1)} %get-tuple-element.33), channel_id=1, source_target_pairs={{0,16},{16,0},{1,17},{17,1},{2,18},{18,2},{3,19},{19,3},{4,20},{20... | collective-permute-start | bytes 1572872 | tf_op jit(solution)/shard_map/ppermute | solution.py:410
  80.7 4.2 %collective-permute-start.10 = (bf16[16,128,128]{2,1,0:T(8,128)(2,1)S(1)}, bf16[16,128,128]{2,1,0:T(8,128)(2,1)S(1)}, u32[]{:S(2)}, u32[]{:S(2)}) collective-permute-start(bf16[16,128,128]{2,1,0:T(8,128)(2,1)S(1)} %get-tuple-element.28), channel_id=1, source_target_pairs={{0,16},{16,0},{1,17},{17,1},{2,18},{18,2},{3,19},{19,3},{4,20},{20... | collective-permute-start | bytes 1572872 | tf_op jit(solution)/shard_map/ppermute | solution.py:410
  81.0 3.9 %collective-permute-start.11 = (bf16[16,128,128]{2,1,0:T(8,128)(2,1)S(1)}, bf16[16,128,128]{2,1,0:T(8,128)(2,1)S(1)}, u32[]{:S(2)}, u32[]{:S(2)}) collective-permute-start(bf16[16,128,128]{2,1,0:T(8,128)(2,1)S(1)} %get-tuple-element.30), channel_id=1, source_target_pairs={{0,16},{16,0},{1,17},{17,1},{2,18},{18,2},{3,19},{19,3},{4,20},{20... | collective-permute-start | bytes 1572872 | tf_op jit(solution)/shard_map/ppermute | solution.py:410
  82.6 8.9 %collective-permute-start.13 = (bf16[8,128,128]{2,1,0:T(8,128)(2,1)S(1)}, bf16[8,128,128]{2,1,0:T(8,128)(2,1)S(1)}, u32[]{:S(2)}, u32[]{:S(2)}) collective-permute-start(bf16[8,128,128]{2,1,0:T(8,128)(2,1)S(1)} %get-tuple-element.34), channel_id=1, source_target_pairs={{0,1},{1,0},{2,3},{3,2},{4,5},{5,4},{6,7},{7,6},{8,9},{9,8},{10,11... | collective-permute-start | bytes 786440 | tf_op jit(solution)/shard_map/ppermute | solution.py:414
  84.9 9.3 %collective-permute-start.14 = (bf16[8,128,128]{2,1,0:T(8,128)(2,1)S(1)}, bf16[8,128,128]{2,1,0:T(8,128)(2,1)S(1)}, u32[]{:S(2)}, u32[]{:S(2)}) collective-permute-start(bf16[8,128,128]{2,1,0:T(8,128)(2,1)S(1)} %get-tuple-element.35), channel_id=1, source_target_pairs={{0,3},{1,2},{2,1},{3,0},{4,7},{5,6},{6,5},{7,4},{8,11},{9,10},{10,... | collective-permute-start | bytes 786440 | tf_op jit(solution)/shard_map/ppermute | solution.py:414
  84.9 24.1 %collective-permute-start.9 = (bf16[16,128,128]{2,1,0:T(8,128)(2,1)S(1)}, bf16[16,128,128]{2,1,0:T(8,128)(2,1)S(1)}, u32[]{:S(2)}, u32[]{:S(2)}) collective-permute-start(bf16[16,128,128]{2,1,0:T(8,128)(2,1)S(1)} %get-tuple-element.26), channel_id=1, source_target_pairs={{0,16},{16,0},{1,17},{17,1},{2,18},{18,2},{3,19},{19,3},{4,20},{20... | collective-permute-start | bytes 1572872 | tf_op jit(solution)/shard_map/ppermute | solution.py:410
  94.5 14.5 %collective-permute-start.15 = (bf16[16,128,128]{2,1,0:T(8,128)(2,1)S(1)}, bf16[16,128,128]{2,1,0:T(8,128)(2,1)S(1)}, u32[]{:S(2)}, u32[]{:S(2)}) collective-permute-start(bf16[16,128,128]{2,1,0:T(8,128)(2,1)S(1)} %get-tuple-element.36), channel_id=1, source_target_pairs={{0,1},{1,0},{2,3},{3,2},{4,5},{5,4},{6,7},{7,6},{8,9},{9,8},{10,11... | collective-permute-start | bytes 1572872 | tf_op jit(solution)/shard_map/ppermute | solution.py:414
  94.6 14.4 %collective-permute-start.16 = (bf16[16,128,128]{2,1,0:T(8,128)(2,1)S(1)}, bf16[16,128,128]{2,1,0:T(8,128)(2,1)S(1)}, u32[]{:S(2)}, u32[]{:S(2)}) collective-permute-start(bf16[16,128,128]{2,1,0:T(8,128)(2,1)S(1)} %get-tuple-element.37), channel_id=1, source_target_pairs={{0,3},{1,2},{2,1},{3,0},{4,7},{5,6},{6,5},{7,4},{8,11},{9,10},{10,... | collective-permute-start | bytes 1572872 | tf_op jit(solution)/shard_map/ppermute | solution.py:414

commit v14 on v13

--- a/solution.py
+++ b/solution.py
@@ -17,8 +17,9 @@
 QR = G * HR
 C = 2 * QR
 NC = 8
-WIDTHS = (8, 2)
-REST = WIDTHS[-1]
+REST = 2
+STATS_WIDTHS = (16, 4, REST)
+GRAD_WIDTHS = (8, 4, REST)
 SCALE = D**-0.5
 EXP_SCALE = SCALE * math.log2(math.e)
 HIDDEN = -1e30
@@ -56,10 +57,11 @@
         copy.wait()
 
 
-def pack_q_kernel(queries, saved, grads, segment, after, out, counts):
+def pack_q_kernel(queries, saved, grads, segment, after, packed, counts, out, sem):
     del after
     counts[0] = jnp.sum((segment[...] == 0).astype(jnp.int32))
     counts[1] = jnp.sum((segment[...] != 2).astype(jnp.int32))
+    copies = []
     ones = jnp.ones((8, D), BF16)
     row = lax.broadcasted_iota(jnp.int32, (16, D), 0)
     for g in range(8):
@@ -81,6 +83,10 @@
             both = jnp.concatenate([dot, dot], axis=0)
             rounded = both.astype(BF16).astype(F32)
             out[dest, 2 * QR :] = jnp.where(row == 0, rounded, both - rounded).astype(BF16)
+            copies.append(pltpu.make_async_copy(out.at[dest], packed.at[dest], sem))
+            copies[-1].start()
+    for copy in copies:
+        copy.wait()
 
 
 def span_id(xh, xl, y, zh):
@@ -259,9 +265,9 @@
         for (c, b), part in zip(items, parts):
             l_s[c] += part
 
-    def each_plain(step):
+    def each_plain(step, widths):
         done = jnp.int32(0)
-        for width in WIDTHS:
+        for width in widths:
 
             def some(i, carry, width=width, done=done):
                 at = [done + width * i + k for k in range(width)]
@@ -273,7 +279,7 @@
             lax.fori_loop(0, count, some, 0)
             done = done + count * width
 
-    each_plain(add_weights)
+    each_plain(add_weights, STATS_WIDTHS)
 
     @pl.when(jnp.logical_not(jnp.max(l_s[...]) < LARGE))
     def _():
@@ -327,7 +333,7 @@
             dq_s[c] += jnp.dot(kt_s[b], score_grad, preferred_element_type=F32)
 
     grad_step([(c, full_blocks(c)) for c in range(NC)], True)
-    each_plain(grad_step)
+    each_plain(grad_step, GRAD_WIDTHS)
 
     def finish(c, carry):
         dq = (dq_s[c] * SCALE).T.astype(BF16)
@@ -427,7 +433,8 @@
         pack_q_kernel,
         out_shape=[bf16(16, 2 * QR + 16, D), jax.ShapeDtypeStruct((2,), jnp.int32)],
         in_specs=[IN_VMEM] * 4 + [ANYWHERE],
-        out_specs=[IN_VMEM, IN_SMEM],
+        out_specs=[pl.BlockSpec(memory_space=pltpu.HBM), IN_SMEM],
+        scratch_shapes=[pltpu.VMEM((16, 2 * QR + 16, D), BF16), pltpu.SemaphoreType.DMA],
         compiler_params=pltpu.CompilerParams(vmem_limit_bytes=16 << 20),
     )(queries, attn_out, out_grad, segment.reshape(64, 128), own)
     qpay = exchange(q_packed)

time: 125 us -> 130 us (1.040)
  starting transfers between devices: 11.8 us -> 20.2 us
  waiting for transfers between devices: 25.8 us -> 20.8 us
  Pallas kernels: 37.8 us -> 39.7 us
    ppermute x8, starting transfers between devices: 6.91 us -> 15.2 us  [swap(): return lax.ppermute(array, 'y', [(i, i ^ distance) for i in range(4)])]
    ppermute x8, waiting for transfers between devices: 22.7 us -> 15.4 us  [swap(): return lax.ppermute(array, 'y', [(i, i ^ distance) for i in range(4)])]
    pallas_call x1, Pallas kernels: 1.25 us -> 4.72 us  [body(): pl.pallas_call(pack_q_kernel, out_shape=[bf16(16, 2 * QR + 16, D), jax.Sh...]
    all_to_all x1, waiting for transfers between devices: 1.52 us -> 4 us  [exchange(): lax.all_to_all(array, SPREAD, split_axis=0, concat_axis=0, tiled=True)]
    pallas_call x1, Pallas kernels: 32.5 us -> 31 us  [body(): pl.pallas_call(attention_kernel, out_shape=[bf16(16, QR, D)] + [group] *...]
  transfers between devices with their start and end apart: 18 -> 18, of which waited for: 9 -> 7; matrix products, arithmetic and copies ran while one was open for 0% -> 0% of each run, Pallas kernels for 1% -> 4%
where the time goes in v14:
time: 130 us; the launch traced here: 129 us
  blocking collectives  46.5 us (36%)
  Pallas kernels  39.7 us (31%)
  waiting for transfers between devices  20.8 us (16%)
  starting transfers between devices  20.2 us (16%)
    all_to_all x3, blocking collectives, exchange(): lax.all_to_all(array, SPREAD, split_axis=0, concat_axis=0, tiled=True)  46.5 us
    pallas_call x1, Pallas kernels, body(): pl.pallas_call(attention_kernel, out_shape=[bf16(16, QR, D)] + [group] *...  31 us
    ppermute x8, waiting for transfers between devices, swap(): return lax.ppermute(array, 'y', [(i, i ^ distance) for i in range(4)])  15.4 us
    ppermute x8, starting transfers between devices, swap(): return lax.ppermute(array, 'y', [(i, i ^ distance) for i in range(4)])  15.2 us
    pallas_call x1, Pallas kernels, body(): pl.pallas_call(pack_q_kernel, out_shape=[bf16(16, 2 * QR + 16, D), jax.Sh...  4.72 us
    all_to_all x1, waiting for transfers between devices, exchange(): lax.all_to_all(array, SPREAD, split_axis=0, concat_axis=0, tiled=True)  4 us
    all_to_all x1, starting transfers between devices, exchange(): lax.all_to_all(array, SPREAD, split_axis=0, concat_axis=0, tiled=True)  3.83 us
  transfers between devices with their start and end apart: 18, of which 7 were waited for; matrix products, arithmetic and copies ran while one was open for 0% of the time, Pallas kernels for 4%

profile of v14, /device:TPU:0, one launch (start us, length us, event | category | flops | bytes accessed | tf_op | source)
XLA Modules:
  0.0 129.1 jit_solution(17957930885367802827)
XLA Ops:
  0.7 1.9 %shard_map.94 = bf16[16,128,128]{2,1,0:T(8,128)(2,1)} custom-call(bf16[64,1024]{1,0:T(8,128)(2,1)} %keys.1, bf16[64,1024]{1,0:T(8,128)(2,1)} %values.1), custom_call_target="tpu_custom_call" | custom-call | tf_op jit(solution)/shard_map/pallas_call | solution.py:424
  2.5 19.5 %all_to_all.20.after.refs_0_ = bf16[16,128,128]{2,1,0:T(8,128)(2,1)S(1)} all-to-all(bf16[16,128,128]{2,1,0:T(8,128)(2,1)} %shard_map.94), channel_id=1, replica_groups=mesh['z'=4,'core'=2,'xh'=2,'xl'=2,'y'=4] {'xh','xl','z'}, dimensions={0} | all-to-all | bytes 1048576 | tf_op jit(solution)/shard_map/all_to_all | solution.py:412
  22.0 3.0 %collective-permute-start.1 = (bf16[16,128,128]{2,1,0:T(8,128)(2,1)S(1)}, bf16[16,128,128]{2,1,0:T(8,128)(2,1)S(1)}, u32[]{:S(2)}, u32[]{:S(2)}) collective-permute-start(bf16[16,128,128]{2,1,0:T(8,128)(2,1)S(1)} %all_to_all.20.after.refs_0_), channel_id=1, source_target_pairs={{0,3},{1,2},{2,1},{3,0},{4,7},{5,6},{6,5},{7,4},{8,11},{9,10},{10,... | collective-permute-start | bytes 1572872 | tf_op jit(solution)/shard_map/ppermute | solution.py:420
  25.0 0.1 collective-permute-start
  25.2 0.0 copy-done.3
  25.2 4.7 %shard_map.95 = (bf16[16,272,128]{2,1,0:T(8,128)(2,1)S(1)}, s32[2]{0:T(128)S(1)}) custom-call(bf16[64,4096]{1,0:T(8,128)(2,1)S(1)} %copy-done.1, bf16[64,4096]{1,0:T(8,128)(2,1)S(1)} %copy-done.2, bf16[64,4096]{1,0:T(8,128)(2,1)S(1)} %copy-done.3, s32[64,128]{1,0:T(8,128)S(1)} %bitcast.1, bf16[16,128,128]{2,1,0:T(8,128)(2,1)S(1)} %all_to_all.20.after.refs_0_), custom_call_target="tpu_custom_call" | custom-call | tf_op jit(solution)/shard_map/pallas_call | solution.py:432
  29.9 1.0 copy-done
  30.9 3.8 %all-to-all-start.1 = ((bf16[16,272,128]{2,1,0:T(8,128)(2,1)}), bf16[16,272,128]{2,1,0:T(8,128)(2,1)S(1)}, u32[]{:S(2)}, u32[]{:S(2)}) async-start(bf16[16,272,128]{2,1,0:T(8,128)(2,1)} %copy-done), calls=%async_computation.1 | async-start | bytes 2228224 | tf_op jit(solution)/shard_map/all_to_all | solution.py:412
  34.8 0.1 collective-permute-start.4
  34.9 0.6 collective-permute-done.1.refs_2_
  35.5 1.4 %collective-permute-start.2 = (bf16[8,128,128]{2,1,0:T(8,128)(2,1)S(1)}, bf16[8,128,128]{2,1,0:T(8,128)(2,1)S(1)}, u32[]{:S(2)}, u32[]{:S(2)}) collective-permute-start(bf16[8,128,128]{2,1,0:T(8,128)(2,1)S(1)} %slice.8), channel_id=1, source_target_pairs={{0,1},{1,0},{2,3},{3,2},{4,5},{5,4},{6,7},{7,6},{8,9},{9,8},{10,11... | collective-permute-start | bytes 786440 | tf_op jit(solution)/shard_map/ppermute | solution.py:420
  36.9 0.2 collective-permute-start.6
  37.1 0.0 collective-permute-done.refs_1_
  37.1 1.7 %collective-permute-start.3 = (bf16[8,128,128]{2,1,0:T(8,128)(2,1)S(1)}, bf16[8,128,128]{2,1,0:T(8,128)(2,1)}, u32[]{:S(2)}, u32[]{:S(2)}) collective-permute-start(bf16[8,128,128]{2,1,0:T(8,128)(2,1)S(1)} %slice.9), channel_id=1, source_target_pairs={{0,3},{1,2},{2,1},{3,0},{4,7},{5,6},{6,5},{7,4},{8,11},{9,10},{10,... | collective-permute-start | bytes 786440 | tf_op jit(solution)/shard_map/ppermute | solution.py:420
  38.8 0.2 collective-permute-start.5
  39.0 4.9 %collective-permute-done.2.refs_3_ = bf16[8,128,128]{2,1,0:T(8,128)(2,1)S(1)} collective-permute-done((bf16[8,128,128]{2,1,0:T(8,128)(2,1)S(1)}, bf16[8,128,128]{2,1,0:T(8,128)(2,1)S(1)}, u32[]{:S(2)}, u32[]{:S(2)}) %collective-permute-start.2) | collective-permute-done | bytes 262176 | tf_op jit(solution)/shard_map/ppermute | solution.py:420
  43.8 0.0 collective-permute-start.7
  43.8 3.2 %collective-permute-done.3.refs_4_ = bf16[8,128,128]{2,1,0:T(8,128)(2,1)} collective-permute-done((bf16[8,128,128]{2,1,0:T(8,128)(2,1)S(1)}, bf16[8,128,128]{2,1,0:T(8,128)(2,1)}, u32[]{:S(2)}, u32[]{:S(2)}) %collective-permute-start.3) | collective-permute-done | bytes 262176 | tf_op jit(solution)/shard_map/ppermute | solution.py:420
  47.0 0.0 collective-permute-start.8
  47.0 0.0 collective-permute-done.4.refs_5_
  47.0 4.0 %all-to-all-done.1.qpay = bf16[16,272,128]{2,1,0:T(8,128)(2,1)S(1)} async-done(((bf16[16,272,128]{2,1,0:T(8,128)(2,1)}), bf16[16,272,128]{2,1,0:T(8,128)(2,1)S(1)}, u32[]{:S(2)}, u32[]{:S(2)}) %all-to-all-start.1) | async-done | bytes 1114144 | tf_op jit(solution)/shard_map/all_to_all | solution.py:412
  51.0 0.0 collective-permute-done.7.refs_8_
  51.0 0.0 collective-permute-done.6.refs_7_
  51.0 0.0 collective-permute-done.8.refs_9_
  51.0 0.0 collective-permute-done.5.refs_6_
  51.1 31.0 %shard_map.96 = (bf16[16,128,128]{2,1,0:T(8,128)(2,1)S(1)}, bf16[16,128,128]{2,1,0:T(8,128)(2,1)S(1)}, bf16[16,128,128]{2,1,0:T(8,128)(2,1)S(1)}, bf16[16,128,12...) custom-call(s32[32]{0:T(128)S(1)} %copy-done.5, ...), custom_call_target="tpu_custom_call" | custom-call | tf_op jit(solution)/shard_map/pallas_call | solution.py:449
  82.1 0.1 collective-permute-start.12
  82.2 0.5 collective-permute-start.10
  82.7 0.1 collective-permute-start.11
  82.8 1.3 %collective-permute-done.12.got = bf16[16,128,128]{2,1,0:T(8,128)(2,1)S(1)} collective-permute-done((bf16[16,128,128]{2,1,0:T(8,128)(2,1)S(1)}, bf16[16,128,128]{2,1,0:T(8,128)(2,1)S(1)}, u32[]{:S(2)}, u32[]{:S(2)}) %collective-permute-start.12) | collective-permute-done | bytes 524320 | tf_op jit(solution)/shard_map/ppermute | solution.py:416
  84.1 0.1 shard_map.97
  84.2 3.8 %collective-permute-start.13 = (bf16[8,128,128]{2,1,0:T(8,128)(2,1)S(1)}, bf16[8,128,128]{2,1,0:T(8,128)(2,1)S(1)}, u32[]{:S(2)}, u32[]{:S(2)}) collective-permute-start(bf16[8,128,128]{2,1,0:T(8,128)(2,1)S(1)} %get-tuple-element.34), channel_id=1, source_target_pairs={{0,1},{1,0},{2,3},{3,2},{4,5},{5,4},{6,7},{7,6},{8,9},{9,8},{10,11... | collective-permute-start | bytes 786440 | tf_op jit(solution)/shard_map/ppermute | solution.py:420
  88.0 2.5 %collective-permute-start.14 = (bf16[8,128,128]{2,1,0:T(8,128)(2,1)S(1)}, bf16[8,128,128]{2,1,0:T(8,128)(2,1)S(1)}, u32[]{:S(2)}, u32[]{:S(2)}) collective-permute-start(bf16[8,128,128]{2,1,0:T(8,128)(2,1)S(1)} %get-tuple-element.35), channel_id=1, source_target_pairs={{0,3},{1,2},{2,1},{3,0},{4,7},{5,6},{6,5},{7,4},{8,11},{9,10},{10,... | collective-permute-start | bytes 786440 | tf_op jit(solution)/shard_map/ppermute | solution.py:420
  90.5 0.0 collective-permute-start.9
  90.5 0.0 collective-permute-done.10.got_1
  90.5 0.0 collective-permute-done.11.got_3
  90.5 4.1 %collective-permute-done.13.from_1 = bf16[8,128,128]{2,1,0:T(8,128)(2,1)S(1)} collective-permute-done((bf16[8,128,128]{2,1,0:T(8,128)(2,1)S(1)}, bf16[8,128,128]{2,1,0:T(8,128)(2,1)S(1)}, u32[]{:S(2)}, u32[]{:S(2)}) %collective-permute-start.13) | collective-permute-done | bytes 262176 | tf_op jit(solution)/shard_map/ppermute | solution.py:420
  94.6 2.7 %collective-permute-done.14.from_3 = bf16[8,128,128]{2,1,0:T(8,128)(2,1)S(1)} collective-permute-done((bf16[8,128,128]{2,1,0:T(8,128)(2,1)S(1)}, bf16[8,128,128]{2,1,0:T(8,128)(2,1)S(1)}, u32[]{:S(2)}, u32[]{:S(2)}) %collective-permute-start.14) | collective-permute-done | bytes 262176 | tf_op jit(solution)/shard_map/ppermute | solution.py:420
  97.3 0.3 shard_map.98
  97.6 0.1 collective-permute-start.15
  97.7 2.6 %collective-permute-start.16 = (bf16[16,128,128]{2,1,0:T(8,128)(2,1)S(1)}, bf16[16,128,128]{2,1,0:T(8,128)(2,1)S(1)}, u32[]{:S(2)}, u32[]{:S(2)}) collective-permute-start(bf16[16,128,128]{2,1,0:T(8,128)(2,1)S(1)} %get-tuple-element.37), channel_id=1, source_target_pairs={{0,3},{1,2},{2,1},{3,0},{4,7},{5,6},{6,5},{7,4},{8,11},{9,10},{10,... | collective-permute-start | bytes 1572872 | tf_op jit(solution)/shard_map/ppermute | solution.py:420
  100.3 13.7 %all_to_all.21.dq = bf16[16,128,128]{2,1,0:T(8,128)(2,1)S(1)} all-to-all(bf16[16,128,128]{2,1,0:T(8,128)(2,1)S(1)} %get-tuple-element.38), channel_id=1, replica_groups=mesh['z'=4,'core'=2,'xh'=2,'xl'=2,'y'=4] {'xh','xl','z'}, dimensions={0} | all-to-all | bytes 1048576 | tf_op jit(solution)/shard_map/all_to_all | solution.py:412
  114.0 0.0 collective-permute-done.9.got
  114.0 0.0 collective-permute-done.15.near_1
  114.0 0.0 collective-permute-done.16.near_3
  114.0 0.9 shard_map.99
  114.9 13.3 %all_to_all.22.got = bf16[16,128,128]{2,1,0:T(8,128)(2,1)S(1)} all-to-all(bf16[16,128,128]{2,1,0:T(8,128)(2,1)S(1)} %get-tuple-element.40), channel_id=1, replica_groups=mesh['z'=4,'core'=2,'xh'=2,'xl'=2,'y'=4] {'xh','xl','z'}, dimensions={0} | all-to-all | bytes 1048576 | tf_op jit(solution)/shard_map/all_to_all | solution.py:412
  128.3 0.8 shard_map.100
  (12 shorter events, 0.1 us)
Async XLA Ops:
  0.6 24.5 %copy-start.4 = (s32[8192]{0:T(1024)S(1)}, s32[8192]{0:T(1024)}, u32[]{:S(2)}) copy-start(s32[8192]{0:T(1024)} %param.12) | copy-start | bytes 98308
  0.6 24.5 %copy-start.3 = (bf16[64,4096]{1,0:T(8,128)(2,1)S(1)}, bf16[64,4096]{1,0:T(8,128)(2,1)}, u32[]{:S(2)}) copy-start(bf16[64,4096]{1,0:T(8,128)(2,1)} %grads.1) | copy-start | bytes 1572868
  0.7 24.5 %copy-start.2 = (bf16[64,4096]{1,0:T(8,128)(2,1)S(1)}, bf16[64,4096]{1,0:T(8,128)(2,1)}, u32[]{:S(2)}) copy-start(bf16[64,4096]{1,0:T(8,128)(2,1)} %saved.1) | copy-start | bytes 1572868
  0.7 24.5 %copy-start.1 = (bf16[64,4096]{1,0:T(8,128)(2,1)S(1)}, bf16[64,4096]{1,0:T(8,128)(2,1)}, u32[]{:S(2)}) copy-start(bf16[64,4096]{1,0:T(8,128)(2,1)} %queries.1) | copy-start | bytes 1572868
  22.0 13.5 %collective-permute-start.1 = (bf16[16,128,128]{2,1,0:T(8,128)(2,1)S(1)}, bf16[16,128,128]{2,1,0:T(8,128)(2,1)S(1)}, u32[]{:S(2)}, u32[]{:S(2)}) collective-permute-start(bf16[16,128,128]{2,1,0:T(8,128)(2,1)S(1)} %all_to_all.20.after.refs_0_), channel_id=1, source_target_pairs={{0,3},{1,2},{2,1},{3,0},{4,7},{5,6},{6,5},{7,4},{8,11},{9,10},{10,... | collective-permute-start | bytes 1572872 | tf_op jit(solution)/shard_map/ppermute | solution.py:420
  25.0 12.1 %collective-permute-start = (bf16[16,128,128]{2,1,0:T(8,128)(2,1)S(1)}, bf16[16,128,128]{2,1,0:T(8,128)(2,1)S(1)}, u32[]{:S(2)}, u32[]{:S(2)}) collective-permute-start(bf16[16,128,128]{2,1,0:T(8,128)(2,1)S(1)} %all_to_all.20.after.refs_0_), channel_id=1, source_target_pairs={{0,1},{1,0},{2,3},{3,2},{4,5},{5,4},{6,7},{7,6},{8,9},{9,8},{10,11... | collective-permute-start | bytes 1572872 | tf_op jit(solution)/shard_map/ppermute | solution.py:420
  29.9 1.0 copy-start
  30.9 20.1 %copy-start.5 = (s32[32]{0:T(128)S(1)}, s32[32]{0:T(128)}, u32[]{:S(2)}) copy-start(s32[32]{0:T(128)} %order.1) | copy-start | bytes 388
  30.9 20.1 %all-to-all-start.1 = ((bf16[16,272,128]{2,1,0:T(8,128)(2,1)}), bf16[16,272,128]{2,1,0:T(8,128)(2,1)S(1)}, u32[]{:S(2)}, u32[]{:S(2)}) async-start(bf16[16,272,128]{2,1,0:T(8,128)(2,1)} %copy-done), calls=%async_computation.1 | async-start | bytes 2228224 | tf_op jit(solution)/shard_map/all_to_all | solution.py:412
  34.8 12.2 %collective-permute-start.4 = (bf16[16,128,128]{2,1,0:T(8,128)(2,1)S(1)}, bf16[16,128,128]{2,1,0:T(8,128)(2,1)S(1)}, u32[]{:S(2)}, u32[]{:S(2)}) collective-permute-start(bf16[16,128,128]{2,1,0:T(8,128)(2,1)S(1)} %all_to_all.20.after.refs_0_), channel_id=1, source_target_pairs={{0,16},{16,0},{1,17},{17,1},{2,18},{18,2},{3,19},{19,3},{4,20},{20... | collective-permute-start | bytes 1572872 | tf_op jit(solution)/shard_map/ppermute | solution.py:416
  35.5 8.3 %collective-permute-start.2 = (bf16[8,128,128]{2,1,0:T(8,128)(2,1)S(1)}, bf16[8,128,128]{2,1,0:T(8,128)(2,1)S(1)}, u32[]{:S(2)}, u32[]{:S(2)}) collective-permute-start(bf16[8,128,128]{2,1,0:T(8,128)(2,1)S(1)} %slice.8), channel_id=1, source_target_pairs={{0,1},{1,0},{2,3},{3,2},{4,5},{5,4},{6,7},{7,6},{8,9},{9,8},{10,11... | collective-permute-start | bytes 786440 | tf_op jit(solution)/shard_map/ppermute | solution.py:420
  36.9 14.2 %collective-permute-start.6 = (bf16[16,128,128]{2,1,0:T(8,128)(2,1)S(1)}, bf16[16,128,128]{2,1,0:T(8,128)(2,1)}, u32[]{:S(2)}, u32[]{:S(2)}) collective-permute-start(bf16[16,128,128]{2,1,0:T(8,128)(2,1)S(1)} %collective-permute-done.1.refs_2_), channel_id=1, source_target_pairs={{0,16},{16,0},{1,17},{17,1},{2,18},{18,2},{3,19},{19,3},{4,20},{20... | collective-permute-start | bytes 1572872 | tf_op jit(solution)/shard_map/ppermute | solution.py:416
  37.1 9.9 %collective-permute-start.3 = (bf16[8,128,128]{2,1,0:T(8,128)(2,1)S(1)}, bf16[8,128,128]{2,1,0:T(8,128)(2,1)}, u32[]{:S(2)}, u32[]{:S(2)}) collective-permute-start(bf16[8,128,128]{2,1,0:T(8,128)(2,1)S(1)} %slice.9), channel_id=1, source_target_pairs={{0,3},{1,2},{2,1},{3,0},{4,7},{5,6},{6,5},{7,4},{8,11},{9,10},{10,... | collective-permute-start | bytes 786440 | tf_op jit(solution)/shard_map/ppermute | solution.py:420
  38.8 12.3 %collective-permute-start.5 = (bf16[16,128,128]{2,1,0:T(8,128)(2,1)S(1)}, bf16[16,128,128]{2,1,0:T(8,128)(2,1)}, u32[]{:S(2)}, u32[]{:S(2)}) collective-permute-start(bf16[16,128,128]{2,1,0:T(8,128)(2,1)S(1)} %collective-permute-done.refs_1_), channel_id=1, source_target_pairs={{0,16},{16,0},{1,17},{17,1},{2,18},{18,2},{3,19},{19,3},{4,20},{20... | collective-permute-start | bytes 1572872 | tf_op jit(solution)/shard_map/ppermute | solution.py:416
  43.8 7.2 %collective-permute-start.7 = (bf16[8,128,128]{2,1,0:T(8,128)(2,1)S(1)}, bf16[8,128,128]{2,1,0:T(8,128)(2,1)}, u32[]{:S(2)}, u32[]{:S(2)}) collective-permute-start(bf16[8,128,128]{2,1,0:T(8,128)(2,1)S(1)} %collective-permute-done.2.refs_3_), channel_id=1, source_target_pairs={{0,16},{16,0},{1,17},{17,1},{2,18},{18,2},{3,19},{19,3},{4,20},{20... | collective-permute-start | bytes 786440 | tf_op jit(solution)/shard_map/ppermute | solution.py:416
  47.0 4.0 %collective-permute-start.8 = (bf16[8,128,128]{2,1,0:T(8,128)(2,1)}, bf16[8,128,128]{2,1,0:T(8,128)(2,1)}, u32[]{:S(2)}, u32[]{:S(2)}) collective-permute-start(bf16[8,128,128]{2,1,0:T(8,128)(2,1)} %collective-permute-done.3.refs_4_), channel_id=1, source_target_pairs={{0,16},{16,0},{1,17},{17,1},{2,18},{18,2},{3,19},{19,3},{4,20},{20... | collective-permute-start | bytes 786440 | tf_op jit(solution)/shard_map/ppermute | solution.py:416
  82.1 2.0 %collective-permute-start.12 = (bf16[16,128,128]{2,1,0:T(8,128)(2,1)S(1)}, bf16[16,128,128]{2,1,0:T(8,128)(2,1)S(1)}, u32[]{:S(2)}, u32[]{:S(2)}) collective-permute-start(bf16[16,128,128]{2,1,0:T(8,128)(2,1)S(1)} %get-tuple-element.33), channel_id=1, source_target_pairs={{0,16},{16,0},{1,17},{17,1},{2,18},{18,2},{3,19},{19,3},{4,20},{20... | collective-permute-start | bytes 1572872 | tf_op jit(solution)/shard_map/ppermute | solution.py:416
  82.2 8.3 %collective-permute-start.10 = (bf16[16,128,128]{2,1,0:T(8,128)(2,1)S(1)}, bf16[16,128,128]{2,1,0:T(8,128)(2,1)S(1)}, u32[]{:S(2)}, u32[]{:S(2)}) collective-permute-start(bf16[16,128,128]{2,1,0:T(8,128)(2,1)S(1)} %get-tuple-element.28), channel_id=1, source_target_pairs={{0,16},{16,0},{1,17},{17,1},{2,18},{18,2},{3,19},{19,3},{4,20},{20... | collective-permute-start | bytes 1572872 | tf_op jit(solution)/shard_map/ppermute | solution.py:416
  82.7 7.9 %collective-permute-start.11 = (bf16[16,128,128]{2,1,0:T(8,128)(2,1)S(1)}, bf16[16,128,128]{2,1,0:T(8,128)(2,1)S(1)}, u32[]{:S(2)}, u32[]{:S(2)}) collective-permute-start(bf16[16,128,128]{2,1,0:T(8,128)(2,1)S(1)} %get-tuple-element.30), channel_id=1, source_target_pairs={{0,16},{16,0},{1,17},{17,1},{2,18},{18,2},{3,19},{19,3},{4,20},{20... | collective-permute-start | bytes 1572872 | tf_op jit(solution)/shard_map/ppermute | solution.py:416
  84.2 10.4 %collective-permute-start.13 = (bf16[8,128,128]{2,1,0:T(8,128)(2,1)S(1)}, bf16[8,128,128]{2,1,0:T(8,128)(2,1)S(1)}, u32[]{:S(2)}, u32[]{:S(2)}) collective-permute-start(bf16[8,128,128]{2,1,0:T(8,128)(2,1)S(1)} %get-tuple-element.34), channel_id=1, source_target_pairs={{0,1},{1,0},{2,3},{3,2},{4,5},{5,4},{6,7},{7,6},{8,9},{9,8},{10,11... | collective-permute-start | bytes 786440 | tf_op jit(solution)/shard_map/ppermute | solution.py:420
  88.0 9.3 %collective-permute-start.14 = (bf16[8,128,128]{2,1,0:T(8,128)(2,1)S(1)}, bf16[8,128,128]{2,1,0:T(8,128)(2,1)S(1)}, u32[]{:S(2)}, u32[]{:S(2)}) collective-permute-start(bf16[8,128,128]{2,1,0:T(8,128)(2,1)S(1)} %get-tuple-element.35), channel_id=1, source_target_pairs={{0,3},{1,2},{2,1},{3,0},{4,7},{5,6},{6,5},{7,4},{8,11},{9,10},{10,... | collective-permute-start | bytes 786440 | tf_op jit(solution)/shard_map/ppermute | solution.py:420
  90.5 23.5 %collective-permute-start.9 = (bf16[16,128,128]{2,1,0:T(8,128)(2,1)S(1)}, bf16[16,128,128]{2,1,0:T(8,128)(2,1)S(1)}, u32[]{:S(2)}, u32[]{:S(2)}) collective-permute-start(bf16[16,128,128]{2,1,0:T(8,128)(2,1)S(1)} %get-tuple-element.26), channel_id=1, source_target_pairs={{0,16},{16,0},{1,17},{17,1},{2,18},{18,2},{3,19},{19,3},{4,20},{20... | collective-permute-start | bytes 1572872 | tf_op jit(solution)/shard_map/ppermute | solution.py:416
  97.6 16.4 %collective-permute-start.15 = (bf16[16,128,128]{2,1,0:T(8,128)(2,1)S(1)}, bf16[16,128,128]{2,1,0:T(8,128)(2,1)S(1)}, u32[]{:S(2)}, u32[]{:S(2)}) collective-permute-start(bf16[16,128,128]{2,1,0:T(8,128)(2,1)S(1)} %get-tuple-element.36), channel_id=1, source_target_pairs={{0,1},{1,0},{2,3},{3,2},{4,5},{5,4},{6,7},{7,6},{8,9},{9,8},{10,11... | collective-permute-start | bytes 1572872 | tf_op jit(solution)/shard_map/ppermute | solution.py:420
  97.7 16.3 %collective-permute-start.16 = (bf16[16,128,128]{2,1,0:T(8,128)(2,1)S(1)}, bf16[16,128,128]{2,1,0:T(8,128)(2,1)S(1)}, u32[]{:S(2)}, u32[]{:S(2)}) collective-permute-start(bf16[16,128,128]{2,1,0:T(8,128)(2,1)S(1)} %get-tuple-element.37), channel_id=1, source_target_pairs={{0,3},{1,2},{2,1},{3,0},{4,7},{5,6},{6,5},{7,4},{8,11},{9,10},{10,... | collective-permute-start | bytes 1572872 | tf_op jit(solution)/shard_map/ppermute | solution.py:420

commit v15 on v14

--- a/solution.py
+++ b/solution.py
@@ -57,11 +57,10 @@
         copy.wait()
 
 
-def pack_q_kernel(queries, saved, grads, segment, after, packed, counts, out, sem):
+def pack_q_kernel(queries, saved, grads, segment, after, out, counts):
     del after
     counts[0] = jnp.sum((segment[...] == 0).astype(jnp.int32))
     counts[1] = jnp.sum((segment[...] != 2).astype(jnp.int32))
-    copies = []
     ones = jnp.ones((8, D), BF16)
     row = lax.broadcasted_iota(jnp.int32, (16, D), 0)
     for g in range(8):
@@ -83,10 +82,6 @@
             both = jnp.concatenate([dot, dot], axis=0)
             rounded = both.astype(BF16).astype(F32)
             out[dest, 2 * QR :] = jnp.where(row == 0, rounded, both - rounded).astype(BF16)
-            copies.append(pltpu.make_async_copy(out.at[dest], packed.at[dest], sem))
-            copies[-1].start()
-    for copy in copies:
-        copy.wait()
 
 
 def span_id(xh, xl, y, zh):
@@ -433,8 +428,7 @@
         pack_q_kernel,
         out_shape=[bf16(16, 2 * QR + 16, D), jax.ShapeDtypeStruct((2,), jnp.int32)],
         in_specs=[IN_VMEM] * 4 + [ANYWHERE],
-        out_specs=[pl.BlockSpec(memory_space=pltpu.HBM), IN_SMEM],
-        scratch_shapes=[pltpu.VMEM((16, 2 * QR + 16, D), BF16), pltpu.SemaphoreType.DMA],
+        out_specs=[IN_VMEM, IN_SMEM],
         compiler_params=pltpu.CompilerParams(vmem_limit_bytes=16 << 20),
     )(queries, attn_out, out_grad, segment.reshape(64, 128), own)
     qpay = exchange(q_packed)

time: 130 us -> 128 us (0.985); the launches traced: 129 us -> 130 us
  Pallas kernels: 39.7 us -> 36.3 us
  waiting for transfers between devices: 20.8 us -> 22.8 us
  starting transfers between devices: 20.2 us -> 21.8 us
    ppermute x8, waiting for transfers between devices: 15.4 us -> 19.7 us  [swap(): return lax.ppermute(array, 'y', [(i, i ^ distance) for i in range(4)])]
    pallas_call x1, Pallas kernels: 4.72 us -> 1.25 us  [body(): pl.pallas_call(pack_q_kernel, out_shape=[bf16(16, 2 * QR + 16, D), jax.Sh...]
    all_to_all x1, waiting for transfers between devices: 4 us -> 1.52 us  [exchange(): lax.all_to_all(array, SPREAD, split_axis=0, concat_axis=0, tiled=True)]
    ppermute x8, starting transfers between devices: 15.2 us -> 16.9 us  [swap(): return lax.ppermute(array, 'y', [(i, i ^ distance) for i in range(4)])]
  transfers between devices with their start and end apart: 18 -> 18, of which waited for: 7 -> 8; matrix products, arithmetic and copies ran while one was open for 0% -> 0% of each run, Pallas kernels for 4% -> 1%
where the time goes in v15:
time: 128 us; the launch traced here: 130 us
  blocking collectives  46.7 us (36%)
  Pallas kernels  36.3 us (28%)
  waiting for transfers between devices  22.8 us (18%)
  starting transfers between devices  21.8 us (17%)
    all_to_all x3, blocking collectives, exchange(): lax.all_to_all(array, SPREAD, split_axis=0, concat_axis=0, tiled=True)  46.7 us
    pallas_call x1, Pallas kernels, body(): pl.pallas_call(attention_kernel, out_shape=[bf16(16, QR, D)] + [group] *...  31.1 us
    ppermute x8, waiting for transfers between devices, swap(): return lax.ppermute(array, 'y', [(i, i ^ distance) for i in range(4)])  19.7 us
    ppermute x8, starting transfers between devices, swap(): return lax.ppermute(array, 'y', [(i, i ^ distance) for i in range(4)])  16.9 us
    all_to_all x1, starting transfers between devices, exchange(): lax.all_to_all(array, SPREAD, split_axis=0, concat_axis=0, tiled=True)  3.83 us
  transfers between devices with their start and end apart: 18, of which 8 were waited for; matrix products, arithmetic and copies ran while one was open for 0% of the time, Pallas kernels for 1%

profile of v15, /device:TPU:0, one launch (start us, length us, event | category | flops | bytes accessed | tf_op | source)
XLA Modules:
  0.0 129.5 jit_solution(16178254081786667943)
XLA Ops:
  0.7 1.9 %shard_map.94 = bf16[16,128,128]{2,1,0:T(8,128)(2,1)} custom-call(bf16[64,1024]{1,0:T(8,128)(2,1)} %keys.1, bf16[64,1024]{1,0:T(8,128)(2,1)} %values.1), custom_call_target="tpu_custom_call" | custom-call | tf_op jit(solution)/shard_map/pallas_call | solution.py:419
  2.5 19.5 %all_to_all.20.after.refs_0_ = bf16[16,128,128]{2,1,0:T(8,128)(2,1)S(1)} all-to-all(bf16[16,128,128]{2,1,0:T(8,128)(2,1)} %shard_map.94), channel_id=1, replica_groups=mesh['z'=4,'core'=2,'xh'=2,'xl'=2,'y'=4] {'xh','xl','z'}, dimensions={0} | all-to-all | bytes 1048576 | tf_op jit(solution)/shard_map/all_to_all | solution.py:407
  22.0 3.0 %collective-permute-start.1 = (bf16[16,128,128]{2,1,0:T(8,128)(2,1)S(1)}, bf16[16,128,128]{2,1,0:T(8,128)(2,1)S(1)}, u32[]{:S(2)}, u32[]{:S(2)}) collective-permute-start(bf16[16,128,128]{2,1,0:T(8,128)(2,1)S(1)} %all_to_all.20.after.refs_0_), channel_id=1, source_target_pairs={{0,3},{1,2},{2,1},{3,0},{4,7},{5,6},{6,5},{7,4},{8,11},{9,10},{10,... | collective-permute-start | bytes 1572872 | tf_op jit(solution)/shard_map/ppermute | solution.py:415
  25.0 0.1 collective-permute-start
  25.2 0.0 copy-done.2
  25.2 1.3 shard_map.95
  26.4 1.0 copy-done
  27.5 3.8 %all-to-all-start.1 = ((bf16[16,272,128]{2,1,0:T(8,128)(2,1)}), bf16[16,272,128]{2,1,0:T(8,128)(2,1)S(1)}, u32[]{:S(2)}, u32[]{:S(2)}) async-start(bf16[16,272,128]{2,1,0:T(8,128)(2,1)} %copy-done), calls=%async_computation.1 | async-start | bytes 2228224 | tf_op jit(solution)/shard_map/all_to_all | solution.py:407
  31.3 0.1 collective-permute-start.4
  31.4 4.1 %collective-permute-done.1.refs_2_ = bf16[16,128,128]{2,1,0:T(8,128)(2,1)S(1)} collective-permute-done((bf16[16,128,128]{2,1,0:T(8,128)(2,1)S(1)}, bf16[16,128,128]{2,1,0:T(8,128)(2,1)S(1)}, u32[]{:S(2)}, u32[]{:S(2)}) %collective-permute-start.1) | collective-permute-done | bytes 524320 | tf_op jit(solution)/shard_map/ppermute | solution.py:415
  35.5 0.4 collective-permute-start.2
  35.9 0.0 collective-permute-start.6
  35.9 2.2 %collective-permute-done.refs_1_ = bf16[16,128,128]{2,1,0:T(8,128)(2,1)S(1)} collective-permute-done((bf16[16,128,128]{2,1,0:T(8,128)(2,1)S(1)}, bf16[16,128,128]{2,1,0:T(8,128)(2,1)S(1)}, u32[]{:S(2)}, u32[]{:S(2)}) %collective-permute-start) | collective-permute-done | bytes 524320 | tf_op jit(solution)/shard_map/ppermute | solution.py:415
  38.2 0.6 collective-permute-start.3
  38.8 0.2 collective-permute-start.5
  39.0 3.6 %collective-permute-done.2.refs_3_ = bf16[8,128,128]{2,1,0:T(8,128)(2,1)S(1)} collective-permute-done((bf16[8,128,128]{2,1,0:T(8,128)(2,1)S(1)}, bf16[8,128,128]{2,1,0:T(8,128)(2,1)S(1)}, u32[]{:S(2)}, u32[]{:S(2)}) %collective-permute-start.2) | collective-permute-done | bytes 262176 | tf_op jit(solution)/shard_map/ppermute | solution.py:415
  42.6 0.0 collective-permute-start.7
  42.6 3.5 %collective-permute-done.3.refs_4_ = bf16[8,128,128]{2,1,0:T(8,128)(2,1)} collective-permute-done((bf16[8,128,128]{2,1,0:T(8,128)(2,1)S(1)}, bf16[8,128,128]{2,1,0:T(8,128)(2,1)}, u32[]{:S(2)}, u32[]{:S(2)}) %collective-permute-start.3) | collective-permute-done | bytes 262176 | tf_op jit(solution)/shard_map/ppermute | solution.py:415
  46.0 0.0 collective-permute-start.8
  46.0 0.0 collective-permute-done.4.refs_5_
  46.0 1.5 %all-to-all-done.1.qpay = bf16[16,272,128]{2,1,0:T(8,128)(2,1)S(1)} async-done(((bf16[16,272,128]{2,1,0:T(8,128)(2,1)}), bf16[16,272,128]{2,1,0:T(8,128)(2,1)S(1)}, u32[]{:S(2)}, u32[]{:S(2)}) %all-to-all-start.1) | async-done | bytes 1114144 | tf_op jit(solution)/shard_map/all_to_all | solution.py:407
  47.6 0.0 collective-permute-done.7.refs_8_
  47.6 0.0 collective-permute-done.6.refs_7_
  47.6 0.3 collective-permute-done.8.refs_9_
  47.9 0.0 collective-permute-done.5.refs_6_
  47.9 31.1 %shard_map.96 = (bf16[16,128,128]{2,1,0:T(8,128)(2,1)S(1)}, bf16[16,128,128]{2,1,0:T(8,128)(2,1)S(1)}, bf16[16,128,128]{2,1,0:T(8,128)(2,1)S(1)}, bf16[16,128,12...) custom-call(s32[32]{0:T(128)S(1)} %copy-done.5, ...), custom_call_target="tpu_custom_call" | custom-call | tf_op jit(solution)/shard_map/pallas_call | solution.py:443
  79.0 0.2 collective-permute-start.12
  79.2 0.4 collective-permute-start.10
  79.6 0.1 collective-permute-start.11
  79.7 1.3 collective-permute-done.12.got
  81.0 0.1 shard_map.97
  81.1 1.4 %collective-permute-start.13 = (bf16[8,128,128]{2,1,0:T(8,128)(2,1)S(1)}, bf16[8,128,128]{2,1,0:T(8,128)(2,1)S(1)}, u32[]{:S(2)}, u32[]{:S(2)}) collective-permute-start(bf16[8,128,128]{2,1,0:T(8,128)(2,1)S(1)} %get-tuple-element.34), channel_id=1, source_target_pairs={{0,1},{1,0},{2,3},{3,2},{4,5},{5,4},{6,7},{7,6},{8,9},{9,8},{10,11... | collective-permute-start | bytes 786440 | tf_op jit(solution)/shard_map/ppermute | solution.py:415
  82.5 8.3 %collective-permute-start.14 = (bf16[8,128,128]{2,1,0:T(8,128)(2,1)S(1)}, bf16[8,128,128]{2,1,0:T(8,128)(2,1)S(1)}, u32[]{:S(2)}, u32[]{:S(2)}) collective-permute-start(bf16[8,128,128]{2,1,0:T(8,128)(2,1)S(1)} %get-tuple-element.35), channel_id=1, source_target_pairs={{0,3},{1,2},{2,1},{3,0},{4,7},{5,6},{6,5},{7,4},{8,11},{9,10},{10,... | collective-permute-start | bytes 786440 | tf_op jit(solution)/shard_map/ppermute | solution.py:415
  90.8 0.0 collective-permute-start.9
  90.8 0.0 collective-permute-done.10.got_1
  90.8 0.0 collective-permute-done.11.got_3
  90.8 0.0 collective-permute-done.13.from_1
  90.8 6.3 %collective-permute-done.14.from_3 = bf16[8,128,128]{2,1,0:T(8,128)(2,1)S(1)} collective-permute-done((bf16[8,128,128]{2,1,0:T(8,128)(2,1)S(1)}, bf16[8,128,128]{2,1,0:T(8,128)(2,1)S(1)}, u32[]{:S(2)}, u32[]{:S(2)}) %collective-permute-start.14) | collective-permute-done | bytes 262176 | tf_op jit(solution)/shard_map/ppermute | solution.py:415
  97.1 0.3 shard_map.98
  97.4 0.1 collective-permute-start.15
  97.5 3.0 %collective-permute-start.16 = (bf16[16,128,128]{2,1,0:T(8,128)(2,1)S(1)}, bf16[16,128,128]{2,1,0:T(8,128)(2,1)S(1)}, u32[]{:S(2)}, u32[]{:S(2)}) collective-permute-start(bf16[16,128,128]{2,1,0:T(8,128)(2,1)S(1)} %get-tuple-element.37), channel_id=1, source_target_pairs={{0,3},{1,2},{2,1},{3,0},{4,7},{5,6},{6,5},{7,4},{8,11},{9,10},{10,... | collective-permute-start | bytes 1572872 | tf_op jit(solution)/shard_map/ppermute | solution.py:415
  100.6 13.9 %all_to_all.21.dq = bf16[16,128,128]{2,1,0:T(8,128)(2,1)S(1)} all-to-all(bf16[16,128,128]{2,1,0:T(8,128)(2,1)S(1)} %get-tuple-element.38), channel_id=1, replica_groups=mesh['z'=4,'core'=2,'xh'=2,'xl'=2,'y'=4] {'xh','xl','z'}, dimensions={0} | all-to-all | bytes 1048576 | tf_op jit(solution)/shard_map/all_to_all | solution.py:407
  114.5 0.0 collective-permute-done.9.got
  114.5 0.0 collective-permute-done.15.near_1
  114.5 0.0 collective-permute-done.16.near_3
  114.5 0.9 shard_map.99
  115.4 13.3 %all_to_all.22.got = bf16[16,128,128]{2,1,0:T(8,128)(2,1)S(1)} all-to-all(bf16[16,128,128]{2,1,0:T(8,128)(2,1)S(1)} %get-tuple-element.40), channel_id=1, replica_groups=mesh['z'=4,'core'=2,'xh'=2,'xl'=2,'y'=4] {'xh','xl','z'}, dimensions={0} | all-to-all | bytes 1048576 | tf_op jit(solution)/shard_map/all_to_all | solution.py:407
  128.8 0.8 shard_map.100
  (12 shorter events, 0.1 us)
Async XLA Ops:
  0.6 24.5 %copy-start.4 = (s32[8192]{0:T(1024)S(1)}, s32[8192]{0:T(1024)}, u32[]{:S(2)}) copy-start(s32[8192]{0:T(1024)} %param.12) | copy-start | bytes 98308
  0.6 24.5 %copy-start.3 = (bf16[64,4096]{1,0:T(8,128)(2,1)S(1)}, bf16[64,4096]{1,0:T(8,128)(2,1)}, u32[]{:S(2)}) copy-start(bf16[64,4096]{1,0:T(8,128)(2,1)} %grads.1) | copy-start | bytes 1572868
  0.7 24.5 %copy-start.2 = (bf16[64,4096]{1,0:T(8,128)(2,1)S(1)}, bf16[64,4096]{1,0:T(8,128)(2,1)}, u32[]{:S(2)}) copy-start(bf16[64,4096]{1,0:T(8,128)(2,1)} %saved.1) | copy-start | bytes 1572868
  0.7 24.5 %copy-start.1 = (bf16[64,4096]{1,0:T(8,128)(2,1)S(1)}, bf16[64,4096]{1,0:T(8,128)(2,1)}, u32[]{:S(2)}) copy-start(bf16[64,4096]{1,0:T(8,128)(2,1)} %queries.1) | copy-start | bytes 1572868
  22.0 13.5 %collective-permute-start.1 = (bf16[16,128,128]{2,1,0:T(8,128)(2,1)S(1)}, bf16[16,128,128]{2,1,0:T(8,128)(2,1)S(1)}, u32[]{:S(2)}, u32[]{:S(2)}) collective-permute-start(bf16[16,128,128]{2,1,0:T(8,128)(2,1)S(1)} %all_to_all.20.after.refs_0_), channel_id=1, source_target_pairs={{0,3},{1,2},{2,1},{3,0},{4,7},{5,6},{6,5},{7,4},{8,11},{9,10},{10,... | collective-permute-start | bytes 1572872 | tf_op jit(solution)/shard_map/ppermute | solution.py:415
  25.0 13.1 %collective-permute-start = (bf16[16,128,128]{2,1,0:T(8,128)(2,1)S(1)}, bf16[16,128,128]{2,1,0:T(8,128)(2,1)S(1)}, u32[]{:S(2)}, u32[]{:S(2)}) collective-permute-start(bf16[16,128,128]{2,1,0:T(8,128)(2,1)S(1)} %all_to_all.20.after.refs_0_), channel_id=1, source_target_pairs={{0,1},{1,0},{2,3},{3,2},{4,5},{5,4},{6,7},{7,6},{8,9},{9,8},{10,11... | collective-permute-start | bytes 1572872 | tf_op jit(solution)/shard_map/ppermute | solution.py:415
  26.4 1.0 copy-start
  27.5 20.4 %copy-start.5 = (s32[32]{0:T(128)S(1)}, s32[32]{0:T(128)}, u32[]{:S(2)}) copy-start(s32[32]{0:T(128)} %order.1) | copy-start | bytes 388
  27.5 20.1 %all-to-all-start.1 = ((bf16[16,272,128]{2,1,0:T(8,128)(2,1)}), bf16[16,272,128]{2,1,0:T(8,128)(2,1)S(1)}, u32[]{:S(2)}, u32[]{:S(2)}) async-start(bf16[16,272,128]{2,1,0:T(8,128)(2,1)} %copy-done), calls=%async_computation.1 | async-start | bytes 2228224 | tf_op jit(solution)/shard_map/all_to_all | solution.py:407
  31.3 14.7 %collective-permute-start.4 = (bf16[16,128,128]{2,1,0:T(8,128)(2,1)S(1)}, bf16[16,128,128]{2,1,0:T(8,128)(2,1)S(1)}, u32[]{:S(2)}, u32[]{:S(2)}) collective-permute-start(bf16[16,128,128]{2,1,0:T(8,128)(2,1)S(1)} %all_to_all.20.after.refs_0_), channel_id=1, source_target_pairs={{0,16},{16,0},{1,17},{17,1},{2,18},{18,2},{3,19},{19,3},{4,20},{20... | collective-permute-start | bytes 1572872 | tf_op jit(solution)/shard_map/ppermute | solution.py:411
  35.5 7.1 %collective-permute-start.2 = (bf16[8,128,128]{2,1,0:T(8,128)(2,1)S(1)}, bf16[8,128,128]{2,1,0:T(8,128)(2,1)S(1)}, u32[]{:S(2)}, u32[]{:S(2)}) collective-permute-start(bf16[8,128,128]{2,1,0:T(8,128)(2,1)S(1)} %slice.8), channel_id=1, source_target_pairs={{0,1},{1,0},{2,3},{3,2},{4,5},{5,4},{6,7},{7,6},{8,9},{9,8},{10,11... | collective-permute-start | bytes 786440 | tf_op jit(solution)/shard_map/ppermute | solution.py:415
  35.9 11.7 %collective-permute-start.6 = (bf16[16,128,128]{2,1,0:T(8,128)(2,1)S(1)}, bf16[16,128,128]{2,1,0:T(8,128)(2,1)}, u32[]{:S(2)}, u32[]{:S(2)}) collective-permute-start(bf16[16,128,128]{2,1,0:T(8,128)(2,1)S(1)} %collective-permute-done.1.refs_2_), channel_id=1, source_target_pairs={{0,16},{16,0},{1,17},{17,1},{2,18},{18,2},{3,19},{19,3},{4,20},{20... | collective-permute-start | bytes 1572872 | tf_op jit(solution)/shard_map/ppermute | solution.py:411
  38.2 7.9 %collective-permute-start.3 = (bf16[8,128,128]{2,1,0:T(8,128)(2,1)S(1)}, bf16[8,128,128]{2,1,0:T(8,128)(2,1)}, u32[]{:S(2)}, u32[]{:S(2)}) collective-permute-start(bf16[8,128,128]{2,1,0:T(8,128)(2,1)S(1)} %slice.9), channel_id=1, source_target_pairs={{0,3},{1,2},{2,1},{3,0},{4,7},{5,6},{6,5},{7,4},{8,11},{9,10},{10,... | collective-permute-start | bytes 786440 | tf_op jit(solution)/shard_map/ppermute | solution.py:415
  38.8 9.2 %collective-permute-start.5 = (bf16[16,128,128]{2,1,0:T(8,128)(2,1)S(1)}, bf16[16,128,128]{2,1,0:T(8,128)(2,1)}, u32[]{:S(2)}, u32[]{:S(2)}) collective-permute-start(bf16[16,128,128]{2,1,0:T(8,128)(2,1)S(1)} %collective-permute-done.refs_1_), channel_id=1, source_target_pairs={{0,16},{16,0},{1,17},{17,1},{2,18},{18,2},{3,19},{19,3},{4,20},{20... | collective-permute-start | bytes 1572872 | tf_op jit(solution)/shard_map/ppermute | solution.py:411
  42.6 5.0 %collective-permute-start.7 = (bf16[8,128,128]{2,1,0:T(8,128)(2,1)S(1)}, bf16[8,128,128]{2,1,0:T(8,128)(2,1)}, u32[]{:S(2)}, u32[]{:S(2)}) collective-permute-start(bf16[8,128,128]{2,1,0:T(8,128)(2,1)S(1)} %collective-permute-done.2.refs_3_), channel_id=1, source_target_pairs={{0,16},{16,0},{1,17},{17,1},{2,18},{18,2},{3,19},{19,3},{4,20},{20... | collective-permute-start | bytes 786440 | tf_op jit(solution)/shard_map/ppermute | solution.py:411
  46.0 1.9 %collective-permute-start.8 = (bf16[8,128,128]{2,1,0:T(8,128)(2,1)}, bf16[8,128,128]{2,1,0:T(8,128)(2,1)}, u32[]{:S(2)}, u32[]{:S(2)}) collective-permute-start(bf16[8,128,128]{2,1,0:T(8,128)(2,1)} %collective-permute-done.3.refs_4_), channel_id=1, source_target_pairs={{0,16},{16,0},{1,17},{17,1},{2,18},{18,2},{3,19},{19,3},{4,20},{20... | collective-permute-start | bytes 786440 | tf_op jit(solution)/shard_map/ppermute | solution.py:411
  79.0 2.0 %collective-permute-start.12 = (bf16[16,128,128]{2,1,0:T(8,128)(2,1)S(1)}, bf16[16,128,128]{2,1,0:T(8,128)(2,1)S(1)}, u32[]{:S(2)}, u32[]{:S(2)}) collective-permute-start(bf16[16,128,128]{2,1,0:T(8,128)(2,1)S(1)} %get-tuple-element.33), channel_id=1, source_target_pairs={{0,16},{16,0},{1,17},{17,1},{2,18},{18,2},{3,19},{19,3},{4,20},{20... | collective-permute-start | bytes 1572872 | tf_op jit(solution)/shard_map/ppermute | solution.py:411
  79.2 11.6 %collective-permute-start.10 = (bf16[16,128,128]{2,1,0:T(8,128)(2,1)S(1)}, bf16[16,128,128]{2,1,0:T(8,128)(2,1)S(1)}, u32[]{:S(2)}, u32[]{:S(2)}) collective-permute-start(bf16[16,128,128]{2,1,0:T(8,128)(2,1)S(1)} %get-tuple-element.28), channel_id=1, source_target_pairs={{0,16},{16,0},{1,17},{17,1},{2,18},{18,2},{3,19},{19,3},{4,20},{20... | collective-permute-start | bytes 1572872 | tf_op jit(solution)/shard_map/ppermute | solution.py:411
  79.6 11.2 %collective-permute-start.11 = (bf16[16,128,128]{2,1,0:T(8,128)(2,1)S(1)}, bf16[16,128,128]{2,1,0:T(8,128)(2,1)S(1)}, u32[]{:S(2)}, u32[]{:S(2)}) collective-permute-start(bf16[16,128,128]{2,1,0:T(8,128)(2,1)S(1)} %get-tuple-element.30), channel_id=1, source_target_pairs={{0,16},{16,0},{1,17},{17,1},{2,18},{18,2},{3,19},{19,3},{4,20},{20... | collective-permute-start | bytes 1572872 | tf_op jit(solution)/shard_map/ppermute | solution.py:411
  81.1 9.7 %collective-permute-start.13 = (bf16[8,128,128]{2,1,0:T(8,128)(2,1)S(1)}, bf16[8,128,128]{2,1,0:T(8,128)(2,1)S(1)}, u32[]{:S(2)}, u32[]{:S(2)}) collective-permute-start(bf16[8,128,128]{2,1,0:T(8,128)(2,1)S(1)} %get-tuple-element.34), channel_id=1, source_target_pairs={{0,1},{1,0},{2,3},{3,2},{4,5},{5,4},{6,7},{7,6},{8,9},{9,8},{10,11... | collective-permute-start | bytes 786440 | tf_op jit(solution)/shard_map/ppermute | solution.py:415
  82.5 14.6 %collective-permute-start.14 = (bf16[8,128,128]{2,1,0:T(8,128)(2,1)S(1)}, bf16[8,128,128]{2,1,0:T(8,128)(2,1)S(1)}, u32[]{:S(2)}, u32[]{:S(2)}) collective-permute-start(bf16[8,128,128]{2,1,0:T(8,128)(2,1)S(1)} %get-tuple-element.35), channel_id=1, source_target_pairs={{0,3},{1,2},{2,1},{3,0},{4,7},{5,6},{6,5},{7,4},{8,11},{9,10},{10,... | collective-permute-start | bytes 786440 | tf_op jit(solution)/shard_map/ppermute | solution.py:415
  90.8 23.7 %collective-permute-start.9 = (bf16[16,128,128]{2,1,0:T(8,128)(2,1)S(1)}, bf16[16,128,128]{2,1,0:T(8,128)(2,1)S(1)}, u32[]{:S(2)}, u32[]{:S(2)}) collective-permute-start(bf16[16,128,128]{2,1,0:T(8,128)(2,1)S(1)} %get-tuple-element.26), channel_id=1, source_target_pairs={{0,16},{16,0},{1,17},{17,1},{2,18},{18,2},{3,19},{19,3},{4,20},{20... | collective-permute-start | bytes 1572872 | tf_op jit(solution)/shard_map/ppermute | solution.py:411
  97.4 17.1 %collective-permute-start.15 = (bf16[16,128,128]{2,1,0:T(8,128)(2,1)S(1)}, bf16[16,128,128]{2,1,0:T(8,128)(2,1)S(1)}, u32[]{:S(2)}, u32[]{:S(2)}) collective-permute-start(bf16[16,128,128]{2,1,0:T(8,128)(2,1)S(1)} %get-tuple-element.36), channel_id=1, source_target_pairs={{0,1},{1,0},{2,3},{3,2},{4,5},{5,4},{6,7},{7,6},{8,9},{9,8},{10,11... | collective-permute-start | bytes 1572872 | tf_op jit(solution)/shard_map/ppermute | solution.py:415
  97.5 17.0 %collective-permute-start.16 = (bf16[16,128,128]{2,1,0:T(8,128)(2,1)S(1)}, bf16[16,128,128]{2,1,0:T(8,128)(2,1)S(1)}, u32[]{:S(2)}, u32[]{:S(2)}) collective-permute-start(bf16[16,128,128]{2,1,0:T(8,128)(2,1)S(1)} %get-tuple-element.37), channel_id=1, source_target_pairs={{0,3},{1,2},{2,1},{3,0},{4,7},{5,6},{6,5},{7,4},{8,11},{9,10},{10,... | collective-permute-start | bytes 1572872 | tf_op jit(solution)/shard_map/ppermute | solution.py:415

commit v16 on v13

--- a/solution.py
+++ b/solution.py
@@ -318,12 +318,11 @@
             weights = weights_of(c, b, masked)
             above = jnp.dot(block_of(v_s, b), ga_s[c], preferred_element_type=F32)
             made.append((weights.astype(BF16), (weights * above).astype(BF16)))
-        for (c, b), (weights, score_grad) in zip(items, made):
-            for ref, term in (
-                (dv_s, jnp.dot(weights, do_s[c], preferred_element_type=F32)),
-                (dk_s, jnp.dot(score_grad, q_s[c], preferred_element_type=F32)),
-            ):
+        for which, ref, rows in ((0, dv_s, do_s), (1, dk_s, q_s)):
+            for (c, b), factors in zip(items, made):
+                term = jnp.dot(factors[which], rows[c], preferred_element_type=F32)
                 ref[pl.ds(2 * b, 2)] += term.reshape(2, 2, 2, R, D)
+        for (c, b), (_, score_grad) in zip(items, made):
             dq_s[c] += jnp.dot(kt_s[b], score_grad, preferred_element_type=F32)
 
     grad_step([(c, full_blocks(c)) for c in range(NC)], True)

time: 125 us -> 130 us (1.040)
  starting transfers between devices: 11.8 us -> 21.5 us
  Pallas kernels: 37.8 us -> 32.4 us
    ppermute x8, starting transfers between devices: 6.91 us -> 16.7 us  [swap(): return lax.ppermute(array, 'y', [(i, i ^ distance) for i in range(4)])]
    pallas_call x1, Pallas kernels: 32.5 us -> 27.1 us  [body(): pl.pallas_call(attention_kernel, out_shape=[bf16(16, QR, D)] + [group] *...]
where the time goes in v16:
time: 130 us; the launch traced here: 128 us
  blocking collectives  46.9 us (36%)
  Pallas kernels  32.4 us (25%)
  waiting for transfers between devices  25.8 us (20%)
  starting transfers between devices  21.5 us (17%)
    all_to_all x3, blocking collectives, exchange(): lax.all_to_all(array, SPREAD, split_axis=0, concat_axis=0, tiled=True)  46.9 us
    pallas_call x1, Pallas kernels, body(): pl.pallas_call(attention_kernel, out_shape=[bf16(16, QR, D)] + [group] *...  27.1 us
    ppermute x8, waiting for transfers between devices, swap(): return lax.ppermute(array, 'y', [(i, i ^ distance) for i in range(4)])  22.7 us
    ppermute x8, starting transfers between devices, swap(): return lax.ppermute(array, 'y', [(i, i ^ distance) for i in range(4)])  16.7 us
    all_to_all x1, starting transfers between devices, exchange(): lax.all_to_all(array, SPREAD, split_axis=0, concat_axis=0, tiled=True)  3.83 us
  transfers between devices with their start and end apart: 18, of which 9 were waited for; matrix products, arithmetic and copies ran while one was open for 0% of the time, Pallas kernels for 1%

profile of v16, /device:TPU:0, one launch (start us, length us, event | category | flops | bytes accessed | tf_op | source)
XLA Modules:
  0.0 128.4 jit_solution(11996746533170789975)
XLA Ops:
  0.7 1.9 %shard_map.94 = bf16[16,128,128]{2,1,0:T(8,128)(2,1)} custom-call(bf16[64,1024]{1,0:T(8,128)(2,1)} %keys.1, bf16[64,1024]{1,0:T(8,128)(2,1)} %values.1), custom_call_target="tpu_custom_call" | custom-call | tf_op jit(solution)/shard_map/pallas_call | solution.py:417
  2.5 19.5 %all_to_all.20.after.refs_0_ = bf16[16,128,128]{2,1,0:T(8,128)(2,1)S(1)} all-to-all(bf16[16,128,128]{2,1,0:T(8,128)(2,1)} %shard_map.94), channel_id=1, replica_groups=mesh['z'=4,'core'=2,'xh'=2,'xl'=2,'y'=4] {'xh','xl','z'}, dimensions={0} | all-to-all | bytes 1048576 | tf_op jit(solution)/shard_map/all_to_all | solution.py:405
  22.0 3.0 %collective-permute-start.1 = (bf16[16,128,128]{2,1,0:T(8,128)(2,1)S(1)}, bf16[16,128,128]{2,1,0:T(8,128)(2,1)S(1)}, u32[]{:S(2)}, u32[]{:S(2)}) collective-permute-start(bf16[16,128,128]{2,1,0:T(8,128)(2,1)S(1)} %all_to_all.20.after.refs_0_), channel_id=1, source_target_pairs={{0,3},{1,2},{2,1},{3,0},{4,7},{5,6},{6,5},{7,4},{8,11},{9,10},{10,... | collective-permute-start | bytes 1572872 | tf_op jit(solution)/shard_map/ppermute | solution.py:413
  25.0 0.1 collective-permute-start
  25.2 0.0 copy-done.2
  25.2 1.3 shard_map.95
  26.4 1.0 copy-done
  27.5 3.8 %all-to-all-start.1 = ((bf16[16,272,128]{2,1,0:T(8,128)(2,1)}), bf16[16,272,128]{2,1,0:T(8,128)(2,1)S(1)}, u32[]{:S(2)}, u32[]{:S(2)}) async-start(bf16[16,272,128]{2,1,0:T(8,128)(2,1)} %copy-done), calls=%async_computation.1 | async-start | bytes 2228224 | tf_op jit(solution)/shard_map/all_to_all | solution.py:405
  31.3 0.1 collective-permute-start.4
  31.4 4.1 %collective-permute-done.1.refs_2_ = bf16[16,128,128]{2,1,0:T(8,128)(2,1)S(1)} collective-permute-done((bf16[16,128,128]{2,1,0:T(8,128)(2,1)S(1)}, bf16[16,128,128]{2,1,0:T(8,128)(2,1)S(1)}, u32[]{:S(2)}, u32[]{:S(2)}) %collective-permute-start.1) | collective-permute-done | bytes 524320 | tf_op jit(solution)/shard_map/ppermute | solution.py:413
  35.5 0.4 collective-permute-start.2
  35.9 0.0 collective-permute-start.6
  35.9 2.2 %collective-permute-done.refs_1_ = bf16[16,128,128]{2,1,0:T(8,128)(2,1)S(1)} collective-permute-done((bf16[16,128,128]{2,1,0:T(8,128)(2,1)S(1)}, bf16[16,128,128]{2,1,0:T(8,128)(2,1)S(1)}, u32[]{:S(2)}, u32[]{:S(2)}) %collective-permute-start) | collective-permute-done | bytes 524320 | tf_op jit(solution)/shard_map/ppermute | solution.py:413
  38.2 0.6 collective-permute-start.3
  38.8 0.2 collective-permute-start.5
  39.0 3.6 %collective-permute-done.2.refs_3_ = bf16[8,128,128]{2,1,0:T(8,128)(2,1)S(1)} collective-permute-done((bf16[8,128,128]{2,1,0:T(8,128)(2,1)S(1)}, bf16[8,128,128]{2,1,0:T(8,128)(2,1)S(1)}, u32[]{:S(2)}, u32[]{:S(2)}) %collective-permute-start.2) | collective-permute-done | bytes 262176 | tf_op jit(solution)/shard_map/ppermute | solution.py:413
  42.6 0.0 collective-permute-start.7
  42.6 3.5 %collective-permute-done.3.refs_4_ = bf16[8,128,128]{2,1,0:T(8,128)(2,1)} collective-permute-done((bf16[8,128,128]{2,1,0:T(8,128)(2,1)S(1)}, bf16[8,128,128]{2,1,0:T(8,128)(2,1)}, u32[]{:S(2)}, u32[]{:S(2)}) %collective-permute-start.3) | collective-permute-done | bytes 262176 | tf_op jit(solution)/shard_map/ppermute | solution.py:413
  46.0 0.0 collective-permute-start.8
  46.0 0.0 collective-permute-done.4.refs_5_
  46.0 1.5 %all-to-all-done.1.qpay = bf16[16,272,128]{2,1,0:T(8,128)(2,1)S(1)} async-done(((bf16[16,272,128]{2,1,0:T(8,128)(2,1)}), bf16[16,272,128]{2,1,0:T(8,128)(2,1)S(1)}, u32[]{:S(2)}, u32[]{:S(2)}) %all-to-all-start.1) | async-done | bytes 1114144 | tf_op jit(solution)/shard_map/all_to_all | solution.py:405
  47.6 0.0 collective-permute-done.7.refs_8_
  47.6 0.0 collective-permute-done.6.refs_7_
  47.6 0.3 collective-permute-done.8.refs_9_
  47.9 0.0 collective-permute-done.5.refs_6_
  47.9 27.1 %shard_map.96 = (bf16[16,128,128]{2,1,0:T(8,128)(2,1)S(1)}, bf16[16,128,128]{2,1,0:T(8,128)(2,1)S(1)}, bf16[16,128,128]{2,1,0:T(8,128)(2,1)S(1)}, bf16[16,128,12...) custom-call(s32[32]{0:T(128)S(1)} %copy-done.5, ...), custom_call_target="tpu_custom_call" | custom-call | tf_op jit(solution)/shard_map/pallas_call | solution.py:441
  75.0 0.2 collective-permute-start.12
  75.3 0.4 collective-permute-start.10
  75.6 0.1 collective-permute-start.11
  75.8 1.3 collective-permute-done.12.got
  77.0 0.1 shard_map.97
  77.1 12.1 %collective-permute-start.13 = (bf16[8,128,128]{2,1,0:T(8,128)(2,1)S(1)}, bf16[8,128,128]{2,1,0:T(8,128)(2,1)S(1)}, u32[]{:S(2)}, u32[]{:S(2)}) collective-permute-start(bf16[8,128,128]{2,1,0:T(8,128)(2,1)S(1)} %get-tuple-element.34), channel_id=1, source_target_pairs={{0,1},{1,0},{2,3},{3,2},{4,5},{5,4},{6,7},{7,6},{8,9},{9,8},{10,11... | collective-permute-start | bytes 786440 | tf_op jit(solution)/shard_map/ppermute | solution.py:413
  89.2 0.0 collective-permute-start.14
  89.2 0.0 collective-permute-start.9
  89.2 0.0 collective-permute-done.10.got_1
  89.2 0.0 collective-permute-done.11.got_3
  89.2 6.6 %collective-permute-done.13.from_1 = bf16[8,128,128]{2,1,0:T(8,128)(2,1)S(1)} collective-permute-done((bf16[8,128,128]{2,1,0:T(8,128)(2,1)S(1)}, bf16[8,128,128]{2,1,0:T(8,128)(2,1)S(1)}, u32[]{:S(2)}, u32[]{:S(2)}) %collective-permute-start.13) | collective-permute-done | bytes 262176 | tf_op jit(solution)/shard_map/ppermute | solution.py:413
  95.8 2.7 %collective-permute-done.14.from_3 = bf16[8,128,128]{2,1,0:T(8,128)(2,1)S(1)} collective-permute-done((bf16[8,128,128]{2,1,0:T(8,128)(2,1)S(1)}, bf16[8,128,128]{2,1,0:T(8,128)(2,1)S(1)}, u32[]{:S(2)}, u32[]{:S(2)}) %collective-permute-start.14) | collective-permute-done | bytes 262176 | tf_op jit(solution)/shard_map/ppermute | solution.py:413
  98.5 0.3 shard_map.98
  98.8 0.1 collective-permute-start.15
  98.9 0.4 collective-permute-start.16
  99.3 14.1 %all_to_all.21.dq = bf16[16,128,128]{2,1,0:T(8,128)(2,1)S(1)} all-to-all(bf16[16,128,128]{2,1,0:T(8,128)(2,1)S(1)} %get-tuple-element.38), channel_id=1, replica_groups=mesh['z'=4,'core'=2,'xh'=2,'xl'=2,'y'=4] {'xh','xl','z'}, dimensions={0} | all-to-all | bytes 1048576 | tf_op jit(solution)/shard_map/all_to_all | solution.py:405
  113.4 0.0 collective-permute-done.9.got
  113.4 0.0 collective-permute-done.15.near_1
  113.4 0.0 collective-permute-done.16.near_3
  113.4 0.9 shard_map.99
  114.3 13.3 %all_to_all.22.got = bf16[16,128,128]{2,1,0:T(8,128)(2,1)S(1)} all-to-all(bf16[16,128,128]{2,1,0:T(8,128)(2,1)S(1)} %get-tuple-element.40), channel_id=1, replica_groups=mesh['z'=4,'core'=2,'xh'=2,'xl'=2,'y'=4] {'xh','xl','z'}, dimensions={0} | all-to-all | bytes 1048576 | tf_op jit(solution)/shard_map/all_to_all | solution.py:405
  127.6 0.8 shard_map.100
  (12 shorter events, 0.1 us)
Async XLA Ops:
  0.6 24.5 %copy-start.4 = (s32[8192]{0:T(1024)S(1)}, s32[8192]{0:T(1024)}, u32[]{:S(2)}) copy-start(s32[8192]{0:T(1024)} %param.12) | copy-start | bytes 98308
  0.6 24.5 %copy-start.3 = (bf16[64,4096]{1,0:T(8,128)(2,1)S(1)}, bf16[64,4096]{1,0:T(8,128)(2,1)}, u32[]{:S(2)}) copy-start(bf16[64,4096]{1,0:T(8,128)(2,1)} %grads.1) | copy-start | bytes 1572868
  0.7 24.5 %copy-start.2 = (bf16[64,4096]{1,0:T(8,128)(2,1)S(1)}, bf16[64,4096]{1,0:T(8,128)(2,1)}, u32[]{:S(2)}) copy-start(bf16[64,4096]{1,0:T(8,128)(2,1)} %saved.1) | copy-start | bytes 1572868
  0.7 24.5 %copy-start.1 = (bf16[64,4096]{1,0:T(8,128)(2,1)S(1)}, bf16[64,4096]{1,0:T(8,128)(2,1)}, u32[]{:S(2)}) copy-start(bf16[64,4096]{1,0:T(8,128)(2,1)} %queries.1) | copy-start | bytes 1572868
  22.0 13.5 %collective-permute-start.1 = (bf16[16,128,128]{2,1,0:T(8,128)(2,1)S(1)}, bf16[16,128,128]{2,1,0:T(8,128)(2,1)S(1)}, u32[]{:S(2)}, u32[]{:S(2)}) collective-permute-start(bf16[16,128,128]{2,1,0:T(8,128)(2,1)S(1)} %all_to_all.20.after.refs_0_), channel_id=1, source_target_pairs={{0,3},{1,2},{2,1},{3,0},{4,7},{5,6},{6,5},{7,4},{8,11},{9,10},{10,... | collective-permute-start | bytes 1572872 | tf_op jit(solution)/shard_map/ppermute | solution.py:413
  25.0 13.1 %collective-permute-start = (bf16[16,128,128]{2,1,0:T(8,128)(2,1)S(1)}, bf16[16,128,128]{2,1,0:T(8,128)(2,1)S(1)}, u32[]{:S(2)}, u32[]{:S(2)}) collective-permute-start(bf16[16,128,128]{2,1,0:T(8,128)(2,1)S(1)} %all_to_all.20.after.refs_0_), channel_id=1, source_target_pairs={{0,1},{1,0},{2,3},{3,2},{4,5},{5,4},{6,7},{7,6},{8,9},{9,8},{10,11... | collective-permute-start | bytes 1572872 | tf_op jit(solution)/shard_map/ppermute | solution.py:413
  26.4 1.0 copy-start
  27.5 20.4 %copy-start.5 = (s32[32]{0:T(128)S(1)}, s32[32]{0:T(128)}, u32[]{:S(2)}) copy-start(s32[32]{0:T(128)} %order.1) | copy-start | bytes 388
  27.5 20.1 %all-to-all-start.1 = ((bf16[16,272,128]{2,1,0:T(8,128)(2,1)}), bf16[16,272,128]{2,1,0:T(8,128)(2,1)S(1)}, u32[]{:S(2)}, u32[]{:S(2)}) async-start(bf16[16,272,128]{2,1,0:T(8,128)(2,1)} %copy-done), calls=%async_computation.1 | async-start | bytes 2228224 | tf_op jit(solution)/shard_map/all_to_all | solution.py:405
  31.3 14.7 %collective-permute-start.4 = (bf16[16,128,128]{2,1,0:T(8,128)(2,1)S(1)}, bf16[16,128,128]{2,1,0:T(8,128)(2,1)S(1)}, u32[]{:S(2)}, u32[]{:S(2)}) collective-permute-start(bf16[16,128,128]{2,1,0:T(8,128)(2,1)S(1)} %all_to_all.20.after.refs_0_), channel_id=1, source_target_pairs={{0,16},{16,0},{1,17},{17,1},{2,18},{18,2},{3,19},{19,3},{4,20},{20... | collective-permute-start | bytes 1572872 | tf_op jit(solution)/shard_map/ppermute | solution.py:409
  35.5 7.1 %collective-permute-start.2 = (bf16[8,128,128]{2,1,0:T(8,128)(2,1)S(1)}, bf16[8,128,128]{2,1,0:T(8,128)(2,1)S(1)}, u32[]{:S(2)}, u32[]{:S(2)}) collective-permute-start(bf16[8,128,128]{2,1,0:T(8,128)(2,1)S(1)} %slice.8), channel_id=1, source_target_pairs={{0,1},{1,0},{2,3},{3,2},{4,5},{5,4},{6,7},{7,6},{8,9},{9,8},{10,11... | collective-permute-start | bytes 786440 | tf_op jit(solution)/shard_map/ppermute | solution.py:413
  35.9 11.7 %collective-permute-start.6 = (bf16[16,128,128]{2,1,0:T(8,128)(2,1)S(1)}, bf16[16,128,128]{2,1,0:T(8,128)(2,1)}, u32[]{:S(2)}, u32[]{:S(2)}) collective-permute-start(bf16[16,128,128]{2,1,0:T(8,128)(2,1)S(1)} %collective-permute-done.1.refs_2_), channel_id=1, source_target_pairs={{0,16},{16,0},{1,17},{17,1},{2,18},{18,2},{3,19},{19,3},{4,20},{20... | collective-permute-start | bytes 1572872 | tf_op jit(solution)/shard_map/ppermute | solution.py:409
  38.2 7.9 %collective-permute-start.3 = (bf16[8,128,128]{2,1,0:T(8,128)(2,1)S(1)}, bf16[8,128,128]{2,1,0:T(8,128)(2,1)}, u32[]{:S(2)}, u32[]{:S(2)}) collective-permute-start(bf16[8,128,128]{2,1,0:T(8,128)(2,1)S(1)} %slice.9), channel_id=1, source_target_pairs={{0,3},{1,2},{2,1},{3,0},{4,7},{5,6},{6,5},{7,4},{8,11},{9,10},{10,... | collective-permute-start | bytes 786440 | tf_op jit(solution)/shard_map/ppermute | solution.py:413
  38.8 9.2 %collective-permute-start.5 = (bf16[16,128,128]{2,1,0:T(8,128)(2,1)S(1)}, bf16[16,128,128]{2,1,0:T(8,128)(2,1)}, u32[]{:S(2)}, u32[]{:S(2)}) collective-permute-start(bf16[16,128,128]{2,1,0:T(8,128)(2,1)S(1)} %collective-permute-done.refs_1_), channel_id=1, source_target_pairs={{0,16},{16,0},{1,17},{17,1},{2,18},{18,2},{3,19},{19,3},{4,20},{20... | collective-permute-start | bytes 1572872 | tf_op jit(solution)/shard_map/ppermute | solution.py:409
  42.6 5.0 %collective-permute-start.7 = (bf16[8,128,128]{2,1,0:T(8,128)(2,1)S(1)}, bf16[8,128,128]{2,1,0:T(8,128)(2,1)}, u32[]{:S(2)}, u32[]{:S(2)}) collective-permute-start(bf16[8,128,128]{2,1,0:T(8,128)(2,1)S(1)} %collective-permute-done.2.refs_3_), channel_id=1, source_target_pairs={{0,16},{16,0},{1,17},{17,1},{2,18},{18,2},{3,19},{19,3},{4,20},{20... | collective-permute-start | bytes 786440 | tf_op jit(solution)/shard_map/ppermute | solution.py:409
  46.0 1.9 %collective-permute-start.8 = (bf16[8,128,128]{2,1,0:T(8,128)(2,1)}, bf16[8,128,128]{2,1,0:T(8,128)(2,1)}, u32[]{:S(2)}, u32[]{:S(2)}) collective-permute-start(bf16[8,128,128]{2,1,0:T(8,128)(2,1)} %collective-permute-done.3.refs_4_), channel_id=1, source_target_pairs={{0,16},{16,0},{1,17},{17,1},{2,18},{18,2},{3,19},{19,3},{4,20},{20... | collective-permute-start | bytes 786440 | tf_op jit(solution)/shard_map/ppermute | solution.py:409
  75.0 2.0 %collective-permute-start.12 = (bf16[16,128,128]{2,1,0:T(8,128)(2,1)S(1)}, bf16[16,128,128]{2,1,0:T(8,128)(2,1)S(1)}, u32[]{:S(2)}, u32[]{:S(2)}) collective-permute-start(bf16[16,128,128]{2,1,0:T(8,128)(2,1)S(1)} %get-tuple-element.33), channel_id=1, source_target_pairs={{0,16},{16,0},{1,17},{17,1},{2,18},{18,2},{3,19},{19,3},{4,20},{20... | collective-permute-start | bytes 1572872 | tf_op jit(solution)/shard_map/ppermute | solution.py:409
  75.3 14.0 %collective-permute-start.10 = (bf16[16,128,128]{2,1,0:T(8,128)(2,1)S(1)}, bf16[16,128,128]{2,1,0:T(8,128)(2,1)S(1)}, u32[]{:S(2)}, u32[]{:S(2)}) collective-permute-start(bf16[16,128,128]{2,1,0:T(8,128)(2,1)S(1)} %get-tuple-element.28), channel_id=1, source_target_pairs={{0,16},{16,0},{1,17},{17,1},{2,18},{18,2},{3,19},{19,3},{4,20},{20... | collective-permute-start | bytes 1572872 | tf_op jit(solution)/shard_map/ppermute | solution.py:409
  75.6 13.6 %collective-permute-start.11 = (bf16[16,128,128]{2,1,0:T(8,128)(2,1)S(1)}, bf16[16,128,128]{2,1,0:T(8,128)(2,1)S(1)}, u32[]{:S(2)}, u32[]{:S(2)}) collective-permute-start(bf16[16,128,128]{2,1,0:T(8,128)(2,1)S(1)} %get-tuple-element.30), channel_id=1, source_target_pairs={{0,16},{16,0},{1,17},{17,1},{2,18},{18,2},{3,19},{19,3},{4,20},{20... | collective-permute-start | bytes 1572872 | tf_op jit(solution)/shard_map/ppermute | solution.py:409
  77.1 18.7 %collective-permute-start.13 = (bf16[8,128,128]{2,1,0:T(8,128)(2,1)S(1)}, bf16[8,128,128]{2,1,0:T(8,128)(2,1)S(1)}, u32[]{:S(2)}, u32[]{:S(2)}) collective-permute-start(bf16[8,128,128]{2,1,0:T(8,128)(2,1)S(1)} %get-tuple-element.34), channel_id=1, source_target_pairs={{0,1},{1,0},{2,3},{3,2},{4,5},{5,4},{6,7},{7,6},{8,9},{9,8},{10,11... | collective-permute-start | bytes 786440 | tf_op jit(solution)/shard_map/ppermute | solution.py:413
  89.2 9.3 %collective-permute-start.14 = (bf16[8,128,128]{2,1,0:T(8,128)(2,1)S(1)}, bf16[8,128,128]{2,1,0:T(8,128)(2,1)S(1)}, u32[]{:S(2)}, u32[]{:S(2)}) collective-permute-start(bf16[8,128,128]{2,1,0:T(8,128)(2,1)S(1)} %get-tuple-element.35), channel_id=1, source_target_pairs={{0,3},{1,2},{2,1},{3,0},{4,7},{5,6},{6,5},{7,4},{8,11},{9,10},{10,... | collective-permute-start | bytes 786440 | tf_op jit(solution)/shard_map/ppermute | solution.py:413
  89.2 24.1 %collective-permute-start.9 = (bf16[16,128,128]{2,1,0:T(8,128)(2,1)S(1)}, bf16[16,128,128]{2,1,0:T(8,128)(2,1)S(1)}, u32[]{:S(2)}, u32[]{:S(2)}) collective-permute-start(bf16[16,128,128]{2,1,0:T(8,128)(2,1)S(1)} %get-tuple-element.26), channel_id=1, source_target_pairs={{0,16},{16,0},{1,17},{17,1},{2,18},{18,2},{3,19},{19,3},{4,20},{20... | collective-permute-start | bytes 1572872 | tf_op jit(solution)/shard_map/ppermute | solution.py:409
  98.8 14.6 %collective-permute-start.15 = (bf16[16,128,128]{2,1,0:T(8,128)(2,1)S(1)}, bf16[16,128,128]{2,1,0:T(8,128)(2,1)S(1)}, u32[]{:S(2)}, u32[]{:S(2)}) collective-permute-start(bf16[16,128,128]{2,1,0:T(8,128)(2,1)S(1)} %get-tuple-element.36), channel_id=1, source_target_pairs={{0,1},{1,0},{2,3},{3,2},{4,5},{5,4},{6,7},{7,6},{8,9},{9,8},{10,11... | collective-permute-start | bytes 1572872 | tf_op jit(solution)/shard_map/ppermute | solution.py:413
  98.9 14.5 %collective-permute-start.16 = (bf16[16,128,128]{2,1,0:T(8,128)(2,1)S(1)}, bf16[16,128,128]{2,1,0:T(8,128)(2,1)S(1)}, u32[]{:S(2)}, u32[]{:S(2)}) collective-permute-start(bf16[16,128,128]{2,1,0:T(8,128)(2,1)S(1)} %get-tuple-element.37), channel_id=1, source_target_pairs={{0,3},{1,2},{2,1},{3,0},{4,7},{5,6},{6,5},{7,4},{8,11},{9,10},{10,... | collective-permute-start | bytes 1572872 | tf_op jit(solution)/shard_map/ppermute | solution.py:413
